TPU v7x, 128 devices: a whole 4x4x4 slice. The times are simulated.
128 devices in a mesh: expert: 32 (over x, y, core), tensor: 4 (over z).
Axes of the slice: x: 4, y: 4, z: 4, core: 2. Of those that a mesh axis runs over, the one named last changes fastest.
Arguments:
- hidden_in: bfloat16 [768, 7168], P('expert', 'tensor'), may hold values from -6 to 6
- norm_gain: float32 [2, 7168], P(None, 'tensor'), may hold values from 0.25 to 1.75
- router: float32 [2, 7168, 32], P(None, 'tensor'), may hold values from -0.0625 to 0.0625
- w_gate: bfloat16 [2, 32, 7168, 1024], P(None, 'expert', None, 'tensor'), may hold values from -0.0625 to 0.0625
- w_up: bfloat16 [2, 32, 7168, 1024], P(None, 'expert', None, 'tensor'), may hold values from -0.0625 to 0.0625
- w_down: bfloat16 [2, 32, 1024, 7168], P(None, 'expert', 'tensor'), may hold values from -0.1875 to 0.1875
- routes: int32 [2, 768, 8], P(None, 'expert'), may hold values from 0 to 31, all different within a row; in each aligned block of 24 rows (0 to 23, 24 to 47, ..., all dimensions but the last counted through in order) at most 12 rows name the same one
Outputs:
- hidden_out: bfloat16 [768, 7168], P('expert', 'tensor')
Inputs may be any that keep to these rules, and one draw needn't show every extreme that they name: `routes`: each token names 8 different experts in each layer. Among the 24 tokens of one index of expert (aligned blocks of rows of one layer), no expert is named by more than 12 tokens, a bound that some block reaches.
All inputs are finite; a program needn't handle non-finite values.
Results may differ from a plain program's by a relative error of at most 0.018.
Values may be sent and summed in bfloat16 or wider, within the bound.
No kernel may reach another device: no remote copies, remote signals or barrier semaphores. Data moves between devices by JAX's collectives and lax.ppermute only.
A program may use at most 128 MiB of HBM per device.

v0:
```python
import jax
import jax.numpy as jnp
from jax import lax
from jax.sharding import PartitionSpec as P

TOP = 8


route_scale = 2.5


def moe_layer(state, gain, router, gate_proj, up_proj, down_proj, chosen):
    token_rows = state.shape[0]
    expert_count = router.shape[1]
    tensor_count = lax.axis_size("tensor")
    full_width = state.shape[1] * tensor_count
    capacity = min(token_rows, 2 * token_rows * TOP // lax.axis_size("expert"))
    slot_total = expert_count * capacity
    values = state.astype(jnp.float32)
    square_sum = lax.psum(jnp.sum(values * values, axis=1), "tensor")
    normed = (values * lax.rsqrt(square_sum / full_width + 1e-06)[:, None] * gain[None, :]).astype(
        jnp.bfloat16
    )
    partial_scores = jnp.dot(normed.astype(jnp.float32), router, precision=lax.Precision.HIGHEST)
    scores = lax.psum(partial_scores, "tensor")
    probs = jax.nn.sigmoid(scores)
    expert_iota = lax.broadcasted_iota(jnp.int32, (1, 1, expert_count), 2)
    picks = chosen[:, :, None] == expert_iota
    picked_probs = jnp.sum(jnp.where(picks, probs[:, None, :], 0.0), axis=2)
    weights = route_scale * picked_probs / jnp.sum(picked_probs, axis=1, keepdims=True)
    flat_picks = picks.reshape(token_rows * TOP, expert_count).astype(jnp.int32)
    ranks = jnp.cumsum(flat_picks, axis=0) - flat_picks
    rank_each = jnp.sum(ranks * flat_picks, axis=1).reshape(token_rows, TOP)
    position = chosen * capacity + rank_each
    slot_iota = lax.broadcasted_iota(jnp.int32, (slot_total, 1, 1), 0)
    dispatch = jnp.any(slot_iota == position[None, :, :], axis=2).astype(jnp.bfloat16)
    full_rows = lax.all_gather(normed, "tensor", axis=1, tiled=True)
    outgoing = jnp.dot(dispatch, full_rows, preferred_element_type=jnp.float32).astype(jnp.bfloat16)
    arrived = lax.all_to_all(outgoing, "expert", split_axis=0, concat_axis=0, tiled=True)
    gate = jnp.dot(arrived, gate_proj, preferred_element_type=jnp.float32)
    up = jnp.dot(arrived, up_proj, preferred_element_type=jnp.float32)
    act = (jax.nn.silu(gate) * up).astype(jnp.bfloat16)
    terms = jnp.dot(act, down_proj, preferred_element_type=jnp.float32)
    expert_out = lax.psum_scatter(
        terms.astype(jnp.bfloat16), "tensor", scatter_dimension=1, tiled=True
    )
    returned = lax.all_to_all(expert_out, "expert", split_axis=0, concat_axis=0, tiled=True)
    select_iota = lax.broadcasted_iota(jnp.int32, (1, 1, slot_total), 2)
    selector = (position[:, :, None] == select_iota).astype(jnp.bfloat16)
    picked_rows = jnp.einsum("rks,sd->rkd", selector, returned, preferred_element_type=jnp.float32)
    mixed = jnp.sum(weights[:, :, None] * picked_rows, axis=1)
    return (values + mixed).astype(jnp.bfloat16)


def body(hidden_in, norm_gain, router, w_gate, w_up, w_down, routes):
    state = hidden_in
    for layer in range(norm_gain.shape[0]):
        state = moe_layer(
            state,
            norm_gain[layer],
            router[layer],
            w_gate[layer, 0],
            w_up[layer, 0],
            w_down[layer, 0],
            routes[layer],
        )
    return state


def solution(mesh):
    placed = (
        P("expert", "tensor"),
        P(None, "tensor"),
        P(None, "tensor", None),
        P(None, "expert", None, "tensor"),
        P(None, "expert", None, "tensor"),
        P(None, "expert", "tensor", None),
        P(None, "expert", None),
    )
    return jax.shard_map(
        body, mesh=mesh, in_specs=placed, out_specs=P("expert", "tensor"), check_vma=False
    )
```

profile of v0, /device:TPU:1, one launch (start us, length us, event | category | flops | bytes accessed | tf_op | source)
XLA Modules:
  0.0 497.0 jit_solution(4682133663514458187)
XLA Ops:
  7.6 10.6 %psum.28 = f32[24]{0:T(128)S(1)} all-reduce(f32[24]{0:T(128)S(1)} %fusion.38), channel_id=1, replica_groups=mesh['expert'=32,'tensor'=4] {'tensor'}, use_global_device_ids=true, to_apply=%region_1.0 | all-reduce | flops 24 | bytes 192 | tf_op jit(solution)/shard_map/psum | solution.py:20
  22.1 10.3 %all_gather.6 = bf16[24,7168]{1,0:T(8,128)(2,1)S(1)} all-gather(bf16[24,1792]{1,0:T(8,128)(2,1)S(1)} %fusion.40), channel_id=1, replica_groups=mesh['expert'=32,'tensor'=4] {'tensor'}, dimensions={1}, use_global_device_ids=true | all-gather | bytes 430080 | tf_op jit(solution)/shard_map/all_gather | solution.py:37
  32.3 4.0 convolution_convert_fusion.3
  36.3 8.0 %all_to_all.32 = bf16[32,12,7168]{2,1,0:T(8,128)(2,1)} reshape(bf16[384,7168]{1,0:T(8,128)(2,1)} %convolution_convert_fusion.3) | data formatting | bytes 11010048 | tf_op jit(solution)/shard_map/all_to_all | solution.py:39
  44.4 96.4 %all_to_all.48 = bf16[32,12,7168]{2,1,0:T(8,128)(2,1)} all-to-all(bf16[32,12,7168]{2,1,0:T(8,128)(2,1)} %all_to_all.32), channel_id=1, replica_groups=mesh['expert'=32,'tensor'=4] {'expert'}, dimensions={0} | all-to-all | bytes 11010048 | tf_op jit(solution)/shard_map/all_to_all | solution.py:39
  140.7 8.2 %all_to_all.34 = bf16[384,7168]{1,0:T(8,128)(2,1)} reshape(bf16[32,12,7168]{2,1,0:T(8,128)(2,1)} %all_to_all.48) | data formatting | bytes 11010048 | tf_op jit(solution)/shard_map/all_to_all | solution.py:39
  149.0 5.4 %fusion.8 = f32[384,256]{1,0:T(8,128)S(1)} fusion(bf16[384,7168]{1,0:T(8,128)(2,1)} %all_to_all.34, bf16[2,1,7168,256]{3,2,1,0:T(8,128)(2,1)} %param.10), kind=kOutput, calls=%fused_computation.12 | convolution fusion | flops 1409286144 | bytes 9568256 | tf_op jit(solution)/shard_map/dot_general | solution.py:40
  158.2 4.0 convolution_convert_fusion.2
  163.6 52.7 %reduce-scatter.3.cloned.1.call-done = bf16[384,1792]{1,0:T(8,128)(2,1)} async-done(((bf16[384,7168]{1,0:T(8,128)(2,1)}), bf16[384,1792]{1,0:T(8,128)(2,1)}) %reduce-scatter.3.cloned.1.call-update) | async-done | bytes 1376272 | tf_op jit(solution)/shard_map/reduce_scatter | solution.py:44
  219.5 7.6 %all-to-all-start.1 = ((bf16[32,12,1792]{2,1,0:T(8,128)(2,1)}), bf16[32,12,1792]{2,1,0:T(8,128)(2,1)S(1)}, u32[]{:S(2)}, u32[]{:S(2)}) async-start(bf16[32,12,1792]{2,1,0:T(8,128)(2,1)} %all_to_all.35), calls=%async_computation.2 | async-start | bytes 3670016 | tf_op jit(solution)/shard_map/all_to_all | solution.py:47
  227.5 12.3 %psum.29 = f32[24,32]{1,0:T(8,128)S(1)} all-reduce(f32[24,32]{1,0:T(8,128)S(1)} %fusion.34), channel_id=1, replica_groups=mesh['expert'=32,'tensor'=4] {'tensor'}, use_global_device_ids=true, to_apply=%region_2.0 | all-reduce | flops 768 | bytes 6144 | tf_op jit(solution)/shard_map/psum | solution.py:25
  240.4 12.2 %all-to-all-done.1 = bf16[32,12,1792]{2,1,0:T(8,128)(2,1)S(1)} async-done(((bf16[32,12,1792]{2,1,0:T(8,128)(2,1)}), bf16[32,12,1792]{2,1,0:T(8,128)(2,1)S(1)}, u32[]{:S(2)}, u32[]{:S(2)}) %all-to-all-start.1) | async-done | bytes 1376288 | tf_op jit(solution)/shard_map/all_to_all | solution.py:47
  253.8 6.5 %psum.30 = f32[24]{0:T(128)S(1)} all-reduce(f32[24]{0:T(128)S(1)} %get-tuple-element.11), channel_id=1, replica_groups=mesh['expert'=32,'tensor'=4] {'tensor'}, use_global_device_ids=true, to_apply=%region_12.13 | all-reduce | flops 24 | bytes 192 | tf_op jit(solution)/shard_map/psum | solution.py:20
  260.4 10.0 %all_gather.7 = bf16[24,7168]{1,0:T(8,128)(2,1)S(1)} all-gather(bf16[24,1792]{1,0:T(8,128)(2,1)S(1)} %fusion.44), channel_id=1, replica_groups=mesh['expert'=32,'tensor'=4] {'tensor'}, dimensions={1}, use_global_device_ids=true | all-gather | bytes 430080 | tf_op jit(solution)/shard_map/all_gather | solution.py:37
  270.4 4.0 convolution_convert_fusion.1
  274.4 8.0 %all_to_all.38 = bf16[32,12,7168]{2,1,0:T(8,128)(2,1)} reshape(bf16[384,7168]{1,0:T(8,128)(2,1)} %convolution_convert_fusion.1) | data formatting | bytes 11010048 | tf_op jit(solution)/shard_map/all_to_all | solution.py:39
  282.5 94.3 %all_to_all.49 = bf16[32,12,7168]{2,1,0:T(8,128)(2,1)} all-to-all(bf16[32,12,7168]{2,1,0:T(8,128)(2,1)} %all_to_all.38), channel_id=1, replica_groups=mesh['expert'=32,'tensor'=4] {'expert'}, dimensions={0} | all-to-all | bytes 11010048 | tf_op jit(solution)/shard_map/all_to_all | solution.py:39
  376.8 8.2 %all_to_all.40 = bf16[384,7168]{1,0:T(8,128)(2,1)} reshape(bf16[32,12,7168]{2,1,0:T(8,128)(2,1)} %all_to_all.49) | data formatting | bytes 11010048 | tf_op jit(solution)/shard_map/all_to_all | solution.py:39
  385.0 5.4 %fusion.3 = f32[384,256]{1,0:T(8,128)S(1)} fusion(bf16[384,7168]{1,0:T(8,128)(2,1)} %all_to_all.40, bf16[2,1,7168,256]{3,2,1,0:T(8,128)(2,1)} %param.10), kind=kOutput, calls=%fused_computation.7 | convolution fusion | flops 1409286144 | bytes 9568256 | tf_op jit(solution)/shard_map/dot_general | solution.py:40
  394.3 4.0 convolution_convert_fusion
  398.3 53.9 %reduce-scatter.5.cloned.1.call-done = bf16[384,1792]{1,0:T(8,128)(2,1)} async-done(((bf16[384,7168]{1,0:T(8,128)(2,1)}), bf16[384,1792]{1,0:T(8,128)(2,1)}) %reduce-scatter.5.cloned.1.call-update) | async-done | bytes 1376272 | tf_op jit(solution)/shard_map/reduce_scatter | solution.py:44
  455.5 7.5 %all-to-all-start.3 = ((bf16[32,12,1792]{2,1,0:T(8,128)(2,1)}), bf16[32,12,1792]{2,1,0:T(8,128)(2,1)S(1)}, u32[]{:S(2)}, u32[]{:S(2)}) async-start(bf16[32,12,1792]{2,1,0:T(8,128)(2,1)} %all_to_all.41), calls=%async_computation.5 | async-start | bytes 3670016 | tf_op jit(solution)/shard_map/all_to_all | solution.py:47
  463.3 12.3 %psum.31 = f32[24,32]{1,0:T(8,128)S(1)} all-reduce(f32[24,32]{1,0:T(8,128)S(1)} %fusion.32), channel_id=1, replica_groups=mesh['expert'=32,'tensor'=4] {'tensor'}, use_global_device_ids=true, to_apply=%region_13.14 | all-reduce | flops 768 | bytes 6144 | tf_op jit(solution)/shard_map/psum | solution.py:25
  476.1 12.4 %all-to-all-done.3 = bf16[32,12,1792]{2,1,0:T(8,128)(2,1)S(1)} async-done(((bf16[32,12,1792]{2,1,0:T(8,128)(2,1)}), bf16[32,12,1792]{2,1,0:T(8,128)(2,1)S(1)}, u32[]{:S(2)}, u32[]{:S(2)}) %all-to-all-start.3) | async-done | bytes 1376288 | tf_op jit(solution)/shard_map/all_to_all | solution.py:47
  (79 shorter events, 24.9 us)
Async XLA Ops:
  6.5 209.7 %reduce-scatter.3.cloned.1.call-start = ((), (), s32[]{:S(2)}) async-start(), calls=%async_computation.6 | async-start | bytes 6881280 | tf_op jit(solution)/shard_map/reduce_scatter | solution.py:44
  149.0 5.4 %copy-start = (bf16[384,7168]{1,0:T(8,128)(2,1)S(1)}, bf16[384,7168]{1,0:T(8,128)(2,1)}, u32[]{:S(2)}) copy-start(bf16[384,7168]{1,0:T(8,128)(2,1)} %all_to_all.34) | copy-start | bytes 16515076
  149.0 9.2 %slice-start = ((s8[7340032]{0:T(1024)(128)(4,1)}), s8[4194304]{0:T(1024)(128)(4,1)S(1)}, s32[]{:S(2)}) async-start(s8[7340032]{0:T(1024)(128)(4,1)} %bitcast.78), calls=%async_computation.8 | async-start | bytes 8388608
  154.4 3.8 slice-start.1
  162.2 65.0 %copy-start.3 = (f32[2,1792,32]{1,2,0:T(8,128)S(1)}, f32[2,1792,32]{1,2,0:T(8,128)}, u32[]{:S(2)}) copy-start(f32[2,1792,32]{1,2,0:T(8,128)} %param.9) | copy-start | bytes 1376260
  219.5 34.1 %copy-start.2 = (bf16[24,1792]{1,0:T(8,128)(2,1)S(1)}, bf16[24,1792]{1,0:T(8,128)(2,1)}, u32[]{:S(2)}) copy-start(bf16[24,1792]{1,0:T(8,128)(2,1)} %param.7) | copy-start | bytes 258052
  219.5 33.1 %all-to-all-start.1 = ((bf16[32,12,1792]{2,1,0:T(8,128)(2,1)}), bf16[32,12,1792]{2,1,0:T(8,128)(2,1)S(1)}, u32[]{:S(2)}, u32[]{:S(2)}) async-start(bf16[32,12,1792]{2,1,0:T(8,128)(2,1)} %all_to_all.35), calls=%async_computation.2 | async-start | bytes 3670016 | tf_op jit(solution)/shard_map/all_to_all | solution.py:47
  227.2 225.1 %reduce-scatter.5.cloned.1.call-start = ((), (), s32[]{:S(2)}) async-start(), calls=%async_computation.7 | async-start | bytes 6881280 | tf_op jit(solution)/shard_map/reduce_scatter | solution.py:44
  385.0 5.4 %copy-start.1 = (bf16[384,7168]{1,0:T(8,128)(2,1)S(1)}, bf16[384,7168]{1,0:T(8,128)(2,1)}, u32[]{:S(2)}) copy-start(bf16[384,7168]{1,0:T(8,128)(2,1)} %all_to_all.40) | copy-start | bytes 16515076
  385.0 9.2 %slice-start.2 = ((s8[7340032]{0:T(1024)(128)(4,1)}), s8[4194304]{0:T(1024)(128)(4,1)S(1)}, s32[]{:S(2)}) async-start(s8[7340032]{0:T(1024)(128)(4,1)} %bitcast.80), calls=%async_computation.10 | async-start | bytes 8388608
  390.4 3.8 slice-start.3
  398.3 64.8 %copy-start.4 = (f32[2,1792,32]{1,2,0:T(8,128)S(1)}, f32[2,1792,32]{1,2,0:T(8,128)}, u32[]{:S(2)}) copy-start(f32[2,1792,32]{1,2,0:T(8,128)} %param.9) | copy-start | bytes 1376260
  455.5 33.0 %all-to-all-start.3 = ((bf16[32,12,1792]{2,1,0:T(8,128)(2,1)}), bf16[32,12,1792]{2,1,0:T(8,128)(2,1)S(1)}, u32[]{:S(2)}, u32[]{:S(2)}) async-start(bf16[32,12,1792]{2,1,0:T(8,128)(2,1)} %all_to_all.41), calls=%async_computation.5 | async-start | bytes 3670016 | tf_op jit(solution)/shard_map/all_to_all | solution.py:47
Sparse Core Ops, SparseCore 0:
  162.4 53.7 reduce-scatter.2
  398.4 53.7 reduce-scatter.4
where the time goes:
time: 498 us; the launch traced here: 497 us
  blocking collectives  253 us (51%)
  waiting for transfers between devices  131 us (26%)
  local copies, waits for them, and re-layouts  42.5 us (9%)
  matrix products  36 us (7%)
  starting transfers between devices  15.1 us (3%)
  between operations  13.8 us (3%)
  other arithmetic  5.75 us (1%)
    all_to_all x2, blocking collectives, moe_layer(): lax.all_to_all(outgoing, 'expert', split_axis=0, concat_axis=0, tiled=True)  191 us
    reduce_scatter x2, waiting for transfers between devices, moe_layer(): lax.psum_scatter(terms.astype(jnp.bfloat16), 'tensor', scatter_dimension=...  107 us
    all_to_all x4, local copies, waits for them, and re-layouts, moe_layer(): lax.all_to_all(outgoing, 'expert', split_axis=0, concat_axis=0, tiled=True)  32.6 us
    all_to_all x2, waiting for transfers between devices, moe_layer(): lax.all_to_all(expert_out, 'expert', split_axis=0, concat_axis=0, tiled=T...  24.6 us
    psum x2, blocking collectives, moe_layer(): scores = lax.psum(partial_scores, 'tensor')  24.6 us
    all_gather x2, blocking collectives, moe_layer(): full_rows = lax.all_gather(normed, 'tensor', axis=1, tiled=True)  20.3 us
    psum x2, blocking collectives, moe_layer(): square_sum = lax.psum(jnp.sum(values * values, axis=1), 'tensor')  17.1 us
    all_to_all x2, starting transfers between devices, moe_layer(): lax.all_to_all(expert_out, 'expert', split_axis=0, concat_axis=0, tiled=T...  15.1 us
  transfers between devices with their start and end apart: 4, of which 4 were waited for; matrix products, arithmetic and copies ran while one was open for 1% of the time, Pallas kernels for 0%

commit v1 on v0

v1 whole, which is shorter than its diff:
```python
import jax
import jax.numpy as jnp
from jax import lax
from jax.sharding import PartitionSpec as P

route_scale = 2.5
bf16, f32 = jnp.bfloat16, jnp.float32


def short(values):
    return lax.reduce_precision(values, 8, 7)


def thirds(values):
    high = short(values)
    middle = short(values - high)
    return [part.astype(bf16) for part in (high, middle, values - high - middle)]


def body(hidden_in, norm_gain, router, w_gate, w_up, w_down, routes):
    rows, part = hidden_in.shape
    layers, width, units = w_gate.shape[0], w_gate.shape[2], w_gate.shape[3]
    experts = router.shape[2]
    quarters = lax.axis_size("tensor")
    capacity = min(rows, 2 * rows * routes.shape[2] // experts)
    slots = experts * capacity
    me = lax.axis_index("expert")

    gains = jnp.stack(thirds(norm_gain), axis=0).reshape(3 * layers, part)
    opening = jnp.concatenate([hidden_in, gains, jnp.zeros((2, part), bf16)], axis=0)
    opening = lax.all_gather(opening, "tensor", axis=1, tiled=True)
    full = opening[:rows]
    gains = opening[rows : rows + 3 * layers].astype(f32).reshape(3, layers, width)
    gains = gains[0] + gains[1] + gains[2]

    state = hidden_in
    for layer in range(layers):
        down = w_down[layer, 0].reshape(units, quarters, part).transpose(1, 0, 2)
        down = lax.all_to_all(down, "tensor", split_axis=0, concat_axis=0)
        down = down.reshape(quarters * units, part)

        if layer:
            full = lax.all_gather(state, "tensor", axis=1, tiled=True)
        values = full.astype(f32)
        scale = lax.rsqrt(jnp.sum(values * values, axis=1) / width + 1e-06)
        normed = (values * scale[:, None] * gains[layer][None, :]).astype(bf16)

        chosen = routes[layer]
        expert_iota = lax.broadcasted_iota(jnp.int32, (1, 1, experts), 2)
        picks = jnp.any(chosen[:, :, None] == expert_iota, axis=1)
        earlier = lax.broadcasted_iota(jnp.int32, (rows, rows), 0) > lax.broadcasted_iota(
            jnp.int32, (rows, rows), 1
        )
        ranks = jnp.dot(earlier.astype(bf16), picks.astype(bf16), preferred_element_type=f32)
        marks = jnp.where(picks, ranks + 1.0, 0.0)
        marks_sent = jnp.pad(marks, ((0, 0), (0, 128 - experts))).astype(bf16)

        sent = jnp.concatenate([normed, marks_sent], axis=1)
        arrived = lax.all_gather(sent, "expert", axis=0, tiled=True)

        own = state.astype(f32) * scale[:, None] * norm_gain[layer][None, :]
        own = own.astype(bf16).astype(f32)
        scores = jnp.dot(own, router[layer], precision=lax.Precision.HIGHEST)
        probs = jax.nn.sigmoid(lax.psum(scores, "tensor"))
        picked = jnp.where(picks, probs, 0.0)
        weights = route_scale * picked / jnp.sum(picked, axis=1, keepdims=True)
        slot_iota = lax.broadcasted_iota(jnp.int32, (1, 1, capacity), 2).astype(f32) + 1.0
        mixer = jnp.where(marks[:, :, None] == slot_iota, weights[:, :, None], 0.0)
        mixer = mixer.reshape(rows, slots)
        mixer = jnp.concatenate(thirds(mixer)[:2], axis=0)

        tokens = arrived[:, :width]
        gate = jnp.dot(tokens, w_gate[layer, 0], preferred_element_type=f32)
        up = jnp.dot(tokens, w_up[layer, 0], preferred_element_type=f32)
        act = (jax.nn.silu(gate) * up).astype(bf16)
        mine = lax.broadcasted_iota(jnp.int32, (1, 128), 1) == me
        mark = jnp.sum(jnp.where(mine, arrived[:, width:].astype(f32), 0.0), axis=1)
        total = mark.shape[0]
        slot = lax.broadcasted_iota(jnp.int32, (slots, total), 0)
        token = lax.broadcasted_iota(jnp.int32, (slots, total), 1)
        inside = (slot // capacity) == (token // rows)
        taken = inside & ((slot % capacity + 1).astype(f32) == mark[None, :])
        act = jnp.dot(taken.astype(bf16), act, preferred_element_type=f32).astype(bf16)

        act = lax.all_gather(act, "tensor", axis=1, tiled=True)
        out = jnp.dot(act, down, preferred_element_type=f32).astype(bf16)
        returned = lax.all_to_all(
            out.reshape(experts, capacity, part), "expert", split_axis=0, concat_axis=0
        ).reshape(slots, part)
        mixed = jnp.dot(mixer, returned, preferred_element_type=f32)
        state = (state.astype(f32) + mixed[:rows] + mixed[rows:]).astype(bf16)
    return state


def solution(mesh):
    placed = (
        P("expert", "tensor"),
        P(None, "tensor"),
        P(None, "tensor", None),
        P(None, "expert", None, "tensor"),
        P(None, "expert", None, "tensor"),
        P(None, "expert", "tensor", None),
        P(None, "expert", None),
    )
    return jax.shard_map(
        body, mesh=mesh, in_specs=placed, out_specs=P("expert", "tensor"), check_vma=False
    )
```

time: 498 us -> 307 us (0.62)
  blocking collectives: 253 us -> 119 us
  waiting for transfers between devices: 131 us -> 63.8 us
  starting transfers between devices: 15.1 us -> 24.5 us
  local copies, waits for them, and re-layouts: 42.5 us -> 36.7 us
    all_to_all x2 -> x1, blocking collectives: 191 us -> 45 us  [body(): down = lax.all_to_all(down, 'tensor', split_axis=0, concat_axis=0)]
    reduce_scatter x2 -> x0, waiting for transfers between devices: 107 us -> none  [moe_layer(): lax.psum_scatter(terms.astype(jnp.bfloat16), 'tensor', scatter_dimension=...]
    all_to_all x2 -> x3, waiting for transfers between devices: 24.6 us -> 61.7 us  [the longest x1 40.9 us: body(): down = lax.all_to_all(down, 'tensor', split_axis=0, concat_axis=0)]
    all_to_all x8 -> x2, local copies, waits for them, and re-layouts: 39.9 us -> 12 us  [body(): down = lax.all_to_all(down, 'tensor', split_axis=0, concat_axis=0)]
    all_gather x2 -> x4, blocking collectives: 20.3 us -> 47.2 us  [the longest x2 24.4 us: body(): act = lax.all_gather(act, 'tensor', axis=1, tiled=True)]
    psum x4 -> x2, blocking collectives: 41.6 us -> 27.1 us  [body(): probs = jax.nn.sigmoid(lax.psum(scores, 'tensor'))]
    unnamed x20 -> x10, local copies, waits for them, and re-layouts: 0.19 us -> 11.9 us
    all_to_all x2 -> x3, starting transfers between devices: 15.1 us -> 24.4 us  [the longest x2 19.7 us: body(): lax.all_to_all(out.reshape(experts, capacity, part), 'expert', split_axis...]
  transfers between devices with their start and end apart: 4 -> 5, of which waited for: 4 -> 4; matrix products, arithmetic and copies ran while one was open for 1% -> 11% of each run, Pallas kernels for 0% -> 0%
where the time goes in v1:
time: 307 us; the launch traced here: 305 us
  blocking collectives  119 us (39%)
  waiting for transfers between devices  63.8 us (21%)
  matrix products  39.7 us (13%)
  local copies, waits for them, and re-layouts  36.7 us (12%)
  starting transfers between devices  24.5 us (8%)
  between operations  13.8 us (4%)
  other arithmetic  7.64 us (2%)
    all_to_all x1, blocking collectives, body(): down = lax.all_to_all(down, 'tensor', split_axis=0, concat_axis=0)  45 us
    all_to_all x1, waiting for transfers between devices, body(): down = lax.all_to_all(down, 'tensor', split_axis=0, concat_axis=0)  40.9 us
    psum x2, blocking collectives, body(): probs = jax.nn.sigmoid(lax.psum(scores, 'tensor'))  27.1 us
    all_gather x2, blocking collectives, body(): act = lax.all_gather(act, 'tensor', axis=1, tiled=True)  24.4 us
    all_to_all x2, waiting for transfers between devices, body(): lax.all_to_all(out.reshape(experts, capacity, part), 'expert', split_axis...  20.8 us
    all_to_all x2, starting transfers between devices, body(): lax.all_to_all(out.reshape(experts, capacity, part), 'expert', split_axis...  19.7 us
    dot_general x2, matrix products, body(): jnp.dot(taken.astype(bf16), act, preferred_element_type=f32).astype(bf16)  17.3 us
    dot_general x2, matrix products, body(): gate = jnp.dot(tokens, w_gate[layer, 0], preferred_element_type=f32)  13.8 us
  transfers between devices with their start and end apart: 5, of which 4 were waited for; matrix products, arithmetic and copies ran while one was open for 11% of the time, Pallas kernels for 0%

profile of v1, /device:TPU:1, one launch (start us, length us, event | category | flops | bytes accessed | tf_op | source)
XLA Modules:
  0.0 305.5 jit_solution(14205487868580988031)
XLA Ops:
  8.4 13.1 %all_gather.18 = bf16[32,7168]{1,0:T(8,128)(2,1)S(1)} all-gather(bf16[32,1792]{1,0:T(8,128)(2,1)S(1)} %maximum_maximum_fusion), channel_id=1, replica_groups=mesh['expert'=32,'tensor'=4] {'tensor'}, dimensions={1}, use_global_device_ids=true | all-gather | bytes 573440 | tf_op jit(solution)/shard_map/all_gather | solution.py:31
  23.8 6.6 %fusion.165 = (bf16[1,1,256,7168]{3,2,1,0:T(8,128)(2,1)}, bf16[1,1,256,7168]{3,2,1,0:T(8,128)(2,1)}) fusion(bf16[2,1,256,7168]{3,2,1,0:T(8,128)(2,1)} %param.12), kind=kLoop, calls=%fused_computation.182 | loop fusion | bytes 14680064 | tf_op jit(solution)/shard_map/slice | solution.py:38
  30.4 5.9 %copy.24 = bf16[1,1,256,7168]{2,3,1,0:T(8,128)(2,1)} copy(bf16[1,1,256,7168]{3,2,1,0:T(8,128)(2,1)} %get-tuple-element.8) | data formatting | bytes 7340032
  36.4 4.7 %all-to-all-start = ((bf16[4,256,1792]{1,2,0:T(8,128)(2,1)}), bf16[4,256,1792]{1,2,0:T(8,128)(2,1)}, u32[]{:S(2)}, u32[]{:S(2)}) async-start(bf16[4,256,1792]{1,2,0:T(8,128)(2,1)} %bitcast.62), calls=%async_computation | async-start | bytes 7340032 | tf_op jit(solution)/shard_map/all_to_all | solution.py:39
  41.2 40.9 %all-to-all-done = bf16[4,256,1792]{1,2,0:T(8,128)(2,1)} async-done(((bf16[4,256,1792]{1,2,0:T(8,128)(2,1)}), bf16[4,256,1792]{1,2,0:T(8,128)(2,1)}, u32[]{:S(2)}, u32[]{:S(2)}) %all-to-all-start) | async-done | bytes 3670048 | tf_op jit(solution)/shard_map/all_to_all | solution.py:39
  82.1 6.0 %copy.20 = bf16[4,256,1792]{2,1,0:T(8,128)(2,1)} copy(bf16[4,256,1792]{1,2,0:T(8,128)(2,1)} %all-to-all-done) | data formatting | bytes 7340032 | tf_op jit(solution)/shard_map/all_to_all | solution.py:39
  88.1 6.9 %fusion.6 = f32[768,256]{1,0:T(8,128)S(1)} fusion(bf16[768,7296]{1,0:T(8,128)(2,1)} %all-gather.3.cloned.1.call-done, bf16[2,1,7168,256]{3,2,1,0:T(8,128)(2,1)} %param.10), kind=kOutput, calls=%fused_computation.6 | convolution fusion | flops 2818572288 | bytes 15466496 | tf_op jit(solution)/shard_map/dot_general | solution.py:73
  96.0 8.7 %fusion.50 = bf16[384,256]{1,0:T(8,128)(2,1)S(1)} fusion(bf16[2,1,7168,256]{3,2,1,0:T(8,128)(2,1)} %param.11, bf16[768,7296]{1,0:T(8,128)(2,1)} %all-gather.3.cloned.1.call-done, f32[768,256]{1,0:T(8,128)S(1)} %fusion.6, f32[768]{0:T(1024)S(1)} %select_reduce_fusion.1, s32[384]{0:T(512)S(1)} %get-tuple-element.27, s32[384]{0:T(512)S(1)} %get-tuple-element.28, ...), kind=kOutput, calls=%fused_computation.30 | convolution fusion | flops 2973204480 | bytes 15680000 | tf_op jit(solution)/shard_map/dot_general | solution.py:83
  104.7 11.6 %all_gather.20 = bf16[384,1024]{1,0:T(8,128)(2,1)S(1)} all-gather(bf16[384,256]{1,0:T(8,128)(2,1)S(1)} %fusion.50), channel_id=1, replica_groups=mesh['expert'=32,'tensor'=4] {'tensor'}, dimensions={1}, use_global_device_ids=true | all-gather | bytes 983040 | tf_op jit(solution)/shard_map/all_gather | solution.py:85
  116.3 3.6 %convolution_convert_fusion.1 = bf16[384,1792]{1,0:T(8,128)(2,1)S(1)} fusion(bf16[384,1024]{1,0:T(8,128)(2,1)S(1)} %all_gather.20, bf16[1024,1792]{1,0:T(8,128)(2,1)} %bitcast.65), kind=kOutput, calls=%fused_computation.17 | convolution fusion | flops 1409974272 | bytes 5832704 | tf_op jit(solution)/shard_map/dot_general | solution.py:86
  121.4 12.0 %all-to-all-start.1 = ((bf16[32,12,1792]{2,1,0:T(8,128)(2,1)}), bf16[32,12,1792]{2,1,0:T(8,128)(2,1)S(1)}, u32[]{:S(2)}, u32[]{:S(2)}) async-start(bf16[32,12,1792]{2,1,0:T(8,128)(2,1)} %reshape.70), calls=%async_computation.1 | async-start | bytes 3670016 | tf_op jit(solution)/shard_map/all_to_all | solution.py:87
  133.9 13.2 %psum.14 = f32[24,32]{1,0:T(8,128)S(1)} all-reduce(f32[24,32]{1,0:T(8,128)S(1)} %fusion.112), channel_id=1, replica_groups=mesh['expert'=32,'tensor'=4] {'tensor'}, use_global_device_ids=true, to_apply=%region_2.3 | all-reduce | flops 768 | bytes 6144 | tf_op jit(solution)/shard_map/psum | solution.py:64
  148.5 10.4 %all-to-all-done.1 = bf16[32,12,1792]{2,1,0:T(8,128)(2,1)S(1)} async-done(((bf16[32,12,1792]{2,1,0:T(8,128)(2,1)}), bf16[32,12,1792]{2,1,0:T(8,128)(2,1)S(1)}, u32[]{:S(2)}, u32[]{:S(2)}) %all-to-all-start.1) | async-done | bytes 1376288 | tf_op jit(solution)/shard_map/all_to_all | solution.py:87
  159.6 9.8 %all_gather.21 = bf16[24,7168]{1,0:T(8,128)(2,1)S(1)} all-gather(bf16[24,1792]{1,0:T(8,128)(2,1)S(1)} %fusion.119), channel_id=1, replica_groups=mesh['expert'=32,'tensor'=4] {'tensor'}, dimensions={1}, use_global_device_ids=true | all-gather | bytes 430080 | tf_op jit(solution)/shard_map/all_gather | solution.py:43
  170.6 5.9 %copy.25 = bf16[1,1,256,7168]{2,3,1,0:T(8,128)(2,1)} copy(bf16[1,1,256,7168]{3,2,1,0:T(8,128)(2,1)} %get-tuple-element.7) | data formatting | bytes 7340032
  176.6 45.0 %all_to_all.20 = bf16[4,256,1792]{1,2,0:T(8,128)(2,1)} all-to-all(bf16[4,256,1792]{1,2,0:T(8,128)(2,1)} %bitcast.63), channel_id=1, replica_groups=mesh['expert'=32,'tensor'=4] {'tensor'}, dimensions={0} | all-to-all | bytes 7340032 | tf_op jit(solution)/shard_map/all_to_all | solution.py:39
  221.6 6.0 %copy.23 = bf16[4,256,1792]{2,1,0:T(8,128)(2,1)} copy(bf16[4,256,1792]{1,2,0:T(8,128)(2,1)} %all_to_all.20) | data formatting | bytes 7340032 | tf_op jit(solution)/shard_map/all_to_all | solution.py:39
  229.7 6.9 %fusion.2 = f32[768,256]{1,0:T(8,128)S(1)} fusion(bf16[768,7296]{1,0:T(8,128)(2,1)} %all-gather.5.cloned.1.call-done, bf16[2,1,7168,256]{3,2,1,0:T(8,128)(2,1)} %param.10), kind=kOutput, calls=%fused_computation.2 | convolution fusion | flops 2818572288 | bytes 15466496 | tf_op jit(solution)/shard_map/dot_general | solution.py:73
  237.6 8.7 %fusion.57 = bf16[384,256]{1,0:T(8,128)(2,1)S(1)} fusion(bf16[2,1,7168,256]{3,2,1,0:T(8,128)(2,1)} %param.11, bf16[768,7296]{1,0:T(8,128)(2,1)} %all-gather.5.cloned.1.call-done, f32[768,256]{1,0:T(8,128)S(1)} %fusion.2, f32[768]{0:T(1024)S(1)} %select_reduce_fusion, s32[384]{0:T(512)S(1)} %get-tuple-element.27, s32[384]{0:T(512)S(1)} %get-tuple-element.28, ...), kind=kOutput, calls=%fused_computation.31 | convolution fusion | flops 2973204480 | bytes 15680000 | tf_op jit(solution)/shard_map/dot_general | solution.py:83
  246.3 12.7 %all_gather.23 = bf16[384,1024]{1,0:T(8,128)(2,1)S(1)} all-gather(bf16[384,256]{1,0:T(8,128)(2,1)S(1)} %fusion.57), channel_id=1, replica_groups=mesh['expert'=32,'tensor'=4] {'tensor'}, dimensions={1}, use_global_device_ids=true | all-gather | bytes 983040 | tf_op jit(solution)/shard_map/all_gather | solution.py:85
  259.0 3.6 %convolution_convert_fusion = bf16[384,1792]{1,0:T(8,128)(2,1)S(1)} fusion(bf16[384,1024]{1,0:T(8,128)(2,1)S(1)} %all_gather.23, bf16[1024,1792]{1,0:T(8,128)(2,1)} %bitcast.64), kind=kOutput, calls=%fused_computation.16 | convolution fusion | flops 1409974272 | bytes 5832704 | tf_op jit(solution)/shard_map/dot_general | solution.py:86
  264.1 7.7 %all-to-all-start.3 = ((bf16[32,12,1792]{2,1,0:T(8,128)(2,1)}), bf16[32,12,1792]{2,1,0:T(8,128)(2,1)S(1)}, u32[]{:S(2)}, u32[]{:S(2)}) async-start(bf16[32,12,1792]{2,1,0:T(8,128)(2,1)} %reshape.73), calls=%async_computation.3 | async-start | bytes 3670016 | tf_op jit(solution)/shard_map/all_to_all | solution.py:87
  272.4 13.9 %psum.15 = f32[24,32]{1,0:T(8,128)S(1)} all-reduce(f32[24,32]{1,0:T(8,128)S(1)} %fusion.110), channel_id=1, replica_groups=mesh['expert'=32,'tensor'=4] {'tensor'}, use_global_device_ids=true, to_apply=%region_7.8 | all-reduce | flops 768 | bytes 6144 | tf_op jit(solution)/shard_map/psum | solution.py:64
  287.0 10.4 %all-to-all-done.3 = bf16[32,12,1792]{2,1,0:T(8,128)(2,1)S(1)} async-done(((bf16[32,12,1792]{2,1,0:T(8,128)(2,1)}), bf16[32,12,1792]{2,1,0:T(8,128)(2,1)S(1)}, u32[]{:S(2)}, u32[]{:S(2)}) %all-to-all-start.3) | async-done | bytes 1376288 | tf_op jit(solution)/shard_map/all_to_all | solution.py:87
  (74 shorter events, 17.4 us)
Async XLA Ops:
  6.5 81.5 %all-gather.3.cloned.1.call-start = ((), (), s32[]{:S(2)}) async-start(), calls=%async_computation.4 | async-start | bytes 11556864 | tf_op jit(solution)/shard_map/all_gather | solution.py:59
  36.4 45.7 %all-to-all-start = ((bf16[4,256,1792]{1,2,0:T(8,128)(2,1)}), bf16[4,256,1792]{1,2,0:T(8,128)(2,1)}, u32[]{:S(2)}, u32[]{:S(2)}) async-start(bf16[4,256,1792]{1,2,0:T(8,128)(2,1)} %bitcast.62), calls=%async_computation | async-start | bytes 7340032 | tf_op jit(solution)/shard_map/all_to_all | solution.py:39
  120.0 13.6 %copy-start.3 = (f32[2,1792]{1,0:T(2,128)S(1)}, f32[2,1792]{1,0:T(2,128)}, u32[]{:S(2)}) copy-start(f32[2,1792]{1,0:T(2,128)} %param.8) | copy-start | bytes 43012
  120.0 13.6 %copy-start = (bf16[24,1792]{1,0:T(8,128)(2,1)S(1)}, bf16[24,1792]{1,0:T(8,128)(2,1)}, u32[]{:S(2)}) copy-start(bf16[24,1792]{1,0:T(8,128)(2,1)} %param.7) | copy-start | bytes 258052
  120.0 13.6 %copy-start.1 = (f32[2,1792,32]{1,2,0:T(8,128)S(1)}, f32[2,1792,32]{1,2,0:T(8,128)}, u32[]{:S(2)}) copy-start(f32[2,1792,32]{1,2,0:T(8,128)} %param.9) | copy-start | bytes 1376260
  121.4 37.5 %all-to-all-start.1 = ((bf16[32,12,1792]{2,1,0:T(8,128)(2,1)}), bf16[32,12,1792]{2,1,0:T(8,128)(2,1)S(1)}, u32[]{:S(2)}, u32[]{:S(2)}) async-start(bf16[32,12,1792]{2,1,0:T(8,128)(2,1)} %reshape.70), calls=%async_computation.1 | async-start | bytes 3670016 | tf_op jit(solution)/shard_map/all_to_all | solution.py:87
  133.5 96.2 %all-gather.5.cloned.1.call-start = ((), (), s32[]{:S(2)}) async-start(), calls=%async_computation.5 | async-start | bytes 11556864 | tf_op jit(solution)/shard_map/all_gather | solution.py:59
  262.6 9.5 %copy-start.2 = (f32[2,1792,32]{1,2,0:T(8,128)S(1)}, f32[2,1792,32]{1,2,0:T(8,128)}, u32[]{:S(2)}) copy-start(f32[2,1792,32]{1,2,0:T(8,128)} %param.9) | copy-start | bytes 1376260
  264.1 33.2 %all-to-all-start.3 = ((bf16[32,12,1792]{2,1,0:T(8,128)(2,1)}), bf16[32,12,1792]{2,1,0:T(8,128)(2,1)S(1)}, u32[]{:S(2)}, u32[]{:S(2)}) async-start(bf16[32,12,1792]{2,1,0:T(8,128)(2,1)} %reshape.73), calls=%async_computation.3 | async-start | bytes 3670016 | tf_op jit(solution)/shard_map/all_to_all | solution.py:87
Sparse Core Ops, SparseCore 0:
  23.9 63.1 all-gather.2
  170.8 58.8 all-gather.4

commit v2 on v1

v2 whole, which is shorter than its diff:
```python
import jax
import jax.numpy as jnp
from jax import lax
from jax.experimental import pallas as pl
from jax.experimental.pallas import tpu as pltpu
from jax.sharding import PartitionSpec as P

route_scale = 2.5
bf16, f32 = jnp.bfloat16, jnp.float32

Y_STEPS = ((2, 6), (6, 2))
X_STEPS = ((8, 24), (24, 8))
SIBLING = (1, 1)


def short(values):
    return lax.reduce_precision(values, 8, 7)


def thirds(values):
    high = short(values)
    middle = short(values - high)
    return [part.astype(bf16) for part in (high, middle, values - high - middle)]


def swap(block, masks):
    count = lax.axis_size("expert")
    return lax.ppermute(block, "expert", [(i, i ^ masks[i & 1]) for i in range(count)])


def z_swap(block, step):
    pairs = []
    for i in range(lax.axis_size("expert")):
        mask = ((1, 3), (3, 1))[i & 1][step]
        pairs += [(i * 4 + z, i * 4 + (z ^ mask)) for z in range(4)]
    return lax.ppermute(block, ("expert", "tensor"), pairs)


def after(block, *others):
    return lax.optimization_barrier((block, *others))[0]


def gate_up_kernel(own_ref, other_ref, gate_ref, up_ref, out_ref):
    rows, units = own_ref.shape[0], gate_ref.shape[-1]

    @pl.when(pl.program_id(0) == 0)
    def _():
        out_ref[...] = jnp.zeros_like(out_ref)

    for start, tokens in ((0, own_ref), (rows, other_ref)):
        for first, weights in ((0, gate_ref), (units, up_ref)):
            out_ref[start : start + rows, first : first + units] += jnp.dot(
                tokens[...], weights[0, 0], preferred_element_type=f32
            )


def gate_up(own, other, w_gate, w_up, layer, first, width):
    depth = 512
    rows, units = own.shape[0], w_gate.shape[-1]
    tokens = pl.BlockSpec((rows, depth), lambda k: (0, k))
    weights = pl.BlockSpec((1, 1, depth, units), lambda k: (layer, 0, first // depth + k, 0))
    return pl.pallas_call(
        gate_up_kernel,
        grid=(width // depth,),
        in_specs=[tokens, tokens, weights, weights],
        out_specs=pl.BlockSpec((2 * rows, 2 * units), lambda k: (0, 0)),
        out_shape=jax.ShapeDtypeStruct((2 * rows, 2 * units), f32),
        cost_estimate=pl.CostEstimate(
            flops=8 * rows * width * units,
            bytes_accessed=4 * (rows + units) * width + 16 * rows * units,
            transcendentals=0,
        ),
    )(own, other, w_gate, w_up)


def down_kernel(z_ref, a0, a1, a2, w0, w1, w2, out_ref):
    total = jnp.dot(a0[...], w0[0, 0], preferred_element_type=f32)
    total += jnp.dot(a1[...], w1[0], preferred_element_type=f32)
    total += jnp.dot(a2[0], w2[0], preferred_element_type=f32)
    total += jnp.dot(a2[1], w2[1], preferred_element_type=f32)
    out_ref[...] = total.astype(out_ref.dtype)


def down_product(z, acts, w_down, layer, first, second):
    slots, units = acts[0].shape
    part = first.shape[-1]
    columns = 256
    steps = part // columns
    return pl.pallas_call(
        down_kernel,
        grid_spec=pltpu.PrefetchScalarGridSpec(
            num_scalar_prefetch=1,
            grid=(steps,),
            in_specs=[
                pl.BlockSpec((slots, units), lambda n, z: (0, 0)),
                pl.BlockSpec((slots, units), lambda n, z: (0, 0)),
                pl.BlockSpec((2, slots, units), lambda n, z: (0, 0, 0)),
                pl.BlockSpec((1, 1, units, columns), lambda n, z: (layer, 0, 0, z[0] * steps + n)),
                pl.BlockSpec((1, units, columns), lambda n, z: (0, 0, n)),
                pl.BlockSpec((2, units, columns), lambda n, z: (0, 0, n)),
            ],
            out_specs=pl.BlockSpec((slots, columns), lambda n, z: (0, n)),
        ),
        out_shape=jax.ShapeDtypeStruct((slots, part), bf16),
        cost_estimate=pl.CostEstimate(
            flops=8 * slots * units * part,
            bytes_accessed=8 * units * (slots + part) + 2 * slots * part,
            transcendentals=0,
        ),
    )(jnp.full((1,), z, jnp.int32), *acts, w_down, first, second)


def body(hidden_in, norm_gain, router, w_gate, w_up, w_down, routes):
    rows, part = hidden_in.shape
    layers, width, units = w_gate.shape[0], w_gate.shape[2], w_gate.shape[3]
    experts = router.shape[2]
    capacity = min(rows, 2 * rows * routes.shape[2] // experts)
    slots = experts * capacity
    chips = experts // 2
    half = width // 2
    me = lax.axis_index("expert")
    core = me & 1
    z = lax.axis_index("tensor")

    gains = jnp.stack(thirds(norm_gain), axis=0).reshape(3 * layers, part)
    opening = jnp.concatenate([hidden_in, gains, jnp.zeros((2, part), bf16)], axis=0)
    opening = lax.all_gather(opening, "tensor", axis=1, tiled=True)
    full = opening[:rows]
    gains = opening[rows : rows + 3 * layers].astype(f32).reshape(3, layers, width)
    gains = gains[0] + gains[1] + gains[2]

    bits = jnp.arange(chips, dtype=jnp.int32)
    sources = []
    for c in range(2):
        masks = [Y_STEPS[0][c], Y_STEPS[1][c], X_STEPS[0][c], X_STEPS[1][c]]
        total = jnp.zeros_like(bits)
        for n, mask in enumerate(masks):
            total = total ^ jnp.where(((bits >> n) & 1) == 1, mask, 0)
        sources.append(total)
    own_source = me ^ jnp.where(core == 1, sources[1], sources[0])
    other_source = (me ^ 1) ^ jnp.where(core == 1, sources[0], sources[1])
    source = jnp.repeat(jnp.concatenate([own_source, other_source]), rows)

    state = hidden_in
    for layer in range(layers):
        if layer:
            full = lax.all_gather(state, "tensor", axis=1, tiled=True)
        values = full.astype(f32)
        scale = lax.rsqrt(jnp.sum(values * values, axis=1) / width + 1e-06)
        normed = (values * scale[:, None] * gains[layer][None, :]).astype(bf16)

        chosen = routes[layer]
        expert_iota = lax.broadcasted_iota(jnp.int32, (1, 1, experts), 2)
        picks = jnp.any(chosen[:, :, None] == expert_iota, axis=1)
        earlier = lax.broadcasted_iota(jnp.int32, (rows, rows), 0) > lax.broadcasted_iota(
            jnp.int32, (rows, rows), 1
        )
        ranks = jnp.dot(earlier.astype(bf16), picks.astype(bf16), preferred_element_type=f32)
        marks = jnp.where(picks, ranks + 1.0, 0.0)
        marks_sent = jnp.pad(marks, ((0, 0), (0, 128 - experts))).astype(bf16)

        held_a = normed[None, :, :half]
        held_b = jnp.concatenate([normed[:, half:], marks_sent], axis=1)[None]
        for step in range(3):
            masks_a = (Y_STEPS + X_STEPS)[step]
            masks_b = (X_STEPS + Y_STEPS)[step]
            got_a, got_b = swap(held_a, masks_a), swap(held_b, masks_b)
            held_a = jnp.concatenate([held_a, got_a])
            held_b = jnp.concatenate([held_b, got_b])
            if step == 0:
                started = got_a
        last_a, last_b = swap(held_a, X_STEPS[1]), swap(held_b, Y_STEPS[1])
        other_a, other_b = swap(held_a, SIBLING), swap(held_b, SIBLING)

        near = jnp.where(core == 1, 3, 1)
        far = near ^ 2

        def columns(mask):
            return lax.dynamic_slice_in_dim(w_down[layer, 0], (z ^ mask) * part, part, axis=1)

        first = jnp.stack([columns(near), columns(2)])
        first = z_swap(after(first, started), 0)
        second = z_swap(jnp.stack([columns(far), first[1]]), 1)

        own = state.astype(f32) * scale[:, None] * norm_gain[layer][None, :]
        own = own.astype(bf16).astype(f32)
        scores = jnp.dot(own, router[layer], precision=lax.Precision.HIGHEST)
        scores = after(scores, started)
        scores = scores + z_swap(scores, 0)
        scores = scores + z_swap(scores, 1)
        probs = jax.nn.sigmoid(scores)
        picked = jnp.where(picks, probs, 0.0)
        weights = route_scale * picked / jnp.sum(picked, axis=1, keepdims=True)

        def by_chip(table):
            table = table.reshape(rows, chips, 2)
            return jnp.where(core == 1, table[:, :, ::-1], table)

        slot_iota = lax.broadcasted_iota(jnp.int32, (1, 1, 1, capacity), 3).astype(f32) + 1.0
        mixer = jnp.where(by_chip(marks)[..., None] == slot_iota, by_chip(weights)[..., None], 0.0)
        mixer = mixer.reshape(rows, slots)
        mixer = jnp.concatenate(thirds(mixer)[:2], axis=0)

        def products(own, other, first):
            flat = [block.reshape(-1, block.shape[2]) for block in (own, other)]
            result = gate_up(*flat, w_gate, w_up, layer, first, half)
            return result.reshape(2, 2, 4, rows, 2 * units)

        sums_a = products(held_a, other_a, 0)
        sums_b = products(held_b, other_b, half)
        more_a = products(last_a, swap(last_a, SIBLING), 0)
        far_b = swap(last_b, SIBLING)
        more_b = products(last_b, far_b, half)
        sums = jnp.concatenate([sums_a, more_a], axis=1)
        sums = sums + jnp.concatenate([sums_b, more_b], axis=1).swapaxes(1, 2)
        sums = sums.reshape(2 * chips * rows, 2 * units)
        act = (jax.nn.silu(sums[:, :units]) * sums[:, units:]).astype(bf16)

        mark = jnp.stack([jnp.concatenate([held_b, last_b]), jnp.concatenate([other_b, far_b])])
        mark = mark[..., half:].astype(f32)
        mine = lax.broadcasted_iota(jnp.int32, (1, 1, 1, 128), 3) == me
        mark = jnp.sum(jnp.where(mine, mark, 0.0), axis=3).astype(jnp.int32)
        mark = mark.reshape(2, 4, 4, rows).swapaxes(1, 2).reshape(-1)
        place = ((source & 1) ^ core) * (slots // 2) + (source >> 1) * capacity + mark - 1
        place = jnp.where(mark > 0, place, -1)
        taken = lax.broadcasted_iota(jnp.int32, (slots, 1), 0) == place[None, :]
        act = jnp.dot(taken.astype(bf16), act, preferred_element_type=f32).astype(bf16)

        act_near = z_swap(act, 0)
        act_far = z_swap(jnp.stack([act, act_near]), 1)
        out = down_product(z, (act, act_near, act_far), w_down, layer, first, second)
        kept, given = out[: slots // 2], out[slots // 2 :]
        shape = (chips, capacity, part)
        out = jnp.concatenate([kept.reshape(shape), swap(given, SIBLING).reshape(shape)], axis=1)
        groups = [list(range(c, experts, 2)) for c in range(2)]
        returned = lax.all_to_all(
            out, "expert", split_axis=0, concat_axis=0, axis_index_groups=groups
        ).reshape(slots, part)
        mixed = jnp.dot(mixer, returned, preferred_element_type=f32)
        state = (state.astype(f32) + mixed[:rows] + mixed[rows:]).astype(bf16)
    return state


def solution(mesh):
    placed = (
        P("expert", "tensor"),
        P(None, "tensor"),
        P(None, "tensor", None),
        P(None, "expert", None, "tensor"),
        P(None, "expert", None, "tensor"),
        P(None, "expert", "tensor", None),
        P(None, "expert", None),
    )
    return jax.shard_map(
        body, mesh=mesh, in_specs=placed, out_specs=P("expert", "tensor"), check_vma=False
    )
```

time: 307 us -> 358 us (1.17)
  blocking collectives: 119 us -> 23.7 us
  Pallas kernels: 0 us -> 74 us
  starting transfers between devices: 24.5 us -> 93.1 us
  waiting for transfers between devices: 63.8 us -> 107 us
  matrix products: 39.7 us -> 2.36 us
  other arithmetic: 7.64 us -> 22.5 us
  between operations: 13.8 us -> 0.99 us
  local copies, waits for them, and re-layouts: 36.7 us -> 32.2 us
    ppermute x0 -> x38, waiting for transfers between devices: none -> 85.2 us  [the longest x26 52 us: swap(): lax.ppermute(block, 'expert', [(i, i ^ masks[i & 1]) for i in range(count)])]
    ppermute x0 -> x38, starting transfers between devices: none -> 81.6 us  [the longest x26 69.7 us: swap(): lax.ppermute(block, 'expert', [(i, i ^ masks[i & 1]) for i in range(count)])]
    pallas_call x0 -> x10, Pallas kernels: none -> 74 us  [the longest x8 59.9 us: gate_up(): pl.pallas_call(gate_up_kernel, grid=(width // depth,), in_specs=[tokens,...]
    all_to_all x1 -> x0, blocking collectives: 45 us -> none  [body(): down = lax.all_to_all(down, 'tensor', split_axis=0, concat_axis=0)]
    all_to_all x3 -> x2, waiting for transfers between devices: 61.7 us -> 22.1 us  [body(): lax.all_to_all(out, 'expert', split_axis=0, concat_axis=0, axis_index_gro...]
    psum x2 -> x0, blocking collectives: 27.1 us -> none  [body(): probs = jax.nn.sigmoid(lax.psum(scores, 'tensor'))]
    all_gather x2 -> x0, blocking collectives: 24.4 us -> none  [body(): act = lax.all_gather(act, 'tensor', axis=1, tiled=True)]
    dot_general x4 -> x0, matrix products: 21 us -> none  [the longest x2 13.8 us: body(): gate = jnp.dot(tokens, w_gate[layer, 0], preferred_element_type=f32)]
  transfers between devices with their start and end apart: 5 -> 40, of which waited for: 4 -> 20; matrix products, arithmetic and copies ran while one was open for 11% -> 11% of each run, Pallas kernels for 0% -> 17%
where the time goes in v2:
time: 358 us; the launch traced here: 356 us
  waiting for transfers between devices  107 us (30%)
  starting transfers between devices  93.1 us (26%)
  Pallas kernels  74 us (21%)
  local copies, waits for them, and re-layouts  32.2 us (9%)
  blocking collectives  23.7 us (7%)
  other arithmetic  22.5 us (6%)
    ppermute x26, starting transfers between devices, swap(): lax.ppermute(block, 'expert', [(i, i ^ masks[i & 1]) for i in range(count)])  69.7 us
    pallas_call x8, Pallas kernels, gate_up(): pl.pallas_call(gate_up_kernel, grid=(width // depth,), in_specs=[tokens,...  59.9 us
    ppermute x26, waiting for transfers between devices, swap(): lax.ppermute(block, 'expert', [(i, i ^ masks[i & 1]) for i in range(count)])  52 us
    ppermute x12, waiting for transfers between devices, z_swap(): return lax.ppermute(block, ('expert', 'tensor'), pairs)  33.1 us
    all_to_all x2, waiting for transfers between devices, body(): lax.all_to_all(out, 'expert', split_axis=0, concat_axis=0, axis_index_gro...  22.1 us
    pallas_call x2, Pallas kernels, down_product(): pl.pallas_call(down_kernel, grid_spec=pltpu.PrefetchScalarGridSpec(num_sc...  14.1 us
    all_gather x1, blocking collectives, body(): opening = lax.all_gather(opening, 'tensor', axis=1, tiled=True)  13.1 us
    ppermute x12, starting transfers between devices, z_swap(): return lax.ppermute(block, ('expert', 'tensor'), pairs)  11.9 us
  transfers between devices with their start and end apart: 40, of which 20 were waited for; matrix products, arithmetic and copies ran while one was open for 11% of the time, Pallas kernels for 17%

profile of v2, /device:TPU:1, one launch (start us, length us, event | category | flops | bytes accessed | tf_op | source)
XLA Modules:
  0.0 356.2 jit_solution(12818798888624048729)
XLA Ops:
  1.9 13.1 %all_gather.6 = bf16[32,7168]{1,0:T(8,128)(2,1)S(1)} all-gather(bf16[32,1792]{1,0:T(8,128)(2,1)S(1)} %maximum_maximum_fusion), channel_id=1, replica_groups=mesh['expert'=32,'tensor'=4] {'tensor'}, dimensions={1}, use_global_device_ids=true | all-gather | bytes 573440 | tf_op jit(solution)/shard_map/all_gather | solution.py:127
  40.6 7.9 %collective-permute-done.10 = bf16[4,24,3584]{2,1,0:T(8,128)(2,1)S(1)} collective-permute-done((bf16[4,24,3584]{2,1,0:T(8,128)(2,1)S(1)}, bf16[4,24,3584]{2,1,0:T(8,128)(2,1)S(1)}, u32[]{:S(2)}, u32[]{:S(2)}) %collective-permute-start.10) | collective-permute-done | bytes 688160 | tf_op jit(solution)/shard_map/ppermute | solution.py:28
  58.7 8.9 %collective-permute-done.12 = bf16[8,24,3584]{2,1,0:T(8,128)(2,1)} collective-permute-done((bf16[8,24,3584]{2,1,0:T(8,128)(2,1)}, bf16[8,24,3584]{2,1,0:T(8,128)(2,1)}, u32[]{:S(2)}, u32[]{:S(2)}) %collective-permute-start.12) | collective-permute-done | bytes 1376288 | tf_op jit(solution)/shard_map/ppermute | solution.py:28
  84.1 7.4 %shard_map.73 = f32[384,512]{1,0:T(8,128)} custom-call(bf16[192,3584]{1,0:T(8,128)(2,1)} %bitcast.15.own_ref, bf16[192,3584]{1,0:T(8,128)(2,1)} %bitcast.16.other_ref, bf16[2,1,7168,256]{3,2,1,0:T(8,128)(2,1)} %gate_ref.15, bf16[2,1,7168,256]{3,2,1,0:T(8,128)(2,1)} %up_ref.15), custom_call_target="tpu_custom_call" | custom-call | flops 1409286144 | bytes 7208960 | tf_op jit(solution)/shard_map/pallas_call | solution.py:62
  91.5 7.5 %shard_map.75 = f32[384,512]{1,0:T(8,128)} custom-call(bf16[192,3712]{1,0:T(8,128)(2,1)} %bitcast.113, bf16[192,3712]{1,0:T(8,128)(2,1)} %bitcast.22.other_ref, bf16[2,1,7168,256]{3,2,1,0:T(8,128)(2,1)} %gate_ref.15, bf16[2,1,7168,256]{3,2,1,0:T(8,128)(2,1)} %up_ref.15), custom_call_target="tpu_custom_call" | custom-call | flops 1409286144 | bytes 7208960 | tf_op jit(solution)/shard_map/pallas_call | solution.py:62
  100.2 7.4 %shard_map.74 = f32[384,512]{1,0:T(8,128)} custom-call(bf16[192,3584]{1,0:T(8,128)(2,1)} %bitcast.18.own_ref, bf16[192,3584]{1,0:T(8,128)(2,1)} %bitcast.19.other_ref, bf16[2,1,7168,256]{3,2,1,0:T(8,128)(2,1)} %gate_ref.15, bf16[2,1,7168,256]{3,2,1,0:T(8,128)(2,1)} %up_ref.15), custom_call_target="tpu_custom_call" | custom-call | flops 1409286144 | bytes 7208960 | tf_op jit(solution)/shard_map/pallas_call | solution.py:62
  110.6 7.6 %shard_map.76 = f32[384,512]{1,0:T(8,128)} custom-call(bf16[192,3712]{1,0:T(8,128)(2,1)} %bitcast.111, bf16[192,3712]{1,0:T(8,128)(2,1)} %bitcast.25.other_ref, bf16[2,1,7168,256]{3,2,1,0:T(8,128)(2,1)} %gate_ref.15, bf16[2,1,7168,256]{3,2,1,0:T(8,128)(2,1)} %up_ref.15), custom_call_target="tpu_custom_call" | custom-call | flops 1409286144 | bytes 7208960 | tf_op jit(solution)/shard_map/pallas_call | solution.py:62
  133.9 7.0 %shard_map.77 = bf16[384,1792]{1,0:T(8,128)(2,1)} custom-call(s32[1]{0:T(128)} %bitcast.9.z_ref, bf16[384,256]{1,0:T(8,128)(2,1)} %copy-done.23, bf16[384,256]{1,0:T(8,128)(2,1)} %copy-done.25, bf16[2,384,256]{2,1,0:T(8,128)(2,1)} %copy-done.30, bf16[2,1,256,7168]{3,2,1,0:T(8,128)(2,1)} %w0.3, bf16[2,256,1792]{2,1,0:T(8,128)(2,1)} %collective-permute-done.16.w1, ...), custom_call_target="tpu_custom_call" | custom-call | flops 1409286144 | bytes 5832704 | tf_op jit(solution)/shard_map/pallas_call | solution.py:89
  149.6 7.7 %all-to-all-start = ((bf16[16,24,1792]{2,1,0:T(8,128)(2,1)}), bf16[16,24,1792]{2,1,0:T(8,128)(2,1)S(1)}, u32[]{:S(2)}, u32[]{:S(2)}) async-start(bf16[16,24,1792]{2,1,0:T(8,128)(2,1)} %pad_maximum_fusion.9), calls=%async_computation | async-start | bytes 2752512 | tf_op jit(solution)/shard_map/all_to_all | solution.py:236
  165.7 10.7 %all-to-all-done = bf16[16,24,1792]{2,1,0:T(8,128)(2,1)S(1)} async-done(((bf16[16,24,1792]{2,1,0:T(8,128)(2,1)}), bf16[16,24,1792]{2,1,0:T(8,128)(2,1)S(1)}, u32[]{:S(2)}, u32[]{:S(2)}) %all-to-all-start) | async-done | bytes 1376288 | tf_op jit(solution)/shard_map/all_to_all | solution.py:236
  176.8 10.7 %all_gather.7 = bf16[24,7168]{1,0:T(8,128)(2,1)S(1)} all-gather(bf16[24,1792]{1,0:T(8,128)(2,1)S(1)} %fusion.33), channel_id=1, replica_groups=mesh['expert'=32,'tensor'=4] {'tensor'}, dimensions={1}, use_global_device_ids=true | all-gather | bytes 430080 | tf_op jit(solution)/shard_map/all_gather | solution.py:147
  193.8 7.7 %collective-permute-done.28 = bf16[2,24,3584]{2,1,0:T(8,128)(2,1)S(1)} collective-permute-done((bf16[2,24,3584]{2,1,0:T(8,128)(2,1)S(1)}, bf16[2,24,3584]{2,1,0:T(8,128)(2,1)S(1)}, u32[]{:S(2)}, u32[]{:S(2)}) %collective-permute-start.28) | collective-permute-done | bytes 344096 | tf_op jit(solution)/shard_map/ppermute | solution.py:28
  203.0 13.4 %collective-permute-done.29 = bf16[4,24,3584]{2,1,0:T(8,128)(2,1)S(1)} collective-permute-done((bf16[4,24,3584]{2,1,0:T(8,128)(2,1)S(1)}, bf16[4,24,3584]{2,1,0:T(8,128)(2,1)S(1)}, u32[]{:S(2)}, u32[]{:S(2)}) %collective-permute-start.29) | collective-permute-done | bytes 688160 | tf_op jit(solution)/shard_map/ppermute | solution.py:28
  217.7 18.2 %collective-permute-start.30 = (bf16[8,24,3584]{2,1,0:T(8,128)(2,1)S(1)}, bf16[8,24,3584]{2,1,0:T(8,128)(2,1)S(1)}, u32[]{:S(2)}, u32[]{:S(2)}) collective-permute-start(bf16[8,24,3584]{2,1,0:T(8,128)(2,1)S(1)} %pad_maximum_fusion.10), channel_id=1, source_target_pairs={{0,4},{4,0},{8,12},{12,8},{16,20},{20,16},{24,28},{28,24},{32,36},... | collective-permute-start | bytes 4128776 | tf_op jit(solution)/shard_map/ppermute | solution.py:28
  236.6 7.7 %collective-permute-start.32 = (bf16[8,24,3584]{2,1,0:T(8,128)(2,1)}, bf16[8,24,3584]{2,1,0:T(8,128)(2,1)}, u32[]{:S(2)}, u32[]{:S(2)}) collective-permute-start(bf16[8,24,3584]{2,1,0:T(8,128)(2,1)} %collective-permute-done.31), channel_id=1, source_target_pairs={{0,4},{4,0},{8,12},{12,8},{16,20},{20,16},{24,28},{28,24},{32,36},... | collective-permute-start | bytes 4128776 | tf_op jit(solution)/shard_map/ppermute | solution.py:28
  244.3 8.0 %collective-permute-start.27 = (bf16[8,24,3712]{2,1,0:T(8,128)(2,1)S(1)}, bf16[8,24,3712]{2,1,0:T(8,128)(2,1)}, u32[]{:S(2)}, u32[]{:S(2)}) collective-permute-start(bf16[8,24,3712]{2,1,0:T(8,128)(2,1)S(1)} %collective-permute-done.25), channel_id=1, source_target_pairs={{0,4},{4,0},{8,12},{12,8},{16,20},{20,16},{24,28},{28,24},{32,36},... | collective-permute-start | bytes 4276232 | tf_op jit(solution)/shard_map/ppermute | solution.py:28
  257.1 7.4 %shard_map.78 = f32[384,512]{1,0:T(8,128)} custom-call(bf16[192,3584]{1,0:T(8,128)(2,1)} %bitcast.117, bf16[192,3584]{1,0:T(8,128)(2,1)} %bitcast.130, bf16[2,1,7168,256]{3,2,1,0:T(8,128)(2,1)} %gate_ref.15, bf16[2,1,7168,256]{3,2,1,0:T(8,128)(2,1)} %up_ref.15), custom_call_target="tpu_custom_call" | custom-call | flops 1409286144 | bytes 7208960 | tf_op jit(solution)/shard_map/pallas_call | solution.py:62
  264.5 7.5 %shard_map.80 = f32[384,512]{1,0:T(8,128)} custom-call(bf16[192,3712]{1,0:T(8,128)(2,1)} %bitcast.114, bf16[192,3712]{1,0:T(8,128)(2,1)} %bitcast.53.other_ref, bf16[2,1,7168,256]{3,2,1,0:T(8,128)(2,1)} %gate_ref.15, bf16[2,1,7168,256]{3,2,1,0:T(8,128)(2,1)} %up_ref.15), custom_call_target="tpu_custom_call" | custom-call | flops 1409286144 | bytes 7208960 | tf_op jit(solution)/shard_map/pallas_call | solution.py:62
  273.2 7.4 %shard_map.79 = f32[384,512]{1,0:T(8,128)} custom-call(bf16[192,3584]{1,0:T(8,128)(2,1)} %bitcast.49.own_ref, bf16[192,3584]{1,0:T(8,128)(2,1)} %bitcast.50.other_ref, bf16[2,1,7168,256]{3,2,1,0:T(8,128)(2,1)} %gate_ref.15, bf16[2,1,7168,256]{3,2,1,0:T(8,128)(2,1)} %up_ref.15), custom_call_target="tpu_custom_call" | custom-call | flops 1409286144 | bytes 7208960 | tf_op jit(solution)/shard_map/pallas_call | solution.py:62
  283.7 7.6 %shard_map.81 = f32[384,512]{1,0:T(8,128)} custom-call(bf16[192,3712]{1,0:T(8,128)(2,1)} %bitcast.112, bf16[192,3712]{1,0:T(8,128)(2,1)} %bitcast.56.other_ref, bf16[2,1,7168,256]{3,2,1,0:T(8,128)(2,1)} %gate_ref.15, bf16[2,1,7168,256]{3,2,1,0:T(8,128)(2,1)} %up_ref.15), custom_call_target="tpu_custom_call" | custom-call | flops 1409286144 | bytes 7208960 | tf_op jit(solution)/shard_map/pallas_call | solution.py:62
  299.5 8.5 %collective-permute-done.34.a2 = bf16[2,384,256]{2,1,0:T(8,128)(2,1)S(1)} collective-permute-done((bf16[2,384,256]{2,1,0:T(8,128)(2,1)S(1)}, bf16[2,384,256]{2,1,0:T(8,128)(2,1)S(1)}, u32[]{:S(2)}, u32[]{:S(2)}) %collective-permute-start.34) | collective-permute-done | bytes 393248 | tf_op jit(solution)/shard_map/ppermute | solution.py:36
  308.7 7.1 %shard_map.82 = bf16[384,1792]{1,0:T(8,128)(2,1)} custom-call(s32[1]{0:T(128)} %bitcast.9.z_ref, bf16[384,256]{1,0:T(8,128)(2,1)} %copy-done.22, bf16[384,256]{1,0:T(8,128)(2,1)} %copy-done.24, bf16[2,384,256]{2,1,0:T(8,128)(2,1)} %copy-done.29, bf16[2,1,256,7168]{3,2,1,0:T(8,128)(2,1)} %w0.3, bf16[2,256,1792]{2,1,0:T(8,128)(2,1)} %copy-done.6, ...), custom_call_target="tpu_custom_call" | custom-call | flops 1409286144 | bytes 5832704 | tf_op jit(solution)/shard_map/pallas_call | solution.py:89
  317.2 8.5 %collective-permute-start.37 = (bf16[192,1792]{1,0:T(8,128)(2,1)S(1)}, bf16[192,1792]{1,0:T(8,128)(2,1)}, u32[]{:S(2)}, u32[]{:S(2)}) collective-permute-start(bf16[192,1792]{1,0:T(8,128)(2,1)S(1)} %get-tuple-element.24), channel_id=1, source_target_pairs={{0,4},{4,0},{8,12},{12,8},{16,20},{20,16},{24,28},{28,24},{32,36},... | collective-permute-start | bytes 2064392 | tf_op jit(solution)/shard_map/ppermute | solution.py:28
  343.8 11.4 %all-to-all-done.1 = bf16[16,24,1792]{2,1,0:T(8,128)(2,1)S(1)} async-done(((bf16[16,24,1792]{2,1,0:T(8,128)(2,1)}), bf16[16,24,1792]{2,1,0:T(8,128)(2,1)S(1)}, u32[]{:S(2)}, u32[]{:S(2)}) %all-to-all-start.1) | async-done | bytes 1376288 | tf_op jit(solution)/shard_map/all_to_all | solution.py:236
  (264 shorter events, 138.9 us)
Async XLA Ops:
  15.5 15.1 %collective-permute-start = (bf16[1,24,3584]{2,1,0:T(8,128)(2,1)S(1)}, bf16[1,24,3584]{2,1,0:T(8,128)(2,1)S(1)}, u32[]{:S(2)}, u32[]{:S(2)}) collective-permute-start(bf16[1,24,3584]{2,1,0:T(8,128)(2,1)S(1)} %get-tuple-element.29), channel_id=1, source_target_pairs={{0,8},{4,28},{8,0},{12,20},{16,24},{20,12},{24,16},{28,4},{32,40},... | collective-permute-start | bytes 516104 | tf_op jit(solution)/shard_map/ppermute | solution.py:28
  18.7 12.1 %collective-permute-start.3 = (bf16[1,24,3712]{2,1,0:T(8,128)(2,1)S(1)}, bf16[1,24,3712]{2,1,0:T(8,128)(2,1)S(1)}, u32[]{:S(2)}, u32[]{:S(2)}) collective-permute-start(bf16[1,24,3712]{2,1,0:T(8,128)(2,1)S(1)} %fusion.27), channel_id=1, source_target_pairs={{0,32},{4,100},{8,40},{12,108},{16,48},{20,116},{24,56},{28,124},{... | collective-permute-start | bytes 534536 | tf_op jit(solution)/shard_map/ppermute | solution.py:28
  37.2 11.3 %collective-permute-start.10 = (bf16[4,24,3584]{2,1,0:T(8,128)(2,1)S(1)}, bf16[4,24,3584]{2,1,0:T(8,128)(2,1)S(1)}, u32[]{:S(2)}, u32[]{:S(2)}) collective-permute-start(bf16[4,24,3584]{2,1,0:T(8,128)(2,1)S(1)} %pad_maximum_fusion.14), channel_id=1, source_target_pairs={{0,32},{4,100},{8,40},{12,108},{16,48},{20,116},{24,56},{28,124},{... | collective-permute-start | bytes 2064392 | tf_op jit(solution)/shard_map/ppermute | solution.py:28
  37.6 12.2 %collective-permute-start.5 = (bf16[4,24,3712]{2,1,0:T(8,128)(2,1)S(1)}, bf16[4,24,3712]{2,1,0:T(8,128)(2,1)S(1)}, u32[]{:S(2)}, u32[]{:S(2)}) collective-permute-start(bf16[4,24,3712]{2,1,0:T(8,128)(2,1)S(1)} %pad_maximum_fusion.12), channel_id=1, source_target_pairs={{0,8},{4,28},{8,0},{12,20},{16,24},{20,12},{24,16},{28,4},{32,40},... | collective-permute-start | bytes 2138120 | tf_op jit(solution)/shard_map/ppermute | solution.py:28
  39.6 37.1 %collective-permute-start.16 = (bf16[2,256,1792]{2,1,0:T(8,128)(2,1)}, bf16[2,256,1792]{2,1,0:T(8,128)(2,1)}, u32[]{:S(2)}, u32[]{:S(2)}) collective-permute-start(bf16[2,256,1792]{2,1,0:T(8,128)(2,1)} %pad_maximum_fusion), channel_id=1, source_target_pairs={{0,1},{1,0},{2,3},{3,2},{4,7},{5,6},{6,5},{7,4},{8,9},{9,8},{10,11... | collective-permute-start | bytes 5505032 | tf_op jit(solution)/shard_map/ppermute | solution.py:36
  49.8 17.8 %collective-permute-start.12 = (bf16[8,24,3584]{2,1,0:T(8,128)(2,1)}, bf16[8,24,3584]{2,1,0:T(8,128)(2,1)}, u32[]{:S(2)}, u32[]{:S(2)}) collective-permute-start(bf16[8,24,3584]{2,1,0:T(8,128)(2,1)} %pad_maximum_fusion.8), channel_id=1, source_target_pairs={{0,96},{4,36},{8,104},{12,44},{16,112},{20,52},{24,120},{28,60},{3... | collective-permute-start | bytes 4128776 | tf_op jit(solution)/shard_map/ppermute | solution.py:28
  50.8 20.7 %collective-permute-start.6 = (bf16[8,24,3712]{2,1,0:T(8,128)(2,1)S(1)}, bf16[8,24,3712]{2,1,0:T(8,128)(2,1)S(1)}, u32[]{:S(2)}, u32[]{:S(2)}) collective-permute-start(bf16[8,24,3712]{2,1,0:T(8,128)(2,1)S(1)} %pad_maximum_fusion.6), channel_id=1, source_target_pairs={{0,24},{4,12},{8,16},{12,4},{16,8},{20,28},{24,0},{28,20},{32,56},... | collective-permute-start | bytes 4276232 | tf_op jit(solution)/shard_map/ppermute | solution.py:28
  52.6 31.5 %collective-permute-start.11 = (bf16[8,24,3584]{2,1,0:T(8,128)(2,1)}, bf16[8,24,3584]{2,1,0:T(8,128)(2,1)}, u32[]{:S(2)}, u32[]{:S(2)}) collective-permute-start(bf16[8,24,3584]{2,1,0:T(8,128)(2,1)} %pad_maximum_fusion.8), channel_id=1, source_target_pairs={{0,4},{4,0},{8,12},{12,8},{16,20},{20,16},{24,28},{28,24},{32,36},... | collective-permute-start | bytes 4128776 | tf_op jit(solution)/shard_map/ppermute | solution.py:28
  58.5 33.0 %collective-permute-start.7 = (bf16[8,24,3712]{2,1,0:T(8,128)(2,1)S(1)}, bf16[8,24,3712]{2,1,0:T(8,128)(2,1)}, u32[]{:S(2)}, u32[]{:S(2)}) collective-permute-start(bf16[8,24,3712]{2,1,0:T(8,128)(2,1)S(1)} %pad_maximum_fusion.6), channel_id=1, source_target_pairs={{0,4},{4,0},{8,12},{12,8},{16,20},{20,16},{24,28},{28,24},{32,36},... | collective-permute-start | bytes 4276232 | tf_op jit(solution)/shard_map/ppermute | solution.py:28
  67.6 32.6 %collective-permute-start.13 = (bf16[8,24,3584]{2,1,0:T(8,128)(2,1)}, bf16[8,24,3584]{2,1,0:T(8,128)(2,1)}, u32[]{:S(2)}, u32[]{:S(2)}) collective-permute-start(bf16[8,24,3584]{2,1,0:T(8,128)(2,1)} %collective-permute-done.12), channel_id=1, source_target_pairs={{0,4},{4,0},{8,12},{12,8},{16,20},{20,16},{24,28},{28,24},{32,36},... | collective-permute-start | bytes 4128776 | tf_op jit(solution)/shard_map/ppermute | solution.py:28
  71.6 36.0 %collective-permute-start.8 = (bf16[8,24,3712]{2,1,0:T(8,128)(2,1)S(1)}, bf16[8,24,3712]{2,1,0:T(8,128)(2,1)}, u32[]{:S(2)}, u32[]{:S(2)}) collective-permute-start(bf16[8,24,3712]{2,1,0:T(8,128)(2,1)S(1)} %collective-permute-done.6), channel_id=1, source_target_pairs={{0,4},{4,0},{8,12},{12,8},{16,20},{20,16},{24,28},{28,24},{32,36},... | collective-permute-start | bytes 4276232 | tf_op jit(solution)/shard_map/ppermute | solution.py:28
  79.4 46.8 %collective-permute-start.17 = (bf16[2,256,1792]{2,1,0:T(8,128)(2,1)}, bf16[2,256,1792]{2,1,0:T(8,128)(2,1)}, u32[]{:S(2)}, u32[]{:S(2)}) collective-permute-start(bf16[2,256,1792]{2,1,0:T(8,128)(2,1)} %pad_maximum_fusion.1), channel_id=1, source_target_pairs={{0,3},{1,2},{2,1},{3,0},{4,5},{5,4},{6,7},{7,6},{8,11},{9,10},{10,... | collective-permute-start | bytes 5505032 | tf_op jit(solution)/shard_map/ppermute | solution.py:36
  149.6 26.9 %all-to-all-start = ((bf16[16,24,1792]{2,1,0:T(8,128)(2,1)}), bf16[16,24,1792]{2,1,0:T(8,128)(2,1)S(1)}, u32[]{:S(2)}, u32[]{:S(2)}) async-start(bf16[16,24,1792]{2,1,0:T(8,128)(2,1)} %pad_maximum_fusion.9), calls=%async_computation | async-start | bytes 2752512 | tf_op jit(solution)/shard_map/all_to_all | solution.py:236
  201.6 14.9 %collective-permute-start.29 = (bf16[4,24,3584]{2,1,0:T(8,128)(2,1)S(1)}, bf16[4,24,3584]{2,1,0:T(8,128)(2,1)S(1)}, u32[]{:S(2)}, u32[]{:S(2)}) collective-permute-start(bf16[4,24,3584]{2,1,0:T(8,128)(2,1)S(1)} %pad_maximum_fusion.15), channel_id=1, source_target_pairs={{0,32},{4,100},{8,40},{12,108},{16,48},{20,116},{24,56},{28,124},{... | collective-permute-start | bytes 2064392 | tf_op jit(solution)/shard_map/ppermute | solution.py:28
  202.3 14.4 %collective-permute-start.24 = (bf16[4,24,3712]{2,1,0:T(8,128)(2,1)S(1)}, bf16[4,24,3712]{2,1,0:T(8,128)(2,1)S(1)}, u32[]{:S(2)}, u32[]{:S(2)}) collective-permute-start(bf16[4,24,3712]{2,1,0:T(8,128)(2,1)S(1)} %pad_maximum_fusion.13), channel_id=1, source_target_pairs={{0,8},{4,28},{8,0},{12,20},{16,24},{20,12},{24,16},{28,4},{32,40},... | collective-permute-start | bytes 2138120 | tf_op jit(solution)/shard_map/ppermute | solution.py:28
  216.6 20.0 %collective-permute-start.31 = (bf16[8,24,3584]{2,1,0:T(8,128)(2,1)S(1)}, bf16[8,24,3584]{2,1,0:T(8,128)(2,1)}, u32[]{:S(2)}, u32[]{:S(2)}) collective-permute-start(bf16[8,24,3584]{2,1,0:T(8,128)(2,1)S(1)} %pad_maximum_fusion.10), channel_id=1, source_target_pairs={{0,96},{4,36},{8,104},{12,44},{16,112},{20,52},{24,120},{28,60},{3... | collective-permute-start | bytes 4128776 | tf_op jit(solution)/shard_map/ppermute | solution.py:28
  216.9 27.4 %collective-permute-start.25 = (bf16[8,24,3712]{2,1,0:T(8,128)(2,1)S(1)}, bf16[8,24,3712]{2,1,0:T(8,128)(2,1)S(1)}, u32[]{:S(2)}, u32[]{:S(2)}) collective-permute-start(bf16[8,24,3712]{2,1,0:T(8,128)(2,1)S(1)} %pad_maximum_fusion.7), channel_id=1, source_target_pairs={{0,24},{4,12},{8,16},{12,4},{16,8},{20,28},{24,0},{28,20},{32,56},... | collective-permute-start | bytes 4276232 | tf_op jit(solution)/shard_map/ppermute | solution.py:28
  217.5 34.9 %collective-permute-start.35 = (bf16[2,256,1792]{2,1,0:T(8,128)(2,1)S(1)}, bf16[2,256,1792]{2,1,0:T(8,128)(2,1)S(1)}, u32[]{:S(2)}, u32[]{:S(2)}) collective-permute-start(bf16[2,256,1792]{2,1,0:T(8,128)(2,1)S(1)} %pad_maximum_fusion.2), channel_id=1, source_target_pairs={{0,1},{1,0},{2,3},{3,2},{4,7},{5,6},{6,5},{7,4},{8,9},{9,8},{10,11... | collective-permute-start | bytes 5505032 | tf_op jit(solution)/shard_map/ppermute | solution.py:36
  217.7 38.3 %collective-permute-start.30 = (bf16[8,24,3584]{2,1,0:T(8,128)(2,1)S(1)}, bf16[8,24,3584]{2,1,0:T(8,128)(2,1)S(1)}, u32[]{:S(2)}, u32[]{:S(2)}) collective-permute-start(bf16[8,24,3584]{2,1,0:T(8,128)(2,1)S(1)} %pad_maximum_fusion.10), channel_id=1, source_target_pairs={{0,4},{4,0},{8,12},{12,8},{16,20},{20,16},{24,28},{28,24},{32,36},... | collective-permute-start | bytes 4128776 | tf_op jit(solution)/shard_map/ppermute | solution.py:28
  235.9 28.6 %collective-permute-start.26 = (bf16[8,24,3712]{2,1,0:T(8,128)(2,1)S(1)}, bf16[8,24,3712]{2,1,0:T(8,128)(2,1)}, u32[]{:S(2)}, u32[]{:S(2)}) collective-permute-start(bf16[8,24,3712]{2,1,0:T(8,128)(2,1)S(1)} %pad_maximum_fusion.7), channel_id=1, source_target_pairs={{0,4},{4,0},{8,12},{12,8},{16,20},{20,16},{24,28},{28,24},{32,36},... | collective-permute-start | bytes 4276232 | tf_op jit(solution)/shard_map/ppermute | solution.py:28
  236.6 36.7 %collective-permute-start.32 = (bf16[8,24,3584]{2,1,0:T(8,128)(2,1)}, bf16[8,24,3584]{2,1,0:T(8,128)(2,1)}, u32[]{:S(2)}, u32[]{:S(2)}) collective-permute-start(bf16[8,24,3584]{2,1,0:T(8,128)(2,1)} %collective-permute-done.31), channel_id=1, source_target_pairs={{0,4},{4,0},{8,12},{12,8},{16,20},{20,16},{24,28},{28,24},{32,36},... | collective-permute-start | bytes 4128776 | tf_op jit(solution)/shard_map/ppermute | solution.py:28
  244.3 36.4 %collective-permute-start.27 = (bf16[8,24,3712]{2,1,0:T(8,128)(2,1)S(1)}, bf16[8,24,3712]{2,1,0:T(8,128)(2,1)}, u32[]{:S(2)}, u32[]{:S(2)}) collective-permute-start(bf16[8,24,3712]{2,1,0:T(8,128)(2,1)S(1)} %collective-permute-done.25), channel_id=1, source_target_pairs={{0,4},{4,0},{8,12},{12,8},{16,20},{20,16},{24,28},{28,24},{32,36},... | collective-permute-start | bytes 4276232 | tf_op jit(solution)/shard_map/ppermute | solution.py:28
  256.0 43.5 %collective-permute-start.36 = (bf16[2,256,1792]{2,1,0:T(8,128)(2,1)}, bf16[2,256,1792]{2,1,0:T(8,128)(2,1)}, u32[]{:S(2)}, u32[]{:S(2)}) collective-permute-start(bf16[2,256,1792]{2,1,0:T(8,128)(2,1)} %pad_maximum_fusion.3), channel_id=1, source_target_pairs={{0,3},{1,2},{2,1},{3,0},{4,5},{5,4},{6,7},{7,6},{8,11},{9,10},{10,... | collective-permute-start | bytes 5505032 | tf_op jit(solution)/shard_map/ppermute | solution.py:36
  330.3 24.9 %all-to-all-start.1 = ((bf16[16,24,1792]{2,1,0:T(8,128)(2,1)}), bf16[16,24,1792]{2,1,0:T(8,128)(2,1)S(1)}, u32[]{:S(2)}, u32[]{:S(2)}) async-start(bf16[16,24,1792]{2,1,0:T(8,128)(2,1)} %pad_maximum_fusion.11), calls=%async_computation.1 | async-start | bytes 2752512 | tf_op jit(solution)/shard_map/all_to_all | solution.py:236
  (49 other events, 405.2 us)

commit v3 on v1

v3 whole, which is shorter than its diff:
```python
import jax
import jax.numpy as jnp
from jax import lax
from jax.experimental import pallas as pl
from jax.experimental.pallas import tpu as pltpu
from jax.sharding import PartitionSpec as P

route_scale = 2.5
bf16, f32 = jnp.bfloat16, jnp.float32

Y_STEPS = ((2, 6), (6, 2))
X_STEPS = ((8, 24), (24, 8))
SIBLING = (1, 1)


def short(values):
    return lax.reduce_precision(values, 8, 7)


def thirds(values):
    high = short(values)
    middle = short(values - high)
    return [part.astype(bf16) for part in (high, middle, values - high - middle)]


def swap(block, masks):
    count = lax.axis_size("expert")
    return lax.ppermute(block, "expert", [(i, i ^ masks[i & 1]) for i in range(count)])


def z_swap(block, mask):
    count = lax.axis_size("tensor")
    return lax.ppermute(block, "tensor", [(i, i ^ mask) for i in range(count)])


def after(block, *others):
    return lax.optimization_barrier((block, *others))[0]


def gate_up_kernel(own_ref, other_ref, gate_ref, up_ref, out_ref):
    units = gate_ref.shape[-1]
    tokens = jnp.concatenate([own_ref[...], other_ref[...]], axis=0)
    gate = jnp.dot(tokens, gate_ref[0, 0], preferred_element_type=f32)
    up = jnp.dot(tokens, up_ref[0, 0], preferred_element_type=f32)

    @pl.when(pl.program_id(0) == 0)
    def _():
        out_ref[:, :units] = gate
        out_ref[:, units:] = up

    @pl.when(pl.program_id(0) > 0)
    def _():
        out_ref[:, :units] += gate
        out_ref[:, units:] += up


def gate_up(own, other, w_gate, w_up, layer, first):
    rows = own.shape[0]
    units = w_gate.shape[-1]
    width = w_gate.shape[2] // 2
    depth = width // 2
    tokens = pl.BlockSpec((rows, depth), lambda k: (0, k))
    weights = pl.BlockSpec((1, 1, depth, units), lambda k: (layer, 0, first // depth + k, 0))
    return pl.pallas_call(
        gate_up_kernel,
        grid=(width // depth,),
        in_specs=[tokens, tokens, weights, weights],
        out_specs=pl.BlockSpec((2 * rows, 2 * units), lambda k: (0, 0)),
        out_shape=jax.ShapeDtypeStruct((2 * rows, 2 * units), f32),
        compiler_params=pltpu.CompilerParams(vmem_limit_bytes=40 << 20),
        cost_estimate=pl.CostEstimate(
            flops=8 * rows * width * units,
            bytes_accessed=4 * (rows + units) * width + 16 * rows * units,
            transcendentals=0,
        ),
    )(own, other, w_gate, w_up)


def down_kernel(z_ref, *refs):
    acts, weights, out_ref = refs[:4], refs[4:-1], refs[-1]
    acts = jnp.concatenate([act[...] for act in acts], axis=1)
    weights = jnp.concatenate([weights[0][0, 0]] + [w[...] for w in weights[1:]], axis=0)
    out_ref[...] = jnp.dot(acts, weights, preferred_element_type=f32).astype(out_ref.dtype)


def down_product(z, acts, slots, w_down, layer, others):
    units = w_down.shape[2]
    part = others[0].shape[-1]
    steps = 2
    columns = part // steps
    act = pl.BlockSpec((slots, units), lambda n, z: (0, 0))
    return pl.pallas_call(
        down_kernel,
        grid_spec=pltpu.PrefetchScalarGridSpec(
            num_scalar_prefetch=1,
            grid=(steps,),
            in_specs=[act] * 4
            + [pl.BlockSpec((1, 1, units, columns), lambda n, z: (layer, 0, 0, z[0] * steps + n))]
            + [pl.BlockSpec((w.shape[0], columns), lambda n, z: (0, n)) for w in others],
            out_specs=pl.BlockSpec((slots, columns), lambda n, z: (0, n)),
        ),
        out_shape=jax.ShapeDtypeStruct((slots, part), bf16),
        compiler_params=pltpu.CompilerParams(vmem_limit_bytes=40 << 20),
        cost_estimate=pl.CostEstimate(
            flops=8 * slots * units * part,
            bytes_accessed=8 * units * (slots + part) + 2 * slots * part,
            transcendentals=0,
        ),
    )(jnp.full((1,), z, jnp.int32), *acts, w_down, *others)


def body(hidden_in, norm_gain, router, w_gate, w_up, w_down, routes):
    rows, part = hidden_in.shape
    layers, width, units = w_gate.shape[0], w_gate.shape[2], w_gate.shape[3]
    experts = router.shape[2]
    capacity = min(rows, 2 * rows * routes.shape[2] // experts)
    slots = experts * capacity
    chips = experts // 2
    half = width // 2
    me = lax.axis_index("expert")
    core = me & 1
    z = lax.axis_index("tensor")

    gains = jnp.stack(thirds(norm_gain), axis=0).reshape(3 * layers, part)
    opening = jnp.concatenate([hidden_in, gains, jnp.zeros((2, part), bf16)], axis=0)
    opening = lax.all_gather(opening, "tensor", axis=1, tiled=True)
    full = opening[:rows]
    gains = opening[rows : rows + 3 * layers].astype(f32).reshape(3, layers, width)
    gains = gains[0] + gains[1] + gains[2]

    bits = jnp.arange(chips, dtype=jnp.int32)
    sources = []
    for c in range(2):
        masks = [Y_STEPS[0][c], Y_STEPS[1][c], X_STEPS[0][c], X_STEPS[1][c]]
        total = jnp.zeros_like(bits)
        for n, mask in enumerate(masks):
            total = total ^ jnp.where(((bits >> n) & 1) == 1, mask, 0)
        sources.append(total)
    own_source = me ^ jnp.where(core == 1, sources[1], sources[0])
    other_source = (me ^ 1) ^ jnp.where(core == 1, sources[0], sources[1])
    source = jnp.concatenate([own_source, other_source])

    expert_iota = lax.broadcasted_iota(jnp.int32, (1, 1, 1, experts), 3)
    picks = jnp.any(routes[..., None] == expert_iota, axis=2)
    earlier = lax.broadcasted_iota(jnp.int32, (rows, rows), 0) >= lax.broadcasted_iota(
        jnp.int32, (rows, rows), 1
    )
    ranks = jnp.einsum("st,lte->lse", earlier.astype(bf16), picks.astype(bf16), preferred_element_type=f32)
    marks = jnp.where(picks, ranks, 0.0)
    marks_sent = jnp.pad(marks, ((0, 0), (0, 0), (0, 128 - experts))).astype(bf16)

    state = hidden_in
    for layer in range(layers):
        if layer:
            full = lax.all_gather(state, "tensor", axis=1, tiled=True)
        values = full.astype(f32)
        scale = lax.rsqrt(jnp.sum(values * values, axis=1) / width + 1e-06)
        normed = (values * scale[:, None] * gains[layer][None, :]).astype(bf16)

        def columns(mask, first, count, *bound):
            column = (after(z, *bound) ^ mask) * part
            block = lax.dynamic_slice(w_down, (layer, 0, first, column), (1, 1, count, part))
            return z_swap(block.reshape(count, part), mask)

        held_a = normed[None, :, :half]
        held_b = jnp.concatenate([normed[:, half:], marks_sent[layer]], axis=1)[None]
        near = [columns(mask, 0, units // 2, normed) for mask in (1, 3)]
        for step in range(3):
            if step == 2:
                held_a, held_b, *near = lax.optimization_barrier((held_a, held_b, *near))
                more = [columns(mask, units // 2, units // 2, held_a, held_b) for mask in (1, 3)]
            got_a = swap(held_a, (Y_STEPS + X_STEPS)[step])
            got_b = swap(held_b, (X_STEPS + Y_STEPS)[step])
            held_a = jnp.concatenate([held_a, got_a])
            held_b = jnp.concatenate([held_b, got_b])
        held_a, held_b, *more = lax.optimization_barrier((held_a, held_b, *more))
        far = columns(2, 0, units, held_a, held_b)
        last_a, last_b = swap(held_a, X_STEPS[1]), swap(held_b, Y_STEPS[1])
        other_a, other_b = swap(held_a, SIBLING), swap(held_b, SIBLING)

        def products(own, other, first):
            flat = [block.reshape(-1, block.shape[2]) for block in (own, other)]
            return gate_up(*flat, w_gate, w_up, layer, first)

        sums_a = products(held_a, other_a, 0)
        sums_b = products(held_b, other_b, half)
        last_a, last_b, sums_a, sums_b, far = lax.optimization_barrier(
            (last_a, last_b, sums_a, sums_b, far)
        )
        last_other_a, last_other_b = swap(last_a, SIBLING), swap(last_b, SIBLING)
        more_a = products(last_a, last_other_a, 0)
        more_b = products(last_b, last_other_b, half)

        mine = lax.broadcasted_iota(jnp.int32, (1, 1, 128), 2) == me
        mark = [
            jnp.sum(jnp.where(mine, block[:, :, half:].astype(f32), 0.0), axis=2)
            for block in (held_b, last_b, other_b, last_other_b)
        ]
        mark = jnp.concatenate(mark).reshape(2, 4, 4, rows).swapaxes(1, 2).reshape(2 * chips, rows)
        mark = mark.astype(jnp.int32)
        slot = jnp.where(mark > 0, source[:, None] * capacity + mark - 1, -1).reshape(1, -1)
        taken = (lax.broadcasted_iota(jnp.int32, (slots, 1), 0) == slot).astype(bf16)

        def in_order(held, last):
            blocks = (2, 2, 4, rows, 2 * units)
            return jnp.concatenate([held.reshape(blocks), last.reshape(blocks)], axis=1)

        sums = in_order(sums_a, more_a) + in_order(sums_b, more_b).swapaxes(1, 2)
        sums = sums.reshape(2 * chips * rows, 2 * units)
        act = (jax.nn.silu(sums[:, :units]) * sums[:, units:]).astype(bf16)
        act = jnp.dot(taken, act, preferred_element_type=f32).astype(bf16)


        own = state.astype(f32) * scale[:, None] * norm_gain[layer][None, :]
        own = own.astype(bf16).astype(f32)
        scores = jnp.dot(own, router[layer], precision=lax.Precision.HIGHEST)
        scores = jnp.pad(jnp.concatenate(thirds(scores), axis=1), ((0, 0), (0, units - 3 * experts)))
        act = jnp.concatenate([act, scores], axis=0)
        acts = [act] + [z_swap(act, mask) for mask in (1, 3, 2)]
        scores = sum(block[slots:].astype(f32) for block in acts)
        scores = sum(scores[:, experts * n : experts * (n + 1)] for n in range(3))
        others = [near[0], more[0], near[1], more[1], far]
        out = down_product(z, acts, slots, w_down, layer, others)
        probs = jax.nn.sigmoid(scores)
        picked = jnp.where(picks[layer], probs, 0.0)
        weights = route_scale * picked / jnp.sum(picked, axis=1, keepdims=True)
        slot_iota = lax.broadcasted_iota(jnp.int32, (1, 1, capacity), 2).astype(f32) + 1.0
        mixer = jnp.where(marks[layer][:, :, None] == slot_iota, weights[:, :, None], 0.0)
        mixer = jnp.concatenate(thirds(mixer.reshape(rows, slots))[:2], axis=0)

        returned = lax.all_to_all(
            out.reshape(experts, capacity, part), "expert", split_axis=0, concat_axis=0
        ).reshape(slots, part)
        mixed = jnp.dot(mixer, returned, preferred_element_type=f32)
        state = (state.astype(f32) + mixed[:rows] + mixed[rows:]).astype(bf16)
    return state


def solution(mesh):
    placed = (
        P("expert", "tensor"),
        P(None, "tensor"),
        P(None, "tensor", None),
        P(None, "expert", None, "tensor"),
        P(None, "expert", None, "tensor"),
        P(None, "expert", "tensor", None),
        P(None, "expert", None),
    )
    return jax.shard_map(
        body, mesh=mesh, in_specs=placed, out_specs=P("expert", "tensor"), check_vma=False
    )
```

time: 307 us -> 310 us (level)
  blocking collectives: 119 us -> 22.7 us
  waiting for transfers between devices: 63.8 us -> 119 us
  matrix products: 39.7 us -> 2.93 us
  starting transfers between devices: 24.5 us -> 59.3 us
  Pallas kernels: 0 us -> 32.7 us
  local copies, waits for them, and re-layouts: 36.7 us -> 58.3 us
  between operations: 13.8 us -> 1.11 us
  other arithmetic: 7.64 us -> 11.9 us
    ppermute x0 -> x40, waiting for transfers between devices: none -> 72.8 us  [the longest x16 39.4 us: z_swap(): return lax.ppermute(block, 'tensor', [(i, i ^ mask) for i in range(count)])]
    all_to_all x1 -> x0, blocking collectives: 45 us -> none  [body(): down = lax.all_to_all(down, 'tensor', split_axis=0, concat_axis=0)]
    ppermute x0 -> x40, starting transfers between devices: none -> 44.6 us  [the longest x24 28.9 us: swap(): lax.ppermute(block, 'expert', [(i, i ^ masks[i & 1]) for i in range(count)])]
    all_to_all x1 -> x0, waiting for transfers between devices: 40.9 us -> none  [body(): down = lax.all_to_all(down, 'tensor', split_axis=0, concat_axis=0)]
    dot_general x8 -> x3, matrix products: 38.6 us -> 1.73 us  [the longest x2 0.99 us: body(): act = jnp.dot(taken, act, preferred_element_type=f32).astype(bf16)]
    pallas_call x0 -> x10, Pallas kernels: none -> 32.7 us  [the longest x8 27.8 us: gate_up(): pl.pallas_call(gate_up_kernel, grid=(width // depth,), in_specs=[tokens,...]
    unnamed x10 -> x145, local copies, waits for them, and re-layouts: 11.9 us -> 39.7 us
    psum x2 -> x0, blocking collectives: 27.1 us -> none  [body(): probs = jax.nn.sigmoid(lax.psum(scores, 'tensor'))]
  transfers between devices with their start and end apart: 5 -> 42, of which waited for: 4 -> 27; matrix products, arithmetic and copies ran while one was open for 11% -> 6% of each run, Pallas kernels for 0% -> 7%
where the time goes in v3:
time: 310 us; the launch traced here: 308 us
  waiting for transfers between devices  119 us (38%)
  starting transfers between devices  59.3 us (19%)
  local copies, waits for them, and re-layouts  58.3 us (19%)
  Pallas kernels  32.7 us (11%)
  blocking collectives  22.7 us (7%)
  other arithmetic  11.9 us (4%)
    all_to_all x2, waiting for transfers between devices, body(): lax.all_to_all(out.reshape(experts, capacity, part), 'expert', split_axis...  46.5 us
    unnamed x145, local copies, waits for them, and re-layouts  39.7 us
    ppermute x16, waiting for transfers between devices, z_swap(): return lax.ppermute(block, 'tensor', [(i, i ^ mask) for i in range(count)])  39.4 us
    ppermute x24, waiting for transfers between devices, swap(): lax.ppermute(block, 'expert', [(i, i ^ masks[i & 1]) for i in range(count)])  33.4 us
    ppermute x24, starting transfers between devices, swap(): lax.ppermute(block, 'expert', [(i, i ^ masks[i & 1]) for i in range(count)])  28.9 us
    pallas_call x8, Pallas kernels, gate_up(): pl.pallas_call(gate_up_kernel, grid=(width // depth,), in_specs=[tokens,...  27.8 us
    ppermute x16, starting transfers between devices, z_swap(): return lax.ppermute(block, 'tensor', [(i, i ^ mask) for i in range(count)])  15.7 us
    all_to_all x2, starting transfers between devices, body(): lax.all_to_all(out.reshape(experts, capacity, part), 'expert', split_axis...  14.7 us
  transfers between devices with their start and end apart: 42, of which 27 were waited for; matrix products, arithmetic and copies ran while one was open for 6% of the time, Pallas kernels for 7%

profile of v3, /device:TPU:1, one launch (start us, length us, event | category | flops | bytes accessed | tf_op | source)
XLA Modules:
  0.0 308.2 jit_solution(11083025708468618928)
XLA Ops:
  1.9 13.1 %all_gather.6 = bf16[32,7168]{1,0:T(8,128)(2,1)S(1)} all-gather(bf16[32,1792]{1,0:T(8,128)(2,1)S(1)} %maximum_maximum_fusion), channel_id=1, replica_groups=mesh['expert'=32,'tensor'=4] {'tensor'}, dimensions={1}, use_global_device_ids=true | all-gather | bytes 573440 | tf_op jit(solution)/shard_map/all_gather | solution.py:126
  25.9 5.8 %collective-permute-done.1 = bf16[2,24,3584]{2,1,0:T(8,128)(2,1)S(1)} collective-permute-done((bf16[2,24,3584]{2,1,0:T(8,128)(2,1)S(1)}, bf16[2,24,3584]{2,1,0:T(8,128)(2,1)S(1)}, u32[]{:S(2)}, u32[]{:S(2)}) %collective-permute-start.1) | collective-permute-done | bytes 344096 | tf_op jit(solution)/shard_map/ppermute | solution.py:28
  32.3 3.3 %collective-permute-done.4.refs_5_ = bf16[128,1792]{1,0:T(8,128)(2,1)S(1)} collective-permute-done((bf16[128,1792]{1,0:T(8,128)(2,1)S(1)}, bf16[128,1792]{1,0:T(8,128)(2,1)S(1)}, u32[]{:S(2)}, u32[]{:S(2)}) %collective-permute-start.4) | collective-permute-done | bytes 458784 | tf_op jit(solution)/shard_map/ppermute | solution.py:33
  40.6 7.9 %collective-permute-done.6 = bf16[4,24,3584]{2,1,0:T(8,128)(2,1)S(1)} collective-permute-done((bf16[4,24,3584]{2,1,0:T(8,128)(2,1)S(1)}, bf16[4,24,3584]{2,1,0:T(8,128)(2,1)S(1)}, u32[]{:S(2)}, u32[]{:S(2)}) %collective-permute-start.6) | collective-permute-done | bytes 688160 | tf_op jit(solution)/shard_map/ppermute | solution.py:28
  61.9 3.4 %shard_map.73 = f32[384,512]{1,0:T(8,128)S(1)} custom-call(bf16[192,3584]{1,0:T(8,128)(2,1)S(1)} %bitcast.120, bf16[192,3584]{1,0:T(8,128)(2,1)} %bitcast.17.other_ref, bf16[2,1,7168,256]{3,2,1,0:T(8,128)(2,1)S(1)} %copy-done, bf16[2,1,7168,256]{3,2,1,0:T(8,128)(2,1)} %up_ref.15), custom_call_target="tpu_custom_call" | custom-call | flops 1409286144 | bytes 7208960 | tf_op jit(solution)/shard_map/pallas_call | solution.py:64
  66.2 3.5 %shard_map.74 = f32[384,512]{1,0:T(8,128)S(1)} custom-call(bf16[192,3712]{1,0:T(8,128)(2,1)S(1)} %bitcast.117, bf16[192,3712]{1,0:T(8,128)(2,1)} %bitcast.19.other_ref, bf16[2,1,7168,256]{3,2,1,0:T(8,128)(2,1)S(1)} %copy-done, bf16[2,1,7168,256]{3,2,1,0:T(8,128)(2,1)} %up_ref.15), custom_call_target="tpu_custom_call" | custom-call | flops 1409286144 | bytes 7208960 | tf_op jit(solution)/shard_map/pallas_call | solution.py:64
  70.6 6.7 %collective-permute-done.14.refs_9_ = bf16[256,1792]{1,0:T(8,128)(2,1)S(1)} collective-permute-done((bf16[256,1792]{1,0:T(8,128)(2,1)S(1)}, bf16[256,1792]{1,0:T(8,128)(2,1)S(1)}, u32[]{:S(2)}, u32[]{:S(2)}) %collective-permute-start.14) | collective-permute-done | bytes 917536 | tf_op jit(solution)/shard_map/ppermute | solution.py:33
  78.3 4.9 %collective-permute-start.16 = (bf16[8,24,3584]{2,1,0:T(8,128)(2,1)}, bf16[8,24,3584]{2,1,0:T(8,128)(2,1)S(1)}, u32[]{:S(2)}, u32[]{:S(2)}) collective-permute-start(bf16[8,24,3584]{2,1,0:T(8,128)(2,1)} %collective-permute-done.10), channel_id=1, source_target_pairs={{0,4},{4,0},{8,12},{12,8},{16,20},{20,16},{24,28},{28,24},{32,36},... | collective-permute-start | bytes 4128776 | tf_op jit(solution)/shard_map/ppermute | solution.py:28
  92.9 3.4 %shard_map.75 = f32[384,512]{1,0:T(8,128)S(1)} custom-call(bf16[192,3584]{1,0:T(8,128)(2,1)} %bitcast.24.own_ref, bf16[192,3584]{1,0:T(8,128)(2,1)S(1)} %bitcast.130, bf16[2,1,7168,256]{3,2,1,0:T(8,128)(2,1)S(1)} %copy-done.1, bf16[2,1,7168,256]{3,2,1,0:T(8,128)(2,1)} %up_ref.15), custom_call_target="tpu_custom_call" | custom-call | flops 1409286144 | bytes 7208960 | tf_op jit(solution)/shard_map/pallas_call | solution.py:64
  101.6 3.7 %shard_map.76 = f32[384,512]{1,0:T(8,128)S(1)} custom-call(bf16[192,3712]{1,0:T(8,128)(2,1)} %bitcast.28.own_ref, bf16[192,3712]{1,0:T(8,128)(2,1)} %bitcast.29.other_ref, bf16[2,1,7168,256]{3,2,1,0:T(8,128)(2,1)S(1)} %copy-done.2, bf16[2,1,7168,256]{3,2,1,0:T(8,128)(2,1)} %up_ref.15), custom_call_target="tpu_custom_call" | custom-call | flops 1409286144 | bytes 7208960 | tf_op jit(solution)/shard_map/pallas_call | solution.py:64
  115.0 3.4 %collective-permute-done.19.refs_3_ = bf16[408,256]{1,0:T(8,128)(2,1)S(1)} collective-permute-done((bf16[408,256]{1,0:T(8,128)(2,1)S(1)}, bf16[408,256]{1,0:T(8,128)(2,1)S(1)}, u32[]{:S(2)}, u32[]{:S(2)}) %collective-permute-start.19) | collective-permute-done | bytes 208928 | tf_op jit(solution)/shard_map/ppermute | solution.py:33
  123.3 3.3 %reshape.240 = bf16[32,12,1792]{2,1,0:T(8,128)(2,1)} reshape(bf16[384,1792]{1,0:T(8,128)(2,1)} %copy-done.8) | data formatting | bytes 2752512 | tf_op jit(solution)/shard_map/reshape | solution.py:232
  126.6 9.1 %all-to-all-start = ((bf16[32,12,1792]{2,1,0:T(8,128)(2,1)}), bf16[32,12,1792]{2,1,0:T(8,128)(2,1)S(1)}, u32[]{:S(2)}, u32[]{:S(2)}) async-start(bf16[32,12,1792]{2,1,0:T(8,128)(2,1)} %reshape.240), calls=%async_computation | async-start | bytes 3670016 | tf_op jit(solution)/shard_map/all_to_all | solution.py:231
  138.3 22.9 %all-to-all-done = bf16[32,12,1792]{2,1,0:T(8,128)(2,1)S(1)} async-done(((bf16[32,12,1792]{2,1,0:T(8,128)(2,1)}), bf16[32,12,1792]{2,1,0:T(8,128)(2,1)S(1)}, u32[]{:S(2)}, u32[]{:S(2)}) %all-to-all-start) | async-done | bytes 1376288 | tf_op jit(solution)/shard_map/all_to_all | solution.py:231
  162.5 9.6 %all_gather.7 = bf16[24,7168]{1,0:T(8,128)(2,1)S(1)} all-gather(bf16[24,1792]{1,0:T(8,128)(2,1)S(1)} %fusion.27), channel_id=1, replica_groups=mesh['expert'=32,'tensor'=4] {'tensor'}, dimensions={1}, use_global_device_ids=true | all-gather | bytes 430080 | tf_op jit(solution)/shard_map/all_gather | solution.py:155
  179.1 6.0 %collective-permute-done.21 = bf16[2,24,3584]{2,1,0:T(8,128)(2,1)S(1)} collective-permute-done((bf16[2,24,3584]{2,1,0:T(8,128)(2,1)S(1)}, bf16[2,24,3584]{2,1,0:T(8,128)(2,1)S(1)}, u32[]{:S(2)}, u32[]{:S(2)}) %collective-permute-start.21) | collective-permute-done | bytes 344096 | tf_op jit(solution)/shard_map/ppermute | solution.py:28
  216.4 3.3 %shard_map.78 = f32[384,512]{1,0:T(8,128)S(1)} custom-call(bf16[192,3584]{1,0:T(8,128)(2,1)S(1)} %bitcast.119, bf16[192,3584]{1,0:T(8,128)(2,1)} %bitcast.46.other_ref, bf16[2,1,7168,256]{3,2,1,0:T(8,128)(2,1)S(1)} %copy-done.3, bf16[2,1,7168,256]{3,2,1,0:T(8,128)(2,1)} %up_ref.15), custom_call_target="tpu_custom_call" | custom-call | flops 1409286144 | bytes 7208960 | tf_op jit(solution)/shard_map/pallas_call | solution.py:64
  220.8 3.5 %shard_map.79 = f32[384,512]{1,0:T(8,128)S(1)} custom-call(bf16[192,3712]{1,0:T(8,128)(2,1)S(1)} %bitcast.118, bf16[192,3712]{1,0:T(8,128)(2,1)} %bitcast.48.other_ref, bf16[2,1,7168,256]{3,2,1,0:T(8,128)(2,1)S(1)} %copy-done.3, bf16[2,1,7168,256]{3,2,1,0:T(8,128)(2,1)} %up_ref.15), custom_call_target="tpu_custom_call" | custom-call | flops 1409286144 | bytes 7208960 | tf_op jit(solution)/shard_map/pallas_call | solution.py:64
  225.2 10.5 %collective-permute-done.34.refs_9_ = bf16[256,1792]{1,0:T(8,128)(2,1)S(1)} collective-permute-done((bf16[256,1792]{1,0:T(8,128)(2,1)S(1)}, bf16[256,1792]{1,0:T(8,128)(2,1)S(1)}, u32[]{:S(2)}, u32[]{:S(2)}) %collective-permute-start.34) | collective-permute-done | bytes 917536 | tf_op jit(solution)/shard_map/ppermute | solution.py:33
  240.3 3.5 %shard_map.80 = f32[384,512]{1,0:T(8,128)S(1)} custom-call(bf16[192,3584]{1,0:T(8,128)(2,1)} %bitcast.53.own_ref, bf16[192,3584]{1,0:T(8,128)(2,1)S(1)} %bitcast.131, bf16[2,1,7168,256]{3,2,1,0:T(8,128)(2,1)S(1)} %copy-done.3, bf16[2,1,7168,256]{3,2,1,0:T(8,128)(2,1)} %up_ref.15), custom_call_target="tpu_custom_call" | custom-call | flops 1409286144 | bytes 7208960 | tf_op jit(solution)/shard_map/pallas_call | solution.py:64
  251.4 3.5 %shard_map.81 = f32[384,512]{1,0:T(8,128)S(1)} custom-call(bf16[192,3712]{1,0:T(8,128)(2,1)} %bitcast.57.own_ref, bf16[192,3712]{1,0:T(8,128)(2,1)S(1)} %bitcast.129, bf16[2,1,7168,256]{3,2,1,0:T(8,128)(2,1)S(1)} %copy-done.4, bf16[2,1,7168,256]{3,2,1,0:T(8,128)(2,1)} %up_ref.15), custom_call_target="tpu_custom_call" | custom-call | flops 1409286144 | bytes 7208960 | tf_op jit(solution)/shard_map/pallas_call | solution.py:64
  272.4 3.3 %reshape.260 = bf16[32,12,1792]{2,1,0:T(8,128)(2,1)} reshape(bf16[384,1792]{1,0:T(8,128)(2,1)} %copy-done.7) | data formatting | bytes 2752512 | tf_op jit(solution)/shard_map/reshape | solution.py:232
  275.7 5.6 %all-to-all-start.1 = ((bf16[32,12,1792]{2,1,0:T(8,128)(2,1)}), bf16[32,12,1792]{2,1,0:T(8,128)(2,1)S(1)}, u32[]{:S(2)}, u32[]{:S(2)}) async-start(bf16[32,12,1792]{2,1,0:T(8,128)(2,1)} %reshape.260), calls=%async_computation.1 | async-start | bytes 3670016 | tf_op jit(solution)/shard_map/all_to_all | solution.py:231
  283.2 23.7 %all-to-all-done.1 = bf16[32,12,1792]{2,1,0:T(8,128)(2,1)S(1)} async-done(((bf16[32,12,1792]{2,1,0:T(8,128)(2,1)}), bf16[32,12,1792]{2,1,0:T(8,128)(2,1)S(1)}, u32[]{:S(2)}, u32[]{:S(2)}) %all-to-all-start.1) | async-done | bytes 1376288 | tf_op jit(solution)/shard_map/all_to_all | solution.py:231
  (313 shorter events, 140.2 us)
Async XLA Ops:
  23.7 11.9 %collective-permute-start.4 = (bf16[128,1792]{1,0:T(8,128)(2,1)S(1)}, bf16[128,1792]{1,0:T(8,128)(2,1)S(1)}, u32[]{:S(2)}, u32[]{:S(2)}) collective-permute-start(bf16[128,1792]{1,0:T(8,128)(2,1)S(1)} %get-tuple-element.90), channel_id=1, source_target_pairs={{0,1},{1,0},{2,3},{3,2},{4,5},{5,4},{6,7},{7,6},{8,9},{9,8},{10,11... | collective-permute-start | bytes 1376264 | tf_op jit(solution)/shard_map/ppermute | solution.py:33
  23.8 12.6 %collective-permute-start.5 = (bf16[128,1792]{1,0:T(8,128)(2,1)S(1)}, bf16[128,1792]{1,0:T(8,128)(2,1)S(1)}, u32[]{:S(2)}, u32[]{:S(2)}) collective-permute-start(bf16[128,1792]{1,0:T(8,128)(2,1)S(1)} %get-tuple-element.89), channel_id=1, source_target_pairs={{0,3},{1,2},{2,1},{3,0},{4,7},{5,6},{6,5},{7,4},{8,11},{9,10},{10,... | collective-permute-start | bytes 1376264 | tf_op jit(solution)/shard_map/ppermute | solution.py:33
  37.2 11.3 %collective-permute-start.6 = (bf16[4,24,3584]{2,1,0:T(8,128)(2,1)S(1)}, bf16[4,24,3584]{2,1,0:T(8,128)(2,1)S(1)}, u32[]{:S(2)}, u32[]{:S(2)}) collective-permute-start(bf16[4,24,3584]{2,1,0:T(8,128)(2,1)S(1)} %pad_maximum_fusion.8), channel_id=1, source_target_pairs={{0,32},{4,100},{8,40},{12,108},{16,48},{20,116},{24,56},{28,124},{... | collective-permute-start | bytes 2064392 | tf_op jit(solution)/shard_map/ppermute | solution.py:28
  37.2 11.6 %collective-permute-start.7 = (bf16[4,24,3712]{2,1,0:T(8,128)(2,1)S(1)}, bf16[4,24,3712]{2,1,0:T(8,128)(2,1)}, u32[]{:S(2)}, u32[]{:S(2)}) collective-permute-start(bf16[4,24,3712]{2,1,0:T(8,128)(2,1)S(1)} %pad_maximum_fusion.6), channel_id=1, source_target_pairs={{0,8},{4,28},{8,0},{12,20},{16,24},{20,12},{24,16},{28,4},{32,40},... | collective-permute-start | bytes 2138120 | tf_op jit(solution)/shard_map/ppermute | solution.py:28
  38.4 11.6 %collective-permute-start.8 = (bf16[128,1792]{1,0:T(8,128)(2,1)S(1)}, bf16[128,1792]{1,0:T(8,128)(2,1)S(1)}, u32[]{:S(2)}, u32[]{:S(2)}) collective-permute-start(bf16[128,1792]{1,0:T(8,128)(2,1)S(1)} %get-tuple-element.88), channel_id=1, source_target_pairs={{0,1},{1,0},{2,3},{3,2},{4,5},{5,4},{6,7},{7,6},{8,9},{9,8},{10,11... | collective-permute-start | bytes 1376264 | tf_op jit(solution)/shard_map/ppermute | solution.py:33
  39.3 11.6 %collective-permute-start.9 = (bf16[128,1792]{1,0:T(8,128)(2,1)S(1)}, bf16[128,1792]{1,0:T(8,128)(2,1)S(1)}, u32[]{:S(2)}, u32[]{:S(2)}) collective-permute-start(bf16[128,1792]{1,0:T(8,128)(2,1)S(1)} %get-tuple-element.87), channel_id=1, source_target_pairs={{0,3},{1,2},{2,1},{3,0},{4,7},{5,6},{6,5},{7,4},{8,11},{9,10},{10,... | collective-permute-start | bytes 1376264 | tf_op jit(solution)/shard_map/ppermute | solution.py:33
  54.3 11.9 %collective-permute-start.13 = (bf16[8,24,3712]{2,1,0:T(8,128)(2,1)S(1)}, bf16[8,24,3712]{2,1,0:T(8,128)(2,1)}, u32[]{:S(2)}, u32[]{:S(2)}) collective-permute-start(bf16[8,24,3712]{2,1,0:T(8,128)(2,1)S(1)} %pad_maximum_fusion.2), channel_id=1, source_target_pairs={{0,4},{4,0},{8,12},{12,8},{16,20},{20,16},{24,28},{28,24},{32,36},... | collective-permute-start | bytes 4276232 | tf_op jit(solution)/shard_map/ppermute | solution.py:28
  54.3 24.0 %collective-permute-start.11 = (bf16[8,24,3712]{2,1,0:T(8,128)(2,1)S(1)}, bf16[8,24,3712]{2,1,0:T(8,128)(2,1)}, u32[]{:S(2)}, u32[]{:S(2)}) collective-permute-start(bf16[8,24,3712]{2,1,0:T(8,128)(2,1)S(1)} %pad_maximum_fusion.2), channel_id=1, source_target_pairs={{0,24},{4,12},{8,16},{12,4},{16,8},{20,28},{24,0},{28,20},{32,56},... | collective-permute-start | bytes 4276232 | tf_op jit(solution)/shard_map/ppermute | solution.py:28
  55.0 23.4 %collective-permute-start.10 = (bf16[8,24,3584]{2,1,0:T(8,128)(2,1)S(1)}, bf16[8,24,3584]{2,1,0:T(8,128)(2,1)}, u32[]{:S(2)}, u32[]{:S(2)}) collective-permute-start(bf16[8,24,3584]{2,1,0:T(8,128)(2,1)S(1)} %pad_maximum_fusion.4), channel_id=1, source_target_pairs={{0,96},{4,36},{8,104},{12,44},{16,112},{20,52},{24,120},{28,60},{3... | collective-permute-start | bytes 4128776 | tf_op jit(solution)/shard_map/ppermute | solution.py:28
  57.9 19.4 %collective-permute-start.14 = (bf16[256,1792]{1,0:T(8,128)(2,1)S(1)}, bf16[256,1792]{1,0:T(8,128)(2,1)S(1)}, u32[]{:S(2)}, u32[]{:S(2)}) collective-permute-start(bf16[256,1792]{1,0:T(8,128)(2,1)S(1)} %dynamic-slice_bitcast_fusion.1), channel_id=1, source_target_pairs={{0,2},{1,3},{2,0},{3,1},{4,6},{5,7},{6,4},{7,5},{8,10},{9,11},{10,... | collective-permute-start | bytes 2752520 | tf_op jit(solution)/shard_map/ppermute | solution.py:33
  83.3 14.0 %collective-permute-start.15 = (bf16[8,24,3712]{2,1,0:T(8,128)(2,1)}, bf16[8,24,3712]{2,1,0:T(8,128)(2,1)}, u32[]{:S(2)}, u32[]{:S(2)}) collective-permute-start(bf16[8,24,3712]{2,1,0:T(8,128)(2,1)} %collective-permute-done.11), channel_id=1, source_target_pairs={{0,4},{4,0},{8,12},{12,8},{16,20},{20,16},{24,28},{28,24},{32,36},... | collective-permute-start | bytes 4276232 | tf_op jit(solution)/shard_map/ppermute | solution.py:28
  107.8 10.5 %collective-permute-start.19 = (bf16[408,256]{1,0:T(8,128)(2,1)S(1)}, bf16[408,256]{1,0:T(8,128)(2,1)S(1)}, u32[]{:S(2)}, u32[]{:S(2)}) collective-permute-start(bf16[408,256]{1,0:T(8,128)(2,1)S(1)} %pad_maximum_fusion.14.refs_0_), channel_id=1, source_target_pairs={{0,2},{1,3},{2,0},{3,1},{4,6},{5,7},{6,4},{7,5},{8,10},{9,11},{10,... | collective-permute-start | bytes 626696 | tf_op jit(solution)/shard_map/ppermute | solution.py:33
  126.6 34.6 %all-to-all-start = ((bf16[32,12,1792]{2,1,0:T(8,128)(2,1)}), bf16[32,12,1792]{2,1,0:T(8,128)(2,1)S(1)}, u32[]{:S(2)}, u32[]{:S(2)}) async-start(bf16[32,12,1792]{2,1,0:T(8,128)(2,1)} %reshape.240), calls=%async_computation | async-start | bytes 3670016 | tf_op jit(solution)/shard_map/all_to_all | solution.py:231
  175.5 10.1 %collective-permute-start.24 = (bf16[128,1792]{1,0:T(8,128)(2,1)S(1)}, bf16[128,1792]{1,0:T(8,128)(2,1)S(1)}, u32[]{:S(2)}, u32[]{:S(2)}) collective-permute-start(bf16[128,1792]{1,0:T(8,128)(2,1)S(1)} %get-tuple-element.86), channel_id=1, source_target_pairs={{0,1},{1,0},{2,3},{3,2},{4,5},{5,4},{6,7},{7,6},{8,9},{9,8},{10,11... | collective-permute-start | bytes 1376264 | tf_op jit(solution)/shard_map/ppermute | solution.py:33
  175.9 10.9 %collective-permute-start.25 = (bf16[128,1792]{1,0:T(8,128)(2,1)S(1)}, bf16[128,1792]{1,0:T(8,128)(2,1)S(1)}, u32[]{:S(2)}, u32[]{:S(2)}) collective-permute-start(bf16[128,1792]{1,0:T(8,128)(2,1)S(1)} %get-tuple-element.85), channel_id=1, source_target_pairs={{0,3},{1,2},{2,1},{3,0},{4,7},{5,6},{6,5},{7,4},{8,11},{9,10},{10,... | collective-permute-start | bytes 1376264 | tf_op jit(solution)/shard_map/ppermute | solution.py:33
  187.6 11.0 %collective-permute-start.26 = (bf16[4,24,3584]{2,1,0:T(8,128)(2,1)S(1)}, bf16[4,24,3584]{2,1,0:T(8,128)(2,1)S(1)}, u32[]{:S(2)}, u32[]{:S(2)}) collective-permute-start(bf16[4,24,3584]{2,1,0:T(8,128)(2,1)S(1)} %pad_maximum_fusion.9), channel_id=1, source_target_pairs={{0,32},{4,100},{8,40},{12,108},{16,48},{20,116},{24,56},{28,124},{... | collective-permute-start | bytes 2064392 | tf_op jit(solution)/shard_map/ppermute | solution.py:28
  189.8 12.0 %collective-permute-start.27 = (bf16[4,24,3712]{2,1,0:T(8,128)(2,1)S(1)}, bf16[4,24,3712]{2,1,0:T(8,128)(2,1)}, u32[]{:S(2)}, u32[]{:S(2)}) collective-permute-start(bf16[4,24,3712]{2,1,0:T(8,128)(2,1)S(1)} %pad_maximum_fusion.7), channel_id=1, source_target_pairs={{0,8},{4,28},{8,0},{12,20},{16,24},{20,12},{24,16},{28,4},{32,40},... | collective-permute-start | bytes 2138120 | tf_op jit(solution)/shard_map/ppermute | solution.py:28
  194.2 11.0 %collective-permute-start.29 = (bf16[128,1792]{1,0:T(8,128)(2,1)S(1)}, bf16[128,1792]{1,0:T(8,128)(2,1)S(1)}, u32[]{:S(2)}, u32[]{:S(2)}) collective-permute-start(bf16[128,1792]{1,0:T(8,128)(2,1)S(1)} %get-tuple-element.83), channel_id=1, source_target_pairs={{0,3},{1,2},{2,1},{3,0},{4,7},{5,6},{6,5},{7,4},{8,11},{9,10},{10,... | collective-permute-start | bytes 1376264 | tf_op jit(solution)/shard_map/ppermute | solution.py:33
  209.2 11.5 %collective-permute-start.33 = (bf16[8,24,3712]{2,1,0:T(8,128)(2,1)S(1)}, bf16[8,24,3712]{2,1,0:T(8,128)(2,1)}, u32[]{:S(2)}, u32[]{:S(2)}) collective-permute-start(bf16[8,24,3712]{2,1,0:T(8,128)(2,1)S(1)} %pad_maximum_fusion.3), channel_id=1, source_target_pairs={{0,4},{4,0},{8,12},{12,8},{16,20},{20,16},{24,28},{28,24},{32,36},... | collective-permute-start | bytes 4276232 | tf_op jit(solution)/shard_map/ppermute | solution.py:28
  209.2 27.4 %collective-permute-start.31 = (bf16[8,24,3712]{2,1,0:T(8,128)(2,1)S(1)}, bf16[8,24,3712]{2,1,0:T(8,128)(2,1)}, u32[]{:S(2)}, u32[]{:S(2)}) collective-permute-start(bf16[8,24,3712]{2,1,0:T(8,128)(2,1)S(1)} %pad_maximum_fusion.3), channel_id=1, source_target_pairs={{0,24},{4,12},{8,16},{12,4},{16,8},{20,28},{24,0},{28,20},{32,56},... | collective-permute-start | bytes 4276232 | tf_op jit(solution)/shard_map/ppermute | solution.py:28
  209.2 27.4 %collective-permute-start.30 = (bf16[8,24,3584]{2,1,0:T(8,128)(2,1)S(1)}, bf16[8,24,3584]{2,1,0:T(8,128)(2,1)}, u32[]{:S(2)}, u32[]{:S(2)}) collective-permute-start(bf16[8,24,3584]{2,1,0:T(8,128)(2,1)S(1)} %pad_maximum_fusion.5), channel_id=1, source_target_pairs={{0,96},{4,36},{8,104},{12,44},{16,112},{20,52},{24,120},{28,60},{3... | collective-permute-start | bytes 4128776 | tf_op jit(solution)/shard_map/ppermute | solution.py:28
  212.1 23.6 %collective-permute-start.34 = (bf16[256,1792]{1,0:T(8,128)(2,1)S(1)}, bf16[256,1792]{1,0:T(8,128)(2,1)S(1)}, u32[]{:S(2)}, u32[]{:S(2)}) collective-permute-start(bf16[256,1792]{1,0:T(8,128)(2,1)S(1)} %dynamic-slice_bitcast_fusion), channel_id=1, source_target_pairs={{0,2},{1,3},{2,0},{3,1},{4,6},{5,7},{6,4},{7,5},{8,10},{9,11},{10,... | collective-permute-start | bytes 2752520 | tf_op jit(solution)/shard_map/ppermute | solution.py:33
  257.4 10.1 %collective-permute-start.39 = (bf16[408,256]{1,0:T(8,128)(2,1)S(1)}, bf16[408,256]{1,0:T(8,128)(2,1)S(1)}, u32[]{:S(2)}, u32[]{:S(2)}) collective-permute-start(bf16[408,256]{1,0:T(8,128)(2,1)S(1)} %pad_maximum_fusion.15.refs_0_), channel_id=1, source_target_pairs={{0,2},{1,3},{2,0},{3,1},{4,6},{5,7},{6,4},{7,5},{8,10},{9,11},{10,... | collective-permute-start | bytes 626696 | tf_op jit(solution)/shard_map/ppermute | solution.py:33
  275.7 31.2 %all-to-all-start.1 = ((bf16[32,12,1792]{2,1,0:T(8,128)(2,1)}), bf16[32,12,1792]{2,1,0:T(8,128)(2,1)S(1)}, u32[]{:S(2)}, u32[]{:S(2)}) async-start(bf16[32,12,1792]{2,1,0:T(8,128)(2,1)} %reshape.260), calls=%async_computation.1 | async-start | bytes 3670016 | tf_op jit(solution)/shard_map/all_to_all | solution.py:231
  (90 other events, 668.5 us)

commit v4 on v1

v4 whole, which is shorter than its diff:
```python
import functools

import jax
import jax.numpy as jnp
from jax import lax
from jax.experimental import pallas as pl
from jax.experimental.pallas import tpu as pltpu
from jax.sharding import PartitionSpec as P

route_scale = 2.5
bf16, f32 = jnp.bfloat16, jnp.float32

ORDER = (0, 1, 3, 2)


def short(values):
    return lax.reduce_precision(values, 8, 7)


def thirds(values):
    high = short(values)
    middle = short(values - high)
    return [part.astype(bf16) for part in (high, middle, values - high - middle)]


def z_swap(block, mask):
    count = lax.axis_size("tensor")
    return lax.ppermute(block, "tensor", [(i, i ^ mask) for i in range(count)])


def after(block, *others):
    return lax.optimization_barrier((block, *others))[0]


def gate_up_kernel(z_ref, tokens_ref, gate_ref, up_ref, act_ref, gate_sum, up_sum):
    step = pl.program_id(0)
    gate = jnp.dot(tokens_ref[...], gate_ref[0, 0], preferred_element_type=f32)
    up = jnp.dot(tokens_ref[...], up_ref[0, 0], preferred_element_type=f32)

    @pl.when(step == 0)
    def _():
        gate_sum[...] = gate
        up_sum[...] = up

    @pl.when(step > 0)
    def _():
        gate_sum[...] += gate
        up_sum[...] += up

    @pl.when(step == pl.num_programs(0) - 1)
    def _():
        gate = gate_sum[...]
        act_ref[...] = (gate / (1.0 + jnp.exp(-gate)) * up_sum[...]).astype(act_ref.dtype)


def gate_up(z, tokens, w_gate, w_up, layer):
    rows, units = tokens.shape[0], w_gate.shape[-1]
    depth = w_gate.shape[2] // 4
    weights = pl.BlockSpec((1, 1, depth, units), lambda k, z: (layer, 0, z[0] ^ k ^ (k >> 1), 0))
    return pl.pallas_call(
        gate_up_kernel,
        grid_spec=pltpu.PrefetchScalarGridSpec(
            num_scalar_prefetch=1,
            grid=(4,),
            in_specs=[pl.BlockSpec((rows, depth), lambda k, z: (0, k)), weights, weights],
            out_specs=pl.BlockSpec((rows, units), lambda k, z: (0, 0)),
            scratch_shapes=[pltpu.VMEM((rows, units), f32)] * 2,
        ),
        out_shape=jax.ShapeDtypeStruct((rows, units), bf16),
        cost_estimate=pl.CostEstimate(
            flops=16 * rows * depth * units,
            bytes_accessed=8 * (rows + 2 * units) * depth + 2 * rows * units,
            transcendentals=rows * units,
        ),
    )(jnp.full((1,), z, jnp.int32), tokens, w_gate, w_up)


def down_kernel(capacity, padded, z_ref, *refs):
    acts, weights, out_ref, held = refs[:4], refs[4:-2], refs[-2], refs[-1]

    @pl.when(pl.program_id(0) == 0)
    def _():
        slots = acts[0].shape[0]
        row = lax.broadcasted_iota(jnp.int32, (slots // capacity * padded, slots), 0)
        slot = lax.broadcasted_iota(jnp.int32, row.shape, 1)
        place = row % padded
        here = (place < capacity) & (row // padded * capacity + place == slot)
        joined = jnp.concatenate([act[...] for act in acts], axis=1)
        spread = jnp.dot(here.astype(bf16), joined, preferred_element_type=f32)
        held[...] = spread.astype(bf16)

    weights = jnp.concatenate([weights[0][0, 0]] + [w[...] for w in weights[1:]], axis=0)
    out_ref[...] = jnp.dot(held[...], weights, preferred_element_type=f32).astype(out_ref.dtype)


def down_product(z, acts, slots, capacity, padded, w_down, layer, others):
    units = w_down.shape[2]
    part = others[0].shape[-1]
    rows = slots // capacity * padded
    steps = 2
    columns = part // steps
    act = pl.BlockSpec((slots, units), lambda n, z: (0, 0))
    return pl.pallas_call(
        functools.partial(down_kernel, capacity, padded),
        grid_spec=pltpu.PrefetchScalarGridSpec(
            num_scalar_prefetch=1,
            grid=(steps,),
            in_specs=[act] * 4
            + [pl.BlockSpec((1, 1, units, columns), lambda n, z: (layer, 0, 0, z[0] * steps + n))]
            + [pl.BlockSpec((w.shape[0], columns), lambda n, z: (0, n)) for w in others],
            out_specs=pl.BlockSpec((rows, columns), lambda n, z: (0, n)),
            scratch_shapes=[pltpu.VMEM((rows, 4 * units), bf16)],
        ),
        out_shape=jax.ShapeDtypeStruct((rows, part), bf16),
        cost_estimate=pl.CostEstimate(
            flops=8 * rows * units * (part + slots),
            bytes_accessed=8 * units * (slots + part) + 2 * rows * part,
            transcendentals=0,
        ),
    )(jnp.full((1,), z, jnp.int32), *acts, w_down, *others)


def body(hidden_in, norm_gain, router, w_gate, w_up, w_down, routes):
    rows, part = hidden_in.shape
    layers, width, units = w_gate.shape[0], w_gate.shape[2], w_gate.shape[3]
    experts = router.shape[2]
    capacity = min(rows, 2 * rows * routes.shape[2] // experts)
    slots = experts * capacity
    padded = -(-capacity // 16) * 16
    me = lax.axis_index("expert")
    z = lax.axis_index("tensor")

    expert_iota = lax.broadcasted_iota(jnp.int32, (1, 1, 1, experts), 3)
    picks = jnp.any(routes[..., None] == expert_iota, axis=2)
    earlier = lax.broadcasted_iota(jnp.int32, (rows, rows), 0) >= lax.broadcasted_iota(
        jnp.int32, (rows, rows), 1
    )
    ranks = jnp.einsum("st,lte->lse", earlier.astype(bf16), picks.astype(bf16), preferred_element_type=f32)
    marks = jnp.where(picks, ranks, 0.0)
    marks_sent = jnp.pad(marks, ((0, 0), (0, 0), (0, 128 - experts))).astype(bf16)

    def spread(block):
        return [block] + [z_swap(block, mask) for mask in ORDER[1:]]

    def columns(layer, mask, first, count, *bound):
        column = (after(z, *bound) ^ mask) * part
        block = lax.dynamic_slice(w_down, (layer, 0, first, column), (1, 1, count, part))
        return z_swap(block.reshape(count, part), mask)

    state = hidden_in
    gains = jnp.stack(thirds(norm_gain), axis=0).reshape(3 * layers, part)
    gains = spread(jnp.pad(gains, ((0, 8 - 3 * layers), (0, 0))))
    gains = [
        block[: 3 * layers].astype(f32).reshape(3, layers, part).sum(axis=0) for block in gains
    ]
    for layer in range(layers):
        blocks = [block.astype(f32) for block in spread(state)]
        scale = sum(jnp.sum(block * block, axis=1) for block in blocks)
        scale = lax.rsqrt(scale / width + 1e-06)
        normed = [
            (block * scale[:, None] * gain[layer][None, :]).astype(bf16)
            for block, gain in zip(blocks, gains)
        ]

        sent = jnp.concatenate(normed + [marks_sent[layer]], axis=1)
        arrived = lax.all_gather(sent, "expert", axis=0, tiled=True)
        others = [columns(layer, mask, 0, units, sent) for mask in ORDER[1:]]
        arrived, *others = lax.optimization_barrier((arrived, *others))
        act = gate_up(z, arrived, w_gate, w_up, layer)

        mine = lax.broadcasted_iota(jnp.int32, (1, 128), 1) == me
        mark = jnp.sum(jnp.where(mine, arrived[:, width:].astype(f32), 0.0), axis=1).astype(jnp.int32)
        source = lax.broadcasted_iota(jnp.int32, (experts, rows), 0).reshape(-1)
        slot = jnp.where(mark > 0, source * capacity + mark - 1, -1)[None, :]
        taken = (lax.broadcasted_iota(jnp.int32, (slots, 1), 0) == slot).astype(bf16)

        act = jnp.dot(taken, act, preferred_element_type=f32).astype(bf16)

        own = state.astype(f32) * scale[:, None] * norm_gain[layer][None, :]
        own = own.astype(bf16).astype(f32)
        scores = jnp.dot(own, router[layer], precision=lax.Precision.HIGHEST)
        scores = jnp.pad(jnp.concatenate(thirds(scores), axis=1), ((0, 0), (0, units - 3 * experts)))
        act = jnp.concatenate([act, scores], axis=0)
        acts = spread(act)
        scores = sum(block[slots:].astype(f32) for block in acts)
        scores = sum(scores[:, experts * n : experts * (n + 1)] for n in range(3))
        out = down_product(z, acts, slots, capacity, padded, w_down, layer, others)
        probs = jax.nn.sigmoid(scores)
        picked = jnp.where(picks[layer], probs, 0.0)
        weights = route_scale * picked / jnp.sum(picked, axis=1, keepdims=True)
        slot_iota = lax.broadcasted_iota(jnp.int32, (1, 1, padded), 2).astype(f32) + 1.0
        mixer = jnp.where(marks[layer][:, :, None] == slot_iota, weights[:, :, None], 0.0)
        mixer = jnp.concatenate(thirds(mixer.reshape(rows, experts * padded))[:2], axis=0)

        returned = lax.all_to_all(
            out.reshape(experts, padded, part), "expert", split_axis=0, concat_axis=0
        ).reshape(experts * padded, part)
        mixed = jnp.dot(mixer, returned, preferred_element_type=f32)
        state = (state.astype(f32) + mixed[:rows] + mixed[rows:]).astype(bf16)
    return state


def solution(mesh):
    placed = (
        P("expert", "tensor"),
        P(None, "tensor"),
        P(None, "tensor", None),
        P(None, "expert", None, "tensor"),
        P(None, "expert", None, "tensor"),
        P(None, "expert", "tensor", None),
        P(None, "expert", None),
    )
    return jax.shard_map(
        body, mesh=mesh, in_specs=placed, out_specs=P("expert", "tensor"), check_vma=False
    )
```

time: 307 us -> 294 us (0.958)
  blocking collectives: 119 us -> 0 us
  waiting for transfers between devices: 63.8 us -> 178 us
  matrix products: 39.7 us -> 5.13 us
  Pallas kernels: 0 us -> 34 us
  local copies, waits for them, and re-layouts: 36.7 us -> 11.3 us
  starting transfers between devices: 24.5 us -> 40.5 us
    ppermute x0 -> x21, waiting for transfers between devices: none -> 95.9 us  [z_swap(): return lax.ppermute(block, 'tensor', [(i, i ^ mask) for i in range(count)])]
    all_gather x4 -> x0, blocking collectives: 47.2 us -> none  [the longest x2 24.4 us: body(): act = lax.all_gather(act, 'tensor', axis=1, tiled=True)]
    all_to_all x1 -> x0, blocking collectives: 45 us -> none  [body(): down = lax.all_to_all(down, 'tensor', split_axis=0, concat_axis=0)]
    dot_general x8 -> x3, matrix products: 38.6 us -> 2.76 us  [the longest x2 2.64 us: body(): act = jnp.dot(taken, act, preferred_element_type=f32).astype(bf16)]
    pallas_call x0 -> x4, Pallas kernels: none -> 34 us  [the longest x2 21.8 us: gate_up(): pl.pallas_call(gate_up_kernel, grid_spec=pltpu.PrefetchScalarGridSpec(num...]
    all_gather x2, waiting for transfers between devices: 2.08 us -> 35.4 us  [body(): arrived = lax.all_gather(sent, 'expert', axis=0, tiled=True)]
    psum x2 -> x0, blocking collectives: 27.1 us -> none  [body(): probs = jax.nn.sigmoid(lax.psum(scores, 'tensor'))]
    ppermute x0 -> x21, starting transfers between devices: none -> 27 us  [z_swap(): return lax.ppermute(block, 'tensor', [(i, i ^ mask) for i in range(count)])]
  transfers between devices with their start and end apart: 5 -> 25, of which waited for: 4 -> 18; matrix products, arithmetic and copies ran while one was open for 11% -> 5% of each run, Pallas kernels for 0% -> 0%
where the time goes in v4:
time: 294 us; the launch traced here: 293 us
  waiting for transfers between devices  178 us (61%)
  starting transfers between devices  40.5 us (14%)
  Pallas kernels  34 us (12%)
  between operations  13.9 us (5%)
  local copies, waits for them, and re-layouts  11.3 us (4%)
  other arithmetic  9.86 us (3%)
  matrix products  5.13 us (2%)
    ppermute x21, waiting for transfers between devices, z_swap(): return lax.ppermute(block, 'tensor', [(i, i ^ mask) for i in range(count)])  95.9 us
    all_to_all x2, waiting for transfers between devices, body(): lax.all_to_all(out.reshape(experts, padded, part), 'expert', split_axis=0...  47 us
    all_gather x2, waiting for transfers between devices, body(): arrived = lax.all_gather(sent, 'expert', axis=0, tiled=True)  35.4 us
    ppermute x21, starting transfers between devices, z_swap(): return lax.ppermute(block, 'tensor', [(i, i ^ mask) for i in range(count)])  27 us
    pallas_call x2, Pallas kernels, gate_up(): pl.pallas_call(gate_up_kernel, grid_spec=pltpu.PrefetchScalarGridSpec(num...  21.8 us
    all_to_all x2, starting transfers between devices, body(): lax.all_to_all(out.reshape(experts, padded, part), 'expert', split_axis=0...  13.4 us
    pallas_call x2, Pallas kernels, down_product(): pl.pallas_call(functools.partial(down_kernel, capacity, padded), grid_spe...  12.1 us
  transfers between devices with their start and end apart: 25, of which 18 were waited for; matrix products, arithmetic and copies ran while one was open for 5% of the time, Pallas kernels for 0%

profile of v4, /device:TPU:1, one launch (start us, length us, event | category | flops | bytes accessed | tf_op | source)
XLA Modules:
  0.0 293.0 jit_solution(9694143307177590943)
XLA Ops:
  6.5 2.5 collective-permute-start
  9.0 2.2 collective-permute-start.1
  13.2 2.2 collective-permute-start.4
  19.0 2.9 collective-permute-done.5
  24.5 3.5 %dynamic-slice_bitcast_fusion.3 = (bf16[256,1792]{1,0:T(8,128)(2,1)}, bf16[256,1792]{1,0:T(8,128)(2,1)}, bf16[256,1792]{1,0:T(8,128)(2,1)}) fusion(bf16[2,1,256,7168]{3,2,1,0:T(8,128)(2,1)} %refs_4_.3, s32[]{:T(128)S(6)} %select_n.63, s32[]{:T(128)S(6)} %select_n.62, s32[]{:T(128)S(6)} %select_n.61), kind=kLoop, calls=%fused_computation.11 | loop fusion | bytes 5505036 | tf_op jit(solution)/shard_map/reshape | solution.py:148
  32.7 14.2 %collective-permute-done.6.refs_5_ = bf16[256,1792]{1,0:T(8,128)(2,1)S(1)} collective-permute-done((bf16[256,1792]{1,0:T(8,128)(2,1)}, bf16[256,1792]{1,0:T(8,128)(2,1)S(1)}, u32[]{:S(2)}, u32[]{:S(2)}) %collective-permute-start.6) | collective-permute-done | bytes 917536 | tf_op jit(solution)/shard_map/ppermute | solution.py:28
  46.9 2.8 collective-permute-done.7.refs_6_
  49.7 17.3 %collective-permute-done.8.refs_7_ = bf16[256,1792]{1,0:T(8,128)(2,1)S(1)} collective-permute-done((bf16[256,1792]{1,0:T(8,128)(2,1)}, bf16[256,1792]{1,0:T(8,128)(2,1)S(1)}, u32[]{:S(2)}, u32[]{:S(2)}) %collective-permute-start.8) | collective-permute-done | bytes 917536 | tf_op jit(solution)/shard_map/ppermute | solution.py:28
  67.0 19.6 %all-gather.3.cloned.1.call-done.tokens_ref = bf16[768,7296]{1,0:T(8,128)(2,1)} async-done(((bf16[24,7296]{1,0:T(8,128)(2,1)}), bf16[768,7296]{1,0:T(8,128)(2,1)}) %all-gather.3.cloned.1.call-update) | async-done | bytes 11206672 | tf_op jit(solution)/shard_map/all_gather | solution.py:166
  87.7 10.9 %shard_map.73 = bf16[768,256]{1,0:T(8,128)(2,1)} custom-call(s32[1]{0:T(128)} %bitcast.12.z_ref, bf16[768,7296]{1,0:T(8,128)(2,1)} %all-gather.3.cloned.1.call-done.tokens_ref, bf16[2,1,7168,256]{3,2,1,0:T(8,128)(2,1)} %gate_ref.3, bf16[2,1,7168,256]{3,2,1,0:T(8,128)(2,1)} %up_ref.3), custom_call_target="tpu_custom_call" | custom-call | flops 5637144576 | bytes 18743296 | tf_op jit(solution)/shard_map/pallas_call | solution.py:60
  100.0 2.7 collective-permute-start.10
  103.4 8.7 %collective-permute-done.10.refs_2_ = bf16[408,256]{1,0:T(8,128)(2,1)S(1)} collective-permute-done((bf16[408,256]{1,0:T(8,128)(2,1)S(1)}, bf16[408,256]{1,0:T(8,128)(2,1)S(1)}, u32[]{:S(2)}, u32[]{:S(2)}) %collective-permute-start.10) | collective-permute-done | bytes 208928 | tf_op jit(solution)/shard_map/ppermute | solution.py:28
  113.6 6.1 %shard_map.74 = bf16[512,1792]{1,0:T(8,128)(2,1)} custom-call(s32[1]{0:T(128)} %bitcast.12.z_ref, bf16[408,256]{1,0:T(8,128)(2,1)} %copy-done.8, bf16[408,256]{1,0:T(8,128)(2,1)} %copy-done.14, bf16[408,256]{1,0:T(8,128)(2,1)} %copy-done.12, bf16[408,256]{1,0:T(8,128)(2,1)} %copy-done.13, bf16[2,1,256,7168]{3,2,1,0:T(8,128)(2,1)} %refs_4_.3, ...), custom_call_target="tpu_custom_call" | custom-call | flops 2281701376 | bytes 6291456 | tf_op jit(solution)/shard_map/pallas_call | solution.py:103
  119.7 6.4 %all-to-all-start = ((bf16[32,16,1792]{2,1,0:T(8,128)(2,1)}), bf16[32,16,1792]{2,1,0:T(8,128)(2,1)S(1)}, u32[]{:S(2)}, u32[]{:S(2)}) async-start(bf16[32,16,1792]{2,1,0:T(8,128)(2,1)} %bitcast.69), calls=%async_computation | async-start | bytes 3670016 | tf_op jit(solution)/shard_map/all_to_all | solution.py:195
  128.1 23.4 %all-to-all-done = bf16[32,16,1792]{2,1,0:T(8,128)(2,1)S(1)} async-done(((bf16[32,16,1792]{2,1,0:T(8,128)(2,1)}), bf16[32,16,1792]{2,1,0:T(8,128)(2,1)S(1)}, u32[]{:S(2)}, u32[]{:S(2)}) %all-to-all-start) | async-done | bytes 1835040 | tf_op jit(solution)/shard_map/all_to_all | solution.py:195
  167.2 15.9 %collective-permute-done.15.refs_5_ = bf16[256,1792]{1,0:T(8,128)(2,1)S(1)} collective-permute-done((bf16[256,1792]{1,0:T(8,128)(2,1)S(1)}, bf16[256,1792]{1,0:T(8,128)(2,1)S(1)}, u32[]{:S(2)}, u32[]{:S(2)}) %collective-permute-start.15) | collective-permute-done | bytes 917536 | tf_op jit(solution)/shard_map/ppermute | solution.py:28
  185.1 18.0 %collective-permute-done.17.refs_7_ = bf16[256,1792]{1,0:T(8,128)(2,1)S(1)} collective-permute-done((bf16[256,1792]{1,0:T(8,128)(2,1)S(1)}, bf16[256,1792]{1,0:T(8,128)(2,1)S(1)}, u32[]{:S(2)}, u32[]{:S(2)}) %collective-permute-start.17) | collective-permute-done | bytes 917536 | tf_op jit(solution)/shard_map/ppermute | solution.py:28
  203.1 15.8 %all-gather.5.cloned.1.call-done.tokens_ref = bf16[768,7296]{1,0:T(8,128)(2,1)} async-done(((bf16[24,7296]{1,0:T(8,128)(2,1)}), bf16[768,7296]{1,0:T(8,128)(2,1)}) %all-gather.5.cloned.1.call-update) | async-done | bytes 11206672 | tf_op jit(solution)/shard_map/all_gather | solution.py:166
  219.0 10.9 %shard_map.75 = bf16[768,256]{1,0:T(8,128)(2,1)} custom-call(s32[1]{0:T(128)} %bitcast.12.z_ref, bf16[768,7296]{1,0:T(8,128)(2,1)} %all-gather.5.cloned.1.call-done.tokens_ref, bf16[2,1,7168,256]{3,2,1,0:T(8,128)(2,1)} %gate_ref.3, bf16[2,1,7168,256]{3,2,1,0:T(8,128)(2,1)} %up_ref.3), custom_call_target="tpu_custom_call" | custom-call | flops 5637144576 | bytes 18743296 | tf_op jit(solution)/shard_map/pallas_call | solution.py:60
  236.3 2.7 collective-permute-done.18.refs_1_
  238.9 5.0 %collective-permute-done.19.refs_2_ = bf16[408,256]{1,0:T(8,128)(2,1)S(1)} collective-permute-done((bf16[408,256]{1,0:T(8,128)(2,1)S(1)}, bf16[408,256]{1,0:T(8,128)(2,1)S(1)}, u32[]{:S(2)}, u32[]{:S(2)}) %collective-permute-start.19) | collective-permute-done | bytes 208928 | tf_op jit(solution)/shard_map/ppermute | solution.py:28
  246.5 6.1 %shard_map.76 = bf16[512,1792]{1,0:T(8,128)(2,1)} custom-call(s32[1]{0:T(128)} %bitcast.12.z_ref, bf16[408,256]{1,0:T(8,128)(2,1)} %copy-done.7, bf16[408,256]{1,0:T(8,128)(2,1)} %copy-done.15, bf16[408,256]{1,0:T(8,128)(2,1)} %copy-done.16, bf16[408,256]{1,0:T(8,128)(2,1)} %copy-done.17, bf16[2,1,256,7168]{3,2,1,0:T(8,128)(2,1)} %refs_4_.3, ...), custom_call_target="tpu_custom_call" | custom-call | flops 2281701376 | bytes 6291456 | tf_op jit(solution)/shard_map/pallas_call | solution.py:103
  252.6 7.0 %all-to-all-start.1 = ((bf16[32,16,1792]{2,1,0:T(8,128)(2,1)}), bf16[32,16,1792]{2,1,0:T(8,128)(2,1)S(1)}, u32[]{:S(2)}, u32[]{:S(2)}) async-start(bf16[32,16,1792]{2,1,0:T(8,128)(2,1)} %bitcast.70), calls=%async_computation.1 | async-start | bytes 3670016 | tf_op jit(solution)/shard_map/all_to_all | solution.py:195
  261.4 23.6 %all-to-all-done.1 = bf16[32,16,1792]{2,1,0:T(8,128)(2,1)S(1)} async-done(((bf16[32,16,1792]{2,1,0:T(8,128)(2,1)}), bf16[32,16,1792]{2,1,0:T(8,128)(2,1)S(1)}, u32[]{:S(2)}, u32[]{:S(2)}) %all-to-all-start.1) | async-done | bytes 1835040 | tf_op jit(solution)/shard_map/all_to_all | solution.py:195
  (151 shorter events, 48.7 us)
Async XLA Ops:
  6.5 80.1 %all-gather.3.cloned.1.call-start = ((), (), s32[]{:S(2)}) async-start(), calls=%async_computation.2 | async-start | bytes 11556864 | tf_op jit(solution)/shard_map/all_gather | solution.py:166
  6.5 15.4 %collective-permute-start = (bf16[24,1792]{1,0:T(8,128)(2,1)}, bf16[24,1792]{1,0:T(8,128)(2,1)S(1)}, u32[]{:S(2)}, u32[]{:S(2)}) collective-permute-start(bf16[24,1792]{1,0:T(8,128)(2,1)} %param.7), channel_id=1, source_target_pairs={{0,1},{1,0},{2,3},{3,2},{4,5},{5,4},{6,7},{7,6},{8,9},{9,8},{10,11... | collective-permute-start | bytes 258056 | tf_op jit(solution)/shard_map/ppermute | solution.py:28
  9.0 13.1 %collective-permute-start.1 = (bf16[24,1792]{1,0:T(8,128)(2,1)}, bf16[24,1792]{1,0:T(8,128)(2,1)S(1)}, u32[]{:S(2)}, u32[]{:S(2)}) collective-permute-start(bf16[24,1792]{1,0:T(8,128)(2,1)} %param.7), channel_id=1, source_target_pairs={{0,3},{1,2},{2,1},{3,0},{4,7},{5,6},{6,5},{7,4},{8,11},{9,10},{10,... | collective-permute-start | bytes 258056 | tf_op jit(solution)/shard_map/ppermute | solution.py:28
  11.2 11.0 %collective-permute-start.2 = (bf16[24,1792]{1,0:T(8,128)(2,1)}, bf16[24,1792]{1,0:T(8,128)(2,1)S(1)}, u32[]{:S(2)}, u32[]{:S(2)}) collective-permute-start(bf16[24,1792]{1,0:T(8,128)(2,1)} %param.7), channel_id=1, source_target_pairs={{0,2},{1,3},{2,0},{3,1},{4,6},{5,7},{6,4},{7,5},{8,10},{9,11},{10,... | collective-permute-start | bytes 258056 | tf_op jit(solution)/shard_map/ppermute | solution.py:28
  13.1 4.4 %collective-permute-start.3 = (bf16[8,1792]{1,0:T(8,128)(2,1)S(1)}, bf16[8,1792]{1,0:T(8,128)(2,1)S(1)}, u32[]{:S(2)}, u32[]{:S(2)}) collective-permute-start(bf16[8,1792]{1,0:T(8,128)(2,1)S(1)} %pad.17), channel_id=1, source_target_pairs={{0,1},{1,0},{2,3},{3,2},{4,5},{5,4},{6,7},{7,6},{8,9},{9,8},{10,11... | collective-permute-start | bytes 86024 | tf_op jit(solution)/shard_map/ppermute | solution.py:28
  13.2 5.6 %collective-permute-start.4 = (bf16[8,1792]{1,0:T(8,128)(2,1)S(1)}, bf16[8,1792]{1,0:T(8,128)(2,1)S(1)}, u32[]{:S(2)}, u32[]{:S(2)}) collective-permute-start(bf16[8,1792]{1,0:T(8,128)(2,1)S(1)} %pad.17), channel_id=1, source_target_pairs={{0,3},{1,2},{2,1},{3,0},{4,7},{5,6},{6,5},{7,4},{8,11},{9,10},{10,... | collective-permute-start | bytes 86024 | tf_op jit(solution)/shard_map/ppermute | solution.py:28
  17.5 4.3 %collective-permute-start.5 = (bf16[8,1792]{1,0:T(8,128)(2,1)S(1)}, bf16[8,1792]{1,0:T(8,128)(2,1)S(1)}, u32[]{:S(2)}, u32[]{:S(2)}) collective-permute-start(bf16[8,1792]{1,0:T(8,128)(2,1)S(1)} %pad.17), channel_id=1, source_target_pairs={{0,2},{1,3},{2,0},{3,1},{4,6},{5,7},{6,4},{7,5},{8,10},{9,11},{10,... | collective-permute-start | bytes 86024 | tf_op jit(solution)/shard_map/ppermute | solution.py:28
  28.0 18.9 %collective-permute-start.6 = (bf16[256,1792]{1,0:T(8,128)(2,1)}, bf16[256,1792]{1,0:T(8,128)(2,1)S(1)}, u32[]{:S(2)}, u32[]{:S(2)}) collective-permute-start(bf16[256,1792]{1,0:T(8,128)(2,1)} %get-tuple-element.48), channel_id=1, source_target_pairs={{0,1},{1,0},{2,3},{3,2},{4,5},{5,4},{6,7},{7,6},{8,9},{9,8},{10,11... | collective-permute-start | bytes 2752520 | tf_op jit(solution)/shard_map/ppermute | solution.py:28
  28.7 21.0 %collective-permute-start.7 = (bf16[256,1792]{1,0:T(8,128)(2,1)}, bf16[256,1792]{1,0:T(8,128)(2,1)S(1)}, u32[]{:S(2)}, u32[]{:S(2)}) collective-permute-start(bf16[256,1792]{1,0:T(8,128)(2,1)} %get-tuple-element.47), channel_id=1, source_target_pairs={{0,3},{1,2},{2,1},{3,0},{4,7},{5,6},{6,5},{7,4},{8,11},{9,10},{10,... | collective-permute-start | bytes 2752520 | tf_op jit(solution)/shard_map/ppermute | solution.py:28
  29.3 37.7 %collective-permute-start.8 = (bf16[256,1792]{1,0:T(8,128)(2,1)}, bf16[256,1792]{1,0:T(8,128)(2,1)S(1)}, u32[]{:S(2)}, u32[]{:S(2)}) collective-permute-start(bf16[256,1792]{1,0:T(8,128)(2,1)} %get-tuple-element.46), channel_id=1, source_target_pairs={{0,2},{1,3},{2,0},{3,1},{4,6},{5,7},{6,4},{7,5},{8,10},{9,11},{10,... | collective-permute-start | bytes 2752520 | tf_op jit(solution)/shard_map/ppermute | solution.py:28
  100.0 12.1 %collective-permute-start.10 = (bf16[408,256]{1,0:T(8,128)(2,1)S(1)}, bf16[408,256]{1,0:T(8,128)(2,1)S(1)}, u32[]{:S(2)}, u32[]{:S(2)}) collective-permute-start(bf16[408,256]{1,0:T(8,128)(2,1)S(1)} %pad_maximum_fusion.refs_0_), channel_id=1, source_target_pairs={{0,3},{1,2},{2,1},{3,0},{4,7},{5,6},{6,5},{7,4},{8,11},{9,10},{10,... | collective-permute-start | bytes 626696 | tf_op jit(solution)/shard_map/ppermute | solution.py:28
  102.8 9.4 %collective-permute-start.11 = (bf16[408,256]{1,0:T(8,128)(2,1)S(1)}, bf16[408,256]{1,0:T(8,128)(2,1)S(1)}, u32[]{:S(2)}, u32[]{:S(2)}) collective-permute-start(bf16[408,256]{1,0:T(8,128)(2,1)S(1)} %pad_maximum_fusion.refs_0_), channel_id=1, source_target_pairs={{0,2},{1,3},{2,0},{3,1},{4,6},{5,7},{6,4},{7,5},{8,10},{9,11},{10,... | collective-permute-start | bytes 626696 | tf_op jit(solution)/shard_map/ppermute | solution.py:28
  103.2 9.6 %collective-permute-start.9 = (bf16[408,256]{1,0:T(8,128)(2,1)S(1)}, bf16[408,256]{1,0:T(8,128)(2,1)S(1)}, u32[]{:S(2)}, u32[]{:S(2)}) collective-permute-start(bf16[408,256]{1,0:T(8,128)(2,1)S(1)} %pad_maximum_fusion.refs_0_), channel_id=1, source_target_pairs={{0,1},{1,0},{2,3},{3,2},{4,5},{5,4},{6,7},{7,6},{8,9},{9,8},{10,11... | collective-permute-start | bytes 626696 | tf_op jit(solution)/shard_map/ppermute | solution.py:28
  119.7 31.9 %all-to-all-start = ((bf16[32,16,1792]{2,1,0:T(8,128)(2,1)}), bf16[32,16,1792]{2,1,0:T(8,128)(2,1)S(1)}, u32[]{:S(2)}, u32[]{:S(2)}) async-start(bf16[32,16,1792]{2,1,0:T(8,128)(2,1)} %bitcast.69), calls=%async_computation | async-start | bytes 3670016 | tf_op jit(solution)/shard_map/all_to_all | solution.py:195
  126.1 92.9 %all-gather.5.cloned.1.call-start = ((), (), s32[]{:S(2)}) async-start(), calls=%async_computation.3 | async-start | bytes 11556864 | tf_op jit(solution)/shard_map/all_gather | solution.py:166
  153.4 4.5 %collective-permute-start.13 = (bf16[24,1792]{1,0:T(8,128)(2,1)S(1)}, bf16[24,1792]{1,0:T(8,128)(2,1)S(1)}, u32[]{:S(2)}, u32[]{:S(2)}) collective-permute-start(bf16[24,1792]{1,0:T(8,128)(2,1)S(1)} %get-tuple-element.38), channel_id=1, source_target_pairs={{0,3},{1,2},{2,1},{3,0},{4,7},{5,6},{6,5},{7,4},{8,11},{9,10},{10,... | collective-permute-start | bytes 258056 | tf_op jit(solution)/shard_map/ppermute | solution.py:28
  155.3 4.9 %collective-permute-start.14 = (bf16[24,1792]{1,0:T(8,128)(2,1)S(1)}, bf16[24,1792]{1,0:T(8,128)(2,1)S(1)}, u32[]{:S(2)}, u32[]{:S(2)}) collective-permute-start(bf16[24,1792]{1,0:T(8,128)(2,1)S(1)} %get-tuple-element.38), channel_id=1, source_target_pairs={{0,2},{1,3},{2,0},{3,1},{4,6},{5,7},{6,4},{7,5},{8,10},{9,11},{10,... | collective-permute-start | bytes 258056 | tf_op jit(solution)/shard_map/ppermute | solution.py:28
  163.5 19.6 %collective-permute-start.15 = (bf16[256,1792]{1,0:T(8,128)(2,1)S(1)}, bf16[256,1792]{1,0:T(8,128)(2,1)S(1)}, u32[]{:S(2)}, u32[]{:S(2)}) collective-permute-start(bf16[256,1792]{1,0:T(8,128)(2,1)S(1)} %get-tuple-element.45), channel_id=1, source_target_pairs={{0,1},{1,0},{2,3},{3,2},{4,5},{5,4},{6,7},{7,6},{8,9},{9,8},{10,11... | collective-permute-start | bytes 2752520 | tf_op jit(solution)/shard_map/ppermute | solution.py:28
  164.0 21.1 %collective-permute-start.16 = (bf16[256,1792]{1,0:T(8,128)(2,1)S(1)}, bf16[256,1792]{1,0:T(8,128)(2,1)S(1)}, u32[]{:S(2)}, u32[]{:S(2)}) collective-permute-start(bf16[256,1792]{1,0:T(8,128)(2,1)S(1)} %get-tuple-element.44), channel_id=1, source_target_pairs={{0,3},{1,2},{2,1},{3,0},{4,7},{5,6},{6,5},{7,4},{8,11},{9,10},{10,... | collective-permute-start | bytes 2752520 | tf_op jit(solution)/shard_map/ppermute | solution.py:28
  164.7 38.4 %collective-permute-start.17 = (bf16[256,1792]{1,0:T(8,128)(2,1)S(1)}, bf16[256,1792]{1,0:T(8,128)(2,1)S(1)}, u32[]{:S(2)}, u32[]{:S(2)}) collective-permute-start(bf16[256,1792]{1,0:T(8,128)(2,1)S(1)} %get-tuple-element.43), channel_id=1, source_target_pairs={{0,2},{1,3},{2,0},{3,1},{4,6},{5,7},{6,4},{7,5},{8,10},{9,11},{10,... | collective-permute-start | bytes 2752520 | tf_op jit(solution)/shard_map/ppermute | solution.py:28
  232.3 6.6 %collective-permute-start.18 = (bf16[408,256]{1,0:T(8,128)(2,1)S(1)}, bf16[408,256]{1,0:T(8,128)(2,1)S(1)}, u32[]{:S(2)}, u32[]{:S(2)}) collective-permute-start(bf16[408,256]{1,0:T(8,128)(2,1)S(1)} %pad_maximum_fusion.1.refs_0_), channel_id=1, source_target_pairs={{0,1},{1,0},{2,3},{3,2},{4,5},{5,4},{6,7},{7,6},{8,9},{9,8},{10,11... | collective-permute-start | bytes 626696 | tf_op jit(solution)/shard_map/ppermute | solution.py:28
  233.7 10.2 %collective-permute-start.19 = (bf16[408,256]{1,0:T(8,128)(2,1)S(1)}, bf16[408,256]{1,0:T(8,128)(2,1)S(1)}, u32[]{:S(2)}, u32[]{:S(2)}) collective-permute-start(bf16[408,256]{1,0:T(8,128)(2,1)S(1)} %pad_maximum_fusion.1.refs_0_), channel_id=1, source_target_pairs={{0,3},{1,2},{2,1},{3,0},{4,7},{5,6},{6,5},{7,4},{8,11},{9,10},{10,... | collective-permute-start | bytes 626696 | tf_op jit(solution)/shard_map/ppermute | solution.py:28
  235.6 10.3 %collective-permute-start.20 = (bf16[408,256]{1,0:T(8,128)(2,1)S(1)}, bf16[408,256]{1,0:T(8,128)(2,1)S(1)}, u32[]{:S(2)}, u32[]{:S(2)}) collective-permute-start(bf16[408,256]{1,0:T(8,128)(2,1)S(1)} %pad_maximum_fusion.1.refs_0_), channel_id=1, source_target_pairs={{0,2},{1,3},{2,0},{3,1},{4,6},{5,7},{6,4},{7,5},{8,10},{9,11},{10,... | collective-permute-start | bytes 626696 | tf_op jit(solution)/shard_map/ppermute | solution.py:28
  252.6 32.5 %all-to-all-start.1 = ((bf16[32,16,1792]{2,1,0:T(8,128)(2,1)}), bf16[32,16,1792]{2,1,0:T(8,128)(2,1)S(1)}, u32[]{:S(2)}, u32[]{:S(2)}) async-start(bf16[32,16,1792]{2,1,0:T(8,128)(2,1)} %bitcast.70), calls=%async_computation.1 | async-start | bytes 3670016 | tf_op jit(solution)/shard_map/all_to_all | solution.py:195
  (20 other events, 313.0 us)
Sparse Core Ops, SparseCore 0:
  24.6 62.0 all-gather.2
  161.6 57.2 all-gather.4

commit v5 on v4

--- a/solution.py
+++ b/solution.py
@@ -10,6 +10,9 @@
 route_scale = 2.5
 bf16, f32 = jnp.bfloat16, jnp.float32
 
+Y_STEPS = ((2, 6), (6, 2))
+X_STEPS = ((8, 24), (24, 8))
+SIBLING = (1, 1)
 ORDER = (0, 1, 3, 2)
 
 
@@ -23,6 +26,11 @@
     return [part.astype(bf16) for part in (high, middle, values - high - middle)]
 
 
+def swap(block, masks):
+    count = lax.axis_size("expert")
+    return lax.ppermute(block, "expert", [(i, i ^ masks[i & 1]) for i in range(count)])
+
+
 def z_swap(block, mask):
     count = lax.axis_size("tensor")
     return lax.ppermute(block, "tensor", [(i, i ^ mask) for i in range(count)])
@@ -32,65 +40,96 @@
     return lax.optimization_barrier((block, *others))[0]
 
 
-def gate_up_kernel(z_ref, tokens_ref, gate_ref, up_ref, act_ref, gate_sum, up_sum):
+def first_kernel(z_ref, t0, t1, t2, t3, gate_ref, up_ref, out_ref):
+    units = gate_ref.shape[-1]
+    tokens = jnp.concatenate([t0[...], t1[...], t2[...], t3[...]], axis=0)
+    out_ref[:, :units] = jnp.dot(tokens, gate_ref[0, 0], preferred_element_type=f32)
+    out_ref[:, units:] = jnp.dot(tokens, up_ref[0, 0], preferred_element_type=f32)
+
+
+def first_products(z, tokens, w_gate, w_up, layer, mask):
+    rows, units = tokens[0].shape[0], w_gate.shape[-1]
+    depth = w_gate.shape[2] // 4
+    weights = pl.BlockSpec((1, 1, depth, units), lambda k, z: (layer, 0, z[0] ^ mask, 0))
+    return pl.pallas_call(
+        first_kernel,
+        grid_spec=pltpu.PrefetchScalarGridSpec(
+            num_scalar_prefetch=1,
+            grid=(1,),
+            in_specs=[pl.BlockSpec((rows, depth), lambda k, z: (0, 0))] * 4 + [weights, weights],
+            out_specs=pl.BlockSpec((4 * rows, 2 * units), lambda k, z: (0, 0)),
+        ),
+        out_shape=jax.ShapeDtypeStruct((4 * rows, 2 * units), f32),
+        cost_estimate=pl.CostEstimate(
+            flops=16 * rows * depth * units,
+            bytes_accessed=8 * rows * depth + 4 * units * depth + 32 * rows * units,
+            transcendentals=0,
+        ),
+    )(jnp.full((1,), z, jnp.int32), *tokens, w_gate, w_up)
+
+
+def gate_up_kernel(rows, z_ref, places_ref, tokens_ref, gate_ref, up_ref, a_ref, b_ref, act_ref, held):
+    units = gate_ref.shape[-1]
     step = pl.program_id(0)
-    gate = jnp.dot(tokens_ref[...], gate_ref[0, 0], preferred_element_type=f32)
-    up = jnp.dot(tokens_ref[...], up_ref[0, 0], preferred_element_type=f32)
 
     @pl.when(step == 0)
     def _():
-        gate_sum[...] = gate
-        up_sum[...] = up
-
-    @pl.when(step > 0)
-    def _():
-        gate_sum[...] += gate
-        up_sum[...] += up
+        for block in range(held.shape[0] // rows):
+            first = pl.multiple_of(places_ref[0, block] * rows, rows)
+            second = pl.multiple_of(places_ref[1, block] * rows, rows)
+            held[block * rows : (block + 1) * rows] = (
+                a_ref[pl.ds(first, rows)] + b_ref[pl.ds(second, rows)]
+            )
+
+    held[:, :units] += jnp.dot(tokens_ref[...], gate_ref[0, 0], preferred_element_type=f32)
+    held[:, units:] += jnp.dot(tokens_ref[...], up_ref[0, 0], preferred_element_type=f32)
 
     @pl.when(step == pl.num_programs(0) - 1)
     def _():
-        gate = gate_sum[...]
-        act_ref[...] = (gate / (1.0 + jnp.exp(-gate)) * up_sum[...]).astype(act_ref.dtype)
-
-
-def gate_up(z, tokens, w_gate, w_up, layer):
-    rows, units = tokens.shape[0], w_gate.shape[-1]
+        gate = held[:, :units]
+        act_ref[...] = (gate / (1.0 + jnp.exp(-gate)) * held[:, units:]).astype(act_ref.dtype)
+
+
+def gate_up(z, places, tokens, w_gate, w_up, layer, sums_a, sums_b, rows):
+    total, units = tokens.shape[0], w_gate.shape[-1]
     depth = w_gate.shape[2] // 4
-    weights = pl.BlockSpec((1, 1, depth, units), lambda k, z: (layer, 0, z[0] ^ k ^ (k >> 1), 0))
+    weights = pl.BlockSpec((1, 1, depth, units), lambda k, z, p: (layer, 0, z[0] ^ k, 0))
+    sums = pl.BlockSpec((total, 2 * units), lambda k, z, p: (0, 0))
     return pl.pallas_call(
-        gate_up_kernel,
+        functools.partial(gate_up_kernel, rows),
         grid_spec=pltpu.PrefetchScalarGridSpec(
-            num_scalar_prefetch=1,
-            grid=(4,),
-            in_specs=[pl.BlockSpec((rows, depth), lambda k, z: (0, k)), weights, weights],
-            out_specs=pl.BlockSpec((rows, units), lambda k, z: (0, 0)),
-            scratch_shapes=[pltpu.VMEM((rows, units), f32)] * 2,
-        ),
-        out_shape=jax.ShapeDtypeStruct((rows, units), bf16),
+            num_scalar_prefetch=2,
+            grid=(2,),
+            in_specs=[
+                pl.BlockSpec((total, depth), lambda k, z, p: (0, k)),
+                weights,
+                weights,
+                sums,
+                sums,
+            ],
+            out_specs=pl.BlockSpec((total, units), lambda k, z, p: (0, 0)),
+            scratch_shapes=[pltpu.VMEM((total, 2 * units), f32)],
+        ),
+        out_shape=jax.ShapeDtypeStruct((total, units), bf16),
+        compiler_params=pltpu.CompilerParams(vmem_limit_bytes=48 << 20),
         cost_estimate=pl.CostEstimate(
-            flops=16 * rows * depth * units,
-            bytes_accessed=8 * (rows + 2 * units) * depth + 2 * rows * units,
-            transcendentals=rows * units,
-        ),
-    )(jnp.full((1,), z, jnp.int32), tokens, w_gate, w_up)
+            flops=8 * total * depth * units,
+            bytes_accessed=4 * (total + 2 * units) * depth + 18 * total * units,
+            transcendentals=total * units,
+        ),
+    )(jnp.full((1,), z, jnp.int32), places, tokens, w_gate, w_up, sums_a, sums_b)
 
 
 def down_kernel(capacity, padded, z_ref, *refs):
-    acts, weights, out_ref, held = refs[:4], refs[4:-2], refs[-2], refs[-1]
-
-    @pl.when(pl.program_id(0) == 0)
-    def _():
-        slots = acts[0].shape[0]
-        row = lax.broadcasted_iota(jnp.int32, (slots // capacity * padded, slots), 0)
-        slot = lax.broadcasted_iota(jnp.int32, row.shape, 1)
-        place = row % padded
-        here = (place < capacity) & (row // padded * capacity + place == slot)
-        joined = jnp.concatenate([act[...] for act in acts], axis=1)
-        spread = jnp.dot(here.astype(bf16), joined, preferred_element_type=f32)
-        held[...] = spread.astype(bf16)
-
+    acts, weights, out_ref = refs[:4], refs[4:-1], refs[-1]
+    acts = jnp.concatenate([act[...] for act in acts], axis=1)
     weights = jnp.concatenate([weights[0][0, 0]] + [w[...] for w in weights[1:]], axis=0)
-    out_ref[...] = jnp.dot(held[...], weights, preferred_element_type=f32).astype(out_ref.dtype)
+    product = jnp.dot(acts, weights, preferred_element_type=f32)
+    blank = jnp.zeros((padded - capacity, product.shape[1]), f32)
+    for block in range(product.shape[0] // capacity):
+        here = product[block * capacity : (block + 1) * capacity]
+        here = jnp.concatenate([here, blank], axis=0).astype(out_ref.dtype)
+        out_ref[block * padded : (block + 1) * padded] = here
 
 
 def down_product(z, acts, slots, capacity, padded, w_down, layer, others):
@@ -109,11 +148,10 @@
             + [pl.BlockSpec((1, 1, units, columns), lambda n, z: (layer, 0, 0, z[0] * steps + n))]
             + [pl.BlockSpec((w.shape[0], columns), lambda n, z: (0, n)) for w in others],
             out_specs=pl.BlockSpec((rows, columns), lambda n, z: (0, n)),
-            scratch_shapes=[pltpu.VMEM((rows, 4 * units), bf16)],
         ),
         out_shape=jax.ShapeDtypeStruct((rows, part), bf16),
         cost_estimate=pl.CostEstimate(
-            flops=8 * rows * units * (part + slots),
+            flops=8 * slots * units * part,
             bytes_accessed=8 * units * (slots + part) + 2 * rows * part,
             transcendentals=0,
         ),
@@ -129,6 +167,19 @@
     padded = -(-capacity // 16) * 16
     me = lax.axis_index("expert")
     z = lax.axis_index("tensor")
+
+    away = lax.broadcasted_iota(jnp.int32, (experts,), 0) ^ me
+    odd = ((away ^ me) & 1) == 1
+
+    def turns(distance):
+        low, high = (distance & 1) ^ (distance >> 1), distance >> 1
+        return jnp.where(odd, high, low) + 2 * jnp.where(odd, low, high)
+
+    along_y, along_x = turns((away >> 1) & 3), turns(away >> 3)
+    other = (away & 1) * (experts // 2)
+    places = jnp.stack([other + along_y + 4 * along_x, other + along_x + 4 * along_y])
+    in_place = places[1][:, None] == lax.broadcasted_iota(jnp.int32, (1, experts), 1)
+    in_place = in_place.astype(bf16)
 
     expert_iota = lax.broadcasted_iota(jnp.int32, (1, 1, 1, experts), 3)
     picks = jnp.any(routes[..., None] == expert_iota, axis=2)
@@ -162,14 +213,37 @@
             for block, gain in zip(blocks, gains)
         ]
 
-        sent = jnp.concatenate(normed + [marks_sent[layer]], axis=1)
+        sent = jnp.concatenate(normed[:2], axis=1)
         arrived = lax.all_gather(sent, "expert", axis=0, tiled=True)
-        others = [columns(layer, mask, 0, units, sent) for mask in ORDER[1:]]
-        arrived, *others = lax.optimization_barrier((arrived, *others))
-        act = gate_up(z, arrived, w_gate, w_up, layer)
-
-        mine = lax.broadcasted_iota(jnp.int32, (1, 128), 1) == me
-        mark = jnp.sum(jnp.where(mine, arrived[:, width:].astype(f32), 0.0), axis=1).astype(jnp.int32)
+        held_a = normed[2][None]
+        held_b = jnp.concatenate([normed[3], marks_sent[layer]], axis=1)[None]
+        near = [columns(layer, mask, 0, units, sent) for mask in ORDER[1:3]]
+        for step in range(3):
+            got_a = swap(held_a, (Y_STEPS + X_STEPS)[step])
+            got_b = swap(held_b, (X_STEPS + Y_STEPS)[step])
+            held_a = jnp.concatenate([held_a, got_a])
+            held_b = jnp.concatenate([held_b, got_b])
+        held_a, held_b, *near = lax.optimization_barrier((held_a, held_b, *near))
+        far = columns(layer, ORDER[3], 0, units, held_a)
+        last_a, last_b = swap(held_a, X_STEPS[1]), swap(held_b, Y_STEPS[1])
+        all_a = [held_a, last_a, swap(held_a, SIBLING), swap(last_a, SIBLING)]
+        all_b = [held_b, last_b, swap(held_b, SIBLING), swap(last_b, SIBLING)]
+
+        def products(tokens, mask):
+            flat = [block.reshape(-1, block.shape[2]) for block in tokens]
+            return first_products(z, flat, w_gate, w_up, layer, mask)
+
+        sums_a, sums_b = products(all_a, ORDER[2]), products(all_b, ORDER[3])
+        mine = lax.broadcasted_iota(jnp.int32, (1, 1, 128), 2) == me
+        mark = [jnp.sum(jnp.where(mine, block[:, :, part:].astype(f32), 0.0), axis=2) for block in all_b]
+        mark = jnp.dot(in_place, jnp.concatenate(mark).astype(bf16), preferred_element_type=f32)
+        mark = mark.astype(jnp.int32).reshape(-1)
+        arrived, sums_a, sums_b, mark, far = lax.optimization_barrier(
+            (arrived, sums_a, sums_b, mark, far)
+        )
+        others = near + [far]
+        act = gate_up(z, places, arrived, w_gate, w_up, layer, sums_a, sums_b, rows)
+
         source = lax.broadcasted_iota(jnp.int32, (experts, rows), 0).reshape(-1)
         slot = jnp.where(mark > 0, source * capacity + mark - 1, -1)[None, :]
         taken = (lax.broadcasted_iota(jnp.int32, (slots, 1), 0) == slot).astype(bf16)

time: 294 us -> 320 us (1.088)
  starting transfers between devices: 40.5 us -> 110 us
  waiting for transfers between devices: 178 us -> 123 us
  Pallas kernels: 34 us -> 42.9 us
  local copies, waits for them, and re-layouts: 11.3 us -> 15.4 us
    ppermute x0 -> x24, starting transfers between devices: none -> 67.1 us  [swap(): lax.ppermute(block, 'expert', [(i, i ^ masks[i & 1]) for i in range(count)])]
    ppermute x21, waiting for transfers between devices: 95.9 us -> 41.8 us  [z_swap(): return lax.ppermute(block, 'tensor', [(i, i ^ mask) for i in range(count)])]
    all_gather x2, waiting for transfers between devices: 35.4 us -> 0.01 us  [body(): arrived = lax.all_gather(sent, 'expert', axis=0, tiled=True)]
    ppermute x0 -> x24, waiting for transfers between devices: none -> 33.8 us  [swap(): lax.ppermute(block, 'expert', [(i, i ^ masks[i & 1]) for i in range(count)])]
    pallas_call x2 -> x6, Pallas kernels: 21.8 us -> 33.3 us  [the longest x4 20.4 us: first_products(): pl.pallas_call(first_kernel, grid_spec=pltpu.PrefetchScalarGridSpec(num_s...]
    reshape x2 -> x4, local copies, waits for them, and re-layouts: 5.45 us -> 7.69 us  [columns(): return z_swap(block.reshape(count, part), mask)]
  transfers between devices with their start and end apart: 25 -> 49, of which waited for: 18 -> 25; matrix products, arithmetic and copies ran while one was open for 5% -> 6% of each run, Pallas kernels for 0% -> 6%
where the time goes in v5:
time: 320 us; the launch traced here: 319 us
  waiting for transfers between devices  123 us (38%)
  starting transfers between devices  110 us (34%)
  Pallas kernels  42.9 us (13%)
  local copies, waits for them, and re-layouts  15.4 us (5%)
  between operations  14.2 us (4%)
  other arithmetic  11.3 us (4%)
    ppermute x24, starting transfers between devices, swap(): lax.ppermute(block, 'expert', [(i, i ^ masks[i & 1]) for i in range(count)])  67.1 us
    all_to_all x2, waiting for transfers between devices, body(): lax.all_to_all(out.reshape(experts, padded, part), 'expert', split_axis=0...  47 us
    ppermute x21, waiting for transfers between devices, z_swap(): return lax.ppermute(block, 'tensor', [(i, i ^ mask) for i in range(count)])  41.8 us
    ppermute x24, waiting for transfers between devices, swap(): lax.ppermute(block, 'expert', [(i, i ^ masks[i & 1]) for i in range(count)])  33.8 us
    ppermute x21, starting transfers between devices, z_swap(): return lax.ppermute(block, 'tensor', [(i, i ^ mask) for i in range(count)])  28.4 us
    pallas_call x4, Pallas kernels, first_products(): pl.pallas_call(first_kernel, grid_spec=pltpu.PrefetchScalarGridSpec(num_s...  20.4 us
    all_to_all x2, starting transfers between devices, body(): lax.all_to_all(out.reshape(experts, padded, part), 'expert', split_axis=0...  14.5 us
    pallas_call x2, Pallas kernels, gate_up(): pl.pallas_call(functools.partial(gate_up_kernel, rows), grid_spec=pltpu.P...  12.9 us
  transfers between devices with their start and end apart: 49, of which 25 were waited for; matrix products, arithmetic and copies ran while one was open for 6% of the time, Pallas kernels for 6%

profile of v5, /device:TPU:1, one launch (start us, length us, event | category | flops | bytes accessed | tf_op | source)
XLA Modules:
  0.0 319.2 jit_solution(11925392671241602534)
XLA Ops:
  7.4 4.7 %collective-permute-start.4 = (bf16[8,1792]{1,0:T(8,128)(2,1)S(1)}, bf16[8,1792]{1,0:T(8,128)(2,1)S(1)}, u32[]{:S(2)}, u32[]{:S(2)}) collective-permute-start(bf16[8,1792]{1,0:T(8,128)(2,1)S(1)} %pad.17), channel_id=1, source_target_pairs={{0,3},{1,2},{2,1},{3,0},{4,7},{5,6},{6,5},{7,4},{8,11},{9,10},{10,... | collective-permute-start | bytes 86024 | tf_op jit(solution)/shard_map/ppermute | solution.py:36
  41.9 6.6 %collective-permute-done.7 = bf16[4,24,1792]{2,1,0:T(8,128)(2,1)S(1)} collective-permute-done((bf16[4,24,1792]{2,1,0:T(8,128)(2,1)S(1)}, bf16[4,24,1792]{2,1,0:T(8,128)(2,1)S(1)}, u32[]{:S(2)}, u32[]{:S(2)}) %collective-permute-start.7) | collective-permute-done | bytes 344096 | tf_op jit(solution)/shard_map/ppermute | solution.py:31
  51.3 13.4 %collective-permute-start.18 = (bf16[8,24,1920]{2,1,0:T(8,128)(2,1)S(1)}, bf16[8,24,1920]{2,1,0:T(8,128)(2,1)}, u32[]{:S(2)}, u32[]{:S(2)}) collective-permute-start(bf16[8,24,1920]{2,1,0:T(8,128)(2,1)S(1)} %pad_maximum_fusion), channel_id=1, source_target_pairs={{0,4},{4,0},{8,12},{12,8},{16,20},{20,16},{24,28},{28,24},{32,36},... | collective-permute-start | bytes 2211848 | tf_op jit(solution)/shard_map/ppermute | solution.py:31
  64.9 15.7 %collective-permute-start.16 = (bf16[8,24,1792]{2,1,0:T(8,128)(2,1)}, bf16[8,24,1792]{2,1,0:T(8,128)(2,1)}, u32[]{:S(2)}, u32[]{:S(2)}) collective-permute-start(bf16[8,24,1792]{2,1,0:T(8,128)(2,1)} %collective-permute-done.14), channel_id=1, source_target_pairs={{0,4},{4,0},{8,12},{12,8},{16,20},{20,16},{24,28},{28,24},{32,36},... | collective-permute-start | bytes 2064392 | tf_op jit(solution)/shard_map/ppermute | solution.py:31
  86.3 5.0 %shard_map.73.a_ref = f32[768,512]{1,0:T(8,128)} custom-call(s32[1]{0:T(128)} %bitcast.8.z_ref, bf16[192,1792]{1,0:T(8,128)(2,1)} %bitcast.95, bf16[192,1792]{1,0:T(8,128)(2,1)} %bitcast.15.t1, bf16[192,1792]{1,0:T(8,128)(2,1)} %bitcast.16.t2, bf16[192,1792]{1,0:T(8,128)(2,1)} %bitcast.17.t3, bf16[2,1,7168,256]{3,2,1,0:T(8,128)(2,1)} %gate_ref.11, ...), custom_call_target="tpu_custom_call" | custom-call | flops 1409286144 | bytes 6160384 | tf_op jit(solution)/shard_map/pallas_call | solution.py:54
  92.8 5.2 %shard_map.74.b_ref = f32[768,512]{1,0:T(8,128)} custom-call(s32[1]{0:T(128)} %bitcast.8.z_ref, bf16[192,1920]{1,0:T(8,128)(2,1)} %bitcast.93, bf16[192,1920]{1,0:T(8,128)(2,1)} %bitcast.97, bf16[192,1920]{1,0:T(8,128)(2,1)} %bitcast.20.t2, bf16[192,1920]{1,0:T(8,128)(2,1)} %bitcast.21.t3, bf16[2,1,7168,256]{3,2,1,0:T(8,128)(2,1)} %gate_ref.11, ...), custom_call_target="tpu_custom_call" | custom-call | flops 1409286144 | bytes 6160384 | tf_op jit(solution)/shard_map/pallas_call | solution.py:54
  98.0 8.5 %collective-permute-done.20.refs_7_ = bf16[256,1792]{1,0:T(8,128)(2,1)} collective-permute-done((bf16[256,1792]{1,0:T(8,128)(2,1)}, bf16[256,1792]{1,0:T(8,128)(2,1)}, u32[]{:S(2)}, u32[]{:S(2)}) %collective-permute-start.20) | collective-permute-done | bytes 917536 | tf_op jit(solution)/shard_map/ppermute | solution.py:36
  107.8 6.4 %shard_map.75 = bf16[768,256]{1,0:T(8,128)(2,1)S(1)} custom-call(s32[1]{0:T(128)} %bitcast.8.z_ref, s32[2,32]{1,0:T(2,128)S(1)} %pad_add_fusion.places_ref, bf16[768,3584]{1,0:T(8,128)(2,1)} %all-gather.3.cloned.1.call-done.tokens_ref, bf16[2,1,7168,256]{3,2,1,0:T(8,128)(2,1)} %gate_ref.11, bf16[2,1,7168,256]{3,2,1,0:T(8,128)(2,1)} %up_ref.11, ...), custom_call_target="tpu_custom_call" | custom-call | flops 2818572288 | bytes 12713984 | tf_op jit(solution)/shard_map/pallas_call | solution.py:98
  120.4 5.6 %collective-permute-done.22.refs_2_ = bf16[408,256]{1,0:T(8,128)(2,1)S(1)} collective-permute-done((bf16[408,256]{1,0:T(8,128)(2,1)S(1)}, bf16[408,256]{1,0:T(8,128)(2,1)S(1)}, u32[]{:S(2)}, u32[]{:S(2)}) %collective-permute-start.22) | collective-permute-done | bytes 208928 | tf_op jit(solution)/shard_map/ppermute | solution.py:36
  127.9 4.8 %shard_map.76 = bf16[512,1792]{1,0:T(8,128)(2,1)} custom-call(s32[1]{0:T(128)} %bitcast.8.z_ref, bf16[408,256]{1,0:T(8,128)(2,1)} %copy-done.16, bf16[408,256]{1,0:T(8,128)(2,1)} %copy-done.19, bf16[408,256]{1,0:T(8,128)(2,1)} %copy-done.20, bf16[408,256]{1,0:T(8,128)(2,1)} %copy-done.21, bf16[2,1,256,7168]{3,2,1,0:T(8,128)(2,1)} %refs_4_.3, ...), custom_call_target="tpu_custom_call" | custom-call | flops 1409286144 | bytes 6291456 | tf_op jit(solution)/shard_map/pallas_call | solution.py:142
  132.7 7.0 %all-to-all-start = ((bf16[32,16,1792]{2,1,0:T(8,128)(2,1)}), bf16[32,16,1792]{2,1,0:T(8,128)(2,1)S(1)}, u32[]{:S(2)}, u32[]{:S(2)}) async-start(bf16[32,16,1792]{2,1,0:T(8,128)(2,1)} %bitcast.89), calls=%async_computation | async-start | bytes 3670016 | tf_op jit(solution)/shard_map/all_to_all | solution.py:269
  141.8 23.4 %all-to-all-done = bf16[32,16,1792]{2,1,0:T(8,128)(2,1)S(1)} async-done(((bf16[32,16,1792]{2,1,0:T(8,128)(2,1)}), bf16[32,16,1792]{2,1,0:T(8,128)(2,1)S(1)}, u32[]{:S(2)}, u32[]{:S(2)}) %all-to-all-start) | async-done | bytes 1835040 | tf_op jit(solution)/shard_map/all_to_all | solution.py:269
  184.5 3.7 %collective-permute-done.28 = bf16[2,24,1792]{2,1,0:T(8,128)(2,1)S(1)} collective-permute-done((bf16[2,24,1792]{2,1,0:T(8,128)(2,1)S(1)}, bf16[2,24,1792]{2,1,0:T(8,128)(2,1)S(1)}, u32[]{:S(2)}, u32[]{:S(2)}) %collective-permute-start.28) | collective-permute-done | bytes 172064 | tf_op jit(solution)/shard_map/ppermute | solution.py:31
  191.3 6.6 %collective-permute-done.29 = bf16[4,24,1792]{2,1,0:T(8,128)(2,1)S(1)} collective-permute-done((bf16[4,24,1792]{2,1,0:T(8,128)(2,1)S(1)}, bf16[4,24,1792]{2,1,0:T(8,128)(2,1)S(1)}, u32[]{:S(2)}, u32[]{:S(2)}) %collective-permute-start.29) | collective-permute-done | bytes 344096 | tf_op jit(solution)/shard_map/ppermute | solution.py:31
  199.2 10.5 %collective-permute-start.36 = (bf16[8,24,1792]{2,1,0:T(8,128)(2,1)S(1)}, bf16[8,24,1792]{2,1,0:T(8,128)(2,1)}, u32[]{:S(2)}, u32[]{:S(2)}) collective-permute-start(bf16[8,24,1792]{2,1,0:T(8,128)(2,1)S(1)} %pad_maximum_fusion.3), channel_id=1, source_target_pairs={{0,4},{4,0},{8,12},{12,8},{16,20},{20,16},{24,28},{28,24},{32,36},... | collective-permute-start | bytes 2064392 | tf_op jit(solution)/shard_map/ppermute | solution.py:31
  209.7 4.6 %collective-permute-done.35 = bf16[8,24,1792]{2,1,0:T(8,128)(2,1)} collective-permute-done((bf16[8,24,1792]{2,1,0:T(8,128)(2,1)S(1)}, bf16[8,24,1792]{2,1,0:T(8,128)(2,1)}, u32[]{:S(2)}, u32[]{:S(2)}) %collective-permute-start.35) | collective-permute-done | bytes 688160 | tf_op jit(solution)/shard_map/ppermute | solution.py:31
  214.3 12.9 %collective-permute-start.37 = (bf16[8,24,1792]{2,1,0:T(8,128)(2,1)}, bf16[8,24,1792]{2,1,0:T(8,128)(2,1)}, u32[]{:S(2)}, u32[]{:S(2)}) collective-permute-start(bf16[8,24,1792]{2,1,0:T(8,128)(2,1)} %collective-permute-done.35), channel_id=1, source_target_pairs={{0,4},{4,0},{8,12},{12,8},{16,20},{20,16},{24,28},{28,24},{32,36},... | collective-permute-start | bytes 2064392 | tf_op jit(solution)/shard_map/ppermute | solution.py:31
  231.7 5.0 %shard_map.77.a_ref = f32[768,512]{1,0:T(8,128)} custom-call(s32[1]{0:T(128)} %bitcast.8.z_ref, bf16[192,1792]{1,0:T(8,128)(2,1)} %bitcast.96, bf16[192,1792]{1,0:T(8,128)(2,1)} %bitcast.34.t1, bf16[192,1792]{1,0:T(8,128)(2,1)} %bitcast.35.t2, bf16[192,1792]{1,0:T(8,128)(2,1)} %bitcast.36.t3, bf16[2,1,7168,256]{3,2,1,0:T(8,128)(2,1)} %gate_ref.11, ...), custom_call_target="tpu_custom_call" | custom-call | flops 1409286144 | bytes 6160384 | tf_op jit(solution)/shard_map/pallas_call | solution.py:54
  238.2 5.2 %shard_map.78.b_ref = f32[768,512]{1,0:T(8,128)} custom-call(s32[1]{0:T(128)} %bitcast.8.z_ref, bf16[192,1920]{1,0:T(8,128)(2,1)} %bitcast.94, bf16[192,1920]{1,0:T(8,128)(2,1)} %bitcast.98, bf16[192,1920]{1,0:T(8,128)(2,1)} %bitcast.39.t2, bf16[192,1920]{1,0:T(8,128)(2,1)} %bitcast.40.t3, bf16[2,1,7168,256]{3,2,1,0:T(8,128)(2,1)} %gate_ref.11, ...), custom_call_target="tpu_custom_call" | custom-call | flops 1409286144 | bytes 6160384 | tf_op jit(solution)/shard_map/pallas_call | solution.py:54
  243.4 10.3 %collective-permute-done.41.refs_7_ = bf16[256,1792]{1,0:T(8,128)(2,1)} collective-permute-done((bf16[256,1792]{1,0:T(8,128)(2,1)}, bf16[256,1792]{1,0:T(8,128)(2,1)}, u32[]{:S(2)}, u32[]{:S(2)}) %collective-permute-start.41) | collective-permute-done | bytes 917536 | tf_op jit(solution)/shard_map/ppermute | solution.py:36
  255.1 6.4 %shard_map.79 = bf16[768,256]{1,0:T(8,128)(2,1)S(1)} custom-call(s32[1]{0:T(128)} %bitcast.8.z_ref, s32[2,32]{1,0:T(2,128)S(1)} %pad_add_fusion.places_ref, bf16[768,3584]{1,0:T(8,128)(2,1)} %all-gather.5.cloned.1.call-done.tokens_ref, bf16[2,1,7168,256]{3,2,1,0:T(8,128)(2,1)} %gate_ref.11, bf16[2,1,7168,256]{3,2,1,0:T(8,128)(2,1)} %up_ref.11, ...), custom_call_target="tpu_custom_call" | custom-call | flops 2818572288 | bytes 12713984 | tf_op jit(solution)/shard_map/pallas_call | solution.py:98
  273.5 4.8 %shard_map.80 = bf16[512,1792]{1,0:T(8,128)(2,1)} custom-call(s32[1]{0:T(128)} %bitcast.8.z_ref, bf16[408,256]{1,0:T(8,128)(2,1)} %copy-done.15, bf16[408,256]{1,0:T(8,128)(2,1)} %copy-done.22, bf16[408,256]{1,0:T(8,128)(2,1)} %copy-done.23, bf16[408,256]{1,0:T(8,128)(2,1)} %copy-done.24, bf16[2,1,256,7168]{3,2,1,0:T(8,128)(2,1)} %refs_4_.3, ...), custom_call_target="tpu_custom_call" | custom-call | flops 1409286144 | bytes 6291456 | tf_op jit(solution)/shard_map/pallas_call | solution.py:142
  278.3 7.5 %all-to-all-start.1 = ((bf16[32,16,1792]{2,1,0:T(8,128)(2,1)}), bf16[32,16,1792]{2,1,0:T(8,128)(2,1)S(1)}, u32[]{:S(2)}, u32[]{:S(2)}) async-start(bf16[32,16,1792]{2,1,0:T(8,128)(2,1)} %bitcast.90), calls=%async_computation.1 | async-start | bytes 3670016 | tf_op jit(solution)/shard_map/all_to_all | solution.py:269
  287.7 23.6 %all-to-all-done.1 = bf16[32,16,1792]{2,1,0:T(8,128)(2,1)S(1)} async-done(((bf16[32,16,1792]{2,1,0:T(8,128)(2,1)}), bf16[32,16,1792]{2,1,0:T(8,128)(2,1)S(1)}, u32[]{:S(2)}, u32[]{:S(2)}) %all-to-all-start.1) | async-done | bytes 1835040 | tf_op jit(solution)/shard_map/all_to_all | solution.py:269
  (238 shorter events, 97.5 us)
Async XLA Ops:
  6.5 99.9 %all-gather.3.cloned.1.call-start = ((), (), s32[]{:S(2)}) async-start(), calls=%async_computation.2 | async-start | bytes 5677056 | tf_op jit(solution)/shard_map/all_gather | solution.py:217
  25.5 24.5 %collective-permute-start.12 = (bf16[256,1792]{1,0:T(8,128)(2,1)S(1)}, bf16[256,1792]{1,0:T(8,128)(2,1)S(1)}, u32[]{:S(2)}, u32[]{:S(2)}) collective-permute-start(bf16[256,1792]{1,0:T(8,128)(2,1)S(1)} %get-tuple-element.78), channel_id=1, source_target_pairs={{0,1},{1,0},{2,3},{3,2},{4,5},{5,4},{6,7},{7,6},{8,9},{9,8},{10,11... | collective-permute-start | bytes 2752520 | tf_op jit(solution)/shard_map/ppermute | solution.py:36
  26.4 23.7 %collective-permute-start.13 = (bf16[256,1792]{1,0:T(8,128)(2,1)S(1)}, bf16[256,1792]{1,0:T(8,128)(2,1)S(1)}, u32[]{:S(2)}, u32[]{:S(2)}) collective-permute-start(bf16[256,1792]{1,0:T(8,128)(2,1)S(1)} %get-tuple-element.77), channel_id=1, source_target_pairs={{0,3},{1,2},{2,1},{3,0},{4,7},{5,6},{6,5},{7,4},{8,11},{9,10},{10,... | collective-permute-start | bytes 2752520 | tf_op jit(solution)/shard_map/ppermute | solution.py:36
  37.1 11.4 %collective-permute-start.7 = (bf16[4,24,1792]{2,1,0:T(8,128)(2,1)S(1)}, bf16[4,24,1792]{2,1,0:T(8,128)(2,1)S(1)}, u32[]{:S(2)}, u32[]{:S(2)}) collective-permute-start(bf16[4,24,1792]{2,1,0:T(8,128)(2,1)S(1)} %pad_maximum_fusion.6), channel_id=1, source_target_pairs={{0,32},{4,100},{8,40},{12,108},{16,48},{20,116},{24,56},{28,124},{... | collective-permute-start | bytes 1032200 | tf_op jit(solution)/shard_map/ppermute | solution.py:31
  51.1 29.5 %collective-permute-start.17 = (bf16[8,24,1920]{2,1,0:T(8,128)(2,1)S(1)}, bf16[8,24,1920]{2,1,0:T(8,128)(2,1)S(1)}, u32[]{:S(2)}, u32[]{:S(2)}) collective-permute-start(bf16[8,24,1920]{2,1,0:T(8,128)(2,1)S(1)} %pad_maximum_fusion), channel_id=1, source_target_pairs={{0,24},{4,12},{8,16},{12,4},{16,8},{20,28},{24,0},{28,20},{32,56},... | collective-permute-start | bytes 2211848 | tf_op jit(solution)/shard_map/ppermute | solution.py:31
  51.1 13.8 %collective-permute-start.14 = (bf16[8,24,1792]{2,1,0:T(8,128)(2,1)S(1)}, bf16[8,24,1792]{2,1,0:T(8,128)(2,1)}, u32[]{:S(2)}, u32[]{:S(2)}) collective-permute-start(bf16[8,24,1792]{2,1,0:T(8,128)(2,1)S(1)} %pad_maximum_fusion.2), channel_id=1, source_target_pairs={{0,96},{4,36},{8,104},{12,44},{16,112},{20,52},{24,120},{28,60},{3... | collective-permute-start | bytes 2064392 | tf_op jit(solution)/shard_map/ppermute | solution.py:31
  51.3 40.0 %collective-permute-start.18 = (bf16[8,24,1920]{2,1,0:T(8,128)(2,1)S(1)}, bf16[8,24,1920]{2,1,0:T(8,128)(2,1)}, u32[]{:S(2)}, u32[]{:S(2)}) collective-permute-start(bf16[8,24,1920]{2,1,0:T(8,128)(2,1)S(1)} %pad_maximum_fusion), channel_id=1, source_target_pairs={{0,4},{4,0},{8,12},{12,8},{16,20},{20,16},{24,28},{28,24},{32,36},... | collective-permute-start | bytes 2211848 | tf_op jit(solution)/shard_map/ppermute | solution.py:31
  64.8 21.5 %collective-permute-start.15 = (bf16[8,24,1792]{2,1,0:T(8,128)(2,1)S(1)}, bf16[8,24,1792]{2,1,0:T(8,128)(2,1)}, u32[]{:S(2)}, u32[]{:S(2)}) collective-permute-start(bf16[8,24,1792]{2,1,0:T(8,128)(2,1)S(1)} %pad_maximum_fusion.2), channel_id=1, source_target_pairs={{0,4},{4,0},{8,12},{12,8},{16,20},{20,16},{24,28},{28,24},{32,36},... | collective-permute-start | bytes 2064392 | tf_op jit(solution)/shard_map/ppermute | solution.py:31
  64.9 21.5 %collective-permute-start.16 = (bf16[8,24,1792]{2,1,0:T(8,128)(2,1)}, bf16[8,24,1792]{2,1,0:T(8,128)(2,1)}, u32[]{:S(2)}, u32[]{:S(2)}) collective-permute-start(bf16[8,24,1792]{2,1,0:T(8,128)(2,1)} %collective-permute-done.14), channel_id=1, source_target_pairs={{0,4},{4,0},{8,12},{12,8},{16,20},{20,16},{24,28},{28,24},{32,36},... | collective-permute-start | bytes 2064392 | tf_op jit(solution)/shard_map/ppermute | solution.py:31
  80.5 10.8 %collective-permute-start.19 = (bf16[8,24,1920]{2,1,0:T(8,128)(2,1)S(1)}, bf16[8,24,1920]{2,1,0:T(8,128)(2,1)}, u32[]{:S(2)}, u32[]{:S(2)}) collective-permute-start(bf16[8,24,1920]{2,1,0:T(8,128)(2,1)S(1)} %collective-permute-done.17), channel_id=1, source_target_pairs={{0,4},{4,0},{8,12},{12,8},{16,20},{20,16},{24,28},{28,24},{32,36},... | collective-permute-start | bytes 2211848 | tf_op jit(solution)/shard_map/ppermute | solution.py:31
  83.1 23.4 %collective-permute-start.20 = (bf16[256,1792]{1,0:T(8,128)(2,1)}, bf16[256,1792]{1,0:T(8,128)(2,1)}, u32[]{:S(2)}, u32[]{:S(2)}) collective-permute-start(bf16[256,1792]{1,0:T(8,128)(2,1)} %dynamic-slice_bitcast_fusion.3), channel_id=1, source_target_pairs={{0,2},{1,3},{2,0},{3,1},{4,6},{5,7},{6,4},{7,5},{8,10},{9,11},{10,... | collective-permute-start | bytes 2752520 | tf_op jit(solution)/shard_map/ppermute | solution.py:36
  115.7 10.2 %collective-permute-start.22 = (bf16[408,256]{1,0:T(8,128)(2,1)S(1)}, bf16[408,256]{1,0:T(8,128)(2,1)S(1)}, u32[]{:S(2)}, u32[]{:S(2)}) collective-permute-start(bf16[408,256]{1,0:T(8,128)(2,1)S(1)} %pad_maximum_fusion.8.refs_0_), channel_id=1, source_target_pairs={{0,3},{1,2},{2,1},{3,0},{4,7},{5,6},{6,5},{7,4},{8,11},{9,10},{10,... | collective-permute-start | bytes 626696 | tf_op jit(solution)/shard_map/ppermute | solution.py:36
  132.7 32.5 %all-to-all-start = ((bf16[32,16,1792]{2,1,0:T(8,128)(2,1)}), bf16[32,16,1792]{2,1,0:T(8,128)(2,1)S(1)}, u32[]{:S(2)}, u32[]{:S(2)}) async-start(bf16[32,16,1792]{2,1,0:T(8,128)(2,1)} %bitcast.89), calls=%async_computation | async-start | bytes 3670016 | tf_op jit(solution)/shard_map/all_to_all | solution.py:269
  139.8 113.9 %all-gather.5.cloned.1.call-start = ((), (), s32[]{:S(2)}) async-start(), calls=%async_computation.3 | async-start | bytes 5677056 | tf_op jit(solution)/shard_map/all_gather | solution.py:217
  176.4 21.9 %collective-permute-start.33 = (bf16[256,1792]{1,0:T(8,128)(2,1)S(1)}, bf16[256,1792]{1,0:T(8,128)(2,1)S(1)}, u32[]{:S(2)}, u32[]{:S(2)}) collective-permute-start(bf16[256,1792]{1,0:T(8,128)(2,1)S(1)} %get-tuple-element.76), channel_id=1, source_target_pairs={{0,1},{1,0},{2,3},{3,2},{4,5},{5,4},{6,7},{7,6},{8,9},{9,8},{10,11... | collective-permute-start | bytes 2752520 | tf_op jit(solution)/shard_map/ppermute | solution.py:36
  176.9 21.4 %collective-permute-start.34 = (bf16[256,1792]{1,0:T(8,128)(2,1)S(1)}, bf16[256,1792]{1,0:T(8,128)(2,1)S(1)}, u32[]{:S(2)}, u32[]{:S(2)}) collective-permute-start(bf16[256,1792]{1,0:T(8,128)(2,1)S(1)} %get-tuple-element.75), channel_id=1, source_target_pairs={{0,3},{1,2},{2,1},{3,0},{4,7},{5,6},{6,5},{7,4},{8,11},{9,10},{10,... | collective-permute-start | bytes 2752520 | tf_op jit(solution)/shard_map/ppermute | solution.py:36
  188.2 9.7 %collective-permute-start.29 = (bf16[4,24,1792]{2,1,0:T(8,128)(2,1)S(1)}, bf16[4,24,1792]{2,1,0:T(8,128)(2,1)S(1)}, u32[]{:S(2)}, u32[]{:S(2)}) collective-permute-start(bf16[4,24,1792]{2,1,0:T(8,128)(2,1)S(1)} %pad_maximum_fusion.7), channel_id=1, source_target_pairs={{0,32},{4,100},{8,40},{12,108},{16,48},{20,116},{24,56},{28,124},{... | collective-permute-start | bytes 1032200 | tf_op jit(solution)/shard_map/ppermute | solution.py:31
  198.3 15.9 %collective-permute-start.35 = (bf16[8,24,1792]{2,1,0:T(8,128)(2,1)S(1)}, bf16[8,24,1792]{2,1,0:T(8,128)(2,1)}, u32[]{:S(2)}, u32[]{:S(2)}) collective-permute-start(bf16[8,24,1792]{2,1,0:T(8,128)(2,1)S(1)} %pad_maximum_fusion.3), channel_id=1, source_target_pairs={{0,96},{4,36},{8,104},{12,44},{16,112},{20,52},{24,120},{28,60},{3... | collective-permute-start | bytes 2064392 | tf_op jit(solution)/shard_map/ppermute | solution.py:31
  198.6 28.6 %collective-permute-start.38 = (bf16[8,24,1920]{2,1,0:T(8,128)(2,1)S(1)}, bf16[8,24,1920]{2,1,0:T(8,128)(2,1)S(1)}, u32[]{:S(2)}, u32[]{:S(2)}) collective-permute-start(bf16[8,24,1920]{2,1,0:T(8,128)(2,1)S(1)} %pad_maximum_fusion.1), channel_id=1, source_target_pairs={{0,24},{4,12},{8,16},{12,4},{16,8},{20,28},{24,0},{28,20},{32,56},... | collective-permute-start | bytes 2211848 | tf_op jit(solution)/shard_map/ppermute | solution.py:31
  199.2 32.5 %collective-permute-start.36 = (bf16[8,24,1792]{2,1,0:T(8,128)(2,1)S(1)}, bf16[8,24,1792]{2,1,0:T(8,128)(2,1)}, u32[]{:S(2)}, u32[]{:S(2)}) collective-permute-start(bf16[8,24,1792]{2,1,0:T(8,128)(2,1)S(1)} %pad_maximum_fusion.3), channel_id=1, source_target_pairs={{0,4},{4,0},{8,12},{12,8},{16,20},{20,16},{24,28},{28,24},{32,36},... | collective-permute-start | bytes 2064392 | tf_op jit(solution)/shard_map/ppermute | solution.py:31
  214.3 17.4 %collective-permute-start.37 = (bf16[8,24,1792]{2,1,0:T(8,128)(2,1)}, bf16[8,24,1792]{2,1,0:T(8,128)(2,1)}, u32[]{:S(2)}, u32[]{:S(2)}) collective-permute-start(bf16[8,24,1792]{2,1,0:T(8,128)(2,1)} %collective-permute-done.35), channel_id=1, source_target_pairs={{0,4},{4,0},{8,12},{12,8},{16,20},{20,16},{24,28},{28,24},{32,36},... | collective-permute-start | bytes 2064392 | tf_op jit(solution)/shard_map/ppermute | solution.py:31
  227.2 9.6 %collective-permute-start.39 = (bf16[8,24,1920]{2,1,0:T(8,128)(2,1)S(1)}, bf16[8,24,1920]{2,1,0:T(8,128)(2,1)}, u32[]{:S(2)}, u32[]{:S(2)}) collective-permute-start(bf16[8,24,1920]{2,1,0:T(8,128)(2,1)S(1)} %pad_maximum_fusion.1), channel_id=1, source_target_pairs={{0,4},{4,0},{8,12},{12,8},{16,20},{20,16},{24,28},{28,24},{32,36},... | collective-permute-start | bytes 2211848 | tf_op jit(solution)/shard_map/ppermute | solution.py:31
  230.0 23.6 %collective-permute-start.41 = (bf16[256,1792]{1,0:T(8,128)(2,1)}, bf16[256,1792]{1,0:T(8,128)(2,1)}, u32[]{:S(2)}, u32[]{:S(2)}) collective-permute-start(bf16[256,1792]{1,0:T(8,128)(2,1)} %dynamic-slice_bitcast_fusion), channel_id=1, source_target_pairs={{0,2},{1,3},{2,0},{3,1},{4,6},{5,7},{6,4},{7,5},{8,10},{9,11},{10,... | collective-permute-start | bytes 2752520 | tf_op jit(solution)/shard_map/ppermute | solution.py:36
  278.3 33.0 %all-to-all-start.1 = ((bf16[32,16,1792]{2,1,0:T(8,128)(2,1)}), bf16[32,16,1792]{2,1,0:T(8,128)(2,1)S(1)}, u32[]{:S(2)}, u32[]{:S(2)}) async-start(bf16[32,16,1792]{2,1,0:T(8,128)(2,1)} %bitcast.90), calls=%async_computation.1 | async-start | bytes 3670016 | tf_op jit(solution)/shard_map/all_to_all | solution.py:269
  (52 other events, 587.4 us)
Sparse Core Ops, SparseCore 0:
  23.7 54.8 all-gather.2
  174.9 49.7 all-gather.4

commit v6 on v4

v6 whole, which is shorter than its diff:
```python
import functools

import jax
import jax.numpy as jnp
from jax import lax
from jax.experimental import pallas as pl
from jax.experimental.pallas import tpu as pltpu
from jax.sharding import PartitionSpec as P

route_scale = 2.5
bf16, f32 = jnp.bfloat16, jnp.float32

SIBLING = (1, 1)
ORDER = (0, 1, 3, 2)


def short(values):
    return lax.reduce_precision(values, 8, 7)


def thirds(values):
    high = short(values)
    middle = short(values - high)
    return [part.astype(bf16) for part in (high, middle, values - high - middle)]


def swap(block, masks):
    count = lax.axis_size("expert")
    return lax.ppermute(block, "expert", [(i, i ^ masks[i & 1]) for i in range(count)])


def z_swap(block, mask):
    count = lax.axis_size("tensor")
    return lax.ppermute(block, "tensor", [(i, i ^ mask) for i in range(count)])


def after(block, *others):
    return lax.optimization_barrier((block, *others))[0]


def gate_up_kernel(layer, z_ref, tokens_ref, gate_ref, up_ref, act_ref, tokens, weights, sums, sems):
    steps, depth = weights.shape[1:3]
    copies = []
    for step, mask in enumerate(ORDER):
        features = pl.ds(pl.multiple_of((z_ref[0] ^ mask) * depth, depth), depth)
        parts = [
            (tokens_ref.at[:, pl.ds(step * depth, depth)], tokens.at[step]),
            (gate_ref.at[layer, 0, features], weights.at[0, step]),
            (up_ref.at[layer, 0, features], weights.at[1, step]),
        ]
        copies.append(
            [pltpu.make_async_copy(*part, sems.at[n, step]) for n, part in enumerate(parts)]
        )
    for copy in sum(copies, []):
        copy.start()
    for step in range(steps):
        for copy in copies[step]:
            copy.wait()
        gate = jnp.dot(tokens[step], weights[0, step], preferred_element_type=f32)
        up = jnp.dot(tokens[step], weights[1, step], preferred_element_type=f32)
        if step == 0:
            sums[0], sums[1] = gate, up
        elif step < steps - 1:
            sums[0] += gate
            sums[1] += up
        else:
            gate += sums[0]
            up += sums[1]
            act_ref[...] = (gate / (1.0 + jnp.exp(-gate)) * up).astype(act_ref.dtype)


def gate_up(z, tokens, w_gate, w_up, layer):
    rows, units = tokens.shape[0], w_gate.shape[-1]
    steps = len(ORDER)
    depth = w_gate.shape[2] // steps
    outside = pl.BlockSpec(memory_space=pl.ANY)
    return pl.pallas_call(
        functools.partial(gate_up_kernel, layer),
        in_specs=[pl.BlockSpec(memory_space=pltpu.SMEM)] + [outside] * 3,
        out_specs=pl.BlockSpec(memory_space=pltpu.VMEM),
        out_shape=jax.ShapeDtypeStruct((rows, units), bf16),
        scratch_shapes=[
            pltpu.VMEM((steps, rows, depth), bf16),
            pltpu.VMEM((2, steps, depth, units), bf16),
            pltpu.VMEM((2, rows, units), f32),
            pltpu.SemaphoreType.DMA((3, steps)),
        ],
        compiler_params=pltpu.CompilerParams(vmem_limit_bytes=58 << 20),
        cost_estimate=pl.CostEstimate(
            flops=16 * rows * depth * units,
            bytes_accessed=8 * (rows + 2 * units) * depth + 2 * rows * units,
            transcendentals=rows * units,
        ),
    )(jnp.full((1,), z, jnp.int32), tokens, w_gate, w_up)


def down_kernel(z_ref, *refs):
    acts, weights, out_ref = refs[:4], refs[4:-1], refs[-1]
    acts = jnp.concatenate([act[...] for act in acts], axis=1)
    weights = jnp.concatenate([weights[0][0, 0]] + [w[...] for w in weights[1:]], axis=0)
    out_ref[...] = jnp.dot(acts, weights, preferred_element_type=f32).astype(out_ref.dtype)


def down_product(z, acts, slots, w_down, layer, others):
    units = w_down.shape[2]
    part = others[0].shape[-1]
    steps = 2
    columns = part // steps
    act = pl.BlockSpec((slots, units), lambda n, z: (0, 0))
    return pl.pallas_call(
        down_kernel,
        grid_spec=pltpu.PrefetchScalarGridSpec(
            num_scalar_prefetch=1,
            grid=(steps,),
            in_specs=[act] * 4
            + [pl.BlockSpec((1, 1, units, columns), lambda n, z: (layer, 0, 0, z[0] * steps + n))]
            + [pl.BlockSpec((w.shape[0], columns), lambda n, z: (0, n)) for w in others],
            out_specs=pl.BlockSpec((slots, columns), lambda n, z: (0, n)),
        ),
        out_shape=jax.ShapeDtypeStruct((slots, part), bf16),
        cost_estimate=pl.CostEstimate(
            flops=8 * slots * units * part,
            bytes_accessed=8 * units * (slots + part) + 2 * slots * part,
            transcendentals=0,
        ),
    )(jnp.full((1,), z, jnp.int32), *acts, w_down, *others)


def body(hidden_in, norm_gain, router, w_gate, w_up, w_down, routes):
    rows, part = hidden_in.shape
    layers, width, units = w_gate.shape[0], w_gate.shape[2], w_gate.shape[3]
    experts = router.shape[2]
    capacity = min(rows, 2 * rows * routes.shape[2] // experts)
    slots = experts * capacity
    chips = experts // 2
    me = lax.axis_index("expert")
    core = me & 1
    z = lax.axis_index("tensor")

    expert_iota = lax.broadcasted_iota(jnp.int32, (1, 1, 1, experts), 3)
    picks = jnp.any(routes[..., None] == expert_iota, axis=2)
    earlier = lax.broadcasted_iota(jnp.int32, (rows, rows), 0) >= lax.broadcasted_iota(
        jnp.int32, (rows, rows), 1
    )
    ranks = jnp.einsum("st,lte->lse", earlier.astype(bf16), picks.astype(bf16), preferred_element_type=f32)
    marks = jnp.where(picks, ranks, 0.0)
    marks_sent = jnp.concatenate([marks[layer] for layer in range(layers)], axis=1)
    marks_sent = jnp.pad(marks_sent, ((0, 0), (0, 128 - layers * experts))).astype(bf16)

    def spread(block):
        return [block] + [z_swap(block, mask) for mask in ORDER[1:]]

    def columns(layer, mask, first, count, *bound):
        column = (after(z, *bound) ^ mask) * part
        block = lax.dynamic_slice(w_down, (layer, 0, first, column), (1, 1, count, part))
        return z_swap(block.reshape(count, part), mask)

    state = hidden_in
    gains = jnp.stack(thirds(norm_gain), axis=0).reshape(3 * layers, part)
    opening = [state, gains, jnp.zeros((8 - 3 * layers, part), bf16)]
    opening = spread(jnp.concatenate(opening, axis=0))
    gains = [
        block[rows : rows + 3 * layers].astype(f32).reshape(3, layers, part).sum(axis=0)
        for block in opening
    ]
    for layer in range(layers):
        blocks = spread(state) if layer else [block[:rows] for block in opening]
        blocks = [block.astype(f32) for block in blocks]
        scale = sum(jnp.sum(block * block, axis=1) for block in blocks)
        scale = lax.rsqrt(scale / width + 1e-06)
        normed = [
            (block * scale[:, None] * gain[layer][None, :]).astype(bf16)
            for block, gain in zip(blocks, gains)
        ]

        sent = jnp.concatenate(normed if layer else normed + [marks_sent], axis=1)
        arrived = lax.all_gather(sent, "expert", axis=0, tiled=True)
        others = [columns(layer, mask, 0, units, sent) for mask in ORDER[1:]]
        arrived, *others = lax.optimization_barrier((arrived, *others))
        if layer == 0:
            marks_here = arrived[:, width:]
        act = gate_up(z, arrived, w_gate, w_up, layer)

        mine = lax.broadcasted_iota(jnp.int32, (1, 128), 1) == me + layer * experts
        mark = jnp.sum(jnp.where(mine, marks_here.astype(f32), 0.0), axis=1).astype(jnp.int32)
        source = lax.broadcasted_iota(jnp.int32, (experts, rows), 0).reshape(-1)
        slot = jnp.where(mark > 0, source * capacity + mark - 1, -1)[None, :]
        taken = (lax.broadcasted_iota(jnp.int32, (slots, 1), 0) == slot).astype(bf16)
        act = jnp.dot(taken, act, preferred_element_type=f32).astype(bf16)

        own = state.astype(f32) * scale[:, None] * norm_gain[layer][None, :]
        own = own.astype(bf16).astype(f32)
        scores = jnp.dot(own, router[layer], precision=lax.Precision.HIGHEST)
        scores = jnp.pad(jnp.concatenate(thirds(scores), axis=1), ((0, 0), (0, units - 3 * experts)))
        act = jnp.concatenate([act, scores], axis=0)
        acts = spread(act)
        scores = sum(block[slots:].astype(f32) for block in acts)
        scores = sum(scores[:, experts * n : experts * (n + 1)] for n in range(3))
        out = down_product(z, acts, slots, w_down, layer, others)
        probs = jax.nn.sigmoid(after(scores, out))
        picked = jnp.where(picks[layer], probs, 0.0)
        weights = route_scale * picked / jnp.sum(picked, axis=1, keepdims=True)

        def mixer(parity):
            def of_parity(table):
                table = table.reshape(rows, chips, 2)
                return jnp.where(parity == 1, table[:, :, 1], table[:, :, 0])[:, :, None, None]

            shape = (1, 1, 2, capacity)
            slot = lax.broadcasted_iota(jnp.int32, shape, 3).astype(f32) + 1.0
            here = lax.broadcasted_iota(jnp.int32, shape, 2) == core
            table = jnp.where(here & (of_parity(marks[layer]) == slot), of_parity(weights), 0.0)
            return jnp.concatenate(thirds(table.reshape(rows, slots))[:2], axis=0)

        mixers = jnp.concatenate([mixer(core), swap(mixer(1 - core), SIBLING)], axis=0)
        groups = [list(range(parity, experts, 2)) for parity in range(2)]
        returned = lax.all_to_all(
            out.reshape(chips, 2 * capacity, part),
            "expert",
            split_axis=0,
            concat_axis=0,
            axis_index_groups=groups,
        ).reshape(slots, part)
        mixed = jnp.dot(mixers, returned, preferred_element_type=f32).reshape(2, 2, rows, part)
        mixed = mixed[:, 0] + mixed[:, 1]
        state = (state.astype(f32) + mixed[0] + swap(mixed[1], SIBLING)).astype(bf16)
    return state


def solution(mesh):
    placed = (
        P("expert", "tensor"),
        P(None, "tensor"),
        P(None, "tensor", None),
        P(None, "expert", None, "tensor"),
        P(None, "expert", None, "tensor"),
        P(None, "expert", "tensor", None),
        P(None, "expert", None),
    )
    return jax.shard_map(
        body, mesh=mesh, in_specs=placed, out_specs=P("expert", "tensor"), check_vma=False
    )
```

time: 294 us -> 274 us (0.932)
  waiting for transfers between devices: 178 us -> 154 us
  local copies, waits for them, and re-layouts: 11.3 us -> 17.9 us
  Pallas kernels: 34 us -> 27.7 us
  starting transfers between devices: 40.5 us -> 44.9 us
    all_to_all x2, waiting for transfers between devices: 47 us -> 23.1 us  [body(): lax.all_to_all(out.reshape(chips, 2 * capacity, part), 'expert', split_ax...]
    ppermute x0 -> x4, starting transfers between devices: none -> 11.3 us  [swap(): lax.ppermute(block, 'expert', [(i, i ^ masks[i & 1]) for i in range(count)])]
    pallas_call x4, Pallas kernels: 34 us -> 27.7 us  [the longest x2 18.3 us: gate_up(): pl.pallas_call(functools.partial(gate_up_kernel, layer), in_specs=[pl.Blo...]
    all_gather x2, waiting for transfers between devices: 35.4 us -> 29.3 us  [body(): arrived = lax.all_gather(sent, 'expert', axis=0, tiled=True)]
    ppermute x0 -> x4, waiting for transfers between devices: none -> 3.81 us  [swap(): lax.ppermute(block, 'expert', [(i, i ^ masks[i & 1]) for i in range(count)])]
    all_to_all x2, starting transfers between devices: 13.4 us -> 9.74 us  [body(): lax.all_to_all(out.reshape(chips, 2 * capacity, part), 'expert', split_ax...]
    eq x7 -> x10, local copies, waits for them, and re-layouts: 0.83 us -> 4.03 us  [mixer(): of_parity(marks[layer]) == slot]
    ppermute x21 -> x18, starting transfers between devices: 27 us -> 23.9 us  [z_swap(): return lax.ppermute(block, 'tensor', [(i, i ^ mask) for i in range(count)])]
  transfers between devices with their start and end apart: 25 -> 26, of which waited for: 18 -> 25; matrix products, arithmetic and copies ran while one was open for 5% -> 8% of each run, Pallas kernels for 0% -> 0%
where the time goes in v6:
time: 274 us; the launch traced here: 273 us
  waiting for transfers between devices  154 us (56%)
  starting transfers between devices  44.9 us (16%)
  Pallas kernels  27.7 us (10%)
  local copies, waits for them, and re-layouts  17.9 us (7%)
  between operations  14 us (5%)
  other arithmetic  9.76 us (4%)
  matrix products  5 us (2%)
    ppermute x18, waiting for transfers between devices, z_swap(): return lax.ppermute(block, 'tensor', [(i, i ^ mask) for i in range(count)])  97.6 us
    all_gather x2, waiting for transfers between devices, body(): arrived = lax.all_gather(sent, 'expert', axis=0, tiled=True)  29.3 us
    ppermute x18, starting transfers between devices, z_swap(): return lax.ppermute(block, 'tensor', [(i, i ^ mask) for i in range(count)])  23.9 us
    all_to_all x2, waiting for transfers between devices, body(): lax.all_to_all(out.reshape(chips, 2 * capacity, part), 'expert', split_ax...  23.1 us
    pallas_call x2, Pallas kernels, gate_up(): pl.pallas_call(functools.partial(gate_up_kernel, layer), in_specs=[pl.Blo...  18.3 us
    ppermute x4, starting transfers between devices, swap(): lax.ppermute(block, 'expert', [(i, i ^ masks[i & 1]) for i in range(count)])  11.3 us
    all_to_all x2, starting transfers between devices, body(): lax.all_to_all(out.reshape(chips, 2 * capacity, part), 'expert', split_ax...  9.74 us
    pallas_call x2, Pallas kernels, down_product(): pl.pallas_call(down_kernel, grid_spec=pltpu.PrefetchScalarGridSpec(num_sc...  9.38 us
  transfers between devices with their start and end apart: 26, of which 25 were waited for; matrix products, arithmetic and copies ran while one was open for 8% of the time, Pallas kernels for 0%

profile of v6, /device:TPU:1, one launch (start us, length us, event | category | flops | bytes accessed | tf_op | source)
XLA Modules:
  0.0 273.1 jit_solution(10147885167322018018)
XLA Ops:
  8.5 2.5 collective-permute-start
  16.8 2.4 collective-permute-done.2
  21.0 3.4 %dynamic-slice_bitcast_fusion.3 = (bf16[256,1792]{1,0:T(8,128)(2,1)}, bf16[256,1792]{1,0:T(8,128)(2,1)}, bf16[256,1792]{1,0:T(8,128)(2,1)}) fusion(bf16[2,1,256,7168]{3,2,1,0:T(8,128)(2,1)} %refs_4_.3, s32[]{:T(128)S(6)} %select_n.168, s32[]{:T(128)S(6)} %select_n.167, s32[]{:T(128)S(6)} %select_n.166), kind=kLoop, calls=%fused_computation.11 | loop fusion | bytes 5505036 | tf_op jit(solution)/shard_map/reshape | solution.py:156
  31.5 13.5 %collective-permute-done.3.refs_5_ = bf16[256,1792]{1,0:T(8,128)(2,1)S(1)} collective-permute-done((bf16[256,1792]{1,0:T(8,128)(2,1)}, bf16[256,1792]{1,0:T(8,128)(2,1)S(1)}, u32[]{:S(2)}, u32[]{:S(2)}) %collective-permute-start.3) | collective-permute-done | bytes 917536 | tf_op jit(solution)/shard_map/ppermute | solution.py:34
  45.2 21.6 %collective-permute-done.5.refs_7_ = bf16[256,1792]{1,0:T(8,128)(2,1)S(1)} collective-permute-done((bf16[256,1792]{1,0:T(8,128)(2,1)}, bf16[256,1792]{1,0:T(8,128)(2,1)S(1)}, u32[]{:S(2)}, u32[]{:S(2)}) %collective-permute-start.5) | collective-permute-done | bytes 917536 | tf_op jit(solution)/shard_map/ppermute | solution.py:34
  66.8 15.7 %all-gather.3.cloned.1.call-done.tokens_ref = bf16[768,7296]{1,0:T(8,128)(2,1)} async-done(((bf16[24,7296]{1,0:T(8,128)(2,1)}), bf16[768,7296]{1,0:T(8,128)(2,1)}) %all-gather.3.cloned.1.call-update) | async-done | bytes 11206672 | tf_op jit(solution)/shard_map/all_gather | solution.py:177
  83.6 9.2 %shard_map.73 = bf16[768,256]{1,0:T(8,128)(2,1)} custom-call(s32[1]{0:T(128)} %bitcast.14.z_ref, bf16[768,7296]{1,0:T(8,128)(2,1)} %all-gather.3.cloned.1.call-done.tokens_ref, bf16[2,1,7168,256]{3,2,1,0:T(8,128)(2,1)} %gate_ref.3, bf16[2,1,7168,256]{3,2,1,0:T(8,128)(2,1)} %up_ref.3), custom_call_target="tpu_custom_call" | custom-call | flops 5637144576 | bytes 18743296 | tf_op jit(solution)/shard_map/pallas_call | solution.py:77
  98.4 2.3 collective-permute-done.6.refs_1_
  100.7 5.0 %collective-permute-done.7.refs_2_ = bf16[408,256]{1,0:T(8,128)(2,1)S(1)} collective-permute-done((bf16[408,256]{1,0:T(8,128)(2,1)S(1)}, bf16[408,256]{1,0:T(8,128)(2,1)S(1)}, u32[]{:S(2)}, u32[]{:S(2)}) %collective-permute-start.7) | collective-permute-done | bytes 208928 | tf_op jit(solution)/shard_map/ppermute | solution.py:34
  108.3 4.7 %shard_map.74 = bf16[384,1792]{1,0:T(8,128)(2,1)} custom-call(s32[1]{0:T(128)} %bitcast.14.z_ref, bf16[408,256]{1,0:T(8,128)(2,1)} %copy-done.6, bf16[408,256]{1,0:T(8,128)(2,1)} %copy-done.10, bf16[408,256]{1,0:T(8,128)(2,1)} %copy-done.11, bf16[408,256]{1,0:T(8,128)(2,1)} %copy-done.12, bf16[2,1,256,7168]{3,2,1,0:T(8,128)(2,1)} %refs_4_.3, ...), custom_call_target="tpu_custom_call" | custom-call | flops 1409286144 | bytes 5832704 | tf_op jit(solution)/shard_map/pallas_call | solution.py:110
  113.0 4.9 %all-to-all-start = ((bf16[16,24,1792]{2,1,0:T(8,128)(2,1)}), bf16[16,24,1792]{2,1,0:T(8,128)(2,1)S(1)}, u32[]{:S(2)}, u32[]{:S(2)}) async-start(bf16[16,24,1792]{2,1,0:T(8,128)(2,1)} %bitcast.103), calls=%async_computation | async-start | bytes 2752512 | tf_op jit(solution)/shard_map/all_to_all | solution.py:217
  124.1 12.4 %all-to-all-done = bf16[16,24,1792]{2,1,0:T(8,128)(2,1)S(1)} async-done(((bf16[16,24,1792]{2,1,0:T(8,128)(2,1)}), bf16[16,24,1792]{2,1,0:T(8,128)(2,1)S(1)}, u32[]{:S(2)}, u32[]{:S(2)}) %all-to-all-start) | async-done | bytes 1376288 | tf_op jit(solution)/shard_map/all_to_all | solution.py:217
  136.9 4.0 %collective-permute-start.10 = (f32[24,1792]{1,0:T(8,128)S(1)}, f32[24,1792]{1,0:T(8,128)S(1)}, u32[]{:S(2)}, u32[]{:S(2)}) collective-permute-start(f32[24,1792]{1,0:T(8,128)S(1)} %slice_bitcast_fusion.2), channel_id=1, source_target_pairs={{0,4},{4,0},{8,12},{12,8},{16,20},{20,16},{24,28},{28,24},{32,36},... | collective-permute-start | bytes 516104 | tf_op jit(solution)/shard_map/ppermute | solution.py:29
  146.9 2.4 collective-permute-done.13
  156.1 16.4 %collective-permute-done.14.refs_5_ = bf16[256,1792]{1,0:T(8,128)(2,1)S(1)} collective-permute-done((bf16[256,1792]{1,0:T(8,128)(2,1)S(1)}, bf16[256,1792]{1,0:T(8,128)(2,1)S(1)}, u32[]{:S(2)}, u32[]{:S(2)}) %collective-permute-start.14) | collective-permute-done | bytes 917536 | tf_op jit(solution)/shard_map/ppermute | solution.py:34
  173.9 19.8 %collective-permute-done.16.refs_7_ = bf16[256,1792]{1,0:T(8,128)(2,1)} collective-permute-done((bf16[256,1792]{1,0:T(8,128)(2,1)S(1)}, bf16[256,1792]{1,0:T(8,128)(2,1)}, u32[]{:S(2)}, u32[]{:S(2)}) %collective-permute-start.16) | collective-permute-done | bytes 917536 | tf_op jit(solution)/shard_map/ppermute | solution.py:34
  193.7 13.6 %all-gather.5.cloned.1.call-done.tokens_ref = bf16[768,7168]{1,0:T(8,128)(2,1)} async-done(((bf16[24,7168]{1,0:T(8,128)(2,1)}), bf16[768,7168]{1,0:T(8,128)(2,1)}) %all-gather.5.cloned.1.call-update) | async-done | bytes 11010064 | tf_op jit(solution)/shard_map/all_gather | solution.py:177
  207.3 9.1 %shard_map.75 = bf16[768,256]{1,0:T(8,128)(2,1)} custom-call(s32[1]{0:T(128)} %bitcast.14.z_ref, bf16[768,7168]{1,0:T(8,128)(2,1)} %all-gather.5.cloned.1.call-done.tokens_ref, bf16[2,1,7168,256]{3,2,1,0:T(8,128)(2,1)} %gate_ref.3, bf16[2,1,7168,256]{3,2,1,0:T(8,128)(2,1)} %up_ref.3), custom_call_target="tpu_custom_call" | custom-call | flops 5637144576 | bytes 18743296 | tf_op jit(solution)/shard_map/pallas_call | solution.py:77
  221.8 2.6 collective-permute-done.17.refs_1_
  224.4 5.0 %collective-permute-done.18.refs_2_ = bf16[408,256]{1,0:T(8,128)(2,1)S(1)} collective-permute-done((bf16[408,256]{1,0:T(8,128)(2,1)S(1)}, bf16[408,256]{1,0:T(8,128)(2,1)S(1)}, u32[]{:S(2)}, u32[]{:S(2)}) %collective-permute-start.18) | collective-permute-done | bytes 208928 | tf_op jit(solution)/shard_map/ppermute | solution.py:34
  232.0 4.7 %shard_map.76 = bf16[384,1792]{1,0:T(8,128)(2,1)} custom-call(s32[1]{0:T(128)} %bitcast.14.z_ref, bf16[408,256]{1,0:T(8,128)(2,1)} %copy-done.7, bf16[408,256]{1,0:T(8,128)(2,1)} %copy-done.13, bf16[408,256]{1,0:T(8,128)(2,1)} %copy-done.14, bf16[408,256]{1,0:T(8,128)(2,1)} %copy-done.15, bf16[2,1,256,7168]{3,2,1,0:T(8,128)(2,1)} %refs_4_.3, ...), custom_call_target="tpu_custom_call" | custom-call | flops 1409286144 | bytes 5832704 | tf_op jit(solution)/shard_map/pallas_call | solution.py:110
  236.7 4.9 %all-to-all-start.1 = ((bf16[16,24,1792]{2,1,0:T(8,128)(2,1)}), bf16[16,24,1792]{2,1,0:T(8,128)(2,1)S(1)}, u32[]{:S(2)}, u32[]{:S(2)}) async-start(bf16[16,24,1792]{2,1,0:T(8,128)(2,1)} %bitcast.102), calls=%async_computation.1 | async-start | bytes 2752512 | tf_op jit(solution)/shard_map/all_to_all | solution.py:217
  249.5 10.7 %all-to-all-done.1 = bf16[16,24,1792]{2,1,0:T(8,128)(2,1)S(1)} async-done(((bf16[16,24,1792]{2,1,0:T(8,128)(2,1)}), bf16[16,24,1792]{2,1,0:T(8,128)(2,1)S(1)}, u32[]{:S(2)}, u32[]{:S(2)}) %all-to-all-start.1) | async-done | bytes 1376288 | tf_op jit(solution)/shard_map/all_to_all | solution.py:217
  260.6 4.0 %collective-permute-start.21 = (f32[24,1792]{1,0:T(8,128)S(1)}, f32[24,1792]{1,0:T(8,128)S(1)}, u32[]{:S(2)}, u32[]{:S(2)}) collective-permute-start(f32[24,1792]{1,0:T(8,128)S(1)} %slice_bitcast_fusion), channel_id=1, source_target_pairs={{0,4},{4,0},{8,12},{12,8},{16,20},{20,16},{24,28},{28,24},{32,36},... | collective-permute-start | bytes 516104 | tf_op jit(solution)/shard_map/ppermute | solution.py:29
  (184 shorter events, 64.4 us)
Async XLA Ops:
  6.5 75.9 %all-gather.3.cloned.1.call-start = ((), (), s32[]{:S(2)}) async-start(), calls=%async_computation.2 | async-start | bytes 11556864 | tf_op jit(solution)/shard_map/all_gather | solution.py:177
  8.5 8.0 %collective-permute-start = (bf16[32,1792]{1,0:T(8,128)(2,1)S(1)}, bf16[32,1792]{1,0:T(8,128)(2,1)S(1)}, u32[]{:S(2)}, u32[]{:S(2)}) collective-permute-start(bf16[32,1792]{1,0:T(8,128)(2,1)S(1)} %maximum_maximum_fusion), channel_id=1, source_target_pairs={{0,1},{1,0},{2,3},{3,2},{4,5},{5,4},{6,7},{7,6},{8,9},{9,8},{10,11... | collective-permute-start | bytes 344072 | tf_op jit(solution)/shard_map/ppermute | solution.py:34
  11.0 5.7 %collective-permute-start.1 = (bf16[32,1792]{1,0:T(8,128)(2,1)S(1)}, bf16[32,1792]{1,0:T(8,128)(2,1)S(1)}, u32[]{:S(2)}, u32[]{:S(2)}) collective-permute-start(bf16[32,1792]{1,0:T(8,128)(2,1)S(1)} %maximum_maximum_fusion), channel_id=1, source_target_pairs={{0,3},{1,2},{2,1},{3,0},{4,7},{5,6},{6,5},{7,4},{8,11},{9,10},{10,... | collective-permute-start | bytes 344072 | tf_op jit(solution)/shard_map/ppermute | solution.py:34
  13.2 6.0 %collective-permute-start.2 = (bf16[32,1792]{1,0:T(8,128)(2,1)S(1)}, bf16[32,1792]{1,0:T(8,128)(2,1)S(1)}, u32[]{:S(2)}, u32[]{:S(2)}) collective-permute-start(bf16[32,1792]{1,0:T(8,128)(2,1)S(1)} %maximum_maximum_fusion), channel_id=1, source_target_pairs={{0,2},{1,3},{2,0},{3,1},{4,6},{5,7},{6,4},{7,5},{8,10},{9,11},{10,... | collective-permute-start | bytes 344072 | tf_op jit(solution)/shard_map/ppermute | solution.py:34
  24.5 20.5 %collective-permute-start.3 = (bf16[256,1792]{1,0:T(8,128)(2,1)}, bf16[256,1792]{1,0:T(8,128)(2,1)S(1)}, u32[]{:S(2)}, u32[]{:S(2)}) collective-permute-start(bf16[256,1792]{1,0:T(8,128)(2,1)} %get-tuple-element.50), channel_id=1, source_target_pairs={{0,1},{1,0},{2,3},{3,2},{4,5},{5,4},{6,7},{7,6},{8,9},{9,8},{10,11... | collective-permute-start | bytes 2752520 | tf_op jit(solution)/shard_map/ppermute | solution.py:34
  24.5 20.7 %collective-permute-start.4 = (bf16[256,1792]{1,0:T(8,128)(2,1)}, bf16[256,1792]{1,0:T(8,128)(2,1)S(1)}, u32[]{:S(2)}, u32[]{:S(2)}) collective-permute-start(bf16[256,1792]{1,0:T(8,128)(2,1)} %get-tuple-element.49), channel_id=1, source_target_pairs={{0,3},{1,2},{2,1},{3,0},{4,7},{5,6},{6,5},{7,4},{8,11},{9,10},{10,... | collective-permute-start | bytes 2752520 | tf_op jit(solution)/shard_map/ppermute | solution.py:34
  26.6 40.2 %collective-permute-start.5 = (bf16[256,1792]{1,0:T(8,128)(2,1)}, bf16[256,1792]{1,0:T(8,128)(2,1)S(1)}, u32[]{:S(2)}, u32[]{:S(2)}) collective-permute-start(bf16[256,1792]{1,0:T(8,128)(2,1)} %get-tuple-element.48), channel_id=1, source_target_pairs={{0,2},{1,3},{2,0},{3,1},{4,6},{5,7},{6,4},{7,5},{8,10},{9,11},{10,... | collective-permute-start | bytes 2752520 | tf_op jit(solution)/shard_map/ppermute | solution.py:34
  94.1 6.6 %collective-permute-start.6 = (bf16[408,256]{1,0:T(8,128)(2,1)S(1)}, bf16[408,256]{1,0:T(8,128)(2,1)S(1)}, u32[]{:S(2)}, u32[]{:S(2)}) collective-permute-start(bf16[408,256]{1,0:T(8,128)(2,1)S(1)} %pad_maximum_fusion.1.refs_0_), channel_id=1, source_target_pairs={{0,1},{1,0},{2,3},{3,2},{4,5},{5,4},{6,7},{7,6},{8,9},{9,8},{10,11... | collective-permute-start | bytes 626696 | tf_op jit(solution)/shard_map/ppermute | solution.py:34
  95.5 10.2 %collective-permute-start.7 = (bf16[408,256]{1,0:T(8,128)(2,1)S(1)}, bf16[408,256]{1,0:T(8,128)(2,1)S(1)}, u32[]{:S(2)}, u32[]{:S(2)}) collective-permute-start(bf16[408,256]{1,0:T(8,128)(2,1)S(1)} %pad_maximum_fusion.1.refs_0_), channel_id=1, source_target_pairs={{0,3},{1,2},{2,1},{3,0},{4,7},{5,6},{6,5},{7,4},{8,11},{9,10},{10,... | collective-permute-start | bytes 626696 | tf_op jit(solution)/shard_map/ppermute | solution.py:34
  97.4 10.3 %collective-permute-start.8 = (bf16[408,256]{1,0:T(8,128)(2,1)S(1)}, bf16[408,256]{1,0:T(8,128)(2,1)S(1)}, u32[]{:S(2)}, u32[]{:S(2)}) collective-permute-start(bf16[408,256]{1,0:T(8,128)(2,1)S(1)} %pad_maximum_fusion.1.refs_0_), channel_id=1, source_target_pairs={{0,2},{1,3},{2,0},{3,1},{4,6},{5,7},{6,4},{7,5},{8,10},{9,11},{10,... | collective-permute-start | bytes 626696 | tf_op jit(solution)/shard_map/ppermute | solution.py:34
  113.0 23.4 %all-to-all-start = ((bf16[16,24,1792]{2,1,0:T(8,128)(2,1)}), bf16[16,24,1792]{2,1,0:T(8,128)(2,1)S(1)}, u32[]{:S(2)}, u32[]{:S(2)}) async-start(bf16[16,24,1792]{2,1,0:T(8,128)(2,1)} %bitcast.103), calls=%async_computation | async-start | bytes 2752512 | tf_op jit(solution)/shard_map/all_to_all | solution.py:217
  117.9 89.4 %all-gather.5.cloned.1.call-start = ((), (), s32[]{:S(2)}) async-start(), calls=%async_computation.3 | async-start | bytes 11354112 | tf_op jit(solution)/shard_map/all_gather | solution.py:177
  136.9 5.0 %collective-permute-start.10 = (f32[24,1792]{1,0:T(8,128)S(1)}, f32[24,1792]{1,0:T(8,128)S(1)}, u32[]{:S(2)}, u32[]{:S(2)}) collective-permute-start(f32[24,1792]{1,0:T(8,128)S(1)} %slice_bitcast_fusion.2), channel_id=1, source_target_pairs={{0,4},{4,0},{8,12},{12,8},{16,20},{20,16},{24,28},{28,24},{32,36},... | collective-permute-start | bytes 516104 | tf_op jit(solution)/shard_map/ppermute | solution.py:29
  142.0 3.8 %collective-permute-start.11 = (bf16[24,1792]{1,0:T(8,128)(2,1)S(1)}, bf16[24,1792]{1,0:T(8,128)(2,1)S(1)}, u32[]{:S(2)}, u32[]{:S(2)}) collective-permute-start(bf16[24,1792]{1,0:T(8,128)(2,1)S(1)} %get-tuple-element.42), channel_id=1, source_target_pairs={{0,1},{1,0},{2,3},{3,2},{4,5},{5,4},{6,7},{7,6},{8,9},{9,8},{10,11... | collective-permute-start | bytes 258056 | tf_op jit(solution)/shard_map/ppermute | solution.py:34
  142.1 4.6 %collective-permute-start.12 = (bf16[24,1792]{1,0:T(8,128)(2,1)S(1)}, bf16[24,1792]{1,0:T(8,128)(2,1)S(1)}, u32[]{:S(2)}, u32[]{:S(2)}) collective-permute-start(bf16[24,1792]{1,0:T(8,128)(2,1)S(1)} %get-tuple-element.42), channel_id=1, source_target_pairs={{0,3},{1,2},{2,1},{3,0},{4,7},{5,6},{6,5},{7,4},{8,11},{9,10},{10,... | collective-permute-start | bytes 258056 | tf_op jit(solution)/shard_map/ppermute | solution.py:34
  144.4 4.8 %collective-permute-start.13 = (bf16[24,1792]{1,0:T(8,128)(2,1)S(1)}, bf16[24,1792]{1,0:T(8,128)(2,1)S(1)}, u32[]{:S(2)}, u32[]{:S(2)}) collective-permute-start(bf16[24,1792]{1,0:T(8,128)(2,1)S(1)} %get-tuple-element.42), channel_id=1, source_target_pairs={{0,2},{1,3},{2,0},{3,1},{4,6},{5,7},{6,4},{7,5},{8,10},{9,11},{10,... | collective-permute-start | bytes 258056 | tf_op jit(solution)/shard_map/ppermute | solution.py:34
  152.4 20.1 %collective-permute-start.14 = (bf16[256,1792]{1,0:T(8,128)(2,1)S(1)}, bf16[256,1792]{1,0:T(8,128)(2,1)S(1)}, u32[]{:S(2)}, u32[]{:S(2)}) collective-permute-start(bf16[256,1792]{1,0:T(8,128)(2,1)S(1)} %get-tuple-element.47), channel_id=1, source_target_pairs={{0,1},{1,0},{2,3},{3,2},{4,5},{5,4},{6,7},{7,6},{8,9},{9,8},{10,11... | collective-permute-start | bytes 2752520 | tf_op jit(solution)/shard_map/ppermute | solution.py:34
  153.2 20.7 %collective-permute-start.15 = (bf16[256,1792]{1,0:T(8,128)(2,1)S(1)}, bf16[256,1792]{1,0:T(8,128)(2,1)S(1)}, u32[]{:S(2)}, u32[]{:S(2)}) collective-permute-start(bf16[256,1792]{1,0:T(8,128)(2,1)S(1)} %get-tuple-element.46), channel_id=1, source_target_pairs={{0,3},{1,2},{2,1},{3,0},{4,7},{5,6},{6,5},{7,4},{8,11},{9,10},{10,... | collective-permute-start | bytes 2752520 | tf_op jit(solution)/shard_map/ppermute | solution.py:34
  154.1 39.6 %collective-permute-start.16 = (bf16[256,1792]{1,0:T(8,128)(2,1)S(1)}, bf16[256,1792]{1,0:T(8,128)(2,1)}, u32[]{:S(2)}, u32[]{:S(2)}) collective-permute-start(bf16[256,1792]{1,0:T(8,128)(2,1)S(1)} %get-tuple-element.45), channel_id=1, source_target_pairs={{0,2},{1,3},{2,0},{3,1},{4,6},{5,7},{6,4},{7,5},{8,10},{9,11},{10,... | collective-permute-start | bytes 2752520 | tf_op jit(solution)/shard_map/ppermute | solution.py:34
  217.8 6.6 %collective-permute-start.17 = (bf16[408,256]{1,0:T(8,128)(2,1)S(1)}, bf16[408,256]{1,0:T(8,128)(2,1)S(1)}, u32[]{:S(2)}, u32[]{:S(2)}) collective-permute-start(bf16[408,256]{1,0:T(8,128)(2,1)S(1)} %pad_maximum_fusion.2.refs_0_), channel_id=1, source_target_pairs={{0,1},{1,0},{2,3},{3,2},{4,5},{5,4},{6,7},{7,6},{8,9},{9,8},{10,11... | collective-permute-start | bytes 626696 | tf_op jit(solution)/shard_map/ppermute | solution.py:34
  219.2 10.2 %collective-permute-start.18 = (bf16[408,256]{1,0:T(8,128)(2,1)S(1)}, bf16[408,256]{1,0:T(8,128)(2,1)S(1)}, u32[]{:S(2)}, u32[]{:S(2)}) collective-permute-start(bf16[408,256]{1,0:T(8,128)(2,1)S(1)} %pad_maximum_fusion.2.refs_0_), channel_id=1, source_target_pairs={{0,3},{1,2},{2,1},{3,0},{4,7},{5,6},{6,5},{7,4},{8,11},{9,10},{10,... | collective-permute-start | bytes 626696 | tf_op jit(solution)/shard_map/ppermute | solution.py:34
  221.1 10.3 %collective-permute-start.19 = (bf16[408,256]{1,0:T(8,128)(2,1)S(1)}, bf16[408,256]{1,0:T(8,128)(2,1)S(1)}, u32[]{:S(2)}, u32[]{:S(2)}) collective-permute-start(bf16[408,256]{1,0:T(8,128)(2,1)S(1)} %pad_maximum_fusion.2.refs_0_), channel_id=1, source_target_pairs={{0,2},{1,3},{2,0},{3,1},{4,6},{5,7},{6,4},{7,5},{8,10},{9,11},{10,... | collective-permute-start | bytes 626696 | tf_op jit(solution)/shard_map/ppermute | solution.py:34
  236.7 23.4 %all-to-all-start.1 = ((bf16[16,24,1792]{2,1,0:T(8,128)(2,1)}), bf16[16,24,1792]{2,1,0:T(8,128)(2,1)S(1)}, u32[]{:S(2)}, u32[]{:S(2)}) async-start(bf16[16,24,1792]{2,1,0:T(8,128)(2,1)} %bitcast.102), calls=%async_computation.1 | async-start | bytes 2752512 | tf_op jit(solution)/shard_map/all_to_all | solution.py:217
  260.6 5.1 %collective-permute-start.21 = (f32[24,1792]{1,0:T(8,128)S(1)}, f32[24,1792]{1,0:T(8,128)S(1)}, u32[]{:S(2)}, u32[]{:S(2)}) collective-permute-start(f32[24,1792]{1,0:T(8,128)S(1)} %slice_bitcast_fusion), channel_id=1, source_target_pairs={{0,4},{4,0},{8,12},{12,8},{16,20},{20,16},{24,28},{28,24},{32,36},... | collective-permute-start | bytes 516104 | tf_op jit(solution)/shard_map/ppermute | solution.py:29
  (19 other events, 283.8 us)
Sparse Core Ops, SparseCore 0:
  21.1 61.2 all-gather.2
  150.5 56.7 all-gather.4

commit v7 on v6

--- a/solution.py
+++ b/solution.py
@@ -38,7 +38,9 @@
     return lax.optimization_barrier((block, *others))[0]
 
 
-def gate_up_kernel(layer, z_ref, tokens_ref, gate_ref, up_ref, act_ref, tokens, weights, sums, sems):
+def gate_up_kernel(
+    layer, z_ref, tokens_ref, taken_ref, gate_ref, up_ref, act_ref, tokens, weights, sums, sems
+):
     steps, depth = weights.shape[1:3]
     copies = []
     for step, mask in enumerate(ORDER):
@@ -66,58 +68,61 @@
         else:
             gate += sums[0]
             up += sums[1]
-            act_ref[...] = (gate / (1.0 + jnp.exp(-gate)) * up).astype(act_ref.dtype)
-
-
-def gate_up(z, tokens, w_gate, w_up, layer):
+            act = (gate / (1.0 + jnp.exp(-gate)) * up).astype(bf16)
+            slots = jnp.dot(taken_ref[...], act, preferred_element_type=f32)
+            act_ref[...] = slots.astype(act_ref.dtype)
+
+
+def gate_up(z, tokens, taken, w_gate, w_up, layer):
     rows, units = tokens.shape[0], w_gate.shape[-1]
     steps = len(ORDER)
     depth = w_gate.shape[2] // steps
-    outside = pl.BlockSpec(memory_space=pl.ANY)
+    outside, inside = pl.BlockSpec(memory_space=pl.ANY), pl.BlockSpec(memory_space=pltpu.VMEM)
     return pl.pallas_call(
         functools.partial(gate_up_kernel, layer),
-        in_specs=[pl.BlockSpec(memory_space=pltpu.SMEM)] + [outside] * 3,
-        out_specs=pl.BlockSpec(memory_space=pltpu.VMEM),
-        out_shape=jax.ShapeDtypeStruct((rows, units), bf16),
+        in_specs=[pl.BlockSpec(memory_space=pltpu.SMEM), outside, inside, outside, outside],
+        out_specs=inside,
+        out_shape=jax.ShapeDtypeStruct((taken.shape[0], units), bf16),
         scratch_shapes=[
             pltpu.VMEM((steps, rows, depth), bf16),
             pltpu.VMEM((2, steps, depth, units), bf16),
             pltpu.VMEM((2, rows, units), f32),
             pltpu.SemaphoreType.DMA((3, steps)),
         ],
-        compiler_params=pltpu.CompilerParams(vmem_limit_bytes=58 << 20),
+        compiler_params=pltpu.CompilerParams(vmem_limit_bytes=56 << 20),
         cost_estimate=pl.CostEstimate(
             flops=16 * rows * depth * units,
             bytes_accessed=8 * (rows + 2 * units) * depth + 2 * rows * units,
             transcendentals=rows * units,
         ),
-    )(jnp.full((1,), z, jnp.int32), tokens, w_gate, w_up)
-
-
-def down_kernel(z_ref, *refs):
-    acts, weights, out_ref = refs[:4], refs[4:-1], refs[-1]
-    acts = jnp.concatenate([act[...] for act in acts], axis=1)
-    weights = jnp.concatenate([weights[0][0, 0]] + [w[...] for w in weights[1:]], axis=0)
-    out_ref[...] = jnp.dot(acts, weights, preferred_element_type=f32).astype(out_ref.dtype)
-
-
-def down_product(z, acts, slots, w_down, layer, others):
-    units = w_down.shape[2]
+    )(jnp.full((1,), z, jnp.int32), tokens, taken, w_gate, w_up)
+
+
+def down_kernel(layer, z_ref, a0, a1, a2, a3, down_ref, w1, w2, w3, out_ref, own, sem):
+    units, part = own.shape
+    column = pl.multiple_of(z_ref[0] * part, part)
+    copy = pltpu.make_async_copy(down_ref.at[layer, 0, :, pl.ds(column, part)], own, sem)
+    copy.start()
+    acts = jnp.concatenate([a1[...], a2[...], a3[...], a0[...]], axis=1)
+    copy.wait()
+    half = part // 2
+    for n in range(2):
+        columns = slice(n * half, (n + 1) * half)
+        weights = jnp.concatenate([w[:, columns] for w in (w1, w2, w3, own)], axis=0)
+        out_ref[:, columns] = jnp.dot(acts, weights, preferred_element_type=f32).astype(bf16)
+
+
+def down_product(z, acts, w_down, layer, others):
+    slots, units = acts[0].shape
     part = others[0].shape[-1]
-    steps = 2
-    columns = part // steps
-    act = pl.BlockSpec((slots, units), lambda n, z: (0, 0))
+    outside, inside = pl.BlockSpec(memory_space=pl.ANY), pl.BlockSpec(memory_space=pltpu.VMEM)
     return pl.pallas_call(
-        down_kernel,
-        grid_spec=pltpu.PrefetchScalarGridSpec(
-            num_scalar_prefetch=1,
-            grid=(steps,),
-            in_specs=[act] * 4
-            + [pl.BlockSpec((1, 1, units, columns), lambda n, z: (layer, 0, 0, z[0] * steps + n))]
-            + [pl.BlockSpec((w.shape[0], columns), lambda n, z: (0, n)) for w in others],
-            out_specs=pl.BlockSpec((slots, columns), lambda n, z: (0, n)),
-        ),
+        functools.partial(down_kernel, layer),
+        in_specs=[pl.BlockSpec(memory_space=pltpu.SMEM)] + [inside] * 4 + [outside] + [inside] * 3,
+        out_specs=inside,
         out_shape=jax.ShapeDtypeStruct((slots, part), bf16),
+        scratch_shapes=[pltpu.VMEM((units, part), bf16), pltpu.SemaphoreType.DMA],
+        compiler_params=pltpu.CompilerParams(vmem_limit_bytes=48 << 20),
         cost_estimate=pl.CostEstimate(
             flops=8 * slots * units * part,
             bytes_accessed=8 * units * (slots + part) + 2 * slots * part,
@@ -175,29 +180,13 @@
 
         sent = jnp.concatenate(normed if layer else normed + [marks_sent], axis=1)
         arrived = lax.all_gather(sent, "expert", axis=0, tiled=True)
-        others = [columns(layer, mask, 0, units, sent) for mask in ORDER[1:]]
-        arrived, *others = lax.optimization_barrier((arrived, *others))
-        if layer == 0:
-            marks_here = arrived[:, width:]
-        act = gate_up(z, arrived, w_gate, w_up, layer)
-
-        mine = lax.broadcasted_iota(jnp.int32, (1, 128), 1) == me + layer * experts
-        mark = jnp.sum(jnp.where(mine, marks_here.astype(f32), 0.0), axis=1).astype(jnp.int32)
-        source = lax.broadcasted_iota(jnp.int32, (experts, rows), 0).reshape(-1)
-        slot = jnp.where(mark > 0, source * capacity + mark - 1, -1)[None, :]
-        taken = (lax.broadcasted_iota(jnp.int32, (slots, 1), 0) == slot).astype(bf16)
-        act = jnp.dot(taken, act, preferred_element_type=f32).astype(bf16)
 
         own = state.astype(f32) * scale[:, None] * norm_gain[layer][None, :]
         own = own.astype(bf16).astype(f32)
         scores = jnp.dot(own, router[layer], precision=lax.Precision.HIGHEST)
-        scores = jnp.pad(jnp.concatenate(thirds(scores), axis=1), ((0, 0), (0, units - 3 * experts)))
-        act = jnp.concatenate([act, scores], axis=0)
-        acts = spread(act)
-        scores = sum(block[slots:].astype(f32) for block in acts)
-        scores = sum(scores[:, experts * n : experts * (n + 1)] for n in range(3))
-        out = down_product(z, acts, slots, w_down, layer, others)
-        probs = jax.nn.sigmoid(after(scores, out))
+        scores = after(scores, sent)
+        others = [columns(layer, mask, 0, units, scores) for mask in ORDER[1:]]
+        probs = jax.nn.sigmoid(sum(spread(scores)))
         picked = jnp.where(picks[layer], probs, 0.0)
         weights = route_scale * picked / jnp.sum(picked, axis=1, keepdims=True)
 
@@ -213,6 +202,25 @@
             return jnp.concatenate(thirds(table.reshape(rows, slots))[:2], axis=0)
 
         mixers = jnp.concatenate([mixer(core), swap(mixer(1 - core), SIBLING)], axis=0)
+
+        def slots_of(marks_here):
+            mine = lax.broadcasted_iota(jnp.int32, (1, 128), 1) == me + layer * experts
+            mark = jnp.sum(jnp.where(mine, marks_here.astype(f32), 0.0), axis=1).astype(jnp.int32)
+            source = lax.broadcasted_iota(jnp.int32, (experts, rows), 0).reshape(-1)
+            slot = jnp.where(mark > 0, source * capacity + mark - 1, -1)[None, :]
+            return (lax.broadcasted_iota(jnp.int32, (slots, 1), 0) == slot).astype(bf16)
+
+        if layer == 0:
+            arrived, mixers, *others = lax.optimization_barrier((arrived, mixers, *others))
+            marks_here = arrived[:, width:]
+            taken = slots_of(marks_here)
+        else:
+            taken = slots_of(after(marks_here, sent))
+            arrived, mixers, taken, *others = lax.optimization_barrier(
+                (arrived, mixers, taken, *others)
+            )
+        acts = spread(gate_up(z, arrived, taken, w_gate, w_up, layer))
+        out = down_product(z, acts, w_down, layer, others)
         groups = [list(range(parity, experts, 2)) for parity in range(2)]
         returned = lax.all_to_all(
             out.reshape(chips, 2 * capacity, part),

time: 274 us -> 269 us (0.982)
  blocking collectives: 0 us -> 48 us
  waiting for transfers between devices: 154 us -> 108 us
  starting transfers between devices: 44.9 us -> 41 us
  matrix products: 5 us -> 1.33 us
    all_to_all x0 -> x2, blocking collectives: none -> 48 us  [body(): lax.all_to_all(out.reshape(chips, 2 * capacity, part), 'expert', split_ax...]
    all_to_all x2 -> x0, waiting for transfers between devices: 23.1 us -> none  [body(): lax.all_to_all(out.reshape(chips, 2 * capacity, part), 'expert', split_ax...]
    all_gather x2, waiting for transfers between devices: 29.3 us -> 13.8 us  [body(): arrived = lax.all_gather(sent, 'expert', axis=0, tiled=True)]
    all_to_all x2 -> x0, starting transfers between devices: 9.74 us -> none  [body(): lax.all_to_all(out.reshape(chips, 2 * capacity, part), 'expert', split_ax...]
    ppermute x18 -> x24, starting transfers between devices: 23.9 us -> 32.2 us  [z_swap(): return lax.ppermute(block, 'tensor', [(i, i ^ mask) for i in range(count)])]
    ppermute x18 -> x24, waiting for transfers between devices: 97.6 us -> 91.1 us  [z_swap(): return lax.ppermute(block, 'tensor', [(i, i ^ mask) for i in range(count)])]
    pallas_call x2, Pallas kernels: 9.38 us -> 5.96 us  [down_product(): pl.pallas_call(functools.partial(down_kernel, layer), in_specs=[pl.BlockS...]
    pallas_call x2, Pallas kernels: 18.3 us -> 21.2 us  [gate_up(): pl.pallas_call(functools.partial(gate_up_kernel, layer), in_specs=[pl.Blo...]
  transfers between devices with their start and end apart: 26 -> 30, of which waited for: 25 -> 17; matrix products, arithmetic and copies ran while one was open for 8% -> 8% of each run, Pallas kernels for 0% -> 0%
where the time goes in v7:
time: 269 us
  waiting for transfers between devices  108 us (40%)
  blocking collectives  48 us (18%)
  starting transfers between devices  41 us (15%)
  Pallas kernels  27.1 us (10%)
  local copies, waits for them, and re-layouts  19.7 us (7%)
  between operations  14 us (5%)
  other arithmetic  9.81 us (4%)
    ppermute x24, waiting for transfers between devices, z_swap(): return lax.ppermute(block, 'tensor', [(i, i ^ mask) for i in range(count)])  91.1 us
    all_to_all x2, blocking collectives, body(): lax.all_to_all(out.reshape(chips, 2 * capacity, part), 'expert', split_ax...  48 us
    ppermute x24, starting transfers between devices, z_swap(): return lax.ppermute(block, 'tensor', [(i, i ^ mask) for i in range(count)])  32.2 us
    pallas_call x2, Pallas kernels, gate_up(): pl.pallas_call(functools.partial(gate_up_kernel, layer), in_specs=[pl.Blo...  21.2 us
    all_gather x2, waiting for transfers between devices, body(): arrived = lax.all_gather(sent, 'expert', axis=0, tiled=True)  13.8 us
    ppermute x4, starting transfers between devices, swap(): lax.ppermute(block, 'expert', [(i, i ^ masks[i & 1]) for i in range(count)])  8.69 us
    reshape x2, local copies, waits for them, and re-layouts, columns(): return z_swap(block.reshape(count, part), mask)  6.77 us
    pallas_call x2, Pallas kernels, down_product(): pl.pallas_call(functools.partial(down_kernel, layer), in_specs=[pl.BlockS...  5.96 us
  transfers between devices with their start and end apart: 30, of which 17 were waited for; matrix products, arithmetic and copies ran while one was open for 8% of the time, Pallas kernels for 0%

profile of v7, /device:TPU:1, one launch (start us, length us, event | category | flops | bytes accessed | tf_op | source)
XLA Modules:
  0.0 268.7 jit_solution(17625270598682042278)
XLA Ops:
  8.5 4.5 %collective-permute-start.2 = (bf16[32,1792]{1,0:T(8,128)(2,1)S(1)}, bf16[32,1792]{1,0:T(8,128)(2,1)S(1)}, u32[]{:S(2)}, u32[]{:S(2)}) collective-permute-start(bf16[32,1792]{1,0:T(8,128)(2,1)S(1)} %maximum_maximum_fusion), channel_id=1, source_target_pairs={{0,2},{1,3},{2,0},{3,1},{4,6},{5,7},{6,4},{7,5},{8,10},{9,11},{10,... | collective-permute-start | bytes 344072 | tf_op jit(solution)/shard_map/ppermute | solution.py:34
  15.9 2.6 collective-permute-done.1
  23.6 2.6 collective-permute-start.5
  27.7 3.4 %dynamic-slice_bitcast_fusion.3 = (bf16[256,1792]{1,0:T(8,128)(2,1)}, bf16[256,1792]{1,0:T(8,128)(2,1)}, bf16[256,1792]{1,0:T(8,128)(2,1)}) fusion(bf16[2,1,256,7168]{3,2,1,0:T(8,128)(2,1)} %down_ref.3, s32[]{:T(128)S(6)} %select_n.178, s32[]{:T(128)S(6)} %select_n.177, s32[]{:T(128)S(6)} %select_n.176), kind=kLoop, calls=%fused_computation.9 | loop fusion | bytes 5505036 | tf_op jit(solution)/shard_map/reshape | solution.py:161
  37.2 2.3 collective-permute-start.6
  40.4 13.2 %collective-permute-done.9.w3 = bf16[256,1792]{1,0:T(8,128)(2,1)S(1)} collective-permute-done((bf16[256,1792]{1,0:T(8,128)(2,1)}, bf16[256,1792]{1,0:T(8,128)(2,1)S(1)}, u32[]{:S(2)}, u32[]{:S(2)}) %collective-permute-start.9) | collective-permute-done | bytes 917536 | tf_op jit(solution)/shard_map/ppermute | solution.py:34
  53.7 21.3 %collective-permute-done.8.w2 = bf16[256,1792]{1,0:T(8,128)(2,1)S(1)} collective-permute-done((bf16[256,1792]{1,0:T(8,128)(2,1)}, bf16[256,1792]{1,0:T(8,128)(2,1)S(1)}, u32[]{:S(2)}, u32[]{:S(2)}) %collective-permute-start.8) | collective-permute-done | bytes 917536 | tf_op jit(solution)/shard_map/ppermute | solution.py:34
  74.9 7.7 %all-gather.3.cloned.1.call-done.tokens_ref = bf16[768,7296]{1,0:T(8,128)(2,1)} async-done(((bf16[24,7296]{1,0:T(8,128)(2,1)}), bf16[768,7296]{1,0:T(8,128)(2,1)}) %all-gather.3.cloned.1.call-update) | async-done | bytes 11206672 | tf_op jit(solution)/shard_map/all_gather | solution.py:182
  84.6 10.6 %shard_map.73.a0 = bf16[384,256]{1,0:T(8,128)(2,1)} custom-call(s32[1]{0:T(128)} %bitcast.19.z_ref, bf16[768,7296]{1,0:T(8,128)(2,1)} %all-gather.3.cloned.1.call-done.tokens_ref, bf16[384,768]{1,0:T(8,128)(2,1)} %fusion.taken_ref, bf16[2,1,7168,256]{3,2,1,0:T(8,128)(2,1)} %gate_ref.3, bf16[2,1,7168,256]{3,2,1,0:T(8,128)(2,1)} %up_ref.3), custom_call_target="tpu_custom_call" | custom-call | flops 5637144576 | bytes 18743296 | tf_op jit(solution)/shard_map/pallas_call | solution.py:81
  95.2 2.9 %collective-permute-start.12 = (bf16[384,256]{1,0:T(8,128)(2,1)}, bf16[384,256]{1,0:T(8,128)(2,1)S(1)}, u32[]{:S(2)}, u32[]{:S(2)}) collective-permute-start(bf16[384,256]{1,0:T(8,128)(2,1)} %shard_map.73.a0), channel_id=1, source_target_pairs={{0,2},{1,3},{2,0},{3,1},{4,6},{5,7},{6,4},{7,5},{8,10},{9,11},{10,... | collective-permute-start | bytes 589832 | tf_op jit(solution)/shard_map/ppermute | solution.py:34
  98.9 4.3 %collective-permute-done.12.a3 = bf16[384,256]{1,0:T(8,128)(2,1)S(1)} collective-permute-done((bf16[384,256]{1,0:T(8,128)(2,1)}, bf16[384,256]{1,0:T(8,128)(2,1)S(1)}, u32[]{:S(2)}, u32[]{:S(2)}) %collective-permute-start.12) | collective-permute-done | bytes 196640 | tf_op jit(solution)/shard_map/ppermute | solution.py:34
  103.3 4.8 %collective-permute-done.11.a2 = bf16[384,256]{1,0:T(8,128)(2,1)S(1)} collective-permute-done((bf16[384,256]{1,0:T(8,128)(2,1)}, bf16[384,256]{1,0:T(8,128)(2,1)S(1)}, u32[]{:S(2)}, u32[]{:S(2)}) %collective-permute-start.11) | collective-permute-done | bytes 196640 | tf_op jit(solution)/shard_map/ppermute | solution.py:34
  109.0 3.0 %shard_map.74 = bf16[384,1792]{1,0:T(8,128)(2,1)S(1)} custom-call(s32[1]{0:T(128)} %bitcast.19.z_ref, bf16[384,256]{1,0:T(8,128)(2,1)S(1)} %copy-done.1, bf16[384,256]{1,0:T(8,128)(2,1)S(1)} %collective-permute-done.10.a1, bf16[384,256]{1,0:T(8,128)(2,1)S(1)} %collective-permute-done.11.a2, bf16[384,256]{1,0:T(8,128)(2,1)S(1)} %collective-permute-done.12.a3, ...), custom_call_target="tpu_custom_call" | custom-call | flops 1409286144 | bytes 5832704 | tf_op jit(solution)/shard_map/pallas_call | solution.py:119
  112.0 24.0 %all_to_all.10 = bf16[16,24,1792]{2,1,0:T(8,128)(2,1)S(1)} all-to-all(bf16[16,24,1792]{2,1,0:T(8,128)(2,1)S(1)} %bitcast.91), channel_id=1, replica_groups={{0,8,16,24,32,40,48,56,64,72,80,88,96,104,112,120},{4,12,20,28,36,44,52..., dimensions={0} | all-to-all | bytes 2752512 | tf_op jit(solution)/shard_map/all_to_all | solution.py:225
  153.1 3.3 %dynamic-slice_bitcast_fusion = (bf16[256,1792]{1,0:T(8,128)(2,1)}, bf16[256,1792]{1,0:T(8,128)(2,1)}, bf16[256,1792]{1,0:T(8,128)(2,1)}) fusion(bf16[2,1,256,7168]{3,2,1,0:T(8,128)(2,1)} %down_ref.3, s32[]{:T(128)S(6)} %select_n.196, s32[]{:T(128)S(6)} %select_n.195, s32[]{:T(128)S(6)} %select_n.194), kind=kLoop, calls=%fused_computation.6 | loop fusion | bytes 5505036 | tf_op jit(solution)/shard_map/reshape | solution.py:161
  168.0 10.9 %collective-permute-done.23.w3 = bf16[256,1792]{1,0:T(8,128)(2,1)S(1)} collective-permute-done((bf16[256,1792]{1,0:T(8,128)(2,1)}, bf16[256,1792]{1,0:T(8,128)(2,1)S(1)}, u32[]{:S(2)}, u32[]{:S(2)}) %collective-permute-start.23) | collective-permute-done | bytes 917536 | tf_op jit(solution)/shard_map/ppermute | solution.py:34
  178.9 21.2 %collective-permute-done.22.w2 = bf16[256,1792]{1,0:T(8,128)(2,1)S(1)} collective-permute-done((bf16[256,1792]{1,0:T(8,128)(2,1)}, bf16[256,1792]{1,0:T(8,128)(2,1)S(1)}, u32[]{:S(2)}, u32[]{:S(2)}) %collective-permute-start.22) | collective-permute-done | bytes 917536 | tf_op jit(solution)/shard_map/ppermute | solution.py:34
  200.2 6.1 %all-gather.5.cloned.1.call-done.tokens_ref = bf16[768,7168]{1,0:T(8,128)(2,1)} async-done(((bf16[24,7168]{1,0:T(8,128)(2,1)}), bf16[768,7168]{1,0:T(8,128)(2,1)}) %all-gather.5.cloned.1.call-update) | async-done | bytes 11010064 | tf_op jit(solution)/shard_map/all_gather | solution.py:182
  206.3 10.6 %shard_map.75.a0 = bf16[384,256]{1,0:T(8,128)(2,1)} custom-call(s32[1]{0:T(128)} %bitcast.19.z_ref, bf16[768,7168]{1,0:T(8,128)(2,1)} %all-gather.5.cloned.1.call-done.tokens_ref, bf16[384,768]{1,0:T(8,128)(2,1)} %fusion.1.taken_ref, bf16[2,1,7168,256]{3,2,1,0:T(8,128)(2,1)} %gate_ref.3, bf16[2,1,7168,256]{3,2,1,0:T(8,128)(2,1)} %up_ref.3), custom_call_target="tpu_custom_call" | custom-call | flops 5637144576 | bytes 18743296 | tf_op jit(solution)/shard_map/pallas_call | solution.py:81
  216.8 2.9 %collective-permute-start.26 = (bf16[384,256]{1,0:T(8,128)(2,1)}, bf16[384,256]{1,0:T(8,128)(2,1)S(1)}, u32[]{:S(2)}, u32[]{:S(2)}) collective-permute-start(bf16[384,256]{1,0:T(8,128)(2,1)} %shard_map.75.a0), channel_id=1, source_target_pairs={{0,2},{1,3},{2,0},{3,1},{4,6},{5,7},{6,4},{7,5},{8,10},{9,11},{10,... | collective-permute-start | bytes 589832 | tf_op jit(solution)/shard_map/ppermute | solution.py:34
  220.6 4.3 %collective-permute-done.26.a3 = bf16[384,256]{1,0:T(8,128)(2,1)S(1)} collective-permute-done((bf16[384,256]{1,0:T(8,128)(2,1)}, bf16[384,256]{1,0:T(8,128)(2,1)S(1)}, u32[]{:S(2)}, u32[]{:S(2)}) %collective-permute-start.26) | collective-permute-done | bytes 196640 | tf_op jit(solution)/shard_map/ppermute | solution.py:34
  224.9 4.8 %collective-permute-done.25.a2 = bf16[384,256]{1,0:T(8,128)(2,1)S(1)} collective-permute-done((bf16[384,256]{1,0:T(8,128)(2,1)}, bf16[384,256]{1,0:T(8,128)(2,1)S(1)}, u32[]{:S(2)}, u32[]{:S(2)}) %collective-permute-start.25) | collective-permute-done | bytes 196640 | tf_op jit(solution)/shard_map/ppermute | solution.py:34
  230.6 3.0 %shard_map.76 = bf16[384,1792]{1,0:T(8,128)(2,1)S(1)} custom-call(s32[1]{0:T(128)} %bitcast.19.z_ref, bf16[384,256]{1,0:T(8,128)(2,1)S(1)} %copy-done, bf16[384,256]{1,0:T(8,128)(2,1)S(1)} %collective-permute-done.24.a1, bf16[384,256]{1,0:T(8,128)(2,1)S(1)} %collective-permute-done.25.a2, bf16[384,256]{1,0:T(8,128)(2,1)S(1)} %collective-permute-done.26.a3, ...), custom_call_target="tpu_custom_call" | custom-call | flops 1409286144 | bytes 5832704 | tf_op jit(solution)/shard_map/pallas_call | solution.py:119
  233.6 24.0 %all_to_all.11 = bf16[16,24,1792]{2,1,0:T(8,128)(2,1)S(1)} all-to-all(bf16[16,24,1792]{2,1,0:T(8,128)(2,1)S(1)} %bitcast.90), channel_id=1, replica_groups={{0,8,16,24,32,40,48,56,64,72,80,88,96,104,112,120},{4,12,20,28,36,44,52..., dimensions={0} | all-to-all | bytes 2752512 | tf_op jit(solution)/shard_map/all_to_all | solution.py:225
  (170 shorter events, 56.3 us)
Async XLA Ops:
  6.5 76.0 %all-gather.3.cloned.1.call-start = ((), (), s32[]{:S(2)}) async-start(), calls=%async_computation.2 | async-start | bytes 11556864 | tf_op jit(solution)/shard_map/all_gather | solution.py:182
  8.5 7.4 %collective-permute-start.2 = (bf16[32,1792]{1,0:T(8,128)(2,1)S(1)}, bf16[32,1792]{1,0:T(8,128)(2,1)S(1)}, u32[]{:S(2)}, u32[]{:S(2)}) collective-permute-start(bf16[32,1792]{1,0:T(8,128)(2,1)S(1)} %maximum_maximum_fusion), channel_id=1, source_target_pairs={{0,2},{1,3},{2,0},{3,1},{4,6},{5,7},{6,4},{7,5},{8,10},{9,11},{10,... | collective-permute-start | bytes 344072 | tf_op jit(solution)/shard_map/ppermute | solution.py:34
  13.0 5.6 %collective-permute-start.1 = (bf16[32,1792]{1,0:T(8,128)(2,1)S(1)}, bf16[32,1792]{1,0:T(8,128)(2,1)S(1)}, u32[]{:S(2)}, u32[]{:S(2)}) collective-permute-start(bf16[32,1792]{1,0:T(8,128)(2,1)S(1)} %maximum_maximum_fusion), channel_id=1, source_target_pairs={{0,3},{1,2},{2,1},{3,0},{4,7},{5,6},{6,5},{7,4},{8,11},{9,10},{10,... | collective-permute-start | bytes 344072 | tf_op jit(solution)/shard_map/ppermute | solution.py:34
  13.4 5.4 %collective-permute-start = (bf16[32,1792]{1,0:T(8,128)(2,1)S(1)}, bf16[32,1792]{1,0:T(8,128)(2,1)S(1)}, u32[]{:S(2)}, u32[]{:S(2)}) collective-permute-start(bf16[32,1792]{1,0:T(8,128)(2,1)S(1)} %maximum_maximum_fusion), channel_id=1, source_target_pairs={{0,1},{1,0},{2,3},{3,2},{4,5},{5,4},{6,7},{7,6},{8,9},{9,8},{10,11... | collective-permute-start | bytes 344072 | tf_op jit(solution)/shard_map/ppermute | solution.py:34
  20.6 185.7 %all-gather.5.cloned.1.call-start = ((), (), s32[]{:S(2)}) async-start(), calls=%async_computation.3 | async-start | bytes 11354112 | tf_op jit(solution)/shard_map/all_gather | solution.py:182
  23.6 11.1 %collective-permute-start.5 = (f32[24,32]{1,0:T(8,128)S(1)}, f32[24,32]{1,0:T(8,128)S(1)}, u32[]{:S(2)}, u32[]{:S(2)}) collective-permute-start(f32[24,32]{1,0:T(8,128)S(1)} %fusion.5), channel_id=1, source_target_pairs={{0,2},{1,3},{2,0},{3,1},{4,6},{5,7},{6,4},{7,5},{8,10},{9,11},{10,... | collective-permute-start | bytes 9224 | tf_op jit(solution)/shard_map/ppermute | solution.py:34
  26.1 8.6 %collective-permute-start.4 = (f32[24,32]{1,0:T(8,128)S(1)}, f32[24,32]{1,0:T(8,128)S(1)}, u32[]{:S(2)}, u32[]{:S(2)}) collective-permute-start(f32[24,32]{1,0:T(8,128)S(1)} %fusion.5), channel_id=1, source_target_pairs={{0,3},{1,2},{2,1},{3,0},{4,7},{5,6},{6,5},{7,4},{8,11},{9,10},{10,... | collective-permute-start | bytes 9224 | tf_op jit(solution)/shard_map/ppermute | solution.py:34
  27.4 7.3 %collective-permute-start.3 = (f32[24,32]{1,0:T(8,128)S(1)}, f32[24,32]{1,0:T(8,128)S(1)}, u32[]{:S(2)}, u32[]{:S(2)}) collective-permute-start(f32[24,32]{1,0:T(8,128)S(1)} %fusion.5), channel_id=1, source_target_pairs={{0,1},{1,0},{2,3},{3,2},{4,5},{5,4},{6,7},{7,6},{8,9},{9,8},{10,11... | collective-permute-start | bytes 9224 | tf_op jit(solution)/shard_map/ppermute | solution.py:34
  31.2 22.5 %collective-permute-start.9 = (bf16[256,1792]{1,0:T(8,128)(2,1)}, bf16[256,1792]{1,0:T(8,128)(2,1)S(1)}, u32[]{:S(2)}, u32[]{:S(2)}) collective-permute-start(bf16[256,1792]{1,0:T(8,128)(2,1)} %get-tuple-element.58), channel_id=1, source_target_pairs={{0,2},{1,3},{2,0},{3,1},{4,6},{5,7},{6,4},{7,5},{8,10},{9,11},{10,... | collective-permute-start | bytes 2752520 | tf_op jit(solution)/shard_map/ppermute | solution.py:34
  33.4 41.5 %collective-permute-start.8 = (bf16[256,1792]{1,0:T(8,128)(2,1)}, bf16[256,1792]{1,0:T(8,128)(2,1)S(1)}, u32[]{:S(2)}, u32[]{:S(2)}) collective-permute-start(bf16[256,1792]{1,0:T(8,128)(2,1)} %get-tuple-element.59), channel_id=1, source_target_pairs={{0,3},{1,2},{2,1},{3,0},{4,7},{5,6},{6,5},{7,4},{8,11},{9,10},{10,... | collective-permute-start | bytes 2752520 | tf_op jit(solution)/shard_map/ppermute | solution.py:34
  34.7 40.2 %collective-permute-start.7 = (bf16[256,1792]{1,0:T(8,128)(2,1)}, bf16[256,1792]{1,0:T(8,128)(2,1)S(1)}, u32[]{:S(2)}, u32[]{:S(2)}) collective-permute-start(bf16[256,1792]{1,0:T(8,128)(2,1)} %get-tuple-element.60), channel_id=1, source_target_pairs={{0,1},{1,0},{2,3},{3,2},{4,5},{5,4},{6,7},{7,6},{8,9},{9,8},{10,11... | collective-permute-start | bytes 2752520 | tf_op jit(solution)/shard_map/ppermute | solution.py:34
  95.2 8.1 %collective-permute-start.12 = (bf16[384,256]{1,0:T(8,128)(2,1)}, bf16[384,256]{1,0:T(8,128)(2,1)S(1)}, u32[]{:S(2)}, u32[]{:S(2)}) collective-permute-start(bf16[384,256]{1,0:T(8,128)(2,1)} %shard_map.73.a0), channel_id=1, source_target_pairs={{0,2},{1,3},{2,0},{3,1},{4,6},{5,7},{6,4},{7,5},{8,10},{9,11},{10,... | collective-permute-start | bytes 589832 | tf_op jit(solution)/shard_map/ppermute | solution.py:34
  98.1 9.9 %collective-permute-start.11 = (bf16[384,256]{1,0:T(8,128)(2,1)}, bf16[384,256]{1,0:T(8,128)(2,1)S(1)}, u32[]{:S(2)}, u32[]{:S(2)}) collective-permute-start(bf16[384,256]{1,0:T(8,128)(2,1)} %shard_map.73.a0), channel_id=1, source_target_pairs={{0,3},{1,2},{2,1},{3,0},{4,7},{5,6},{6,5},{7,4},{8,11},{9,10},{10,... | collective-permute-start | bytes 589832 | tf_op jit(solution)/shard_map/ppermute | solution.py:34
  98.9 9.1 %collective-permute-start.10 = (bf16[384,256]{1,0:T(8,128)(2,1)}, bf16[384,256]{1,0:T(8,128)(2,1)S(1)}, u32[]{:S(2)}, u32[]{:S(2)}) collective-permute-start(bf16[384,256]{1,0:T(8,128)(2,1)} %shard_map.73.a0), channel_id=1, source_target_pairs={{0,1},{1,0},{2,3},{3,2},{4,5},{5,4},{6,7},{7,6},{8,9},{9,8},{10,11... | collective-permute-start | bytes 589832 | tf_op jit(solution)/shard_map/ppermute | solution.py:34
  141.3 5.8 %collective-permute-start.15 = (bf16[24,1792]{1,0:T(8,128)(2,1)S(1)}, bf16[24,1792]{1,0:T(8,128)(2,1)S(1)}, u32[]{:S(2)}, u32[]{:S(2)}) collective-permute-start(bf16[24,1792]{1,0:T(8,128)(2,1)S(1)} %get-tuple-element.50), channel_id=1, source_target_pairs={{0,3},{1,2},{2,1},{3,0},{4,7},{5,6},{6,5},{7,4},{8,11},{9,10},{10,... | collective-permute-start | bytes 258056 | tf_op jit(solution)/shard_map/ppermute | solution.py:34
  148.7 11.5 %collective-permute-start.19 = (f32[24,32]{1,0:T(8,128)S(1)}, f32[24,32]{1,0:T(8,128)S(1)}, u32[]{:S(2)}, u32[]{:S(2)}) collective-permute-start(f32[24,32]{1,0:T(8,128)S(1)} %fusion.3), channel_id=1, source_target_pairs={{0,2},{1,3},{2,0},{3,1},{4,6},{5,7},{6,4},{7,5},{8,10},{9,11},{10,... | collective-permute-start | bytes 9224 | tf_op jit(solution)/shard_map/ppermute | solution.py:34
  150.8 9.5 %collective-permute-start.18 = (f32[24,32]{1,0:T(8,128)S(1)}, f32[24,32]{1,0:T(8,128)S(1)}, u32[]{:S(2)}, u32[]{:S(2)}) collective-permute-start(f32[24,32]{1,0:T(8,128)S(1)} %fusion.3), channel_id=1, source_target_pairs={{0,3},{1,2},{2,1},{3,0},{4,7},{5,6},{6,5},{7,4},{8,11},{9,10},{10,... | collective-permute-start | bytes 9224 | tf_op jit(solution)/shard_map/ppermute | solution.py:34
  152.9 7.4 %collective-permute-start.17 = (f32[24,32]{1,0:T(8,128)S(1)}, f32[24,32]{1,0:T(8,128)S(1)}, u32[]{:S(2)}, u32[]{:S(2)}) collective-permute-start(f32[24,32]{1,0:T(8,128)S(1)} %fusion.3), channel_id=1, source_target_pairs={{0,1},{1,0},{2,3},{3,2},{4,5},{5,4},{6,7},{7,6},{8,9},{9,8},{10,11... | collective-permute-start | bytes 9224 | tf_op jit(solution)/shard_map/ppermute | solution.py:34
  156.4 22.5 %collective-permute-start.23 = (bf16[256,1792]{1,0:T(8,128)(2,1)}, bf16[256,1792]{1,0:T(8,128)(2,1)S(1)}, u32[]{:S(2)}, u32[]{:S(2)}) collective-permute-start(bf16[256,1792]{1,0:T(8,128)(2,1)} %get-tuple-element.55), channel_id=1, source_target_pairs={{0,2},{1,3},{2,0},{3,1},{4,6},{5,7},{6,4},{7,5},{8,10},{9,11},{10,... | collective-permute-start | bytes 2752520 | tf_op jit(solution)/shard_map/ppermute | solution.py:34
  158.1 42.0 %collective-permute-start.22 = (bf16[256,1792]{1,0:T(8,128)(2,1)}, bf16[256,1792]{1,0:T(8,128)(2,1)S(1)}, u32[]{:S(2)}, u32[]{:S(2)}) collective-permute-start(bf16[256,1792]{1,0:T(8,128)(2,1)} %get-tuple-element.56), channel_id=1, source_target_pairs={{0,3},{1,2},{2,1},{3,0},{4,7},{5,6},{6,5},{7,4},{8,11},{9,10},{10,... | collective-permute-start | bytes 2752520 | tf_op jit(solution)/shard_map/ppermute | solution.py:34
  160.3 39.9 %collective-permute-start.21 = (bf16[256,1792]{1,0:T(8,128)(2,1)}, bf16[256,1792]{1,0:T(8,128)(2,1)S(1)}, u32[]{:S(2)}, u32[]{:S(2)}) collective-permute-start(bf16[256,1792]{1,0:T(8,128)(2,1)} %get-tuple-element.57), channel_id=1, source_target_pairs={{0,1},{1,0},{2,3},{3,2},{4,5},{5,4},{6,7},{7,6},{8,9},{9,8},{10,11... | collective-permute-start | bytes 2752520 | tf_op jit(solution)/shard_map/ppermute | solution.py:34
  216.8 8.0 %collective-permute-start.26 = (bf16[384,256]{1,0:T(8,128)(2,1)}, bf16[384,256]{1,0:T(8,128)(2,1)S(1)}, u32[]{:S(2)}, u32[]{:S(2)}) collective-permute-start(bf16[384,256]{1,0:T(8,128)(2,1)} %shard_map.75.a0), channel_id=1, source_target_pairs={{0,2},{1,3},{2,0},{3,1},{4,6},{5,7},{6,4},{7,5},{8,10},{9,11},{10,... | collective-permute-start | bytes 589832 | tf_op jit(solution)/shard_map/ppermute | solution.py:34
  219.8 9.9 %collective-permute-start.25 = (bf16[384,256]{1,0:T(8,128)(2,1)}, bf16[384,256]{1,0:T(8,128)(2,1)S(1)}, u32[]{:S(2)}, u32[]{:S(2)}) collective-permute-start(bf16[384,256]{1,0:T(8,128)(2,1)} %shard_map.75.a0), channel_id=1, source_target_pairs={{0,3},{1,2},{2,1},{3,0},{4,7},{5,6},{6,5},{7,4},{8,11},{9,10},{10,... | collective-permute-start | bytes 589832 | tf_op jit(solution)/shard_map/ppermute | solution.py:34
  220.6 9.1 %collective-permute-start.24 = (bf16[384,256]{1,0:T(8,128)(2,1)}, bf16[384,256]{1,0:T(8,128)(2,1)S(1)}, u32[]{:S(2)}, u32[]{:S(2)}) collective-permute-start(bf16[384,256]{1,0:T(8,128)(2,1)} %shard_map.75.a0), channel_id=1, source_target_pairs={{0,1},{1,0},{2,3},{3,2},{4,5},{5,4},{6,7},{7,6},{8,9},{9,8},{10,11... | collective-permute-start | bytes 589832 | tf_op jit(solution)/shard_map/ppermute | solution.py:34
  (14 other events, 64.4 us)
Sparse Core Ops, SparseCore 0:
  20.7 61.8 all-gather.2
  148.5 57.7 all-gather.4

commit v8 on v7

--- a/solution.py
+++ b/solution.py
@@ -10,6 +10,8 @@
 route_scale = 2.5
 bf16, f32 = jnp.bfloat16, jnp.float32
 
+Y_STEPS = ((2, 6), (6, 2))
+X_STEPS = ((8, 24), (24, 8))
 SIBLING = (1, 1)
 ORDER = (0, 1, 3, 2)
 
@@ -98,13 +100,18 @@
     )(jnp.full((1,), z, jnp.int32), tokens, taken, w_gate, w_up)
 
 
-def down_kernel(layer, z_ref, a0, a1, a2, a3, down_ref, w1, w2, w3, out_ref, own, sem):
+def down_kernel(layer, z_ref, a0, a1, a2, a3, down_ref, w1, w2, w3, out_ref, own, act, sems):
     units, part = own.shape
     column = pl.multiple_of(z_ref[0] * part, part)
-    copy = pltpu.make_async_copy(down_ref.at[layer, 0, :, pl.ds(column, part)], own, sem)
-    copy.start()
-    acts = jnp.concatenate([a1[...], a2[...], a3[...], a0[...]], axis=1)
-    copy.wait()
+    copies = [
+        pltpu.make_async_copy(down_ref.at[layer, 0, :, pl.ds(column, part)], own, sems.at[0]),
+        pltpu.make_async_copy(a0, act, sems.at[1]),
+    ]
+    for copy in copies:
+        copy.start()
+    for copy in copies:
+        copy.wait()
+    acts = jnp.concatenate([a1[...], a2[...], a3[...], act[...]], axis=1)
     half = part // 2
     for n in range(2):
         columns = slice(n * half, (n + 1) * half)
@@ -118,10 +125,17 @@
     outside, inside = pl.BlockSpec(memory_space=pl.ANY), pl.BlockSpec(memory_space=pltpu.VMEM)
     return pl.pallas_call(
         functools.partial(down_kernel, layer),
-        in_specs=[pl.BlockSpec(memory_space=pltpu.SMEM)] + [inside] * 4 + [outside] + [inside] * 3,
+        in_specs=[pl.BlockSpec(memory_space=pltpu.SMEM), outside]
+        + [inside] * 3
+        + [outside]
+        + [inside] * 3,
         out_specs=inside,
         out_shape=jax.ShapeDtypeStruct((slots, part), bf16),
-        scratch_shapes=[pltpu.VMEM((units, part), bf16), pltpu.SemaphoreType.DMA],
+        scratch_shapes=[
+            pltpu.VMEM((units, part), bf16),
+            pltpu.VMEM((slots, units), bf16),
+            pltpu.SemaphoreType.DMA((2,)),
+        ],
         compiler_params=pltpu.CompilerParams(vmem_limit_bytes=48 << 20),
         cost_estimate=pl.CostEstimate(
             flops=8 * slots * units * part,
@@ -138,9 +152,20 @@
     capacity = min(rows, 2 * rows * routes.shape[2] // experts)
     slots = experts * capacity
     chips = experts // 2
+    quarters = lax.axis_size("tensor")
     me = lax.axis_index("expert")
     core = me & 1
     z = lax.axis_index("tensor")
+
+    away = lax.broadcasted_iota(jnp.int32, (experts,), 0) ^ me
+    odd = ((away ^ me) & 1) == 1
+
+    def turns(distance):
+        low, high = (distance & 1) ^ (distance >> 1), distance >> 1
+        return jnp.where(odd, high, low) + 2 * jnp.where(odd, low, high)
+
+    places = (away & 1) * chips + turns((away >> 1) & 3) + 4 * turns(away >> 3)
+    in_place = places[:, None] == lax.broadcasted_iota(jnp.int32, (1, experts), 1)
 
     expert_iota = lax.broadcasted_iota(jnp.int32, (1, 1, 1, experts), 3)
     picks = jnp.any(routes[..., None] == expert_iota, axis=2)
@@ -159,6 +184,14 @@
         column = (after(z, *bound) ^ mask) * part
         block = lax.dynamic_slice(w_down, (layer, 0, first, column), (1, 1, count, part))
         return z_swap(block.reshape(count, part), mask)
+
+    def slots_of(marks_here, layer):
+        mine = lax.broadcasted_iota(jnp.int32, (1, 1, 128), 2) == me + layer * experts
+        mark = jnp.sum(jnp.where(mine, marks_here, 0.0), axis=2).astype(bf16)
+        mark = jnp.dot(in_place.astype(bf16), mark, preferred_element_type=f32).astype(jnp.int32)
+        source = lax.broadcasted_iota(jnp.int32, (experts, 1), 0)
+        slot = jnp.where(mark > 0, source * capacity + mark - 1, -1).reshape(1, -1)
+        return (lax.broadcasted_iota(jnp.int32, (slots, 1), 0) == slot).astype(bf16)
 
     state = hidden_in
     gains = jnp.stack(thirds(norm_gain), axis=0).reshape(3 * layers, part)
@@ -178,7 +211,7 @@
             for block, gain in zip(blocks, gains)
         ]
 
-        sent = jnp.concatenate(normed if layer else normed + [marks_sent], axis=1)
+        sent = jnp.concatenate(normed, axis=1)
         arrived = lax.all_gather(sent, "expert", axis=0, tiled=True)
 
         own = state.astype(f32) * scale[:, None] * norm_gain[layer][None, :]
@@ -203,23 +236,19 @@
 
         mixers = jnp.concatenate([mixer(core), swap(mixer(1 - core), SIBLING)], axis=0)
 
-        def slots_of(marks_here):
-            mine = lax.broadcasted_iota(jnp.int32, (1, 128), 1) == me + layer * experts
-            mark = jnp.sum(jnp.where(mine, marks_here.astype(f32), 0.0), axis=1).astype(jnp.int32)
-            source = lax.broadcasted_iota(jnp.int32, (experts, rows), 0).reshape(-1)
-            slot = jnp.where(mark > 0, source * capacity + mark - 1, -1)[None, :]
-            return (lax.broadcasted_iota(jnp.int32, (slots, 1), 0) == slot).astype(bf16)
-
         if layer == 0:
-            arrived, mixers, *others = lax.optimization_barrier((arrived, mixers, *others))
-            marks_here = arrived[:, width:]
-            taken = slots_of(marks_here)
+            held = after(marks_sent, scores)[None]
+            for masks in Y_STEPS + X_STEPS:
+                held = jnp.concatenate([held, swap(held, masks)])
+            held = jnp.concatenate([held, swap(held, SIBLING)]).astype(f32)
+            taken = [slots_of(held, each) for each in range(layers)]
+            arrived, mixers, taken, others = lax.optimization_barrier(
+                (arrived, mixers, taken, others)
+            )
         else:
-            taken = slots_of(after(marks_here, sent))
-            arrived, mixers, taken, *others = lax.optimization_barrier(
-                (arrived, mixers, taken, *others)
-            )
-        acts = spread(gate_up(z, arrived, taken, w_gate, w_up, layer))
+            arrived, mixers, others = lax.optimization_barrier((arrived, mixers, others))
+        acts = spread(gate_up(z, arrived, taken[layer], w_gate, w_up, layer))
+        acts[0] = jnp.where(z < quarters, acts[0], 0.0)
         out = down_product(z, acts, w_down, layer, others)
         groups = [list(range(parity, experts, 2)) for parity in range(2)]
         returned = lax.all_to_all(

time: 269 us -> 267 us (level)
  waiting for transfers between devices: 108 us -> 80.2 us
  starting transfers between devices: 41 us -> 52.5 us
  local copies, waits for them, and re-layouts: 19.7 us -> 27.2 us
  other arithmetic: 9.81 us -> 15.6 us
    ppermute x24, waiting for transfers between devices: 91.1 us -> 53.2 us  [z_swap(): return lax.ppermute(block, 'tensor', [(i, i ^ mask) for i in range(count)])]
    ppermute x4 -> x9, starting transfers between devices: 8.69 us -> 21 us  [swap(): lax.ppermute(block, 'expert', [(i, i ^ masks[i & 1]) for i in range(count)])]
    ppermute x4 -> x9, waiting for transfers between devices: 2.86 us -> 10.9 us  [swap(): lax.ppermute(block, 'expert', [(i, i ^ masks[i & 1]) for i in range(count)])]
  transfers between devices with their start and end apart: 30 -> 35, of which waited for: 17 -> 24; matrix products, arithmetic and copies ran while one was open for 8% -> 15% of each run, Pallas kernels for 0% -> 0%
where the time goes in v8:
time: 267 us; the launch traced here: 266 us
  waiting for transfers between devices  80.2 us (30%)
  starting transfers between devices  52.5 us (20%)
  blocking collectives  46.3 us (17%)
  local copies, waits for them, and re-layouts  27.2 us (10%)
  Pallas kernels  27.2 us (10%)
  other arithmetic  15.6 us (6%)
  between operations  14 us (5%)
  matrix products  2.94 us (1%)
    ppermute x24, waiting for transfers between devices, z_swap(): return lax.ppermute(block, 'tensor', [(i, i ^ mask) for i in range(count)])  53.2 us
    all_to_all x2, blocking collectives, body(): lax.all_to_all(out.reshape(chips, 2 * capacity, part), 'expert', split_ax...  46.3 us
    ppermute x24, starting transfers between devices, z_swap(): return lax.ppermute(block, 'tensor', [(i, i ^ mask) for i in range(count)])  31.4 us
    pallas_call x2, Pallas kernels, gate_up(): pl.pallas_call(functools.partial(gate_up_kernel, layer), in_specs=[pl.Blo...  21.2 us
    ppermute x9, starting transfers between devices, swap(): lax.ppermute(block, 'expert', [(i, i ^ masks[i & 1]) for i in range(count)])  21 us
    all_gather x2, waiting for transfers between devices, body(): arrived = lax.all_gather(sent, 'expert', axis=0, tiled=True)  16.1 us
    ppermute x9, waiting for transfers between devices, swap(): lax.ppermute(block, 'expert', [(i, i ^ masks[i & 1]) for i in range(count)])  10.9 us
    reshape x2, local copies, waits for them, and re-layouts, columns(): return z_swap(block.reshape(count, part), mask)  6.89 us
  transfers between devices with their start and end apart: 35, of which 24 were waited for; matrix products, arithmetic and copies ran while one was open for 15% of the time, Pallas kernels for 0%

profile of v8, /device:TPU:1, one launch (start us, length us, event | category | flops | bytes accessed | tf_op | source)
XLA Modules:
  0.0 265.9 jit_solution(16858335498147241598)
XLA Ops:
  8.5 2.5 collective-permute-start
  29.3 3.3 %collective-permute-start.4 = (f32[24,32]{1,0:T(8,128)S(1)}, f32[24,32]{1,0:T(8,128)S(1)}, u32[]{:S(2)}, u32[]{:S(2)}) collective-permute-start(f32[24,32]{1,0:T(8,128)S(1)} %fusion.7), channel_id=1, source_target_pairs={{0,3},{1,2},{2,1},{3,0},{4,7},{5,6},{6,5},{7,4},{8,11},{9,10},{10,... | collective-permute-start | bytes 9224 | tf_op jit(solution)/shard_map/ppermute | solution.py:36
  33.7 3.5 %dynamic-slice_bitcast_fusion.3 = (bf16[256,1792]{1,0:T(8,128)(2,1)}, bf16[256,1792]{1,0:T(8,128)(2,1)}, bf16[256,1792]{1,0:T(8,128)(2,1)}) fusion(bf16[2,1,256,7168]{3,2,1,0:T(8,128)(2,1)} %down_ref.3, s32[]{:T(128)S(6)} %select_n.219, s32[]{:T(128)S(6)} %select_n.218, s32[]{:T(128)S(6)} %select_n.217), kind=kLoop, calls=%fused_computation.11 | loop fusion | bytes 5505036 | tf_op jit(solution)/shard_map/reshape | solution.py:186
  41.1 2.7 %collective-permute-start.7 = (bf16[1,24,128]{2,1,0:T(8,128)(2,1)S(1)}, bf16[1,24,128]{2,1,0:T(8,128)(2,1)S(1)}, u32[]{:S(2)}, u32[]{:S(2)}) collective-permute-start(bf16[1,24,128]{2,1,0:T(8,128)(2,1)S(1)} %bitcast.101), channel_id=1, source_target_pairs={{0,8},{4,28},{8,0},{12,20},{16,24},{20,12},{24,16},{28,4},{32,40},... | collective-permute-start | bytes 18440 | tf_op jit(solution)/shard_map/ppermute | solution.py:31
  54.7 2.5 collective-permute-start.9
  59.7 3.7 %collective-permute-done.10 = bf16[8,24,128]{2,1,0:T(8,128)(2,1)S(1)} collective-permute-done((bf16[8,24,128]{2,1,0:T(8,128)(2,1)S(1)}, bf16[8,24,128]{2,1,0:T(8,128)(2,1)S(1)}, u32[]{:S(2)}, u32[]{:S(2)}) %collective-permute-start.10) | collective-permute-done | bytes 49184 | tf_op jit(solution)/shard_map/ppermute | solution.py:31
  64.0 4.2 %collective-permute-start.11 = (bf16[16,24,128]{2,1,0:T(8,128)(2,1)}, bf16[16,24,128]{2,1,0:T(8,128)(2,1)S(1)}, u32[]{:S(2)}, u32[]{:S(2)}) collective-permute-start(bf16[16,24,128]{2,1,0:T(8,128)(2,1)} %get-tuple-element.73), channel_id=1, source_target_pairs={{0,4},{4,0},{8,12},{12,8},{16,20},{20,16},{24,28},{28,24},{32,36},... | collective-permute-start | bytes 294920 | tf_op jit(solution)/shard_map/ppermute | solution.py:31
  74.2 4.5 %collective-permute-done.14.w3 = bf16[256,1792]{1,0:T(8,128)(2,1)S(1)} collective-permute-done((bf16[256,1792]{1,0:T(8,128)(2,1)}, bf16[256,1792]{1,0:T(8,128)(2,1)S(1)}, u32[]{:S(2)}, u32[]{:S(2)}) %collective-permute-start.14) | collective-permute-done | bytes 917536 | tf_op jit(solution)/shard_map/ppermute | solution.py:36
  78.7 5.0 %all-gather.3.cloned.1.call-done.tokens_ref = bf16[768,7168]{1,0:T(8,128)(2,1)} async-done(((bf16[24,7168]{1,0:T(8,128)(2,1)}), bf16[768,7168]{1,0:T(8,128)(2,1)}) %all-gather.3.cloned.1.call-update) | async-done | bytes 11010064 | tf_op jit(solution)/shard_map/all_gather | solution.py:215
  83.7 10.6 %shard_map.73 = bf16[384,256]{1,0:T(8,128)(2,1)} custom-call(s32[1]{0:T(128)} %bitcast.20.z_ref, bf16[768,7168]{1,0:T(8,128)(2,1)} %all-gather.3.cloned.1.call-done.tokens_ref, bf16[384,768]{1,0:T(8,128)(2,1)} %fusion.taken_ref, bf16[2,1,7168,256]{3,2,1,0:T(8,128)(2,1)} %gate_ref.3, bf16[2,1,7168,256]{3,2,1,0:T(8,128)(2,1)} %up_ref.3), custom_call_target="tpu_custom_call" | custom-call | flops 5637144576 | bytes 18743296 | tf_op jit(solution)/shard_map/pallas_call | solution.py:83
  100.8 4.8 %collective-permute-done.16.a2 = bf16[384,256]{1,0:T(8,128)(2,1)S(1)} collective-permute-done((bf16[384,256]{1,0:T(8,128)(2,1)}, bf16[384,256]{1,0:T(8,128)(2,1)S(1)}, u32[]{:S(2)}, u32[]{:S(2)}) %collective-permute-start.16) | collective-permute-done | bytes 196640 | tf_op jit(solution)/shard_map/ppermute | solution.py:36
  107.5 3.0 %shard_map.74 = bf16[384,1792]{1,0:T(8,128)(2,1)S(1)} custom-call(s32[1]{0:T(128)} %bitcast.20.z_ref, bf16[384,256]{1,0:T(8,128)(2,1)S(1)} %broadcast_select_fusion.1.a0, bf16[384,256]{1,0:T(8,128)(2,1)S(1)} %collective-permute-done.15.a1, bf16[384,256]{1,0:T(8,128)(2,1)S(1)} %collective-permute-done.16.a2, bf16[384,256]{1,0:T(8,128)(2,1)S(1)} %collective-permute-done.17.a3, ...), custom_call_target="tpu_custom_call" | custom-call | flops 1409286144 | bytes 5832704 | tf_op jit(solution)/shard_map/pallas_call | solution.py:126
  110.5 23.3 %all_to_all.10 = bf16[16,24,1792]{2,1,0:T(8,128)(2,1)S(1)} all-to-all(bf16[16,24,1792]{2,1,0:T(8,128)(2,1)S(1)} %bitcast.96), channel_id=1, replica_groups={{0,8,16,24,32,40,48,56,64,72,80,88,96,104,112,120},{4,12,20,28,36,44,52..., dimensions={0} | all-to-all | bytes 2752512 | tf_op jit(solution)/shard_map/all_to_all | solution.py:254
  134.2 3.1 %collective-permute-start.18 = (f32[24,1792]{1,0:T(8,128)S(1)}, f32[24,1792]{1,0:T(8,128)S(1)}, u32[]{:S(2)}, u32[]{:S(2)}) collective-permute-start(f32[24,1792]{1,0:T(8,128)S(1)} %slice_bitcast_fusion.2), channel_id=1, source_target_pairs={{0,4},{4,0},{8,12},{12,8},{16,20},{20,16},{24,28},{28,24},{32,36},... | collective-permute-start | bytes 516104 | tf_op jit(solution)/shard_map/ppermute | solution.py:31
  150.0 3.4 %dynamic-slice_bitcast_fusion = (bf16[256,1792]{1,0:T(8,128)(2,1)}, bf16[256,1792]{1,0:T(8,128)(2,1)}, bf16[256,1792]{1,0:T(8,128)(2,1)}) fusion(bf16[2,1,256,7168]{3,2,1,0:T(8,128)(2,1)} %down_ref.3, s32[]{:T(128)S(6)} %select_n.235, s32[]{:T(128)S(6)} %select_n.234, s32[]{:T(128)S(6)} %select_n.233), kind=kLoop, calls=%fused_computation.8 | loop fusion | bytes 5505036 | tf_op jit(solution)/shard_map/reshape | solution.py:186
  161.3 3.6 %collective-permute-start.25 = (bf16[48,384]{1,0:T(8,128)(2,1)S(1)}, bf16[48,384]{1,0:T(8,128)(2,1)S(1)}, u32[]{:S(2)}, u32[]{:S(2)}) collective-permute-start(bf16[48,384]{1,0:T(8,128)(2,1)S(1)} %pad_maximum_fusion.6), channel_id=1, source_target_pairs={{0,4},{4,0},{8,12},{12,8},{16,20},{20,16},{24,28},{28,24},{32,36},... | collective-permute-start | bytes 110600 | tf_op jit(solution)/shard_map/ppermute | solution.py:31
  165.7 7.1 %collective-permute-done.26.w1 = bf16[256,1792]{1,0:T(8,128)(2,1)S(1)} collective-permute-done((bf16[256,1792]{1,0:T(8,128)(2,1)}, bf16[256,1792]{1,0:T(8,128)(2,1)S(1)}, u32[]{:S(2)}, u32[]{:S(2)}) %collective-permute-start.26) | collective-permute-done | bytes 917536 | tf_op jit(solution)/shard_map/ppermute | solution.py:36
  175.2 17.8 %collective-permute-done.28.w3 = bf16[256,1792]{1,0:T(8,128)(2,1)S(1)} collective-permute-done((bf16[256,1792]{1,0:T(8,128)(2,1)}, bf16[256,1792]{1,0:T(8,128)(2,1)S(1)}, u32[]{:S(2)}, u32[]{:S(2)}) %collective-permute-start.28) | collective-permute-done | bytes 917536 | tf_op jit(solution)/shard_map/ppermute | solution.py:36
  193.0 11.1 %all-gather.5.cloned.1.call-done.tokens_ref = bf16[768,7168]{1,0:T(8,128)(2,1)} async-done(((bf16[24,7168]{1,0:T(8,128)(2,1)}), bf16[768,7168]{1,0:T(8,128)(2,1)}) %all-gather.5.cloned.1.call-update) | async-done | bytes 11010064 | tf_op jit(solution)/shard_map/all_gather | solution.py:215
  204.0 10.6 %shard_map.75 = bf16[384,256]{1,0:T(8,128)(2,1)} custom-call(s32[1]{0:T(128)} %bitcast.20.z_ref, bf16[768,7168]{1,0:T(8,128)(2,1)} %all-gather.5.cloned.1.call-done.tokens_ref, bf16[384,768]{1,0:T(8,128)(2,1)} %fusion.1.taken_ref, bf16[2,1,7168,256]{3,2,1,0:T(8,128)(2,1)} %gate_ref.3, bf16[2,1,7168,256]{3,2,1,0:T(8,128)(2,1)} %up_ref.3), custom_call_target="tpu_custom_call" | custom-call | flops 5637144576 | bytes 18743296 | tf_op jit(solution)/shard_map/pallas_call | solution.py:83
  221.2 4.8 %collective-permute-done.30.a2 = bf16[384,256]{1,0:T(8,128)(2,1)S(1)} collective-permute-done((bf16[384,256]{1,0:T(8,128)(2,1)}, bf16[384,256]{1,0:T(8,128)(2,1)S(1)}, u32[]{:S(2)}, u32[]{:S(2)}) %collective-permute-start.30) | collective-permute-done | bytes 196640 | tf_op jit(solution)/shard_map/ppermute | solution.py:36
  227.8 3.0 %shard_map.76 = bf16[384,1792]{1,0:T(8,128)(2,1)S(1)} custom-call(s32[1]{0:T(128)} %bitcast.20.z_ref, bf16[384,256]{1,0:T(8,128)(2,1)S(1)} %broadcast_select_fusion.a0, bf16[384,256]{1,0:T(8,128)(2,1)S(1)} %collective-permute-done.29.a1, bf16[384,256]{1,0:T(8,128)(2,1)S(1)} %collective-permute-done.30.a2, bf16[384,256]{1,0:T(8,128)(2,1)S(1)} %collective-permute-done.31.a3, ...), custom_call_target="tpu_custom_call" | custom-call | flops 1409286144 | bytes 5832704 | tf_op jit(solution)/shard_map/pallas_call | solution.py:126
  230.8 23.0 %all_to_all.11 = bf16[16,24,1792]{2,1,0:T(8,128)(2,1)S(1)} all-to-all(bf16[16,24,1792]{2,1,0:T(8,128)(2,1)S(1)} %bitcast.95), channel_id=1, replica_groups={{0,8,16,24,32,40,48,56,64,72,80,88,96,104,112,120},{4,12,20,28,36,44,52..., dimensions={0} | all-to-all | bytes 2752512 | tf_op jit(solution)/shard_map/all_to_all | solution.py:254
  254.3 3.1 %collective-permute-start.32 = (f32[24,1792]{1,0:T(8,128)S(1)}, f32[24,1792]{1,0:T(8,128)S(1)}, u32[]{:S(2)}, u32[]{:S(2)}) collective-permute-start(f32[24,1792]{1,0:T(8,128)S(1)} %slice_bitcast_fusion), channel_id=1, source_target_pairs={{0,4},{4,0},{8,12},{12,8},{16,20},{20,16},{24,28},{28,24},{32,36},... | collective-permute-start | bytes 516104 | tf_op jit(solution)/shard_map/ppermute | solution.py:31
  (206 shorter events, 87.9 us)
Async XLA Ops:
  6.5 77.1 %all-gather.3.cloned.1.call-start = ((), (), s32[]{:S(2)}) async-start(), calls=%async_computation.2 | async-start | bytes 11354112 | tf_op jit(solution)/shard_map/all_gather | solution.py:215
  8.5 7.5 %collective-permute-start = (bf16[32,1792]{1,0:T(8,128)(2,1)S(1)}, bf16[32,1792]{1,0:T(8,128)(2,1)S(1)}, u32[]{:S(2)}, u32[]{:S(2)}) collective-permute-start(bf16[32,1792]{1,0:T(8,128)(2,1)S(1)} %maximum_maximum_fusion), channel_id=1, source_target_pairs={{0,1},{1,0},{2,3},{3,2},{4,5},{5,4},{6,7},{7,6},{8,9},{9,8},{10,11... | collective-permute-start | bytes 344072 | tf_op jit(solution)/shard_map/ppermute | solution.py:36
  13.2 6.0 %collective-permute-start.2 = (bf16[32,1792]{1,0:T(8,128)(2,1)S(1)}, bf16[32,1792]{1,0:T(8,128)(2,1)S(1)}, u32[]{:S(2)}, u32[]{:S(2)}) collective-permute-start(bf16[32,1792]{1,0:T(8,128)(2,1)S(1)} %maximum_maximum_fusion), channel_id=1, source_target_pairs={{0,2},{1,3},{2,0},{3,1},{4,6},{5,7},{6,4},{7,5},{8,10},{9,11},{10,... | collective-permute-start | bytes 344072 | tf_op jit(solution)/shard_map/ppermute | solution.py:36
  21.3 182.7 %all-gather.5.cloned.1.call-start = ((), (), s32[]{:S(2)}) async-start(), calls=%async_computation.3 | async-start | bytes 11354112 | tf_op jit(solution)/shard_map/all_gather | solution.py:215
  29.2 10.8 %collective-permute-start.3 = (f32[24,32]{1,0:T(8,128)S(1)}, f32[24,32]{1,0:T(8,128)S(1)}, u32[]{:S(2)}, u32[]{:S(2)}) collective-permute-start(f32[24,32]{1,0:T(8,128)S(1)} %fusion.7), channel_id=1, source_target_pairs={{0,1},{1,0},{2,3},{3,2},{4,5},{5,4},{6,7},{7,6},{8,9},{9,8},{10,11... | collective-permute-start | bytes 9224 | tf_op jit(solution)/shard_map/ppermute | solution.py:36
  29.3 11.8 %collective-permute-start.4 = (f32[24,32]{1,0:T(8,128)S(1)}, f32[24,32]{1,0:T(8,128)S(1)}, u32[]{:S(2)}, u32[]{:S(2)}) collective-permute-start(f32[24,32]{1,0:T(8,128)S(1)} %fusion.7), channel_id=1, source_target_pairs={{0,3},{1,2},{2,1},{3,0},{4,7},{5,6},{6,5},{7,4},{8,11},{9,10},{10,... | collective-permute-start | bytes 9224 | tf_op jit(solution)/shard_map/ppermute | solution.py:36
  32.6 11.2 %collective-permute-start.5 = (f32[24,32]{1,0:T(8,128)S(1)}, f32[24,32]{1,0:T(8,128)S(1)}, u32[]{:S(2)}, u32[]{:S(2)}) collective-permute-start(f32[24,32]{1,0:T(8,128)S(1)} %fusion.7), channel_id=1, source_target_pairs={{0,2},{1,3},{2,0},{3,1},{4,6},{5,7},{6,4},{7,5},{8,10},{9,11},{10,... | collective-permute-start | bytes 9224 | tf_op jit(solution)/shard_map/ppermute | solution.py:36
  37.2 37.0 %collective-permute-start.12 = (bf16[256,1792]{1,0:T(8,128)(2,1)}, bf16[256,1792]{1,0:T(8,128)(2,1)S(1)}, u32[]{:S(2)}, u32[]{:S(2)}) collective-permute-start(bf16[256,1792]{1,0:T(8,128)(2,1)} %get-tuple-element.64), channel_id=1, source_target_pairs={{0,1},{1,0},{2,3},{3,2},{4,5},{5,4},{6,7},{7,6},{8,9},{9,8},{10,11... | collective-permute-start | bytes 2752520 | tf_op jit(solution)/shard_map/ppermute | solution.py:36
  37.2 37.0 %collective-permute-start.13 = (bf16[256,1792]{1,0:T(8,128)(2,1)}, bf16[256,1792]{1,0:T(8,128)(2,1)S(1)}, u32[]{:S(2)}, u32[]{:S(2)}) collective-permute-start(bf16[256,1792]{1,0:T(8,128)(2,1)} %get-tuple-element.63), channel_id=1, source_target_pairs={{0,3},{1,2},{2,1},{3,0},{4,7},{5,6},{6,5},{7,4},{8,11},{9,10},{10,... | collective-permute-start | bytes 2752520 | tf_op jit(solution)/shard_map/ppermute | solution.py:36
  40.0 38.7 %collective-permute-start.14 = (bf16[256,1792]{1,0:T(8,128)(2,1)}, bf16[256,1792]{1,0:T(8,128)(2,1)S(1)}, u32[]{:S(2)}, u32[]{:S(2)}) collective-permute-start(bf16[256,1792]{1,0:T(8,128)(2,1)} %get-tuple-element.62), channel_id=1, source_target_pairs={{0,2},{1,3},{2,0},{3,1},{4,6},{5,7},{6,4},{7,5},{8,10},{9,11},{10,... | collective-permute-start | bytes 2752520 | tf_op jit(solution)/shard_map/ppermute | solution.py:36
  41.1 10.7 %collective-permute-start.7 = (bf16[1,24,128]{2,1,0:T(8,128)(2,1)S(1)}, bf16[1,24,128]{2,1,0:T(8,128)(2,1)S(1)}, u32[]{:S(2)}, u32[]{:S(2)}) collective-permute-start(bf16[1,24,128]{2,1,0:T(8,128)(2,1)S(1)} %bitcast.101), channel_id=1, source_target_pairs={{0,8},{4,28},{8,0},{12,20},{16,24},{20,12},{24,16},{28,4},{32,40},... | collective-permute-start | bytes 18440 | tf_op jit(solution)/shard_map/ppermute | solution.py:31
  50.3 17.9 %collective-permute-start.6 = (bf16[48,384]{1,0:T(8,128)(2,1)S(1)}, bf16[48,384]{1,0:T(8,128)(2,1)S(1)}, u32[]{:S(2)}, u32[]{:S(2)}) collective-permute-start(bf16[48,384]{1,0:T(8,128)(2,1)S(1)} %pad_maximum_fusion.5), channel_id=1, source_target_pairs={{0,4},{4,0},{8,12},{12,8},{16,20},{20,16},{24,28},{28,24},{32,36},... | collective-permute-start | bytes 110600 | tf_op jit(solution)/shard_map/ppermute | solution.py:31
  94.3 6.5 %collective-permute-start.15 = (bf16[384,256]{1,0:T(8,128)(2,1)}, bf16[384,256]{1,0:T(8,128)(2,1)S(1)}, u32[]{:S(2)}, u32[]{:S(2)}) collective-permute-start(bf16[384,256]{1,0:T(8,128)(2,1)} %shard_map.73), channel_id=1, source_target_pairs={{0,1},{1,0},{2,3},{3,2},{4,5},{5,4},{6,7},{7,6},{8,9},{9,8},{10,11... | collective-permute-start | bytes 589832 | tf_op jit(solution)/shard_map/ppermute | solution.py:36
  95.6 10.0 %collective-permute-start.16 = (bf16[384,256]{1,0:T(8,128)(2,1)}, bf16[384,256]{1,0:T(8,128)(2,1)S(1)}, u32[]{:S(2)}, u32[]{:S(2)}) collective-permute-start(bf16[384,256]{1,0:T(8,128)(2,1)} %shard_map.73), channel_id=1, source_target_pairs={{0,3},{1,2},{2,1},{3,0},{4,7},{5,6},{6,5},{7,4},{8,11},{9,10},{10,... | collective-permute-start | bytes 589832 | tf_op jit(solution)/shard_map/ppermute | solution.py:36
  97.5 9.9 %collective-permute-start.17 = (bf16[384,256]{1,0:T(8,128)(2,1)}, bf16[384,256]{1,0:T(8,128)(2,1)S(1)}, u32[]{:S(2)}, u32[]{:S(2)}) collective-permute-start(bf16[384,256]{1,0:T(8,128)(2,1)} %shard_map.73), channel_id=1, source_target_pairs={{0,2},{1,3},{2,0},{3,1},{4,6},{5,7},{6,4},{7,5},{8,10},{9,11},{10,... | collective-permute-start | bytes 589832 | tf_op jit(solution)/shard_map/ppermute | solution.py:36
  146.7 8.6 %collective-permute-start.22 = (f32[24,32]{1,0:T(8,128)S(1)}, f32[24,32]{1,0:T(8,128)S(1)}, u32[]{:S(2)}, u32[]{:S(2)}) collective-permute-start(f32[24,32]{1,0:T(8,128)S(1)} %fusion.5), channel_id=1, source_target_pairs={{0,1},{1,0},{2,3},{3,2},{4,5},{5,4},{6,7},{7,6},{8,9},{9,8},{10,11... | collective-permute-start | bytes 9224 | tf_op jit(solution)/shard_map/ppermute | solution.py:36
  147.5 9.2 %collective-permute-start.23 = (f32[24,32]{1,0:T(8,128)S(1)}, f32[24,32]{1,0:T(8,128)S(1)}, u32[]{:S(2)}, u32[]{:S(2)}) collective-permute-start(f32[24,32]{1,0:T(8,128)S(1)} %fusion.5), channel_id=1, source_target_pairs={{0,3},{1,2},{2,1},{3,0},{4,7},{5,6},{6,5},{7,4},{8,11},{9,10},{10,... | collective-permute-start | bytes 9224 | tf_op jit(solution)/shard_map/ppermute | solution.py:36
  148.6 8.0 %collective-permute-start.24 = (f32[24,32]{1,0:T(8,128)S(1)}, f32[24,32]{1,0:T(8,128)S(1)}, u32[]{:S(2)}, u32[]{:S(2)}) collective-permute-start(f32[24,32]{1,0:T(8,128)S(1)} %fusion.5), channel_id=1, source_target_pairs={{0,2},{1,3},{2,0},{3,1},{4,6},{5,7},{6,4},{7,5},{8,10},{9,11},{10,... | collective-permute-start | bytes 9224 | tf_op jit(solution)/shard_map/ppermute | solution.py:36
  153.4 19.4 %collective-permute-start.26 = (bf16[256,1792]{1,0:T(8,128)(2,1)}, bf16[256,1792]{1,0:T(8,128)(2,1)S(1)}, u32[]{:S(2)}, u32[]{:S(2)}) collective-permute-start(bf16[256,1792]{1,0:T(8,128)(2,1)} %get-tuple-element.61), channel_id=1, source_target_pairs={{0,1},{1,0},{2,3},{3,2},{4,5},{5,4},{6,7},{7,6},{8,9},{9,8},{10,11... | collective-permute-start | bytes 2752520 | tf_op jit(solution)/shard_map/ppermute | solution.py:36
  154.2 21.0 %collective-permute-start.27 = (bf16[256,1792]{1,0:T(8,128)(2,1)}, bf16[256,1792]{1,0:T(8,128)(2,1)S(1)}, u32[]{:S(2)}, u32[]{:S(2)}) collective-permute-start(bf16[256,1792]{1,0:T(8,128)(2,1)} %get-tuple-element.60), channel_id=1, source_target_pairs={{0,3},{1,2},{2,1},{3,0},{4,7},{5,6},{6,5},{7,4},{8,11},{9,10},{10,... | collective-permute-start | bytes 2752520 | tf_op jit(solution)/shard_map/ppermute | solution.py:36
  155.3 37.7 %collective-permute-start.28 = (bf16[256,1792]{1,0:T(8,128)(2,1)}, bf16[256,1792]{1,0:T(8,128)(2,1)S(1)}, u32[]{:S(2)}, u32[]{:S(2)}) collective-permute-start(bf16[256,1792]{1,0:T(8,128)(2,1)} %get-tuple-element.59), channel_id=1, source_target_pairs={{0,2},{1,3},{2,0},{3,1},{4,6},{5,7},{6,4},{7,5},{8,10},{9,11},{10,... | collective-permute-start | bytes 2752520 | tf_op jit(solution)/shard_map/ppermute | solution.py:36
  214.6 6.5 %collective-permute-start.29 = (bf16[384,256]{1,0:T(8,128)(2,1)}, bf16[384,256]{1,0:T(8,128)(2,1)S(1)}, u32[]{:S(2)}, u32[]{:S(2)}) collective-permute-start(bf16[384,256]{1,0:T(8,128)(2,1)} %shard_map.75), channel_id=1, source_target_pairs={{0,1},{1,0},{2,3},{3,2},{4,5},{5,4},{6,7},{7,6},{8,9},{9,8},{10,11... | collective-permute-start | bytes 589832 | tf_op jit(solution)/shard_map/ppermute | solution.py:36
  216.0 10.0 %collective-permute-start.30 = (bf16[384,256]{1,0:T(8,128)(2,1)}, bf16[384,256]{1,0:T(8,128)(2,1)S(1)}, u32[]{:S(2)}, u32[]{:S(2)}) collective-permute-start(bf16[384,256]{1,0:T(8,128)(2,1)} %shard_map.75), channel_id=1, source_target_pairs={{0,3},{1,2},{2,1},{3,0},{4,7},{5,6},{6,5},{7,4},{8,11},{9,10},{10,... | collective-permute-start | bytes 589832 | tf_op jit(solution)/shard_map/ppermute | solution.py:36
  217.9 10.0 %collective-permute-start.31 = (bf16[384,256]{1,0:T(8,128)(2,1)}, bf16[384,256]{1,0:T(8,128)(2,1)S(1)}, u32[]{:S(2)}, u32[]{:S(2)}) collective-permute-start(bf16[384,256]{1,0:T(8,128)(2,1)} %shard_map.75), channel_id=1, source_target_pairs={{0,2},{1,3},{2,0},{3,1},{4,6},{5,7},{6,4},{7,5},{8,10},{9,11},{10,... | collective-permute-start | bytes 589832 | tf_op jit(solution)/shard_map/ppermute | solution.py:36
  (26 other events, 199.2 us)
Sparse Core Ops, SparseCore 0:
  21.4 62.2 all-gather.2
  146.4 57.5 all-gather.4

commit v9 on v8

--- a/solution.py
+++ b/solution.py
@@ -194,13 +194,9 @@
         return (lax.broadcasted_iota(jnp.int32, (slots, 1), 0) == slot).astype(bf16)
 
     state = hidden_in
-    gains = jnp.stack(thirds(norm_gain), axis=0).reshape(3 * layers, part)
-    opening = [state, gains, jnp.zeros((8 - 3 * layers, part), bf16)]
+    opening = [state, norm_gain.astype(bf16), jnp.zeros((8 - layers, part), bf16)]
     opening = spread(jnp.concatenate(opening, axis=0))
-    gains = [
-        block[rows : rows + 3 * layers].astype(f32).reshape(3, layers, part).sum(axis=0)
-        for block in opening
-    ]
+    gains = [block[rows : rows + layers].astype(f32) for block in opening]
     for layer in range(layers):
         blocks = spread(state) if layer else [block[:rows] for block in opening]
         blocks = [block.astype(f32) for block in blocks]

time: 267 us -> 267 us (level)
  no operation moved by 1% of the time
where the time goes in v9:
time: 267 us
  waiting for transfers between devices  80.1 us (30%)
  starting transfers between devices  52.5 us (20%)
  blocking collectives  46.3 us (17%)
  local copies, waits for them, and re-layouts  27.1 us (10%)
  Pallas kernels  27.1 us (10%)
  other arithmetic  16.4 us (6%)
  between operations  13.9 us (5%)
  matrix products  3.03 us (1%)
    ppermute x24, waiting for transfers between devices, z_swap(): return lax.ppermute(block, 'tensor', [(i, i ^ mask) for i in range(count)])  53.3 us
    all_to_all x2, blocking collectives, body(): lax.all_to_all(out.reshape(chips, 2 * capacity, part), 'expert', split_ax...  46.3 us
    ppermute x24, starting transfers between devices, z_swap(): return lax.ppermute(block, 'tensor', [(i, i ^ mask) for i in range(count)])  31.4 us
    pallas_call x2, Pallas kernels, gate_up(): pl.pallas_call(functools.partial(gate_up_kernel, layer), in_specs=[pl.Blo...  21.1 us
    ppermute x9, starting transfers between devices, swap(): lax.ppermute(block, 'expert', [(i, i ^ masks[i & 1]) for i in range(count)])  21 us
    all_gather x2, waiting for transfers between devices, body(): arrived = lax.all_gather(sent, 'expert', axis=0, tiled=True)  15.9 us
    ppermute x9, waiting for transfers between devices, swap(): lax.ppermute(block, 'expert', [(i, i ^ masks[i & 1]) for i in range(count)])  10.9 us
    reshape x2, local copies, waits for them, and re-layouts, columns(): return z_swap(block.reshape(count, part), mask)  6.98 us
  transfers between devices with their start and end apart: 35, of which 24 were waited for; matrix products, arithmetic and copies ran while one was open for 15% of the time, Pallas kernels for 0%

profile of v9, /device:TPU:1, one launch (start us, length us, event | category | flops | bytes accessed | tf_op | source)
XLA Modules:
  0.0 266.5 jit_solution(10413524714667017270)
XLA Ops:
  8.3 2.5 collective-permute-start
  30.0 3.3 %collective-permute-start.4 = (f32[24,32]{1,0:T(8,128)S(1)}, f32[24,32]{1,0:T(8,128)S(1)}, u32[]{:S(2)}, u32[]{:S(2)}) collective-permute-start(f32[24,32]{1,0:T(8,128)S(1)} %fusion.7), channel_id=1, source_target_pairs={{0,3},{1,2},{2,1},{3,0},{4,7},{5,6},{6,5},{7,4},{8,11},{9,10},{10,... | collective-permute-start | bytes 9224 | tf_op jit(solution)/shard_map/ppermute | solution.py:36
  34.3 3.5 %dynamic-slice_bitcast_fusion.3 = (bf16[256,1792]{1,0:T(8,128)(2,1)}, bf16[256,1792]{1,0:T(8,128)(2,1)}, bf16[256,1792]{1,0:T(8,128)(2,1)}) fusion(bf16[2,1,256,7168]{3,2,1,0:T(8,128)(2,1)} %down_ref.3, s32[]{:T(128)S(6)} %select_n.219, s32[]{:T(128)S(6)} %select_n.218, s32[]{:T(128)S(6)} %select_n.217), kind=kLoop, calls=%fused_computation.11 | loop fusion | bytes 5505036 | tf_op jit(solution)/shard_map/reshape | solution.py:186
  41.8 2.7 %collective-permute-start.7 = (bf16[1,24,128]{2,1,0:T(8,128)(2,1)S(1)}, bf16[1,24,128]{2,1,0:T(8,128)(2,1)S(1)}, u32[]{:S(2)}, u32[]{:S(2)}) collective-permute-start(bf16[1,24,128]{2,1,0:T(8,128)(2,1)S(1)} %bitcast.95), channel_id=1, source_target_pairs={{0,8},{4,28},{8,0},{12,20},{16,24},{20,12},{24,16},{28,4},{32,40},... | collective-permute-start | bytes 18440 | tf_op jit(solution)/shard_map/ppermute | solution.py:31
  55.4 2.5 collective-permute-start.9
  60.4 3.6 %collective-permute-done.10 = bf16[8,24,128]{2,1,0:T(8,128)(2,1)S(1)} collective-permute-done((bf16[8,24,128]{2,1,0:T(8,128)(2,1)S(1)}, bf16[8,24,128]{2,1,0:T(8,128)(2,1)S(1)}, u32[]{:S(2)}, u32[]{:S(2)}) %collective-permute-start.10) | collective-permute-done | bytes 49184 | tf_op jit(solution)/shard_map/ppermute | solution.py:31
  64.7 4.2 %collective-permute-start.11 = (bf16[16,24,128]{2,1,0:T(8,128)(2,1)}, bf16[16,24,128]{2,1,0:T(8,128)(2,1)S(1)}, u32[]{:S(2)}, u32[]{:S(2)}) collective-permute-start(bf16[16,24,128]{2,1,0:T(8,128)(2,1)} %get-tuple-element.73), channel_id=1, source_target_pairs={{0,4},{4,0},{8,12},{12,8},{16,20},{20,16},{24,28},{28,24},{32,36},... | collective-permute-start | bytes 294920 | tf_op jit(solution)/shard_map/ppermute | solution.py:31
  75.0 4.4 %collective-permute-done.14.w3 = bf16[256,1792]{1,0:T(8,128)(2,1)S(1)} collective-permute-done((bf16[256,1792]{1,0:T(8,128)(2,1)}, bf16[256,1792]{1,0:T(8,128)(2,1)S(1)}, u32[]{:S(2)}, u32[]{:S(2)}) %collective-permute-start.14) | collective-permute-done | bytes 917536 | tf_op jit(solution)/shard_map/ppermute | solution.py:36
  79.4 4.9 %all-gather.3.cloned.1.call-done.tokens_ref = bf16[768,7168]{1,0:T(8,128)(2,1)} async-done(((bf16[24,7168]{1,0:T(8,128)(2,1)}), bf16[768,7168]{1,0:T(8,128)(2,1)}) %all-gather.3.cloned.1.call-update) | async-done | bytes 11010064 | tf_op jit(solution)/shard_map/all_gather | solution.py:211
  84.3 10.6 %shard_map.73 = bf16[384,256]{1,0:T(8,128)(2,1)} custom-call(s32[1]{0:T(128)} %bitcast.17.z_ref, bf16[768,7168]{1,0:T(8,128)(2,1)} %all-gather.3.cloned.1.call-done.tokens_ref, bf16[384,768]{1,0:T(8,128)(2,1)} %fusion.taken_ref, bf16[2,1,7168,256]{3,2,1,0:T(8,128)(2,1)} %gate_ref.3, bf16[2,1,7168,256]{3,2,1,0:T(8,128)(2,1)} %up_ref.3), custom_call_target="tpu_custom_call" | custom-call | flops 5637144576 | bytes 18743296 | tf_op jit(solution)/shard_map/pallas_call | solution.py:83
  101.4 4.8 %collective-permute-done.16.a2 = bf16[384,256]{1,0:T(8,128)(2,1)S(1)} collective-permute-done((bf16[384,256]{1,0:T(8,128)(2,1)}, bf16[384,256]{1,0:T(8,128)(2,1)S(1)}, u32[]{:S(2)}, u32[]{:S(2)}) %collective-permute-start.16) | collective-permute-done | bytes 196640 | tf_op jit(solution)/shard_map/ppermute | solution.py:36
  108.1 3.0 %shard_map.74 = bf16[384,1792]{1,0:T(8,128)(2,1)S(1)} custom-call(s32[1]{0:T(128)} %bitcast.17.z_ref, bf16[384,256]{1,0:T(8,128)(2,1)S(1)} %broadcast_select_fusion.1.a0, bf16[384,256]{1,0:T(8,128)(2,1)S(1)} %collective-permute-done.15.a1, bf16[384,256]{1,0:T(8,128)(2,1)S(1)} %collective-permute-done.16.a2, bf16[384,256]{1,0:T(8,128)(2,1)S(1)} %collective-permute-done.17.a3, ...), custom_call_target="tpu_custom_call" | custom-call | flops 1409286144 | bytes 5832704 | tf_op jit(solution)/shard_map/pallas_call | solution.py:126
  111.1 23.3 %all_to_all.10 = bf16[16,24,1792]{2,1,0:T(8,128)(2,1)S(1)} all-to-all(bf16[16,24,1792]{2,1,0:T(8,128)(2,1)S(1)} %bitcast.90), channel_id=1, replica_groups={{0,8,16,24,32,40,48,56,64,72,80,88,96,104,112,120},{4,12,20,28,36,44,52..., dimensions={0} | all-to-all | bytes 2752512 | tf_op jit(solution)/shard_map/all_to_all | solution.py:250
  134.9 3.1 %collective-permute-start.18 = (f32[24,1792]{1,0:T(8,128)S(1)}, f32[24,1792]{1,0:T(8,128)S(1)}, u32[]{:S(2)}, u32[]{:S(2)}) collective-permute-start(f32[24,1792]{1,0:T(8,128)S(1)} %slice_bitcast_fusion.2), channel_id=1, source_target_pairs={{0,4},{4,0},{8,12},{12,8},{16,20},{20,16},{24,28},{28,24},{32,36},... | collective-permute-start | bytes 516104 | tf_op jit(solution)/shard_map/ppermute | solution.py:31
  150.6 3.4 %dynamic-slice_bitcast_fusion = (bf16[256,1792]{1,0:T(8,128)(2,1)}, bf16[256,1792]{1,0:T(8,128)(2,1)}, bf16[256,1792]{1,0:T(8,128)(2,1)}) fusion(bf16[2,1,256,7168]{3,2,1,0:T(8,128)(2,1)} %down_ref.3, s32[]{:T(128)S(6)} %select_n.235, s32[]{:T(128)S(6)} %select_n.234, s32[]{:T(128)S(6)} %select_n.233), kind=kLoop, calls=%fused_computation.8 | loop fusion | bytes 5505036 | tf_op jit(solution)/shard_map/reshape | solution.py:186
  162.0 3.6 %collective-permute-start.25 = (bf16[48,384]{1,0:T(8,128)(2,1)S(1)}, bf16[48,384]{1,0:T(8,128)(2,1)S(1)}, u32[]{:S(2)}, u32[]{:S(2)}) collective-permute-start(bf16[48,384]{1,0:T(8,128)(2,1)S(1)} %pad_maximum_fusion.6), channel_id=1, source_target_pairs={{0,4},{4,0},{8,12},{12,8},{16,20},{20,16},{24,28},{28,24},{32,36},... | collective-permute-start | bytes 110600 | tf_op jit(solution)/shard_map/ppermute | solution.py:31
  166.4 7.0 %collective-permute-done.26.w1 = bf16[256,1792]{1,0:T(8,128)(2,1)S(1)} collective-permute-done((bf16[256,1792]{1,0:T(8,128)(2,1)}, bf16[256,1792]{1,0:T(8,128)(2,1)S(1)}, u32[]{:S(2)}, u32[]{:S(2)}) %collective-permute-start.26) | collective-permute-done | bytes 917536 | tf_op jit(solution)/shard_map/ppermute | solution.py:36
  175.7 18.0 %collective-permute-done.28.w3 = bf16[256,1792]{1,0:T(8,128)(2,1)S(1)} collective-permute-done((bf16[256,1792]{1,0:T(8,128)(2,1)}, bf16[256,1792]{1,0:T(8,128)(2,1)S(1)}, u32[]{:S(2)}, u32[]{:S(2)}) %collective-permute-start.28) | collective-permute-done | bytes 917536 | tf_op jit(solution)/shard_map/ppermute | solution.py:36
  193.7 11.0 %all-gather.5.cloned.1.call-done.tokens_ref = bf16[768,7168]{1,0:T(8,128)(2,1)} async-done(((bf16[24,7168]{1,0:T(8,128)(2,1)}), bf16[768,7168]{1,0:T(8,128)(2,1)}) %all-gather.5.cloned.1.call-update) | async-done | bytes 11010064 | tf_op jit(solution)/shard_map/all_gather | solution.py:211
  204.7 10.6 %shard_map.75 = bf16[384,256]{1,0:T(8,128)(2,1)} custom-call(s32[1]{0:T(128)} %bitcast.17.z_ref, bf16[768,7168]{1,0:T(8,128)(2,1)} %all-gather.5.cloned.1.call-done.tokens_ref, bf16[384,768]{1,0:T(8,128)(2,1)} %fusion.1.taken_ref, bf16[2,1,7168,256]{3,2,1,0:T(8,128)(2,1)} %gate_ref.3, bf16[2,1,7168,256]{3,2,1,0:T(8,128)(2,1)} %up_ref.3), custom_call_target="tpu_custom_call" | custom-call | flops 5637144576 | bytes 18743296 | tf_op jit(solution)/shard_map/pallas_call | solution.py:83
  221.8 4.8 %collective-permute-done.30.a2 = bf16[384,256]{1,0:T(8,128)(2,1)S(1)} collective-permute-done((bf16[384,256]{1,0:T(8,128)(2,1)}, bf16[384,256]{1,0:T(8,128)(2,1)S(1)}, u32[]{:S(2)}, u32[]{:S(2)}) %collective-permute-start.30) | collective-permute-done | bytes 196640 | tf_op jit(solution)/shard_map/ppermute | solution.py:36
  228.4 3.0 %shard_map.76 = bf16[384,1792]{1,0:T(8,128)(2,1)S(1)} custom-call(s32[1]{0:T(128)} %bitcast.17.z_ref, bf16[384,256]{1,0:T(8,128)(2,1)S(1)} %broadcast_select_fusion.a0, bf16[384,256]{1,0:T(8,128)(2,1)S(1)} %collective-permute-done.29.a1, bf16[384,256]{1,0:T(8,128)(2,1)S(1)} %collective-permute-done.30.a2, bf16[384,256]{1,0:T(8,128)(2,1)S(1)} %collective-permute-done.31.a3, ...), custom_call_target="tpu_custom_call" | custom-call | flops 1409286144 | bytes 5832704 | tf_op jit(solution)/shard_map/pallas_call | solution.py:126
  231.4 23.0 %all_to_all.11 = bf16[16,24,1792]{2,1,0:T(8,128)(2,1)S(1)} all-to-all(bf16[16,24,1792]{2,1,0:T(8,128)(2,1)S(1)} %bitcast.89), channel_id=1, replica_groups={{0,8,16,24,32,40,48,56,64,72,80,88,96,104,112,120},{4,12,20,28,36,44,52..., dimensions={0} | all-to-all | bytes 2752512 | tf_op jit(solution)/shard_map/all_to_all | solution.py:250
  254.9 3.1 %collective-permute-start.32 = (f32[24,1792]{1,0:T(8,128)S(1)}, f32[24,1792]{1,0:T(8,128)S(1)}, u32[]{:S(2)}, u32[]{:S(2)}) collective-permute-start(f32[24,1792]{1,0:T(8,128)S(1)} %slice_bitcast_fusion), channel_id=1, source_target_pairs={{0,4},{4,0},{8,12},{12,8},{16,20},{20,16},{24,28},{28,24},{32,36},... | collective-permute-start | bytes 516104 | tf_op jit(solution)/shard_map/ppermute | solution.py:31
  (198 shorter events, 88.6 us)
Async XLA Ops:
  6.5 77.8 %all-gather.3.cloned.1.call-start = ((), (), s32[]{:S(2)}) async-start(), calls=%async_computation.2 | async-start | bytes 11354112 | tf_op jit(solution)/shard_map/all_gather | solution.py:211
  8.3 7.5 %collective-permute-start = (bf16[32,1792]{1,0:T(8,128)(2,1)S(1)}, bf16[32,1792]{1,0:T(8,128)(2,1)S(1)}, u32[]{:S(2)}, u32[]{:S(2)}) collective-permute-start(bf16[32,1792]{1,0:T(8,128)(2,1)S(1)} %maximum_maximum_fusion), channel_id=1, source_target_pairs={{0,1},{1,0},{2,3},{3,2},{4,5},{5,4},{6,7},{7,6},{8,9},{9,8},{10,11... | collective-permute-start | bytes 344072 | tf_op jit(solution)/shard_map/ppermute | solution.py:36
  13.1 6.0 %collective-permute-start.2 = (bf16[32,1792]{1,0:T(8,128)(2,1)S(1)}, bf16[32,1792]{1,0:T(8,128)(2,1)S(1)}, u32[]{:S(2)}, u32[]{:S(2)}) collective-permute-start(bf16[32,1792]{1,0:T(8,128)(2,1)S(1)} %maximum_maximum_fusion), channel_id=1, source_target_pairs={{0,2},{1,3},{2,0},{3,1},{4,6},{5,7},{6,4},{7,5},{8,10},{9,11},{10,... | collective-permute-start | bytes 344072 | tf_op jit(solution)/shard_map/ppermute | solution.py:36
  22.0 182.7 %all-gather.5.cloned.1.call-start = ((), (), s32[]{:S(2)}) async-start(), calls=%async_computation.3 | async-start | bytes 11354112 | tf_op jit(solution)/shard_map/all_gather | solution.py:211
  29.9 10.8 %collective-permute-start.3 = (f32[24,32]{1,0:T(8,128)S(1)}, f32[24,32]{1,0:T(8,128)S(1)}, u32[]{:S(2)}, u32[]{:S(2)}) collective-permute-start(f32[24,32]{1,0:T(8,128)S(1)} %fusion.7), channel_id=1, source_target_pairs={{0,1},{1,0},{2,3},{3,2},{4,5},{5,4},{6,7},{7,6},{8,9},{9,8},{10,11... | collective-permute-start | bytes 9224 | tf_op jit(solution)/shard_map/ppermute | solution.py:36
  30.0 11.8 %collective-permute-start.4 = (f32[24,32]{1,0:T(8,128)S(1)}, f32[24,32]{1,0:T(8,128)S(1)}, u32[]{:S(2)}, u32[]{:S(2)}) collective-permute-start(f32[24,32]{1,0:T(8,128)S(1)} %fusion.7), channel_id=1, source_target_pairs={{0,3},{1,2},{2,1},{3,0},{4,7},{5,6},{6,5},{7,4},{8,11},{9,10},{10,... | collective-permute-start | bytes 9224 | tf_op jit(solution)/shard_map/ppermute | solution.py:36
  33.2 11.3 %collective-permute-start.5 = (f32[24,32]{1,0:T(8,128)S(1)}, f32[24,32]{1,0:T(8,128)S(1)}, u32[]{:S(2)}, u32[]{:S(2)}) collective-permute-start(f32[24,32]{1,0:T(8,128)S(1)} %fusion.7), channel_id=1, source_target_pairs={{0,2},{1,3},{2,0},{3,1},{4,6},{5,7},{6,4},{7,5},{8,10},{9,11},{10,... | collective-permute-start | bytes 9224 | tf_op jit(solution)/shard_map/ppermute | solution.py:36
  37.9 37.1 %collective-permute-start.12 = (bf16[256,1792]{1,0:T(8,128)(2,1)}, bf16[256,1792]{1,0:T(8,128)(2,1)S(1)}, u32[]{:S(2)}, u32[]{:S(2)}) collective-permute-start(bf16[256,1792]{1,0:T(8,128)(2,1)} %get-tuple-element.64), channel_id=1, source_target_pairs={{0,1},{1,0},{2,3},{3,2},{4,5},{5,4},{6,7},{7,6},{8,9},{9,8},{10,11... | collective-permute-start | bytes 2752520 | tf_op jit(solution)/shard_map/ppermute | solution.py:36
  37.9 37.1 %collective-permute-start.13 = (bf16[256,1792]{1,0:T(8,128)(2,1)}, bf16[256,1792]{1,0:T(8,128)(2,1)S(1)}, u32[]{:S(2)}, u32[]{:S(2)}) collective-permute-start(bf16[256,1792]{1,0:T(8,128)(2,1)} %get-tuple-element.63), channel_id=1, source_target_pairs={{0,3},{1,2},{2,1},{3,0},{4,7},{5,6},{6,5},{7,4},{8,11},{9,10},{10,... | collective-permute-start | bytes 2752520 | tf_op jit(solution)/shard_map/ppermute | solution.py:36
  40.6 38.7 %collective-permute-start.14 = (bf16[256,1792]{1,0:T(8,128)(2,1)}, bf16[256,1792]{1,0:T(8,128)(2,1)S(1)}, u32[]{:S(2)}, u32[]{:S(2)}) collective-permute-start(bf16[256,1792]{1,0:T(8,128)(2,1)} %get-tuple-element.62), channel_id=1, source_target_pairs={{0,2},{1,3},{2,0},{3,1},{4,6},{5,7},{6,4},{7,5},{8,10},{9,11},{10,... | collective-permute-start | bytes 2752520 | tf_op jit(solution)/shard_map/ppermute | solution.py:36
  41.8 10.7 %collective-permute-start.7 = (bf16[1,24,128]{2,1,0:T(8,128)(2,1)S(1)}, bf16[1,24,128]{2,1,0:T(8,128)(2,1)S(1)}, u32[]{:S(2)}, u32[]{:S(2)}) collective-permute-start(bf16[1,24,128]{2,1,0:T(8,128)(2,1)S(1)} %bitcast.95), channel_id=1, source_target_pairs={{0,8},{4,28},{8,0},{12,20},{16,24},{20,12},{24,16},{28,4},{32,40},... | collective-permute-start | bytes 18440 | tf_op jit(solution)/shard_map/ppermute | solution.py:31
  51.0 17.9 %collective-permute-start.6 = (bf16[48,384]{1,0:T(8,128)(2,1)S(1)}, bf16[48,384]{1,0:T(8,128)(2,1)S(1)}, u32[]{:S(2)}, u32[]{:S(2)}) collective-permute-start(bf16[48,384]{1,0:T(8,128)(2,1)S(1)} %pad_maximum_fusion.5), channel_id=1, source_target_pairs={{0,4},{4,0},{8,12},{12,8},{16,20},{20,16},{24,28},{28,24},{32,36},... | collective-permute-start | bytes 110600 | tf_op jit(solution)/shard_map/ppermute | solution.py:31
  94.9 6.5 %collective-permute-start.15 = (bf16[384,256]{1,0:T(8,128)(2,1)}, bf16[384,256]{1,0:T(8,128)(2,1)S(1)}, u32[]{:S(2)}, u32[]{:S(2)}) collective-permute-start(bf16[384,256]{1,0:T(8,128)(2,1)} %shard_map.73), channel_id=1, source_target_pairs={{0,1},{1,0},{2,3},{3,2},{4,5},{5,4},{6,7},{7,6},{8,9},{9,8},{10,11... | collective-permute-start | bytes 589832 | tf_op jit(solution)/shard_map/ppermute | solution.py:36
  96.2 10.0 %collective-permute-start.16 = (bf16[384,256]{1,0:T(8,128)(2,1)}, bf16[384,256]{1,0:T(8,128)(2,1)S(1)}, u32[]{:S(2)}, u32[]{:S(2)}) collective-permute-start(bf16[384,256]{1,0:T(8,128)(2,1)} %shard_map.73), channel_id=1, source_target_pairs={{0,3},{1,2},{2,1},{3,0},{4,7},{5,6},{6,5},{7,4},{8,11},{9,10},{10,... | collective-permute-start | bytes 589832 | tf_op jit(solution)/shard_map/ppermute | solution.py:36
  98.1 10.0 %collective-permute-start.17 = (bf16[384,256]{1,0:T(8,128)(2,1)}, bf16[384,256]{1,0:T(8,128)(2,1)S(1)}, u32[]{:S(2)}, u32[]{:S(2)}) collective-permute-start(bf16[384,256]{1,0:T(8,128)(2,1)} %shard_map.73), channel_id=1, source_target_pairs={{0,2},{1,3},{2,0},{3,1},{4,6},{5,7},{6,4},{7,5},{8,10},{9,11},{10,... | collective-permute-start | bytes 589832 | tf_op jit(solution)/shard_map/ppermute | solution.py:36
  147.2 8.7 %collective-permute-start.22 = (f32[24,32]{1,0:T(8,128)S(1)}, f32[24,32]{1,0:T(8,128)S(1)}, u32[]{:S(2)}, u32[]{:S(2)}) collective-permute-start(f32[24,32]{1,0:T(8,128)S(1)} %fusion.5), channel_id=1, source_target_pairs={{0,1},{1,0},{2,3},{3,2},{4,5},{5,4},{6,7},{7,6},{8,9},{9,8},{10,11... | collective-permute-start | bytes 9224 | tf_op jit(solution)/shard_map/ppermute | solution.py:36
  148.1 9.2 %collective-permute-start.23 = (f32[24,32]{1,0:T(8,128)S(1)}, f32[24,32]{1,0:T(8,128)S(1)}, u32[]{:S(2)}, u32[]{:S(2)}) collective-permute-start(f32[24,32]{1,0:T(8,128)S(1)} %fusion.5), channel_id=1, source_target_pairs={{0,3},{1,2},{2,1},{3,0},{4,7},{5,6},{6,5},{7,4},{8,11},{9,10},{10,... | collective-permute-start | bytes 9224 | tf_op jit(solution)/shard_map/ppermute | solution.py:36
  149.2 8.1 %collective-permute-start.24 = (f32[24,32]{1,0:T(8,128)S(1)}, f32[24,32]{1,0:T(8,128)S(1)}, u32[]{:S(2)}, u32[]{:S(2)}) collective-permute-start(f32[24,32]{1,0:T(8,128)S(1)} %fusion.5), channel_id=1, source_target_pairs={{0,2},{1,3},{2,0},{3,1},{4,6},{5,7},{6,4},{7,5},{8,10},{9,11},{10,... | collective-permute-start | bytes 9224 | tf_op jit(solution)/shard_map/ppermute | solution.py:36
  154.0 19.4 %collective-permute-start.26 = (bf16[256,1792]{1,0:T(8,128)(2,1)}, bf16[256,1792]{1,0:T(8,128)(2,1)S(1)}, u32[]{:S(2)}, u32[]{:S(2)}) collective-permute-start(bf16[256,1792]{1,0:T(8,128)(2,1)} %get-tuple-element.61), channel_id=1, source_target_pairs={{0,1},{1,0},{2,3},{3,2},{4,5},{5,4},{6,7},{7,6},{8,9},{9,8},{10,11... | collective-permute-start | bytes 2752520 | tf_op jit(solution)/shard_map/ppermute | solution.py:36
  154.8 20.9 %collective-permute-start.27 = (bf16[256,1792]{1,0:T(8,128)(2,1)}, bf16[256,1792]{1,0:T(8,128)(2,1)S(1)}, u32[]{:S(2)}, u32[]{:S(2)}) collective-permute-start(bf16[256,1792]{1,0:T(8,128)(2,1)} %get-tuple-element.60), channel_id=1, source_target_pairs={{0,3},{1,2},{2,1},{3,0},{4,7},{5,6},{6,5},{7,4},{8,11},{9,10},{10,... | collective-permute-start | bytes 2752520 | tf_op jit(solution)/shard_map/ppermute | solution.py:36
  155.9 37.8 %collective-permute-start.28 = (bf16[256,1792]{1,0:T(8,128)(2,1)}, bf16[256,1792]{1,0:T(8,128)(2,1)S(1)}, u32[]{:S(2)}, u32[]{:S(2)}) collective-permute-start(bf16[256,1792]{1,0:T(8,128)(2,1)} %get-tuple-element.59), channel_id=1, source_target_pairs={{0,2},{1,3},{2,0},{3,1},{4,6},{5,7},{6,4},{7,5},{8,10},{9,11},{10,... | collective-permute-start | bytes 2752520 | tf_op jit(solution)/shard_map/ppermute | solution.py:36
  215.3 6.5 %collective-permute-start.29 = (bf16[384,256]{1,0:T(8,128)(2,1)}, bf16[384,256]{1,0:T(8,128)(2,1)S(1)}, u32[]{:S(2)}, u32[]{:S(2)}) collective-permute-start(bf16[384,256]{1,0:T(8,128)(2,1)} %shard_map.75), channel_id=1, source_target_pairs={{0,1},{1,0},{2,3},{3,2},{4,5},{5,4},{6,7},{7,6},{8,9},{9,8},{10,11... | collective-permute-start | bytes 589832 | tf_op jit(solution)/shard_map/ppermute | solution.py:36
  216.6 10.0 %collective-permute-start.30 = (bf16[384,256]{1,0:T(8,128)(2,1)}, bf16[384,256]{1,0:T(8,128)(2,1)S(1)}, u32[]{:S(2)}, u32[]{:S(2)}) collective-permute-start(bf16[384,256]{1,0:T(8,128)(2,1)} %shard_map.75), channel_id=1, source_target_pairs={{0,3},{1,2},{2,1},{3,0},{4,7},{5,6},{6,5},{7,4},{8,11},{9,10},{10,... | collective-permute-start | bytes 589832 | tf_op jit(solution)/shard_map/ppermute | solution.py:36
  218.5 9.9 %collective-permute-start.31 = (bf16[384,256]{1,0:T(8,128)(2,1)}, bf16[384,256]{1,0:T(8,128)(2,1)S(1)}, u32[]{:S(2)}, u32[]{:S(2)}) collective-permute-start(bf16[384,256]{1,0:T(8,128)(2,1)} %shard_map.75), channel_id=1, source_target_pairs={{0,2},{1,3},{2,0},{3,1},{4,6},{5,7},{6,4},{7,5},{8,10},{9,11},{10,... | collective-permute-start | bytes 589832 | tf_op jit(solution)/shard_map/ppermute | solution.py:36
  (26 other events, 202.9 us)
Sparse Core Ops, SparseCore 0:
  22.1 62.1 all-gather.2
  147.0 57.6 all-gather.4

commit v10 on v8

--- a/solution.py
+++ b/solution.py
@@ -40,12 +40,60 @@
     return lax.optimization_barrier((block, *others))[0]
 
 
+def first_kernel(layer, mask, z_ref, own_ref, other_ref, gate_ref, up_ref, out_ref, weights, sems):
+    depth, units = weights.shape[1:]
+    features = pl.ds(pl.multiple_of((z_ref[0] ^ mask) * depth, depth), depth)
+    copies = [
+        pltpu.make_async_copy(source.at[layer, 0, features], weights.at[n], sems.at[n])
+        for n, source in enumerate((gate_ref, up_ref))
+    ]
+    for copy in copies:
+        copy.start()
+    tokens = jnp.concatenate([own_ref[:, :depth], other_ref[:, :depth]], axis=0)
+    for n in range(2):
+        copies[n].wait()
+        product = jnp.dot(tokens, weights[n], preferred_element_type=f32)
+        out_ref[:, n * units : (n + 1) * units] = product
+
+
+def first_products(z, own, other, w_gate, w_up, layer, mask):
+    rows, units = 2 * own.shape[0], w_gate.shape[-1]
+    depth = w_gate.shape[2] // len(ORDER)
+    outside, inside = pl.BlockSpec(memory_space=pl.ANY), pl.BlockSpec(memory_space=pltpu.VMEM)
+    return pl.pallas_call(
+        functools.partial(first_kernel, layer, mask),
+        in_specs=[pl.BlockSpec(memory_space=pltpu.SMEM), inside, inside, outside, outside],
+        out_specs=inside,
+        out_shape=jax.ShapeDtypeStruct((rows, 2 * units), f32),
+        scratch_shapes=[pltpu.VMEM((2, depth, units), bf16), pltpu.SemaphoreType.DMA((2,))],
+        compiler_params=pltpu.CompilerParams(vmem_limit_bytes=48 << 20),
+        cost_estimate=pl.CostEstimate(
+            flops=4 * rows * depth * units,
+            bytes_accessed=2 * depth * (rows + 2 * units) + 8 * rows * units,
+            transcendentals=0,
+        ),
+    )(jnp.full((1,), z, jnp.int32), own, other, w_gate, w_up)
+
+
 def gate_up_kernel(
-    layer, z_ref, tokens_ref, taken_ref, gate_ref, up_ref, act_ref, tokens, weights, sums, sems
+    layer,
+    rows,
+    z_ref,
+    places_ref,
+    tokens_ref,
+    taken_ref,
+    first_ref,
+    gate_ref,
+    up_ref,
+    act_ref,
+    tokens,
+    weights,
+    sums,
+    sems,
 ):
-    steps, depth = weights.shape[1:3]
+    steps, depth, units = weights.shape[1:]
     copies = []
-    for step, mask in enumerate(ORDER):
+    for step, mask in enumerate(ORDER[:steps]):
         features = pl.ds(pl.multiple_of((z_ref[0] ^ mask) * depth, depth), depth)
         parts = [
             (tokens_ref.at[:, pl.ds(step * depth, depth)], tokens.at[step]),
@@ -57,47 +105,49 @@
         )
     for copy in sum(copies, []):
         copy.start()
+    for block in range(sums.shape[0] // rows):
+        place = pl.multiple_of(places_ref[block] * rows, rows)
+        sums[block * rows : (block + 1) * rows] = first_ref[pl.ds(place, rows)]
     for step in range(steps):
         for copy in copies[step]:
             copy.wait()
         gate = jnp.dot(tokens[step], weights[0, step], preferred_element_type=f32)
         up = jnp.dot(tokens[step], weights[1, step], preferred_element_type=f32)
-        if step == 0:
-            sums[0], sums[1] = gate, up
-        elif step < steps - 1:
-            sums[0] += gate
-            sums[1] += up
+        if step < steps - 1:
+            sums[:, :units] += gate
+            sums[:, units:] += up
         else:
-            gate += sums[0]
-            up += sums[1]
+            gate += sums[:, :units]
+            up += sums[:, units:]
             act = (gate / (1.0 + jnp.exp(-gate)) * up).astype(bf16)
             slots = jnp.dot(taken_ref[...], act, preferred_element_type=f32)
             act_ref[...] = slots.astype(act_ref.dtype)
 
 
-def gate_up(z, tokens, taken, w_gate, w_up, layer):
+def gate_up(z, places, tokens, taken, first, w_gate, w_up, layer, block):
     rows, units = tokens.shape[0], w_gate.shape[-1]
-    steps = len(ORDER)
-    depth = w_gate.shape[2] // steps
+    steps = len(ORDER) - 1
+    depth = w_gate.shape[2] // len(ORDER)
     outside, inside = pl.BlockSpec(memory_space=pl.ANY), pl.BlockSpec(memory_space=pltpu.VMEM)
+    scalars = pl.BlockSpec(memory_space=pltpu.SMEM)
     return pl.pallas_call(
-        functools.partial(gate_up_kernel, layer),
-        in_specs=[pl.BlockSpec(memory_space=pltpu.SMEM), outside, inside, outside, outside],
+        functools.partial(gate_up_kernel, layer, block),
+        in_specs=[scalars, scalars, outside, inside, inside, outside, outside],
         out_specs=inside,
         out_shape=jax.ShapeDtypeStruct((taken.shape[0], units), bf16),
         scratch_shapes=[
             pltpu.VMEM((steps, rows, depth), bf16),
             pltpu.VMEM((2, steps, depth, units), bf16),
-            pltpu.VMEM((2, rows, units), f32),
+            pltpu.VMEM((rows, 2 * units), f32),
             pltpu.SemaphoreType.DMA((3, steps)),
         ],
-        compiler_params=pltpu.CompilerParams(vmem_limit_bytes=56 << 20),
+        compiler_params=pltpu.CompilerParams(vmem_limit_bytes=52 << 20),
         cost_estimate=pl.CostEstimate(
-            flops=16 * rows * depth * units,
-            bytes_accessed=8 * (rows + 2 * units) * depth + 2 * rows * units,
+            flops=4 * steps * rows * depth * units,
+            bytes_accessed=2 * steps * (rows + 2 * units) * depth + 8 * rows * units,
             transcendentals=rows * units,
         ),
-    )(jnp.full((1,), z, jnp.int32), tokens, taken, w_gate, w_up)
+    )(jnp.full((1,), z, jnp.int32), places, tokens, taken, first, w_gate, w_up)
 
 
 def down_kernel(layer, z_ref, a0, a1, a2, a3, down_ref, w1, w2, w3, out_ref, own, act, sems):
@@ -180,10 +230,10 @@
     def spread(block):
         return [block] + [z_swap(block, mask) for mask in ORDER[1:]]
 
-    def columns(layer, mask, first, count, *bound):
+    def columns(layer, mask, *bound):
         column = (after(z, *bound) ^ mask) * part
-        block = lax.dynamic_slice(w_down, (layer, 0, first, column), (1, 1, count, part))
-        return z_swap(block.reshape(count, part), mask)
+        block = lax.dynamic_slice(w_down, (layer, 0, 0, column), (1, 1, units, part))
+        return block.reshape(units, part)
 
     def slots_of(marks_here, layer):
         mine = lax.broadcasted_iota(jnp.int32, (1, 1, 128), 2) == me + layer * experts
@@ -211,14 +261,13 @@
             for block, gain in zip(blocks, gains)
         ]
 
-        sent = jnp.concatenate(normed, axis=1)
+        sent = jnp.concatenate(normed[:3], axis=1)
         arrived = lax.all_gather(sent, "expert", axis=0, tiled=True)
 
         own = state.astype(f32) * scale[:, None] * norm_gain[layer][None, :]
         own = own.astype(bf16).astype(f32)
         scores = jnp.dot(own, router[layer], precision=lax.Precision.HIGHEST)
         scores = after(scores, sent)
-        others = [columns(layer, mask, 0, units, scores) for mask in ORDER[1:]]
         probs = jax.nn.sigmoid(sum(spread(scores)))
         picked = jnp.where(picks[layer], probs, 0.0)
         weights = route_scale * picked / jnp.sum(picked, axis=1, keepdims=True)
@@ -236,18 +285,28 @@
 
         mixers = jnp.concatenate([mixer(core), swap(mixer(1 - core), SIBLING)], axis=0)
 
+        held = after(normed[3], sent)
+        held = (jnp.concatenate([held, marks_sent], axis=1) if layer == 0 else held)[None]
+        blocks = [columns(layer, mask, held) for mask in ORDER[1:]]
+        near = [z_swap(block, mask) for block, mask in zip(blocks[:2], ORDER[1:3])]
+        for step, masks in enumerate(Y_STEPS + X_STEPS):
+            if step == 3:
+                held, far, near = lax.optimization_barrier((held, blocks[2], near))
+                far = z_swap(far, ORDER[3])
+            held = jnp.concatenate([held, swap(held, masks)])
+        held, far = lax.optimization_barrier((held, far))
+        others = near + [far]
+        swapped = swap(held, SIBLING)
         if layer == 0:
-            held = after(marks_sent, scores)[None]
-            for masks in Y_STEPS + X_STEPS:
-                held = jnp.concatenate([held, swap(held, masks)])
-            held = jnp.concatenate([held, swap(held, SIBLING)]).astype(f32)
-            taken = [slots_of(held, each) for each in range(layers)]
-            arrived, mixers, taken, others = lax.optimization_barrier(
-                (arrived, mixers, taken, others)
-            )
-        else:
-            arrived, mixers, others = lax.optimization_barrier((arrived, mixers, others))
-        acts = spread(gate_up(z, arrived, taken[layer], w_gate, w_up, layer))
+            marks_all = jnp.concatenate([held[:, :, part:], swapped[:, :, part:]]).astype(f32)
+            taken = [slots_of(marks_all, each) for each in range(layers)]
+        flat = [block.reshape(chips * rows, -1) for block in (held, swapped)]
+        first = first_products(z, *flat, w_gate, w_up, layer, ORDER[3])
+        arrived, mixers, first, taken, others = lax.optimization_barrier(
+            (arrived, mixers, first, taken, others)
+        )
+        act = gate_up(z, places, arrived, taken[layer], first, w_gate, w_up, layer, rows)
+        acts = spread(act)
         acts[0] = jnp.where(z < quarters, acts[0], 0.0)
         out = down_product(z, acts, w_down, layer, others)
         groups = [list(range(parity, experts, 2)) for parity in range(2)]

time: 267 us -> 313 us (1.17)
  waiting for transfers between devices: 80.2 us -> 102 us
  local copies, waits for them, and re-layouts: 27.2 us -> 39.1 us
  starting transfers between devices: 52.5 us -> 61 us
  Pallas kernels: 27.2 us -> 32.6 us
    ppermute x9 -> x14, waiting for transfers between devices: 10.9 us -> 62.3 us  [swap(): lax.ppermute(block, 'expert', [(i, i ^ masks[i & 1]) for i in range(count)])]
    all_gather x2, waiting for transfers between devices: 16.1 us -> 0.02 us  [body(): arrived = lax.all_gather(sent, 'expert', axis=0, tiled=True)]
    ppermute x24, waiting for transfers between devices: 53.2 us -> 39.3 us  [z_swap(): return lax.ppermute(block, 'tensor', [(i, i ^ mask) for i in range(count)])]
    ppermute x9 -> x14, starting transfers between devices: 21 us -> 33.6 us  [swap(): lax.ppermute(block, 'expert', [(i, i ^ masks[i & 1]) for i in range(count)])]
    unnamed x35 -> x53, local copies, waits for them, and re-layouts: 2.54 us -> 8.24 us
    pallas_call x2 -> x4, Pallas kernels: 21.2 us -> 26.6 us  [the longest x2 17.9 us: gate_up(): pl.pallas_call(functools.partial(gate_up_kernel, layer, block), in_specs=...]
    eq x10, local copies, waits for them, and re-layouts: 4.64 us -> 8.96 us  [mixer(): of_parity(marks[layer]) == slot]
    ppermute x24, starting transfers between devices: 31.4 us -> 27.4 us  [z_swap(): return lax.ppermute(block, 'tensor', [(i, i ^ mask) for i in range(count)])]
  transfers between devices with their start and end apart: 35 -> 40, of which waited for: 24 -> 26; matrix products, arithmetic and copies ran while one was open for 15% -> 14% of each run, Pallas kernels for 0% -> 3%
where the time goes in v10:
time: 313 us; the launch traced here: 312 us
  waiting for transfers between devices  102 us (33%)
  starting transfers between devices  61 us (19%)
  blocking collectives  45.1 us (14%)
  local copies, waits for them, and re-layouts  39.1 us (12%)
  Pallas kernels  32.6 us (10%)
  other arithmetic  14.9 us (5%)
  between operations  14.1 us (5%)
  matrix products  4.01 us (1%)
    ppermute x14, waiting for transfers between devices, swap(): lax.ppermute(block, 'expert', [(i, i ^ masks[i & 1]) for i in range(count)])  62.3 us
    all_to_all x2, blocking collectives, body(): lax.all_to_all(out.reshape(chips, 2 * capacity, part), 'expert', split_ax...  45.1 us
    ppermute x24, waiting for transfers between devices, z_swap(): return lax.ppermute(block, 'tensor', [(i, i ^ mask) for i in range(count)])  39.3 us
    ppermute x14, starting transfers between devices, swap(): lax.ppermute(block, 'expert', [(i, i ^ masks[i & 1]) for i in range(count)])  33.6 us
    ppermute x24, starting transfers between devices, z_swap(): return lax.ppermute(block, 'tensor', [(i, i ^ mask) for i in range(count)])  27.4 us
    pallas_call x2, Pallas kernels, gate_up(): pl.pallas_call(functools.partial(gate_up_kernel, layer, block), in_specs=...  17.9 us
    eq x10, local copies, waits for them, and re-layouts, mixer(): of_parity(marks[layer]) == slot  8.96 us
    pallas_call x2, Pallas kernels, first_products(): pl.pallas_call(functools.partial(first_kernel, layer, mask), in_specs=[pl...  8.67 us
  transfers between devices with their start and end apart: 40, of which 26 were waited for; matrix products, arithmetic and copies ran while one was open for 14% of the time, Pallas kernels for 3%

profile of v10, /device:TPU:1, one launch (start us, length us, event | category | flops | bytes accessed | tf_op | source)
XLA Modules:
  0.0 312.3 jit_solution(1174452865826295369)
XLA Ops:
  16.0 3.3 %collective-permute-done.2 = bf16[32,1792]{1,0:T(8,128)(2,1)S(1)} collective-permute-done((bf16[32,1792]{1,0:T(8,128)(2,1)S(1)}, bf16[32,1792]{1,0:T(8,128)(2,1)S(1)}, u32[]{:S(2)}, u32[]{:S(2)}) %collective-permute-start.2) | collective-permute-done | bytes 114720 | tf_op jit(solution)/shard_map/ppermute | solution.py:36
  28.1 2.9 dynamic-slice_bitcast_fusion.3
  35.1 7.9 %collective-permute-done.9 = bf16[4,24,1920]{2,1,0:T(8,128)(2,1)S(1)} collective-permute-done((bf16[4,24,1920]{2,1,0:T(8,128)(2,1)S(1)}, bf16[4,24,1920]{2,1,0:T(8,128)(2,1)S(1)}, u32[]{:S(2)}, u32[]{:S(2)}) %collective-permute-start.9) | collective-permute-done | bytes 368672 | tf_op jit(solution)/shard_map/ppermute | solution.py:31
  43.1 5.2 %collective-permute-done.10.w1 = bf16[256,1792]{1,0:T(8,128)(2,1)S(1)} collective-permute-done((bf16[256,1792]{1,0:T(8,128)(2,1)S(1)}, bf16[256,1792]{1,0:T(8,128)(2,1)S(1)}, u32[]{:S(2)}, u32[]{:S(2)}) %collective-permute-start.10) | collective-permute-done | bytes 917536 | tf_op jit(solution)/shard_map/ppermute | solution.py:36
  54.1 15.4 %collective-permute-done.12 = bf16[8,24,1920]{2,1,0:T(8,128)(2,1)} collective-permute-done((bf16[8,24,1920]{2,1,0:T(8,128)(2,1)S(1)}, bf16[8,24,1920]{2,1,0:T(8,128)(2,1)}, u32[]{:S(2)}, u32[]{:S(2)}) %collective-permute-start.12) | collective-permute-done | bytes 737312 | tf_op jit(solution)/shard_map/ppermute | solution.py:31
  71.8 13.5 %collective-permute-start.14 = (bf16[16,24,1920]{2,1,0:T(8,128)(2,1)S(1)}, bf16[16,24,1920]{2,1,0:T(8,128)(2,1)S(1)}, u32[]{:S(2)}, u32[]{:S(2)}) collective-permute-start(bf16[16,24,1920]{2,1,0:T(8,128)(2,1)S(1)} %pad_maximum_fusion), channel_id=1, source_target_pairs={{0,4},{4,0},{8,12},{12,8},{16,20},{20,16},{24,28},{28,24},{32,36},... | collective-permute-start | bytes 4423688 | tf_op jit(solution)/shard_map/ppermute | solution.py:31
  105.6 4.3 %shard_map.73.first_ref = f32[768,512]{1,0:T(8,128)S(1)} custom-call(s32[1]{0:T(128)} %bitcast.13.z_ref, bf16[384,1920]{1,0:T(8,128)(2,1)S(1)} %bitcast.99, bf16[384,1920]{1,0:T(8,128)(2,1)S(1)} %bitcast.103, bf16[2,1,7168,256]{3,2,1,0:T(8,128)(2,1)} %gate_ref.7, bf16[2,1,7168,256]{3,2,1,0:T(8,128)(2,1)} %up_ref.7), custom_call_target="tpu_custom_call" | custom-call | flops 1409286144 | bytes 6160384 | tf_op jit(solution)/shard_map/pallas_call | solution.py:63
  111.5 8.9 %shard_map.74 = bf16[384,256]{1,0:T(8,128)(2,1)S(1)} custom-call(s32[1]{0:T(128)} %bitcast.13.z_ref, s32[32]{0:T(128)S(1)} %get-tuple-element.137.places_ref, bf16[768,5376]{1,0:T(8,128)(2,1)} %all-gather.3.cloned.1.call-done.tokens_ref, bf16[384,768]{1,0:T(8,128)(2,1)S(1)} %fusion.taken_ref, f32[768,512]{1,0:T(8,128)} %copy-done, ...), custom_call_target="tpu_custom_call" | custom-call | flops 4227858432 | bytes 15335424 | tf_op jit(solution)/shard_map/pallas_call | solution.py:133
  123.8 2.9 collective-permute-done.15.a1
  128.3 4.2 %collective-permute-done.17.a3 = bf16[384,256]{1,0:T(8,128)(2,1)S(1)} collective-permute-done((bf16[384,256]{1,0:T(8,128)(2,1)S(1)}, bf16[384,256]{1,0:T(8,128)(2,1)S(1)}, u32[]{:S(2)}, u32[]{:S(2)}) %collective-permute-start.17) | collective-permute-done | bytes 196640 | tf_op jit(solution)/shard_map/ppermute | solution.py:36
  132.5 3.0 shard_map.75
  135.6 22.0 %all_to_all.10 = bf16[16,24,1792]{2,1,0:T(8,128)(2,1)S(1)} all-to-all(bf16[16,24,1792]{2,1,0:T(8,128)(2,1)S(1)} %bitcast.101), channel_id=1, replica_groups={{0,8,16,24,32,40,48,56,64,72,80,88,96,104,112,120},{4,12,20,28,36,44,52..., dimensions={0} | all-to-all | bytes 2752512 | tf_op jit(solution)/shard_map/all_to_all | solution.py:313
  158.0 3.7 %collective-permute-start.18 = (f32[24,1792]{1,0:T(8,128)S(1)}, f32[24,1792]{1,0:T(8,128)S(1)}, u32[]{:S(2)}, u32[]{:S(2)}) collective-permute-start(f32[24,1792]{1,0:T(8,128)S(1)} %slice_bitcast_fusion.2), channel_id=1, source_target_pairs={{0,4},{4,0},{8,12},{12,8},{16,20},{20,16},{24,28},{28,24},{32,36},... | collective-permute-start | bytes 516104 | tf_op jit(solution)/shard_map/ppermute | solution.py:31
  171.8 3.8 %collective-permute-done.26 = bf16[1,24,1792]{2,1,0:T(8,128)(2,1)S(1)} collective-permute-done((bf16[1,24,1792]{2,1,0:T(8,128)(2,1)S(1)}, bf16[1,24,1792]{2,1,0:T(8,128)(2,1)S(1)}, u32[]{:S(2)}, u32[]{:S(2)}) %collective-permute-start.26) | collective-permute-done | bytes 86048 | tf_op jit(solution)/shard_map/ppermute | solution.py:31
  175.7 2.9 dynamic-slice_bitcast_fusion
  181.2 9.0 %collective-permute-done.28 = bf16[4,24,1792]{2,1,0:T(8,128)(2,1)S(1)} collective-permute-done((bf16[4,24,1792]{2,1,0:T(8,128)(2,1)S(1)}, bf16[4,24,1792]{2,1,0:T(8,128)(2,1)S(1)}, u32[]{:S(2)}, u32[]{:S(2)}) %collective-permute-start.28) | collective-permute-done | bytes 344096 | tf_op jit(solution)/shard_map/ppermute | solution.py:31
  190.3 7.1 %collective-permute-done.29.w1 = bf16[256,1792]{1,0:T(8,128)(2,1)S(1)} collective-permute-done((bf16[256,1792]{1,0:T(8,128)(2,1)S(1)}, bf16[256,1792]{1,0:T(8,128)(2,1)S(1)}, u32[]{:S(2)}, u32[]{:S(2)}) %collective-permute-start.29) | collective-permute-done | bytes 917536 | tf_op jit(solution)/shard_map/ppermute | solution.py:36
  205.6 19.2 %collective-permute-done.31 = bf16[8,24,1792]{2,1,0:T(8,128)(2,1)} collective-permute-done((bf16[8,24,1792]{2,1,0:T(8,128)(2,1)S(1)}, bf16[8,24,1792]{2,1,0:T(8,128)(2,1)}, u32[]{:S(2)}, u32[]{:S(2)}) %collective-permute-start.31) | collective-permute-done | bytes 688160 | tf_op jit(solution)/shard_map/ppermute | solution.py:31
  227.2 3.5 %collective-permute-start.33 = (bf16[16,24,1792]{2,1,0:T(8,128)(2,1)S(1)}, bf16[16,24,1792]{2,1,0:T(8,128)(2,1)S(1)}, u32[]{:S(2)}, u32[]{:S(2)}) collective-permute-start(bf16[16,24,1792]{2,1,0:T(8,128)(2,1)S(1)} %pad_maximum_fusion.1), channel_id=1, source_target_pairs={{0,4},{4,0},{8,12},{12,8},{16,20},{20,16},{24,28},{28,24},{32,36},... | collective-permute-start | bytes 4128776 | tf_op jit(solution)/shard_map/ppermute | solution.py:31
  247.3 4.3 %shard_map.76.first_ref = f32[768,512]{1,0:T(8,128)S(1)} custom-call(s32[1]{0:T(128)} %bitcast.13.z_ref, bf16[384,1792]{1,0:T(8,128)(2,1)S(1)} %bitcast.102, bf16[384,1792]{1,0:T(8,128)(2,1)S(1)} %bitcast.104, bf16[2,1,7168,256]{3,2,1,0:T(8,128)(2,1)} %gate_ref.7, bf16[2,1,7168,256]{3,2,1,0:T(8,128)(2,1)} %up_ref.7), custom_call_target="tpu_custom_call" | custom-call | flops 1409286144 | bytes 6160384 | tf_op jit(solution)/shard_map/pallas_call | solution.py:63
  252.9 9.0 %shard_map.77 = bf16[384,256]{1,0:T(8,128)(2,1)S(1)} custom-call(s32[1]{0:T(128)} %bitcast.13.z_ref, s32[32]{0:T(128)S(1)} %get-tuple-element.137.places_ref, bf16[768,5376]{1,0:T(8,128)(2,1)} %all-gather.5.cloned.1.call-done.tokens_ref, bf16[384,768]{1,0:T(8,128)(2,1)S(1)} %fusion.1.taken_ref, f32[768,512]{1,0:T(8,128)} %copy-done.1, ...), custom_call_target="tpu_custom_call" | custom-call | flops 4227858432 | bytes 15335424 | tf_op jit(solution)/shard_map/pallas_call | solution.py:133
  268.3 4.7 %collective-permute-done.35.a2 = bf16[384,256]{1,0:T(8,128)(2,1)S(1)} collective-permute-done((bf16[384,256]{1,0:T(8,128)(2,1)S(1)}, bf16[384,256]{1,0:T(8,128)(2,1)S(1)}, u32[]{:S(2)}, u32[]{:S(2)}) %collective-permute-start.35) | collective-permute-done | bytes 196640 | tf_op jit(solution)/shard_map/ppermute | solution.py:36
  274.9 3.0 shard_map.78
  277.9 23.1 %all_to_all.11 = bf16[16,24,1792]{2,1,0:T(8,128)(2,1)S(1)} all-to-all(bf16[16,24,1792]{2,1,0:T(8,128)(2,1)S(1)} %bitcast.100), channel_id=1, replica_groups={{0,8,16,24,32,40,48,56,64,72,80,88,96,104,112,120},{4,12,20,28,36,44,52..., dimensions={0} | all-to-all | bytes 2752512 | tf_op jit(solution)/shard_map/all_to_all | solution.py:313
  (240 shorter events, 111.2 us)
Async XLA Ops:
  6.5 104.9 %all-gather.3.cloned.1.call-start = ((), (), s32[]{:S(2)}) async-start(), calls=%async_computation.2 | async-start | bytes 8515584 | tf_op jit(solution)/shard_map/all_gather | solution.py:265
  8.5 10.9 %collective-permute-start = (bf16[32,1792]{1,0:T(8,128)(2,1)S(1)}, bf16[32,1792]{1,0:T(8,128)(2,1)S(1)}, u32[]{:S(2)}, u32[]{:S(2)}) collective-permute-start(bf16[32,1792]{1,0:T(8,128)(2,1)S(1)} %maximum_maximum_fusion), channel_id=1, source_target_pairs={{0,1},{1,0},{2,3},{3,2},{4,5},{5,4},{6,7},{7,6},{8,9},{9,8},{10,11... | collective-permute-start | bytes 344072 | tf_op jit(solution)/shard_map/ppermute | solution.py:36
  11.0 9.6 %collective-permute-start.1 = (bf16[32,1792]{1,0:T(8,128)(2,1)S(1)}, bf16[32,1792]{1,0:T(8,128)(2,1)S(1)}, u32[]{:S(2)}, u32[]{:S(2)}) collective-permute-start(bf16[32,1792]{1,0:T(8,128)(2,1)S(1)} %maximum_maximum_fusion), channel_id=1, source_target_pairs={{0,3},{1,2},{2,1},{3,0},{4,7},{5,6},{6,5},{7,4},{8,11},{9,10},{10,... | collective-permute-start | bytes 344072 | tf_op jit(solution)/shard_map/ppermute | solution.py:36
  22.7 230.2 %all-gather.5.cloned.1.call-start = ((), (), s32[]{:S(2)}) async-start(), calls=%async_computation.3 | async-start | bytes 8515584 | tf_op jit(solution)/shard_map/all_gather | solution.py:265
  31.0 17.3 %collective-permute-start.10 = (bf16[256,1792]{1,0:T(8,128)(2,1)S(1)}, bf16[256,1792]{1,0:T(8,128)(2,1)S(1)}, u32[]{:S(2)}, u32[]{:S(2)}) collective-permute-start(bf16[256,1792]{1,0:T(8,128)(2,1)S(1)} %get-tuple-element.95), channel_id=1, source_target_pairs={{0,1},{1,0},{2,3},{3,2},{4,5},{5,4},{6,7},{7,6},{8,9},{9,8},{10,11... | collective-permute-start | bytes 2752520 | tf_op jit(solution)/shard_map/ppermute | solution.py:36
  31.0 18.2 %collective-permute-start.11 = (bf16[256,1792]{1,0:T(8,128)(2,1)S(1)}, bf16[256,1792]{1,0:T(8,128)(2,1)S(1)}, u32[]{:S(2)}, u32[]{:S(2)}) collective-permute-start(bf16[256,1792]{1,0:T(8,128)(2,1)S(1)} %get-tuple-element.94), channel_id=1, source_target_pairs={{0,3},{1,2},{2,1},{3,0},{4,7},{5,6},{6,5},{7,4},{8,11},{9,10},{10,... | collective-permute-start | bytes 2752520 | tf_op jit(solution)/shard_map/ppermute | solution.py:36
  32.5 10.5 %collective-permute-start.9 = (bf16[4,24,1920]{2,1,0:T(8,128)(2,1)S(1)}, bf16[4,24,1920]{2,1,0:T(8,128)(2,1)S(1)}, u32[]{:S(2)}, u32[]{:S(2)}) collective-permute-start(bf16[4,24,1920]{2,1,0:T(8,128)(2,1)S(1)} %pad_maximum_fusion.4), channel_id=1, source_target_pairs={{0,32},{4,100},{8,40},{12,108},{16,48},{20,116},{24,56},{28,124},{... | collective-permute-start | bytes 1105928 | tf_op jit(solution)/shard_map/ppermute | solution.py:31
  50.1 19.4 %collective-permute-start.12 = (bf16[8,24,1920]{2,1,0:T(8,128)(2,1)S(1)}, bf16[8,24,1920]{2,1,0:T(8,128)(2,1)}, u32[]{:S(2)}, u32[]{:S(2)}) collective-permute-start(bf16[8,24,1920]{2,1,0:T(8,128)(2,1)S(1)} %pad_maximum_fusion.2), channel_id=1, source_target_pairs={{0,96},{4,36},{8,104},{12,44},{16,112},{20,52},{24,120},{28,60},{3... | collective-permute-start | bytes 2211848 | tf_op jit(solution)/shard_map/ppermute | solution.py:31
  51.3 19.5 %collective-permute-start.13 = (bf16[256,1792]{1,0:T(8,128)(2,1)}, bf16[256,1792]{1,0:T(8,128)(2,1)S(1)}, u32[]{:S(2)}, u32[]{:S(2)}) collective-permute-start(bf16[256,1792]{1,0:T(8,128)(2,1)} %get-tuple-element.42), channel_id=1, source_target_pairs={{0,2},{1,3},{2,0},{3,1},{4,6},{5,7},{6,4},{7,5},{8,10},{9,11},{10,... | collective-permute-start | bytes 2752520 | tf_op jit(solution)/shard_map/ppermute | solution.py:36
  71.8 31.3 %collective-permute-start.14 = (bf16[16,24,1920]{2,1,0:T(8,128)(2,1)S(1)}, bf16[16,24,1920]{2,1,0:T(8,128)(2,1)S(1)}, u32[]{:S(2)}, u32[]{:S(2)}) collective-permute-start(bf16[16,24,1920]{2,1,0:T(8,128)(2,1)S(1)} %pad_maximum_fusion), channel_id=1, source_target_pairs={{0,4},{4,0},{8,12},{12,8},{16,20},{20,16},{24,28},{28,24},{32,36},... | collective-permute-start | bytes 4423688 | tf_op jit(solution)/shard_map/ppermute | solution.py:31
  121.3 7.0 %collective-permute-start.16 = (bf16[384,256]{1,0:T(8,128)(2,1)S(1)}, bf16[384,256]{1,0:T(8,128)(2,1)S(1)}, u32[]{:S(2)}, u32[]{:S(2)}) collective-permute-start(bf16[384,256]{1,0:T(8,128)(2,1)S(1)} %shard_map.74), channel_id=1, source_target_pairs={{0,3},{1,2},{2,1},{3,0},{4,7},{5,6},{6,5},{7,4},{8,11},{9,10},{10,... | collective-permute-start | bytes 589832 | tf_op jit(solution)/shard_map/ppermute | solution.py:36
  122.5 10.0 %collective-permute-start.17 = (bf16[384,256]{1,0:T(8,128)(2,1)S(1)}, bf16[384,256]{1,0:T(8,128)(2,1)S(1)}, u32[]{:S(2)}, u32[]{:S(2)}) collective-permute-start(bf16[384,256]{1,0:T(8,128)(2,1)S(1)} %shard_map.74), channel_id=1, source_target_pairs={{0,2},{1,3},{2,0},{3,1},{4,6},{5,7},{6,4},{7,5},{8,10},{9,11},{10,... | collective-permute-start | bytes 589832 | tf_op jit(solution)/shard_map/ppermute | solution.py:36
  178.6 18.8 %collective-permute-start.29 = (bf16[256,1792]{1,0:T(8,128)(2,1)S(1)}, bf16[256,1792]{1,0:T(8,128)(2,1)S(1)}, u32[]{:S(2)}, u32[]{:S(2)}) collective-permute-start(bf16[256,1792]{1,0:T(8,128)(2,1)S(1)} %get-tuple-element.92), channel_id=1, source_target_pairs={{0,1},{1,0},{2,3},{3,2},{4,5},{5,4},{6,7},{7,6},{8,9},{9,8},{10,11... | collective-permute-start | bytes 2752520 | tf_op jit(solution)/shard_map/ppermute | solution.py:36
  179.3 19.7 %collective-permute-start.30 = (bf16[256,1792]{1,0:T(8,128)(2,1)S(1)}, bf16[256,1792]{1,0:T(8,128)(2,1)S(1)}, u32[]{:S(2)}, u32[]{:S(2)}) collective-permute-start(bf16[256,1792]{1,0:T(8,128)(2,1)S(1)} %get-tuple-element.91), channel_id=1, source_target_pairs={{0,3},{1,2},{2,1},{3,0},{4,7},{5,6},{6,5},{7,4},{8,11},{9,10},{10,... | collective-permute-start | bytes 2752520 | tf_op jit(solution)/shard_map/ppermute | solution.py:36
  180.3 9.9 %collective-permute-start.28 = (bf16[4,24,1792]{2,1,0:T(8,128)(2,1)S(1)}, bf16[4,24,1792]{2,1,0:T(8,128)(2,1)S(1)}, u32[]{:S(2)}, u32[]{:S(2)}) collective-permute-start(bf16[4,24,1792]{2,1,0:T(8,128)(2,1)S(1)} %pad_maximum_fusion.5), channel_id=1, source_target_pairs={{0,32},{4,100},{8,40},{12,108},{16,48},{20,116},{24,56},{28,124},{... | collective-permute-start | bytes 1032200 | tf_op jit(solution)/shard_map/ppermute | solution.py:31
  199.9 24.9 %collective-permute-start.31 = (bf16[8,24,1792]{2,1,0:T(8,128)(2,1)S(1)}, bf16[8,24,1792]{2,1,0:T(8,128)(2,1)}, u32[]{:S(2)}, u32[]{:S(2)}) collective-permute-start(bf16[8,24,1792]{2,1,0:T(8,128)(2,1)S(1)} %pad_maximum_fusion.3), channel_id=1, source_target_pairs={{0,96},{4,36},{8,104},{12,44},{16,112},{20,52},{24,120},{28,60},{3... | collective-permute-start | bytes 2064392 | tf_op jit(solution)/shard_map/ppermute | solution.py:31
  199.9 26.3 %collective-permute-start.32 = (bf16[256,1792]{1,0:T(8,128)(2,1)}, bf16[256,1792]{1,0:T(8,128)(2,1)S(1)}, u32[]{:S(2)}, u32[]{:S(2)}) collective-permute-start(bf16[256,1792]{1,0:T(8,128)(2,1)} %get-tuple-element.58), channel_id=1, source_target_pairs={{0,2},{1,3},{2,0},{3,1},{4,6},{5,7},{6,4},{7,5},{8,10},{9,11},{10,... | collective-permute-start | bytes 2752520 | tf_op jit(solution)/shard_map/ppermute | solution.py:36
  202.1 34.4 %collective-permute-start.22 = (f32[24,32]{1,0:T(8,128)S(1)}, f32[24,32]{1,0:T(8,128)}, u32[]{:S(2)}, u32[]{:S(2)}) collective-permute-start(f32[24,32]{1,0:T(8,128)S(1)} %fusion.5), channel_id=1, source_target_pairs={{0,1},{1,0},{2,3},{3,2},{4,5},{5,4},{6,7},{7,6},{8,9},{9,8},{10,11... | collective-permute-start | bytes 9224 | tf_op jit(solution)/shard_map/ppermute | solution.py:36
  203.3 33.1 %collective-permute-start.23 = (f32[24,32]{1,0:T(8,128)S(1)}, f32[24,32]{1,0:T(8,128)}, u32[]{:S(2)}, u32[]{:S(2)}) collective-permute-start(f32[24,32]{1,0:T(8,128)S(1)} %fusion.5), channel_id=1, source_target_pairs={{0,3},{1,2},{2,1},{3,0},{4,7},{5,6},{6,5},{7,4},{8,11},{9,10},{10,... | collective-permute-start | bytes 9224 | tf_op jit(solution)/shard_map/ppermute | solution.py:36
  204.8 31.6 %collective-permute-start.24 = (f32[24,32]{1,0:T(8,128)S(1)}, f32[24,32]{1,0:T(8,128)}, u32[]{:S(2)}, u32[]{:S(2)}) collective-permute-start(f32[24,32]{1,0:T(8,128)S(1)} %fusion.5), channel_id=1, source_target_pairs={{0,2},{1,3},{2,0},{3,1},{4,6},{5,7},{6,4},{7,5},{8,10},{9,11},{10,... | collective-permute-start | bytes 9224 | tf_op jit(solution)/shard_map/ppermute | solution.py:36
  227.2 20.1 %collective-permute-start.33 = (bf16[16,24,1792]{2,1,0:T(8,128)(2,1)S(1)}, bf16[16,24,1792]{2,1,0:T(8,128)(2,1)S(1)}, u32[]{:S(2)}, u32[]{:S(2)}) collective-permute-start(bf16[16,24,1792]{2,1,0:T(8,128)(2,1)S(1)} %pad_maximum_fusion.1), channel_id=1, source_target_pairs={{0,4},{4,0},{8,12},{12,8},{16,20},{20,16},{24,28},{28,24},{32,36},... | collective-permute-start | bytes 4128776 | tf_op jit(solution)/shard_map/ppermute | solution.py:31
  261.8 6.4 %collective-permute-start.34 = (bf16[384,256]{1,0:T(8,128)(2,1)S(1)}, bf16[384,256]{1,0:T(8,128)(2,1)S(1)}, u32[]{:S(2)}, u32[]{:S(2)}) collective-permute-start(bf16[384,256]{1,0:T(8,128)(2,1)S(1)} %shard_map.77), channel_id=1, source_target_pairs={{0,1},{1,0},{2,3},{3,2},{4,5},{5,4},{6,7},{7,6},{8,9},{9,8},{10,11... | collective-permute-start | bytes 589832 | tf_op jit(solution)/shard_map/ppermute | solution.py:36
  263.2 9.8 %collective-permute-start.35 = (bf16[384,256]{1,0:T(8,128)(2,1)S(1)}, bf16[384,256]{1,0:T(8,128)(2,1)S(1)}, u32[]{:S(2)}, u32[]{:S(2)}) collective-permute-start(bf16[384,256]{1,0:T(8,128)(2,1)S(1)} %shard_map.77), channel_id=1, source_target_pairs={{0,3},{1,2},{2,1},{3,0},{4,7},{5,6},{6,5},{7,4},{8,11},{9,10},{10,... | collective-permute-start | bytes 589832 | tf_op jit(solution)/shard_map/ppermute | solution.py:36
  265.1 9.8 %collective-permute-start.36 = (bf16[384,256]{1,0:T(8,128)(2,1)S(1)}, bf16[384,256]{1,0:T(8,128)(2,1)S(1)}, u32[]{:S(2)}, u32[]{:S(2)}) collective-permute-start(bf16[384,256]{1,0:T(8,128)(2,1)S(1)} %shard_map.77), channel_id=1, source_target_pairs={{0,2},{1,3},{2,0},{3,1},{4,6},{5,7},{6,4},{7,5},{8,10},{9,11},{10,... | collective-permute-start | bytes 589832 | tf_op jit(solution)/shard_map/ppermute | solution.py:36
  (42 other events, 406.4 us)
Sparse Core Ops, SparseCore 0:
  22.8 61.0 all-gather.2
  171.1 57.1 all-gather.4

commit v11 on v9

--- a/solution.py
+++ b/solution.py
@@ -194,12 +194,9 @@
         return (lax.broadcasted_iota(jnp.int32, (slots, 1), 0) == slot).astype(bf16)
 
     state = hidden_in
-    opening = [state, norm_gain.astype(bf16), jnp.zeros((8 - layers, part), bf16)]
-    opening = spread(jnp.concatenate(opening, axis=0))
-    gains = [block[rows : rows + layers].astype(f32) for block in opening]
+    gains = spread(norm_gain)
     for layer in range(layers):
-        blocks = spread(state) if layer else [block[:rows] for block in opening]
-        blocks = [block.astype(f32) for block in blocks]
+        blocks = [block.astype(f32) for block in spread(state)]
         scale = sum(jnp.sum(block * block, axis=1) for block in blocks)
         scale = lax.rsqrt(scale / width + 1e-06)
         normed = [

time: 267 us -> 268 us (level)
  local copies, waits for them, and re-layouts: 27.1 us -> 21.5 us
  starting transfers between devices: 52.5 us -> 57.9 us
  waiting for transfers between devices: 80.1 us -> 84.8 us
    all_gather x2, waiting for transfers between devices: 15.9 us -> 22.5 us  [body(): arrived = lax.all_gather(sent, 'expert', axis=0, tiled=True)]
    ppermute x9, starting transfers between devices: 21 us -> 23.8 us  [swap(): lax.ppermute(block, 'expert', [(i, i ^ masks[i & 1]) for i in range(count)])]
    ppermute x24 -> x27, starting transfers between devices: 31.4 us -> 34 us  [z_swap(): return lax.ppermute(block, 'tensor', [(i, i ^ mask) for i in range(count)])]
    ppermute x24 -> x27, waiting for transfers between devices: 53.3 us -> 52.2 us  [z_swap(): return lax.ppermute(block, 'tensor', [(i, i ^ mask) for i in range(count)])]
  transfers between devices with their start and end apart: 35 -> 38, of which waited for: 24 -> 23; matrix products, arithmetic and copies ran while one was open for 15% -> 13% of each run, Pallas kernels for 0% -> 0%
where the time goes in v11:
time: 268 us
  waiting for transfers between devices  84.8 us (32%)
  starting transfers between devices  57.9 us (22%)
  blocking collectives  45.8 us (17%)
  Pallas kernels  27.1 us (10%)
  local copies, waits for them, and re-layouts  21.5 us (8%)
  other arithmetic  13.9 us (5%)
  between operations  13.9 us (5%)
  matrix products  2.96 us (1%)
    ppermute x27, waiting for transfers between devices, z_swap(): return lax.ppermute(block, 'tensor', [(i, i ^ mask) for i in range(count)])  52.2 us
    all_to_all x2, blocking collectives, body(): lax.all_to_all(out.reshape(chips, 2 * capacity, part), 'expert', split_ax...  45.8 us
    ppermute x27, starting transfers between devices, z_swap(): return lax.ppermute(block, 'tensor', [(i, i ^ mask) for i in range(count)])  34 us
    ppermute x9, starting transfers between devices, swap(): lax.ppermute(block, 'expert', [(i, i ^ masks[i & 1]) for i in range(count)])  23.8 us
    all_gather x2, waiting for transfers between devices, body(): arrived = lax.all_gather(sent, 'expert', axis=0, tiled=True)  22.5 us
    pallas_call x2, Pallas kernels, gate_up(): pl.pallas_call(functools.partial(gate_up_kernel, layer), in_specs=[pl.Blo...  21.2 us
    ppermute x9, waiting for transfers between devices, swap(): lax.ppermute(block, 'expert', [(i, i ^ masks[i & 1]) for i in range(count)])  9.99 us
    reshape x2, local copies, waits for them, and re-layouts, columns(): return z_swap(block.reshape(count, part), mask)  6.85 us
  transfers between devices with their start and end apart: 38, of which 23 were waited for; matrix products, arithmetic and copies ran while one was open for 13% of the time, Pallas kernels for 0%

profile of v11, /device:TPU:1, one launch (start us, length us, event | category | flops | bytes accessed | tf_op | source)
XLA Modules:
  0.0 267.8 jit_solution(10059586116974215919)
XLA Ops:
  18.2 2.5 collective-permute-done.5
  33.0 3.4 %dynamic-slice_bitcast_fusion.3 = (bf16[256,1792]{1,0:T(8,128)(2,1)}, bf16[256,1792]{1,0:T(8,128)(2,1)}, bf16[256,1792]{1,0:T(8,128)(2,1)}) fusion(bf16[2,1,256,7168]{3,2,1,0:T(8,128)(2,1)} %down_ref.3, s32[]{:T(128)S(6)} %select_n.219, s32[]{:T(128)S(6)} %select_n.218, s32[]{:T(128)S(6)} %select_n.217), kind=kLoop, calls=%fused_computation.11 | loop fusion | bytes 5505036 | tf_op jit(solution)/shard_map/reshape | solution.py:186
  40.3 2.7 %collective-permute-start.10 = (bf16[1,24,128]{2,1,0:T(8,128)(2,1)S(1)}, bf16[1,24,128]{2,1,0:T(8,128)(2,1)S(1)}, u32[]{:S(2)}, u32[]{:S(2)}) collective-permute-start(bf16[1,24,128]{2,1,0:T(8,128)(2,1)S(1)} %bitcast.97), channel_id=1, source_target_pairs={{0,8},{4,28},{8,0},{12,20},{16,24},{20,12},{24,16},{28,4},{32,40},... | collective-permute-start | bytes 18440 | tf_op jit(solution)/shard_map/ppermute | solution.py:31
  46.1 4.0 %collective-permute-start.9 = (bf16[48,384]{1,0:T(8,128)(2,1)S(1)}, bf16[48,384]{1,0:T(8,128)(2,1)S(1)}, u32[]{:S(2)}, u32[]{:S(2)}) collective-permute-start(bf16[48,384]{1,0:T(8,128)(2,1)S(1)} %pad_maximum_fusion.5), channel_id=1, source_target_pairs={{0,4},{4,0},{8,12},{12,8},{16,20},{20,16},{24,28},{28,24},{32,36},... | collective-permute-start | bytes 110600 | tf_op jit(solution)/shard_map/ppermute | solution.py:31
  53.0 2.5 collective-permute-start.12
  57.9 2.7 %collective-permute-done.13 = bf16[8,24,128]{2,1,0:T(8,128)(2,1)S(1)} collective-permute-done((bf16[8,24,128]{2,1,0:T(8,128)(2,1)S(1)}, bf16[8,24,128]{2,1,0:T(8,128)(2,1)S(1)}, u32[]{:S(2)}, u32[]{:S(2)}) %collective-permute-start.13) | collective-permute-done | bytes 49184 | tf_op jit(solution)/shard_map/ppermute | solution.py:31
  61.2 4.6 %collective-permute-start.14 = (bf16[16,24,128]{2,1,0:T(8,128)(2,1)}, bf16[16,24,128]{2,1,0:T(8,128)(2,1)S(1)}, u32[]{:S(2)}, u32[]{:S(2)}) collective-permute-start(bf16[16,24,128]{2,1,0:T(8,128)(2,1)} %get-tuple-element.69), channel_id=1, source_target_pairs={{0,4},{4,0},{8,12},{12,8},{16,20},{20,16},{24,28},{28,24},{32,36},... | collective-permute-start | bytes 294920 | tf_op jit(solution)/shard_map/ppermute | solution.py:31
  72.0 2.7 %collective-permute-done.17.w3 = bf16[256,1792]{1,0:T(8,128)(2,1)S(1)} collective-permute-done((bf16[256,1792]{1,0:T(8,128)(2,1)}, bf16[256,1792]{1,0:T(8,128)(2,1)S(1)}, u32[]{:S(2)}, u32[]{:S(2)}) %collective-permute-start.17) | collective-permute-done | bytes 917536 | tf_op jit(solution)/shard_map/ppermute | solution.py:36
  74.7 11.5 %all-gather.3.cloned.1.call-done.tokens_ref = bf16[768,7168]{1,0:T(8,128)(2,1)} async-done(((bf16[24,7168]{1,0:T(8,128)(2,1)}), bf16[768,7168]{1,0:T(8,128)(2,1)}) %all-gather.3.cloned.1.call-update) | async-done | bytes 11010064 | tf_op jit(solution)/shard_map/all_gather | solution.py:208
  86.2 10.6 %shard_map.73 = bf16[384,256]{1,0:T(8,128)(2,1)} custom-call(s32[1]{0:T(128)} %bitcast.17.z_ref, bf16[768,7168]{1,0:T(8,128)(2,1)} %all-gather.3.cloned.1.call-done.tokens_ref, bf16[384,768]{1,0:T(8,128)(2,1)} %fusion.taken_ref, bf16[2,1,7168,256]{3,2,1,0:T(8,128)(2,1)} %gate_ref.3, bf16[2,1,7168,256]{3,2,1,0:T(8,128)(2,1)} %up_ref.3), custom_call_target="tpu_custom_call" | custom-call | flops 5637144576 | bytes 18743296 | tf_op jit(solution)/shard_map/pallas_call | solution.py:83
  103.3 4.8 %collective-permute-done.19.a2 = bf16[384,256]{1,0:T(8,128)(2,1)S(1)} collective-permute-done((bf16[384,256]{1,0:T(8,128)(2,1)}, bf16[384,256]{1,0:T(8,128)(2,1)S(1)}, u32[]{:S(2)}, u32[]{:S(2)}) %collective-permute-start.19) | collective-permute-done | bytes 196640 | tf_op jit(solution)/shard_map/ppermute | solution.py:36
  110.0 3.0 %shard_map.74 = bf16[384,1792]{1,0:T(8,128)(2,1)S(1)} custom-call(s32[1]{0:T(128)} %bitcast.17.z_ref, bf16[384,256]{1,0:T(8,128)(2,1)S(1)} %broadcast_select_fusion.1.a0, bf16[384,256]{1,0:T(8,128)(2,1)S(1)} %collective-permute-done.18.a1, bf16[384,256]{1,0:T(8,128)(2,1)S(1)} %collective-permute-done.19.a2, bf16[384,256]{1,0:T(8,128)(2,1)S(1)} %collective-permute-done.20.a3, ...), custom_call_target="tpu_custom_call" | custom-call | flops 1409286144 | bytes 5832704 | tf_op jit(solution)/shard_map/pallas_call | solution.py:126
  113.0 22.8 %all_to_all.10 = bf16[16,24,1792]{2,1,0:T(8,128)(2,1)S(1)} all-to-all(bf16[16,24,1792]{2,1,0:T(8,128)(2,1)S(1)} %bitcast.92), channel_id=1, replica_groups={{0,8,16,24,32,40,48,56,64,72,80,88,96,104,112,120},{4,12,20,28,36,44,52..., dimensions={0} | all-to-all | bytes 2752512 | tf_op jit(solution)/shard_map/all_to_all | solution.py:247
  136.2 3.1 %collective-permute-start.21 = (f32[24,1792]{1,0:T(8,128)S(1)}, f32[24,1792]{1,0:T(8,128)S(1)}, u32[]{:S(2)}, u32[]{:S(2)}) collective-permute-start(f32[24,1792]{1,0:T(8,128)S(1)} %slice_bitcast_fusion.2), channel_id=1, source_target_pairs={{0,4},{4,0},{8,12},{12,8},{16,20},{20,16},{24,28},{28,24},{32,36},... | collective-permute-start | bytes 516104 | tf_op jit(solution)/shard_map/ppermute | solution.py:31
  151.8 3.4 %dynamic-slice_bitcast_fusion = (bf16[256,1792]{1,0:T(8,128)(2,1)}, bf16[256,1792]{1,0:T(8,128)(2,1)}, bf16[256,1792]{1,0:T(8,128)(2,1)}) fusion(bf16[2,1,256,7168]{3,2,1,0:T(8,128)(2,1)} %down_ref.3, s32[]{:T(128)S(6)} %select_n.235, s32[]{:T(128)S(6)} %select_n.234, s32[]{:T(128)S(6)} %select_n.233), kind=kLoop, calls=%fused_computation.8 | loop fusion | bytes 5505036 | tf_op jit(solution)/shard_map/reshape | solution.py:186
  163.1 3.6 %collective-permute-start.28 = (bf16[48,384]{1,0:T(8,128)(2,1)S(1)}, bf16[48,384]{1,0:T(8,128)(2,1)S(1)}, u32[]{:S(2)}, u32[]{:S(2)}) collective-permute-start(bf16[48,384]{1,0:T(8,128)(2,1)S(1)} %pad_maximum_fusion.6), channel_id=1, source_target_pairs={{0,4},{4,0},{8,12},{12,8},{16,20},{20,16},{24,28},{28,24},{32,36},... | collective-permute-start | bytes 110600 | tf_op jit(solution)/shard_map/ppermute | solution.py:31
  167.5 7.1 %collective-permute-done.29.w1 = bf16[256,1792]{1,0:T(8,128)(2,1)S(1)} collective-permute-done((bf16[256,1792]{1,0:T(8,128)(2,1)}, bf16[256,1792]{1,0:T(8,128)(2,1)S(1)}, u32[]{:S(2)}, u32[]{:S(2)}) %collective-permute-start.29) | collective-permute-done | bytes 917536 | tf_op jit(solution)/shard_map/ppermute | solution.py:36
  176.9 18.0 %collective-permute-done.31.w3 = bf16[256,1792]{1,0:T(8,128)(2,1)S(1)} collective-permute-done((bf16[256,1792]{1,0:T(8,128)(2,1)}, bf16[256,1792]{1,0:T(8,128)(2,1)S(1)}, u32[]{:S(2)}, u32[]{:S(2)}) %collective-permute-start.31) | collective-permute-done | bytes 917536 | tf_op jit(solution)/shard_map/ppermute | solution.py:36
  194.9 11.0 %all-gather.5.cloned.1.call-done.tokens_ref = bf16[768,7168]{1,0:T(8,128)(2,1)} async-done(((bf16[24,7168]{1,0:T(8,128)(2,1)}), bf16[768,7168]{1,0:T(8,128)(2,1)}) %all-gather.5.cloned.1.call-update) | async-done | bytes 11010064 | tf_op jit(solution)/shard_map/all_gather | solution.py:208
  205.9 10.6 %shard_map.75 = bf16[384,256]{1,0:T(8,128)(2,1)} custom-call(s32[1]{0:T(128)} %bitcast.17.z_ref, bf16[768,7168]{1,0:T(8,128)(2,1)} %all-gather.5.cloned.1.call-done.tokens_ref, bf16[384,768]{1,0:T(8,128)(2,1)} %fusion.1.taken_ref, bf16[2,1,7168,256]{3,2,1,0:T(8,128)(2,1)} %gate_ref.3, bf16[2,1,7168,256]{3,2,1,0:T(8,128)(2,1)} %up_ref.3), custom_call_target="tpu_custom_call" | custom-call | flops 5637144576 | bytes 18743296 | tf_op jit(solution)/shard_map/pallas_call | solution.py:83
  223.1 4.8 %collective-permute-done.33.a2 = bf16[384,256]{1,0:T(8,128)(2,1)S(1)} collective-permute-done((bf16[384,256]{1,0:T(8,128)(2,1)}, bf16[384,256]{1,0:T(8,128)(2,1)S(1)}, u32[]{:S(2)}, u32[]{:S(2)}) %collective-permute-start.33) | collective-permute-done | bytes 196640 | tf_op jit(solution)/shard_map/ppermute | solution.py:36
  229.7 3.0 %shard_map.76 = bf16[384,1792]{1,0:T(8,128)(2,1)S(1)} custom-call(s32[1]{0:T(128)} %bitcast.17.z_ref, bf16[384,256]{1,0:T(8,128)(2,1)S(1)} %broadcast_select_fusion.a0, bf16[384,256]{1,0:T(8,128)(2,1)S(1)} %collective-permute-done.32.a1, bf16[384,256]{1,0:T(8,128)(2,1)S(1)} %collective-permute-done.33.a2, bf16[384,256]{1,0:T(8,128)(2,1)S(1)} %collective-permute-done.34.a3, ...), custom_call_target="tpu_custom_call" | custom-call | flops 1409286144 | bytes 5832704 | tf_op jit(solution)/shard_map/pallas_call | solution.py:126
  232.7 23.0 %all_to_all.11 = bf16[16,24,1792]{2,1,0:T(8,128)(2,1)S(1)} all-to-all(bf16[16,24,1792]{2,1,0:T(8,128)(2,1)S(1)} %bitcast.91), channel_id=1, replica_groups={{0,8,16,24,32,40,48,56,64,72,80,88,96,104,112,120},{4,12,20,28,36,44,52..., dimensions={0} | all-to-all | bytes 2752512 | tf_op jit(solution)/shard_map/all_to_all | solution.py:247
  256.2 3.1 %collective-permute-start.35 = (f32[24,1792]{1,0:T(8,128)S(1)}, f32[24,1792]{1,0:T(8,128)S(1)}, u32[]{:S(2)}, u32[]{:S(2)}) collective-permute-start(f32[24,1792]{1,0:T(8,128)S(1)} %slice_bitcast_fusion), channel_id=1, source_target_pairs={{0,4},{4,0},{8,12},{12,8},{16,20},{20,16},{24,28},{28,24},{32,36},... | collective-permute-start | bytes 516104 | tf_op jit(solution)/shard_map/ppermute | solution.py:31
  (178 shorter events, 85.4 us)
Async XLA Ops:
  6.5 79.7 %all-gather.3.cloned.1.call-start = ((), (), s32[]{:S(2)}) async-start(), calls=%async_computation.2 | async-start | bytes 11354112 | tf_op jit(solution)/shard_map/all_gather | solution.py:208
  6.5 14.8 %collective-permute-start = (bf16[24,1792]{1,0:T(8,128)(2,1)}, bf16[24,1792]{1,0:T(8,128)(2,1)S(1)}, u32[]{:S(2)}, u32[]{:S(2)}) collective-permute-start(bf16[24,1792]{1,0:T(8,128)(2,1)} %param.7), channel_id=1, source_target_pairs={{0,1},{1,0},{2,3},{3,2},{4,5},{5,4},{6,7},{7,6},{8,9},{9,8},{10,11... | collective-permute-start | bytes 258056 | tf_op jit(solution)/shard_map/ppermute | solution.py:36
  9.0 12.5 %collective-permute-start.1 = (bf16[24,1792]{1,0:T(8,128)(2,1)}, bf16[24,1792]{1,0:T(8,128)(2,1)S(1)}, u32[]{:S(2)}, u32[]{:S(2)}) collective-permute-start(bf16[24,1792]{1,0:T(8,128)(2,1)} %param.7), channel_id=1, source_target_pairs={{0,3},{1,2},{2,1},{3,0},{4,7},{5,6},{6,5},{7,4},{8,11},{9,10},{10,... | collective-permute-start | bytes 258056 | tf_op jit(solution)/shard_map/ppermute | solution.py:36
  11.2 10.4 %collective-permute-start.2 = (bf16[24,1792]{1,0:T(8,128)(2,1)}, bf16[24,1792]{1,0:T(8,128)(2,1)S(1)}, u32[]{:S(2)}, u32[]{:S(2)}) collective-permute-start(bf16[24,1792]{1,0:T(8,128)(2,1)} %param.7), channel_id=1, source_target_pairs={{0,2},{1,3},{2,0},{3,1},{4,6},{5,7},{6,4},{7,5},{8,10},{9,11},{10,... | collective-permute-start | bytes 258056 | tf_op jit(solution)/shard_map/ppermute | solution.py:36
  23.6 182.3 %all-gather.5.cloned.1.call-start = ((), (), s32[]{:S(2)}) async-start(), calls=%async_computation.3 | async-start | bytes 11354112 | tf_op jit(solution)/shard_map/all_gather | solution.py:208
  29.6 9.3 %collective-permute-start.6 = (f32[24,32]{1,0:T(8,128)S(1)}, f32[24,32]{1,0:T(8,128)S(1)}, u32[]{:S(2)}, u32[]{:S(2)}) collective-permute-start(f32[24,32]{1,0:T(8,128)S(1)} %fusion.7), channel_id=1, source_target_pairs={{0,1},{1,0},{2,3},{3,2},{4,5},{5,4},{6,7},{7,6},{8,9},{9,8},{10,11... | collective-permute-start | bytes 9224 | tf_op jit(solution)/shard_map/ppermute | solution.py:36
  30.5 9.8 %collective-permute-start.7 = (f32[24,32]{1,0:T(8,128)S(1)}, f32[24,32]{1,0:T(8,128)S(1)}, u32[]{:S(2)}, u32[]{:S(2)}) collective-permute-start(f32[24,32]{1,0:T(8,128)S(1)} %fusion.7), channel_id=1, source_target_pairs={{0,3},{1,2},{2,1},{3,0},{4,7},{5,6},{6,5},{7,4},{8,11},{9,10},{10,... | collective-permute-start | bytes 9224 | tf_op jit(solution)/shard_map/ppermute | solution.py:36
  31.7 11.3 %collective-permute-start.8 = (f32[24,32]{1,0:T(8,128)S(1)}, f32[24,32]{1,0:T(8,128)S(1)}, u32[]{:S(2)}, u32[]{:S(2)}) collective-permute-start(f32[24,32]{1,0:T(8,128)S(1)} %fusion.7), channel_id=1, source_target_pairs={{0,2},{1,3},{2,0},{3,1},{4,6},{5,7},{6,4},{7,5},{8,10},{9,11},{10,... | collective-permute-start | bytes 9224 | tf_op jit(solution)/shard_map/ppermute | solution.py:36
  36.4 35.6 %collective-permute-start.15 = (bf16[256,1792]{1,0:T(8,128)(2,1)}, bf16[256,1792]{1,0:T(8,128)(2,1)S(1)}, u32[]{:S(2)}, u32[]{:S(2)}) collective-permute-start(bf16[256,1792]{1,0:T(8,128)(2,1)} %get-tuple-element.60), channel_id=1, source_target_pairs={{0,1},{1,0},{2,3},{3,2},{4,5},{5,4},{6,7},{7,6},{8,9},{9,8},{10,11... | collective-permute-start | bytes 2752520 | tf_op jit(solution)/shard_map/ppermute | solution.py:36
  37.2 34.8 %collective-permute-start.16 = (bf16[256,1792]{1,0:T(8,128)(2,1)}, bf16[256,1792]{1,0:T(8,128)(2,1)S(1)}, u32[]{:S(2)}, u32[]{:S(2)}) collective-permute-start(bf16[256,1792]{1,0:T(8,128)(2,1)} %get-tuple-element.59), channel_id=1, source_target_pairs={{0,3},{1,2},{2,1},{3,0},{4,7},{5,6},{6,5},{7,4},{8,11},{9,10},{10,... | collective-permute-start | bytes 2752520 | tf_op jit(solution)/shard_map/ppermute | solution.py:36
  38.9 35.7 %collective-permute-start.17 = (bf16[256,1792]{1,0:T(8,128)(2,1)}, bf16[256,1792]{1,0:T(8,128)(2,1)S(1)}, u32[]{:S(2)}, u32[]{:S(2)}) collective-permute-start(bf16[256,1792]{1,0:T(8,128)(2,1)} %get-tuple-element.58), channel_id=1, source_target_pairs={{0,2},{1,3},{2,0},{3,1},{4,6},{5,7},{6,4},{7,5},{8,10},{9,11},{10,... | collective-permute-start | bytes 2752520 | tf_op jit(solution)/shard_map/ppermute | solution.py:36
  40.3 9.8 %collective-permute-start.10 = (bf16[1,24,128]{2,1,0:T(8,128)(2,1)S(1)}, bf16[1,24,128]{2,1,0:T(8,128)(2,1)S(1)}, u32[]{:S(2)}, u32[]{:S(2)}) collective-permute-start(bf16[1,24,128]{2,1,0:T(8,128)(2,1)S(1)} %bitcast.97), channel_id=1, source_target_pairs={{0,8},{4,28},{8,0},{12,20},{16,24},{20,12},{24,16},{28,4},{32,40},... | collective-permute-start | bytes 18440 | tf_op jit(solution)/shard_map/ppermute | solution.py:31
  46.1 19.8 %collective-permute-start.9 = (bf16[48,384]{1,0:T(8,128)(2,1)S(1)}, bf16[48,384]{1,0:T(8,128)(2,1)S(1)}, u32[]{:S(2)}, u32[]{:S(2)}) collective-permute-start(bf16[48,384]{1,0:T(8,128)(2,1)S(1)} %pad_maximum_fusion.5), channel_id=1, source_target_pairs={{0,4},{4,0},{8,12},{12,8},{16,20},{20,16},{24,28},{28,24},{32,36},... | collective-permute-start | bytes 110600 | tf_op jit(solution)/shard_map/ppermute | solution.py:31
  98.1 10.0 %collective-permute-start.19 = (bf16[384,256]{1,0:T(8,128)(2,1)}, bf16[384,256]{1,0:T(8,128)(2,1)S(1)}, u32[]{:S(2)}, u32[]{:S(2)}) collective-permute-start(bf16[384,256]{1,0:T(8,128)(2,1)} %shard_map.73), channel_id=1, source_target_pairs={{0,3},{1,2},{2,1},{3,0},{4,7},{5,6},{6,5},{7,4},{8,11},{9,10},{10,... | collective-permute-start | bytes 589832 | tf_op jit(solution)/shard_map/ppermute | solution.py:36
  100.0 9.9 %collective-permute-start.20 = (bf16[384,256]{1,0:T(8,128)(2,1)}, bf16[384,256]{1,0:T(8,128)(2,1)S(1)}, u32[]{:S(2)}, u32[]{:S(2)}) collective-permute-start(bf16[384,256]{1,0:T(8,128)(2,1)} %shard_map.73), channel_id=1, source_target_pairs={{0,2},{1,3},{2,0},{3,1},{4,6},{5,7},{6,4},{7,5},{8,10},{9,11},{10,... | collective-permute-start | bytes 589832 | tf_op jit(solution)/shard_map/ppermute | solution.py:36
  148.5 8.7 %collective-permute-start.25 = (f32[24,32]{1,0:T(8,128)S(1)}, f32[24,32]{1,0:T(8,128)S(1)}, u32[]{:S(2)}, u32[]{:S(2)}) collective-permute-start(f32[24,32]{1,0:T(8,128)S(1)} %fusion.5), channel_id=1, source_target_pairs={{0,1},{1,0},{2,3},{3,2},{4,5},{5,4},{6,7},{7,6},{8,9},{9,8},{10,11... | collective-permute-start | bytes 9224 | tf_op jit(solution)/shard_map/ppermute | solution.py:36
  149.3 9.2 %collective-permute-start.26 = (f32[24,32]{1,0:T(8,128)S(1)}, f32[24,32]{1,0:T(8,128)S(1)}, u32[]{:S(2)}, u32[]{:S(2)}) collective-permute-start(f32[24,32]{1,0:T(8,128)S(1)} %fusion.5), channel_id=1, source_target_pairs={{0,3},{1,2},{2,1},{3,0},{4,7},{5,6},{6,5},{7,4},{8,11},{9,10},{10,... | collective-permute-start | bytes 9224 | tf_op jit(solution)/shard_map/ppermute | solution.py:36
  150.5 8.0 %collective-permute-start.27 = (f32[24,32]{1,0:T(8,128)S(1)}, f32[24,32]{1,0:T(8,128)S(1)}, u32[]{:S(2)}, u32[]{:S(2)}) collective-permute-start(f32[24,32]{1,0:T(8,128)S(1)} %fusion.5), channel_id=1, source_target_pairs={{0,2},{1,3},{2,0},{3,1},{4,6},{5,7},{6,4},{7,5},{8,10},{9,11},{10,... | collective-permute-start | bytes 9224 | tf_op jit(solution)/shard_map/ppermute | solution.py:36
  155.2 19.4 %collective-permute-start.29 = (bf16[256,1792]{1,0:T(8,128)(2,1)}, bf16[256,1792]{1,0:T(8,128)(2,1)S(1)}, u32[]{:S(2)}, u32[]{:S(2)}) collective-permute-start(bf16[256,1792]{1,0:T(8,128)(2,1)} %get-tuple-element.57), channel_id=1, source_target_pairs={{0,1},{1,0},{2,3},{3,2},{4,5},{5,4},{6,7},{7,6},{8,9},{9,8},{10,11... | collective-permute-start | bytes 2752520 | tf_op jit(solution)/shard_map/ppermute | solution.py:36
  156.0 20.9 %collective-permute-start.30 = (bf16[256,1792]{1,0:T(8,128)(2,1)}, bf16[256,1792]{1,0:T(8,128)(2,1)S(1)}, u32[]{:S(2)}, u32[]{:S(2)}) collective-permute-start(bf16[256,1792]{1,0:T(8,128)(2,1)} %get-tuple-element.56), channel_id=1, source_target_pairs={{0,3},{1,2},{2,1},{3,0},{4,7},{5,6},{6,5},{7,4},{8,11},{9,10},{10,... | collective-permute-start | bytes 2752520 | tf_op jit(solution)/shard_map/ppermute | solution.py:36
  157.1 37.8 %collective-permute-start.31 = (bf16[256,1792]{1,0:T(8,128)(2,1)}, bf16[256,1792]{1,0:T(8,128)(2,1)S(1)}, u32[]{:S(2)}, u32[]{:S(2)}) collective-permute-start(bf16[256,1792]{1,0:T(8,128)(2,1)} %get-tuple-element.55), channel_id=1, source_target_pairs={{0,2},{1,3},{2,0},{3,1},{4,6},{5,7},{6,4},{7,5},{8,10},{9,11},{10,... | collective-permute-start | bytes 2752520 | tf_op jit(solution)/shard_map/ppermute | solution.py:36
  216.5 6.5 %collective-permute-start.32 = (bf16[384,256]{1,0:T(8,128)(2,1)}, bf16[384,256]{1,0:T(8,128)(2,1)S(1)}, u32[]{:S(2)}, u32[]{:S(2)}) collective-permute-start(bf16[384,256]{1,0:T(8,128)(2,1)} %shard_map.75), channel_id=1, source_target_pairs={{0,1},{1,0},{2,3},{3,2},{4,5},{5,4},{6,7},{7,6},{8,9},{9,8},{10,11... | collective-permute-start | bytes 589832 | tf_op jit(solution)/shard_map/ppermute | solution.py:36
  217.9 10.0 %collective-permute-start.33 = (bf16[384,256]{1,0:T(8,128)(2,1)}, bf16[384,256]{1,0:T(8,128)(2,1)S(1)}, u32[]{:S(2)}, u32[]{:S(2)}) collective-permute-start(bf16[384,256]{1,0:T(8,128)(2,1)} %shard_map.75), channel_id=1, source_target_pairs={{0,3},{1,2},{2,1},{3,0},{4,7},{5,6},{6,5},{7,4},{8,11},{9,10},{10,... | collective-permute-start | bytes 589832 | tf_op jit(solution)/shard_map/ppermute | solution.py:36
  219.8 10.0 %collective-permute-start.34 = (bf16[384,256]{1,0:T(8,128)(2,1)}, bf16[384,256]{1,0:T(8,128)(2,1)S(1)}, u32[]{:S(2)}, u32[]{:S(2)}) collective-permute-start(bf16[384,256]{1,0:T(8,128)(2,1)} %shard_map.75), channel_id=1, source_target_pairs={{0,2},{1,3},{2,0},{3,1},{4,6},{5,7},{6,4},{7,5},{8,10},{9,11},{10,... | collective-permute-start | bytes 589832 | tf_op jit(solution)/shard_map/ppermute | solution.py:36
  (20 other events, 117.2 us)
Sparse Core Ops, SparseCore 0:
  23.7 62.4 all-gather.2
  148.3 57.6 all-gather.4

commit v12 on v11

--- a/solution.py
+++ b/solution.py
@@ -38,6 +38,54 @@
 
 def after(block, *others):
     return lax.optimization_barrier((block, *others))[0]
+
+
+def opening_kernel(state_ref, gain_ref, out_ref):
+    gain = gain_ref[...]
+    high = gain.astype(bf16).astype(f32)
+    middle = (gain - high).astype(bf16).astype(f32)
+    parts = [state_ref[...].astype(f32), high, middle, gain - high - middle]
+    rest = out_ref.shape[0] - sum(part.shape[0] for part in parts)
+    parts.append(jnp.zeros((rest, out_ref.shape[1]), f32))
+    out_ref[...] = jnp.concatenate(parts, axis=0).astype(bf16)
+
+
+def join(state, gain):
+    inside = pl.BlockSpec(memory_space=pltpu.VMEM)
+    return pl.pallas_call(
+        opening_kernel,
+        in_specs=[inside, inside],
+        out_specs=inside,
+        out_shape=jax.ShapeDtypeStruct((state.shape[0] + 8, state.shape[1]), bf16),
+    )(state, gain)
+
+
+def norm_kernel(layer, layers, b0, b1, b2, b3, g0, g1, g2, g3, out_ref, scale_ref):
+    rows, width = out_ref.shape
+    part = width // len(ORDER)
+    blocks = [block[...].astype(f32)[:rows] for block in (b0, b1, b2, b3)]
+    scale = sum(jnp.sum(block * block, axis=1, keepdims=True) for block in blocks)
+    scale = lax.rsqrt(scale / width + 1e-06)
+    scale_ref[...] = jnp.broadcast_to(scale, scale_ref.shape)
+    for n, (block, gains) in enumerate(zip(blocks, (g0, g1, g2, g3))):
+        terms = gains[...].astype(f32)[rows:]
+        gain = sum(terms[k * layers + layer : k * layers + layer + 1] for k in range(3))
+        out_ref[:, n * part : (n + 1) * part] = (block * scale * gain).astype(bf16)
+
+
+def normalize(blocks, openings, rows, layer, layers):
+    inside = pl.BlockSpec(memory_space=pltpu.VMEM)
+    width = len(blocks) * blocks[0].shape[1]
+    normed, scale = pl.pallas_call(
+        functools.partial(norm_kernel, layer, layers),
+        in_specs=[inside] * 8,
+        out_specs=(inside, inside),
+        out_shape=(
+            jax.ShapeDtypeStruct((rows, width), bf16),
+            jax.ShapeDtypeStruct((rows, 128), f32),
+        ),
+    )(*blocks, *openings)
+    return normed, scale[:, 0]
 
 
 def gate_up_kernel(
@@ -194,17 +242,10 @@
         return (lax.broadcasted_iota(jnp.int32, (slots, 1), 0) == slot).astype(bf16)
 
     state = hidden_in
-    gains = spread(norm_gain)
+    openings = spread(join(state, norm_gain))
     for layer in range(layers):
-        blocks = [block.astype(f32) for block in spread(state)]
-        scale = sum(jnp.sum(block * block, axis=1) for block in blocks)
-        scale = lax.rsqrt(scale / width + 1e-06)
-        normed = [
-            (block * scale[:, None] * gain[layer][None, :]).astype(bf16)
-            for block, gain in zip(blocks, gains)
-        ]
-
-        sent = jnp.concatenate(normed, axis=1)
+        blocks = spread(state) if layer else openings
+        sent, scale = normalize(blocks, openings, rows, layer, layers)
         arrived = lax.all_gather(sent, "expert", axis=0, tiled=True)
 
         own = state.astype(f32) * scale[:, None] * norm_gain[layer][None, :]

time: 268 us -> 269 us (level)
  starting transfers between devices: 57.9 us -> 51.7 us
  Pallas kernels: 27.1 us -> 33.1 us
  local copies, waits for them, and re-layouts: 21.5 us -> 26.8 us
  other arithmetic: 13.9 us -> 10.2 us
  waiting for transfers between devices: 84.8 us -> 81.7 us
    all_gather x2, waiting for transfers between devices: 22.5 us -> 14.7 us  [body(): arrived = lax.all_gather(sent, 'expert', axis=0, tiled=True)]
    pallas_call x0 -> x3, Pallas kernels: none -> 6.01 us  [the longest x2 4.43 us: normalize(): pl.pallas_call(functools.partial(norm_kernel, layer, layers), in_specs=[i...]
    ppermute x27 -> x24, waiting for transfers between devices: 52.2 us -> 55.8 us  [z_swap(): return lax.ppermute(block, 'tensor', [(i, i ^ mask) for i in range(count)])]
    ppermute x27 -> x24, starting transfers between devices: 34 us -> 30.5 us  [z_swap(): return lax.ppermute(block, 'tensor', [(i, i ^ mask) for i in range(count)])]
  transfers between devices with their start and end apart: 38 -> 35, of which waited for: 23 -> 24; matrix products, arithmetic and copies ran while one was open for 13% -> 14% of each run, Pallas kernels for 0% -> 0%
where the time goes in v12:
time: 269 us; the launch traced here: 268 us
  waiting for transfers between devices  81.7 us (30%)
  starting transfers between devices  51.7 us (19%)
  blocking collectives  46.3 us (17%)
  Pallas kernels  33.1 us (12%)
  local copies, waits for them, and re-layouts  26.8 us (10%)
  between operations  13.9 us (5%)
  other arithmetic  10.2 us (4%)
  matrix products  3.99 us (1%)
    ppermute x24, waiting for transfers between devices, z_swap(): return lax.ppermute(block, 'tensor', [(i, i ^ mask) for i in range(count)])  55.8 us
    all_to_all x2, blocking collectives, body(): lax.all_to_all(out.reshape(chips, 2 * capacity, part), 'expert', split_ax...  46.3 us
    ppermute x24, starting transfers between devices, z_swap(): return lax.ppermute(block, 'tensor', [(i, i ^ mask) for i in range(count)])  30.5 us
    pallas_call x2, Pallas kernels, gate_up(): pl.pallas_call(functools.partial(gate_up_kernel, layer), in_specs=[pl.Blo...  21.2 us
    ppermute x9, starting transfers between devices, swap(): lax.ppermute(block, 'expert', [(i, i ^ masks[i & 1]) for i in range(count)])  21.1 us
    all_gather x2, waiting for transfers between devices, body(): arrived = lax.all_gather(sent, 'expert', axis=0, tiled=True)  14.7 us
    ppermute x9, waiting for transfers between devices, swap(): lax.ppermute(block, 'expert', [(i, i ^ masks[i & 1]) for i in range(count)])  11.2 us
    reshape x2, local copies, waits for them, and re-layouts, columns(): return z_swap(block.reshape(count, part), mask)  6.98 us
  transfers between devices with their start and end apart: 35, of which 24 were waited for; matrix products, arithmetic and copies ran while one was open for 14% of the time, Pallas kernels for 0%

profile of v12, /device:TPU:1, one launch (start us, length us, event | category | flops | bytes accessed | tf_op | source)
XLA Modules:
  0.0 267.7 jit_solution(5858848792983538293)
XLA Ops:
  13.9 2.7 collective-permute-done.1.b2.g2
  30.3 2.7 collective-permute-start.4
  34.0 3.6 %dynamic-slice_bitcast_fusion.3 = (bf16[256,1792]{1,0:T(8,128)(2,1)}, bf16[256,1792]{1,0:T(8,128)(2,1)}, bf16[256,1792]{1,0:T(8,128)(2,1)}) fusion(bf16[2,1,256,7168]{3,2,1,0:T(8,128)(2,1)} %down_ref.3, s32[]{:T(128)S(6)} %select_n.219, s32[]{:T(128)S(6)} %select_n.218, s32[]{:T(128)S(6)} %select_n.217), kind=kLoop, calls=%fused_computation.11 | loop fusion | bytes 5505036 | tf_op jit(solution)/shard_map/reshape | solution.py:234
  41.4 2.7 %collective-permute-start.7 = (bf16[1,24,128]{2,1,0:T(8,128)(2,1)S(1)}, bf16[1,24,128]{2,1,0:T(8,128)(2,1)S(1)}, u32[]{:S(2)}, u32[]{:S(2)}) collective-permute-start(bf16[1,24,128]{2,1,0:T(8,128)(2,1)S(1)} %bitcast.94), channel_id=1, source_target_pairs={{0,8},{4,28},{8,0},{12,20},{16,24},{20,12},{24,16},{28,4},{32,40},... | collective-permute-start | bytes 18440 | tf_op jit(solution)/shard_map/ppermute | solution.py:31
  60.3 3.6 %collective-permute-done.10 = bf16[8,24,128]{2,1,0:T(8,128)(2,1)S(1)} collective-permute-done((bf16[8,24,128]{2,1,0:T(8,128)(2,1)S(1)}, bf16[8,24,128]{2,1,0:T(8,128)(2,1)S(1)}, u32[]{:S(2)}, u32[]{:S(2)}) %collective-permute-start.10) | collective-permute-done | bytes 49184 | tf_op jit(solution)/shard_map/ppermute | solution.py:31
  64.5 4.0 %collective-permute-start.11 = (bf16[16,24,128]{2,1,0:T(8,128)(2,1)}, bf16[16,24,128]{2,1,0:T(8,128)(2,1)S(1)}, u32[]{:S(2)}, u32[]{:S(2)}) collective-permute-start(bf16[16,24,128]{2,1,0:T(8,128)(2,1)} %get-tuple-element.69), channel_id=1, source_target_pairs={{0,4},{4,0},{8,12},{12,8},{16,20},{20,16},{24,28},{28,24},{32,36},... | collective-permute-start | bytes 294920 | tf_op jit(solution)/shard_map/ppermute | solution.py:31
  74.9 4.2 %collective-permute-done.14.w3 = bf16[256,1792]{1,0:T(8,128)(2,1)S(1)} collective-permute-done((bf16[256,1792]{1,0:T(8,128)(2,1)}, bf16[256,1792]{1,0:T(8,128)(2,1)S(1)}, u32[]{:S(2)}, u32[]{:S(2)}) %collective-permute-start.14) | collective-permute-done | bytes 917536 | tf_op jit(solution)/shard_map/ppermute | solution.py:36
  79.1 4.7 %all-gather.3.cloned.1.call-done.tokens_ref = bf16[768,7168]{1,0:T(8,128)(2,1)} async-done(((bf16[24,7168]{1,0:T(8,128)(2,1)}), bf16[768,7168]{1,0:T(8,128)(2,1)}) %all-gather.3.cloned.1.call-update) | async-done | bytes 11010064 | tf_op jit(solution)/shard_map/all_gather | solution.py:249
  83.8 10.6 %shard_map.75 = bf16[384,256]{1,0:T(8,128)(2,1)} custom-call(s32[1]{0:T(128)} %bitcast.17.z_ref, bf16[768,7168]{1,0:T(8,128)(2,1)} %all-gather.3.cloned.1.call-done.tokens_ref, bf16[384,768]{1,0:T(8,128)(2,1)} %fusion.taken_ref, bf16[2,1,7168,256]{3,2,1,0:T(8,128)(2,1)} %gate_ref.3, bf16[2,1,7168,256]{3,2,1,0:T(8,128)(2,1)} %up_ref.3), custom_call_target="tpu_custom_call" | custom-call | flops 5637144576 | bytes 18743296 | tf_op jit(solution)/shard_map/pallas_call | solution.py:131
  101.0 4.7 %collective-permute-done.16.a2 = bf16[384,256]{1,0:T(8,128)(2,1)S(1)} collective-permute-done((bf16[384,256]{1,0:T(8,128)(2,1)}, bf16[384,256]{1,0:T(8,128)(2,1)S(1)}, u32[]{:S(2)}, u32[]{:S(2)}) %collective-permute-start.16) | collective-permute-done | bytes 196640 | tf_op jit(solution)/shard_map/ppermute | solution.py:36
  107.5 3.0 %shard_map.76 = bf16[384,1792]{1,0:T(8,128)(2,1)S(1)} custom-call(s32[1]{0:T(128)} %bitcast.17.z_ref, bf16[384,256]{1,0:T(8,128)(2,1)S(1)} %broadcast_select_fusion.1.a0, bf16[384,256]{1,0:T(8,128)(2,1)S(1)} %collective-permute-done.15.a1, bf16[384,256]{1,0:T(8,128)(2,1)S(1)} %collective-permute-done.16.a2, bf16[384,256]{1,0:T(8,128)(2,1)S(1)} %collective-permute-done.17.a3, ...), custom_call_target="tpu_custom_call" | custom-call | flops 1409286144 | bytes 5832704 | tf_op jit(solution)/shard_map/pallas_call | solution.py:174
  110.5 23.3 %all_to_all.10 = bf16[16,24,1792]{2,1,0:T(8,128)(2,1)S(1)} all-to-all(bf16[16,24,1792]{2,1,0:T(8,128)(2,1)S(1)} %bitcast.89), channel_id=1, replica_groups={{0,8,16,24,32,40,48,56,64,72,80,88,96,104,112,120},{4,12,20,28,36,44,52..., dimensions={0} | all-to-all | bytes 2752512 | tf_op jit(solution)/shard_map/all_to_all | solution.py:288
  134.2 3.1 %collective-permute-start.18 = (f32[24,1792]{1,0:T(8,128)S(1)}, f32[24,1792]{1,0:T(8,128)S(1)}, u32[]{:S(2)}, u32[]{:S(2)}) collective-permute-start(f32[24,1792]{1,0:T(8,128)S(1)} %slice_bitcast_fusion.2), channel_id=1, source_target_pairs={{0,4},{4,0},{8,12},{12,8},{16,20},{20,16},{24,28},{28,24},{32,36},... | collective-permute-start | bytes 516104 | tf_op jit(solution)/shard_map/ppermute | solution.py:31
  153.3 3.4 %dynamic-slice_bitcast_fusion = (bf16[256,1792]{1,0:T(8,128)(2,1)}, bf16[256,1792]{1,0:T(8,128)(2,1)}, bf16[256,1792]{1,0:T(8,128)(2,1)}) fusion(bf16[2,1,256,7168]{3,2,1,0:T(8,128)(2,1)} %down_ref.3, s32[]{:T(128)S(6)} %select_n.235, s32[]{:T(128)S(6)} %select_n.234, s32[]{:T(128)S(6)} %select_n.233), kind=kLoop, calls=%fused_computation.8 | loop fusion | bytes 5505036 | tf_op jit(solution)/shard_map/reshape | solution.py:234
  164.7 3.7 %collective-permute-start.25 = (bf16[48,384]{1,0:T(8,128)(2,1)S(1)}, bf16[48,384]{1,0:T(8,128)(2,1)S(1)}, u32[]{:S(2)}, u32[]{:S(2)}) collective-permute-start(bf16[48,384]{1,0:T(8,128)(2,1)S(1)} %pad_maximum_fusion.4), channel_id=1, source_target_pairs={{0,4},{4,0},{8,12},{12,8},{16,20},{20,16},{24,28},{28,24},{32,36},... | collective-permute-start | bytes 110600 | tf_op jit(solution)/shard_map/ppermute | solution.py:31
  169.2 6.8 %collective-permute-done.26.w1 = bf16[256,1792]{1,0:T(8,128)(2,1)S(1)} collective-permute-done((bf16[256,1792]{1,0:T(8,128)(2,1)}, bf16[256,1792]{1,0:T(8,128)(2,1)S(1)}, u32[]{:S(2)}, u32[]{:S(2)}) %collective-permute-start.26) | collective-permute-done | bytes 917536 | tf_op jit(solution)/shard_map/ppermute | solution.py:36
  176.0 2.8 %collective-permute-done.27.w2 = bf16[256,1792]{1,0:T(8,128)(2,1)S(1)} collective-permute-done((bf16[256,1792]{1,0:T(8,128)(2,1)}, bf16[256,1792]{1,0:T(8,128)(2,1)S(1)}, u32[]{:S(2)}, u32[]{:S(2)}) %collective-permute-start.27) | collective-permute-done | bytes 917536 | tf_op jit(solution)/shard_map/ppermute | solution.py:36
  178.8 17.0 %collective-permute-done.28.w3 = bf16[256,1792]{1,0:T(8,128)(2,1)S(1)} collective-permute-done((bf16[256,1792]{1,0:T(8,128)(2,1)}, bf16[256,1792]{1,0:T(8,128)(2,1)S(1)}, u32[]{:S(2)}, u32[]{:S(2)}) %collective-permute-start.28) | collective-permute-done | bytes 917536 | tf_op jit(solution)/shard_map/ppermute | solution.py:36
  195.8 10.0 %all-gather.5.cloned.1.call-done.tokens_ref = bf16[768,7168]{1,0:T(8,128)(2,1)} async-done(((bf16[24,7168]{1,0:T(8,128)(2,1)}), bf16[768,7168]{1,0:T(8,128)(2,1)}) %all-gather.5.cloned.1.call-update) | async-done | bytes 11010064 | tf_op jit(solution)/shard_map/all_gather | solution.py:249
  205.8 10.6 %shard_map.78 = bf16[384,256]{1,0:T(8,128)(2,1)} custom-call(s32[1]{0:T(128)} %bitcast.17.z_ref, bf16[768,7168]{1,0:T(8,128)(2,1)} %all-gather.5.cloned.1.call-done.tokens_ref, bf16[384,768]{1,0:T(8,128)(2,1)} %fusion.1.taken_ref, bf16[2,1,7168,256]{3,2,1,0:T(8,128)(2,1)} %gate_ref.3, bf16[2,1,7168,256]{3,2,1,0:T(8,128)(2,1)} %up_ref.3), custom_call_target="tpu_custom_call" | custom-call | flops 5637144576 | bytes 18743296 | tf_op jit(solution)/shard_map/pallas_call | solution.py:131
  223.0 4.8 %collective-permute-done.30.a2 = bf16[384,256]{1,0:T(8,128)(2,1)S(1)} collective-permute-done((bf16[384,256]{1,0:T(8,128)(2,1)}, bf16[384,256]{1,0:T(8,128)(2,1)S(1)}, u32[]{:S(2)}, u32[]{:S(2)}) %collective-permute-start.30) | collective-permute-done | bytes 196640 | tf_op jit(solution)/shard_map/ppermute | solution.py:36
  229.6 3.0 %shard_map.79 = bf16[384,1792]{1,0:T(8,128)(2,1)S(1)} custom-call(s32[1]{0:T(128)} %bitcast.17.z_ref, bf16[384,256]{1,0:T(8,128)(2,1)S(1)} %broadcast_select_fusion.a0, bf16[384,256]{1,0:T(8,128)(2,1)S(1)} %collective-permute-done.29.a1, bf16[384,256]{1,0:T(8,128)(2,1)S(1)} %collective-permute-done.30.a2, bf16[384,256]{1,0:T(8,128)(2,1)S(1)} %collective-permute-done.31.a3, ...), custom_call_target="tpu_custom_call" | custom-call | flops 1409286144 | bytes 5832704 | tf_op jit(solution)/shard_map/pallas_call | solution.py:174
  232.6 23.0 %all_to_all.11 = bf16[16,24,1792]{2,1,0:T(8,128)(2,1)S(1)} all-to-all(bf16[16,24,1792]{2,1,0:T(8,128)(2,1)S(1)} %bitcast.88), channel_id=1, replica_groups={{0,8,16,24,32,40,48,56,64,72,80,88,96,104,112,120},{4,12,20,28,36,44,52..., dimensions={0} | all-to-all | bytes 2752512 | tf_op jit(solution)/shard_map/all_to_all | solution.py:288
  256.1 3.1 %collective-permute-start.32 = (f32[24,1792]{1,0:T(8,128)S(1)}, f32[24,1792]{1,0:T(8,128)S(1)}, u32[]{:S(2)}, u32[]{:S(2)}) collective-permute-start(f32[24,1792]{1,0:T(8,128)S(1)} %slice_bitcast_fusion), channel_id=1, source_target_pairs={{0,4},{4,0},{8,12},{12,8},{16,20},{20,16},{24,28},{28,24},{32,36},... | collective-permute-start | bytes 516104 | tf_op jit(solution)/shard_map/ppermute | solution.py:31
  (189 shorter events, 92.7 us)
Async XLA Ops:
  6.5 77.3 %all-gather.3.cloned.1.call-start = ((), (), s32[]{:S(2)}) async-start(), calls=%async_computation.2 | async-start | bytes 11354112 | tf_op jit(solution)/shard_map/all_gather | solution.py:249
  10.6 6.0 %collective-permute-start.1 = (bf16[32,1792]{1,0:T(8,128)(2,1)}, bf16[32,1792]{1,0:T(8,128)(2,1)S(1)}, u32[]{:S(2)}, u32[]{:S(2)}) collective-permute-start(bf16[32,1792]{1,0:T(8,128)(2,1)} %shard_map.73.b0.g0), channel_id=1, source_target_pairs={{0,3},{1,2},{2,1},{3,0},{4,7},{5,6},{6,5},{7,4},{8,11},{9,10},{10,... | collective-permute-start | bytes 344072 | tf_op jit(solution)/shard_map/ppermute | solution.py:36
  12.8 6.2 %collective-permute-start.2 = (bf16[32,1792]{1,0:T(8,128)(2,1)}, bf16[32,1792]{1,0:T(8,128)(2,1)S(1)}, u32[]{:S(2)}, u32[]{:S(2)}) collective-permute-start(bf16[32,1792]{1,0:T(8,128)(2,1)} %shard_map.73.b0.g0), channel_id=1, source_target_pairs={{0,2},{1,3},{2,0},{3,1},{4,6},{5,7},{6,4},{7,5},{8,10},{9,11},{10,... | collective-permute-start | bytes 344072 | tf_op jit(solution)/shard_map/ppermute | solution.py:36
  22.0 183.9 %all-gather.5.cloned.1.call-start = ((), (), s32[]{:S(2)}) async-start(), calls=%async_computation.3 | async-start | bytes 11354112 | tf_op jit(solution)/shard_map/all_gather | solution.py:249
  30.2 10.2 %collective-permute-start.3 = (f32[24,32]{1,0:T(8,128)S(1)}, f32[24,32]{1,0:T(8,128)S(1)}, u32[]{:S(2)}, u32[]{:S(2)}) collective-permute-start(f32[24,32]{1,0:T(8,128)S(1)} %fusion.7), channel_id=1, source_target_pairs={{0,1},{1,0},{2,3},{3,2},{4,5},{5,4},{6,7},{7,6},{8,9},{9,8},{10,11... | collective-permute-start | bytes 9224 | tf_op jit(solution)/shard_map/ppermute | solution.py:36
  30.3 11.2 %collective-permute-start.4 = (f32[24,32]{1,0:T(8,128)S(1)}, f32[24,32]{1,0:T(8,128)S(1)}, u32[]{:S(2)}, u32[]{:S(2)}) collective-permute-start(f32[24,32]{1,0:T(8,128)S(1)} %fusion.7), channel_id=1, source_target_pairs={{0,3},{1,2},{2,1},{3,0},{4,7},{5,6},{6,5},{7,4},{8,11},{9,10},{10,... | collective-permute-start | bytes 9224 | tf_op jit(solution)/shard_map/ppermute | solution.py:36
  32.9 11.2 %collective-permute-start.5 = (f32[24,32]{1,0:T(8,128)S(1)}, f32[24,32]{1,0:T(8,128)S(1)}, u32[]{:S(2)}, u32[]{:S(2)}) collective-permute-start(f32[24,32]{1,0:T(8,128)S(1)} %fusion.7), channel_id=1, source_target_pairs={{0,2},{1,3},{2,0},{3,1},{4,6},{5,7},{6,4},{7,5},{8,10},{9,11},{10,... | collective-permute-start | bytes 9224 | tf_op jit(solution)/shard_map/ppermute | solution.py:36
  37.6 37.3 %collective-permute-start.12 = (bf16[256,1792]{1,0:T(8,128)(2,1)}, bf16[256,1792]{1,0:T(8,128)(2,1)S(1)}, u32[]{:S(2)}, u32[]{:S(2)}) collective-permute-start(bf16[256,1792]{1,0:T(8,128)(2,1)} %get-tuple-element.60), channel_id=1, source_target_pairs={{0,1},{1,0},{2,3},{3,2},{4,5},{5,4},{6,7},{7,6},{8,9},{9,8},{10,11... | collective-permute-start | bytes 2752520 | tf_op jit(solution)/shard_map/ppermute | solution.py:36
  37.6 37.3 %collective-permute-start.13 = (bf16[256,1792]{1,0:T(8,128)(2,1)}, bf16[256,1792]{1,0:T(8,128)(2,1)S(1)}, u32[]{:S(2)}, u32[]{:S(2)}) collective-permute-start(bf16[256,1792]{1,0:T(8,128)(2,1)} %get-tuple-element.59), channel_id=1, source_target_pairs={{0,3},{1,2},{2,1},{3,0},{4,7},{5,6},{6,5},{7,4},{8,11},{9,10},{10,... | collective-permute-start | bytes 2752520 | tf_op jit(solution)/shard_map/ppermute | solution.py:36
  40.3 38.8 %collective-permute-start.14 = (bf16[256,1792]{1,0:T(8,128)(2,1)}, bf16[256,1792]{1,0:T(8,128)(2,1)S(1)}, u32[]{:S(2)}, u32[]{:S(2)}) collective-permute-start(bf16[256,1792]{1,0:T(8,128)(2,1)} %get-tuple-element.58), channel_id=1, source_target_pairs={{0,2},{1,3},{2,0},{3,1},{4,6},{5,7},{6,4},{7,5},{8,10},{9,11},{10,... | collective-permute-start | bytes 2752520 | tf_op jit(solution)/shard_map/ppermute | solution.py:36
  41.4 10.7 %collective-permute-start.7 = (bf16[1,24,128]{2,1,0:T(8,128)(2,1)S(1)}, bf16[1,24,128]{2,1,0:T(8,128)(2,1)S(1)}, u32[]{:S(2)}, u32[]{:S(2)}) collective-permute-start(bf16[1,24,128]{2,1,0:T(8,128)(2,1)S(1)} %bitcast.94), channel_id=1, source_target_pairs={{0,8},{4,28},{8,0},{12,20},{16,24},{20,12},{24,16},{28,4},{32,40},... | collective-permute-start | bytes 18440 | tf_op jit(solution)/shard_map/ppermute | solution.py:31
  50.6 18.0 %collective-permute-start.6 = (bf16[48,384]{1,0:T(8,128)(2,1)S(1)}, bf16[48,384]{1,0:T(8,128)(2,1)S(1)}, u32[]{:S(2)}, u32[]{:S(2)}) collective-permute-start(bf16[48,384]{1,0:T(8,128)(2,1)S(1)} %pad_maximum_fusion.3), channel_id=1, source_target_pairs={{0,4},{4,0},{8,12},{12,8},{16,20},{20,16},{24,28},{28,24},{32,36},... | collective-permute-start | bytes 110600 | tf_op jit(solution)/shard_map/ppermute | solution.py:31
  94.4 6.5 %collective-permute-start.15 = (bf16[384,256]{1,0:T(8,128)(2,1)}, bf16[384,256]{1,0:T(8,128)(2,1)S(1)}, u32[]{:S(2)}, u32[]{:S(2)}) collective-permute-start(bf16[384,256]{1,0:T(8,128)(2,1)} %shard_map.75), channel_id=1, source_target_pairs={{0,1},{1,0},{2,3},{3,2},{4,5},{5,4},{6,7},{7,6},{8,9},{9,8},{10,11... | collective-permute-start | bytes 589832 | tf_op jit(solution)/shard_map/ppermute | solution.py:36
  95.6 10.0 %collective-permute-start.16 = (bf16[384,256]{1,0:T(8,128)(2,1)}, bf16[384,256]{1,0:T(8,128)(2,1)S(1)}, u32[]{:S(2)}, u32[]{:S(2)}) collective-permute-start(bf16[384,256]{1,0:T(8,128)(2,1)} %shard_map.75), channel_id=1, source_target_pairs={{0,3},{1,2},{2,1},{3,0},{4,7},{5,6},{6,5},{7,4},{8,11},{9,10},{10,... | collective-permute-start | bytes 589832 | tf_op jit(solution)/shard_map/ppermute | solution.py:36
  97.5 9.9 %collective-permute-start.17 = (bf16[384,256]{1,0:T(8,128)(2,1)}, bf16[384,256]{1,0:T(8,128)(2,1)S(1)}, u32[]{:S(2)}, u32[]{:S(2)}) collective-permute-start(bf16[384,256]{1,0:T(8,128)(2,1)} %shard_map.75), channel_id=1, source_target_pairs={{0,2},{1,3},{2,0},{3,1},{4,6},{5,7},{6,4},{7,5},{8,10},{9,11},{10,... | collective-permute-start | bytes 589832 | tf_op jit(solution)/shard_map/ppermute | solution.py:36
  150.0 8.7 %collective-permute-start.22 = (f32[24,32]{1,0:T(8,128)S(1)}, f32[24,32]{1,0:T(8,128)S(1)}, u32[]{:S(2)}, u32[]{:S(2)}) collective-permute-start(f32[24,32]{1,0:T(8,128)S(1)} %fusion.5), channel_id=1, source_target_pairs={{0,1},{1,0},{2,3},{3,2},{4,5},{5,4},{6,7},{7,6},{8,9},{9,8},{10,11... | collective-permute-start | bytes 9224 | tf_op jit(solution)/shard_map/ppermute | solution.py:36
  150.8 9.2 %collective-permute-start.23 = (f32[24,32]{1,0:T(8,128)S(1)}, f32[24,32]{1,0:T(8,128)S(1)}, u32[]{:S(2)}, u32[]{:S(2)}) collective-permute-start(f32[24,32]{1,0:T(8,128)S(1)} %fusion.5), channel_id=1, source_target_pairs={{0,3},{1,2},{2,1},{3,0},{4,7},{5,6},{6,5},{7,4},{8,11},{9,10},{10,... | collective-permute-start | bytes 9224 | tf_op jit(solution)/shard_map/ppermute | solution.py:36
  152.0 8.1 %collective-permute-start.24 = (f32[24,32]{1,0:T(8,128)S(1)}, f32[24,32]{1,0:T(8,128)S(1)}, u32[]{:S(2)}, u32[]{:S(2)}) collective-permute-start(f32[24,32]{1,0:T(8,128)S(1)} %fusion.5), channel_id=1, source_target_pairs={{0,2},{1,3},{2,0},{3,1},{4,6},{5,7},{6,4},{7,5},{8,10},{9,11},{10,... | collective-permute-start | bytes 9224 | tf_op jit(solution)/shard_map/ppermute | solution.py:36
  156.8 19.3 %collective-permute-start.26 = (bf16[256,1792]{1,0:T(8,128)(2,1)}, bf16[256,1792]{1,0:T(8,128)(2,1)S(1)}, u32[]{:S(2)}, u32[]{:S(2)}) collective-permute-start(bf16[256,1792]{1,0:T(8,128)(2,1)} %get-tuple-element.57), channel_id=1, source_target_pairs={{0,1},{1,0},{2,3},{3,2},{4,5},{5,4},{6,7},{7,6},{8,9},{9,8},{10,11... | collective-permute-start | bytes 2752520 | tf_op jit(solution)/shard_map/ppermute | solution.py:36
  157.5 21.3 %collective-permute-start.27 = (bf16[256,1792]{1,0:T(8,128)(2,1)}, bf16[256,1792]{1,0:T(8,128)(2,1)S(1)}, u32[]{:S(2)}, u32[]{:S(2)}) collective-permute-start(bf16[256,1792]{1,0:T(8,128)(2,1)} %get-tuple-element.56), channel_id=1, source_target_pairs={{0,3},{1,2},{2,1},{3,0},{4,7},{5,6},{6,5},{7,4},{8,11},{9,10},{10,... | collective-permute-start | bytes 2752520 | tf_op jit(solution)/shard_map/ppermute | solution.py:36
  158.7 37.2 %collective-permute-start.28 = (bf16[256,1792]{1,0:T(8,128)(2,1)}, bf16[256,1792]{1,0:T(8,128)(2,1)S(1)}, u32[]{:S(2)}, u32[]{:S(2)}) collective-permute-start(bf16[256,1792]{1,0:T(8,128)(2,1)} %get-tuple-element.55), channel_id=1, source_target_pairs={{0,2},{1,3},{2,0},{3,1},{4,6},{5,7},{6,4},{7,5},{8,10},{9,11},{10,... | collective-permute-start | bytes 2752520 | tf_op jit(solution)/shard_map/ppermute | solution.py:36
  216.4 6.5 %collective-permute-start.29 = (bf16[384,256]{1,0:T(8,128)(2,1)}, bf16[384,256]{1,0:T(8,128)(2,1)S(1)}, u32[]{:S(2)}, u32[]{:S(2)}) collective-permute-start(bf16[384,256]{1,0:T(8,128)(2,1)} %shard_map.78), channel_id=1, source_target_pairs={{0,1},{1,0},{2,3},{3,2},{4,5},{5,4},{6,7},{7,6},{8,9},{9,8},{10,11... | collective-permute-start | bytes 589832 | tf_op jit(solution)/shard_map/ppermute | solution.py:36
  217.8 10.0 %collective-permute-start.30 = (bf16[384,256]{1,0:T(8,128)(2,1)}, bf16[384,256]{1,0:T(8,128)(2,1)S(1)}, u32[]{:S(2)}, u32[]{:S(2)}) collective-permute-start(bf16[384,256]{1,0:T(8,128)(2,1)} %shard_map.78), channel_id=1, source_target_pairs={{0,3},{1,2},{2,1},{3,0},{4,7},{5,6},{6,5},{7,4},{8,11},{9,10},{10,... | collective-permute-start | bytes 589832 | tf_op jit(solution)/shard_map/ppermute | solution.py:36
  219.7 9.9 %collective-permute-start.31 = (bf16[384,256]{1,0:T(8,128)(2,1)}, bf16[384,256]{1,0:T(8,128)(2,1)S(1)}, u32[]{:S(2)}, u32[]{:S(2)}) collective-permute-start(bf16[384,256]{1,0:T(8,128)(2,1)} %shard_map.78), channel_id=1, source_target_pairs={{0,2},{1,3},{2,0},{3,1},{4,6},{5,7},{6,4},{7,5},{8,10},{9,11},{10,... | collective-permute-start | bytes 589832 | tf_op jit(solution)/shard_map/ppermute | solution.py:36
  (31 other events, 198.1 us)
Sparse Core Ops, SparseCore 0:
  22.1 61.6 all-gather.2
  148.0 57.7 all-gather.4
